TPU v7x, 32 devices: a whole 2x2x4 slice. The times are simulated.
32 devices in a mesh: gx: 8 (over z, y), gy: 4 (over x, core).
Axes of the slice: x: 2, y: 2, z: 4, core: 2. Of those that a mesh axis runs over, the one named last changes fastest.
Arguments:
- intensity: float32 [512, 512, 512], P('gx', 'gy'), may hold values from -48 to 48
- template: int32 [32, 32, 32], replicated, may hold values from 0 to 1, as said below
Outputs:
- pdf: float32 [512, 512, 512], P('gx', 'gy')
Inputs may be any that keep to these rules, and one draw needn't show every extreme that they name: template marks the cells of the period near its corner, within a drawn radius, and a few other cells.
All inputs are finite; a program needn't handle non-finite values.
Results may differ from a plain program's by a relative error of at most 0.0003.
Values sent between devices are 32-bit elements; how exact they have to be, the bound alone decides.
No kernel may reach another device: no remote copies, remote signals or barrier semaphores. Data moves between devices by JAX's collectives and lax.ppermute only.
A program may use at most 192 MiB of HBM per device.

v0:
```python
import math

import jax
import jax.numpy as jnp
from jax import lax
from jax.experimental import pallas as pl
from jax.experimental.pallas import tpu as pltpu
from jax.sharding import PartitionSpec as P

SWEEPS = 2

AXIS_ORDERS = ((0, 1, 2), (0, 2, 1), (1, 0, 2), (1, 2, 0), (2, 0, 1), (2, 1, 0))

HIGH = lax.Precision.HIGH


def ring(axis):
    peers = lax.axis_size(axis)
    up = [(i, (i + 1) % peers) for i in range(peers)]
    return up, [(j, i) for i, j in up]


def halos(block):
    rows, cols, _ = block.shape
    up, down = ring("gx")
    right, left = ring("gy")
    top = lax.ppermute(block[rows - SWEEPS :], "gx", up)
    bottom = lax.ppermute(block[:SWEEPS], "gx", down)
    before = lax.ppermute(block[:, cols - SWEEPS :], "gy", right)
    after = lax.ppermute(block[:, :SWEEPS], "gy", left)
    sides = jnp.concatenate([before, after], axis=1)
    above = lax.ppermute(sides[rows - SWEEPS :], "gx", up)
    below = lax.ppermute(sides[:SWEEPS], "gx", down)
    free = (8 - SWEEPS, 8 - SWEEPS), (0, 0)
    inner = jnp.pad(sides, ((SWEEPS, SWEEPS),) + free)
    sides = jnp.pad(jnp.concatenate([above, sides, below], axis=0), ((0, 0),) + free)
    return (block[:SWEEPS], block[:SWEEPS], inner), (top, bottom, sides)


def mirror(values, axis):
    return jnp.roll(jnp.flip(values, axis), 1, axis)


def symmetric_marks(marks):
    for flip_axis in range(3):
        marks = jnp.maximum(marks, mirror(marks, flip_axis))
    united = marks
    for axis_order in AXIS_ORDERS[1:]:
        united = jnp.maximum(united, jnp.transpose(marks, axis_order))
    return united


def cosine_table(length):
    position = jnp.arange(length, dtype=jnp.int32)
    phases = jnp.mod(position[:, None] * position[None, : length // 2 + 1], length)
    return jnp.cos(phases.astype(jnp.float32) * (2.0 * math.pi / length)) / math.sqrt(length)


MARGIN = 16
CHUNK = 16
STEP_ROWS = 16
PART_STEP = 8
VMEM_BYTES = 56 * 1024 * 1024


def split(values):
    high = values.astype(jnp.bfloat16)
    low = (values - high.astype(jnp.float32)).astype(jnp.bfloat16)
    return high, low


def fill_block(step, base, steps):
    return jnp.where(step < steps, base[0] + step, base[1] + step - steps)


def fill_kernel(
    base, here, above, below, top, bottom, sides, marks, table_high, table_low,
    given, kept, alternate, edge, punched, once, high, low, folded,
):
    step_rows, cols, length = here.shape
    step = fill_block(pl.program_id(0), base, pl.num_programs(0) // 2)
    is_given = pl.program_id(0) < pl.num_programs(0) // 2
    first_row = step * step_rows
    local_row = pl.program_id(0) * step_rows
    period = marks.shape[0]
    lane = lax.broadcasted_iota(jnp.int32, (128, 128), 1)
    signs = jnp.where(lax.broadcasted_iota(jnp.int32, (128, 128), 0) % 2 == 0, 1.0, -1.0)

    @pl.when(pl.program_id(0) == 0)
    def _():
        edge[...] = jnp.zeros_like(edge)

    def holes(row, start, size):
        row = lax.rem(first_row + row, period)
        start = start % period
        if start + size <= period:
            part = marks[row, pl.ds(start, size), :]
        else:
            part = jnp.concatenate(
                [marks[row, pl.ds(start, period - start), :], marks[row, pl.ds(0, start + size - period), :]],
                axis=0,
            )
        return jnp.concatenate([part] * (length // 128), axis=1)

    def punch(row, start, values):
        kept = jnp.where(holes(row, start, values.shape[0]) > 0.0, 0.0, values)
        punched[row, pl.ds(start, values.shape[0]), :] = kept

    def punch_row(row, source, index):
        full = first_row + row
        punch(row, MARGIN - 8, sides[full, pl.ds(0, 8), :])
        punch(row, MARGIN + cols, sides[full, pl.ds(8, 8), :])
        for c in range(0, cols, CHUNK):
            punch(row, MARGIN + c, source[index, pl.ds(c, CHUNK), :])

    def neighbours(ref, row, start):
        middle = ref[row, pl.ds(start, CHUNK), :]
        total = ref[row - 1, pl.ds(start, CHUNK), :] + ref[row + 1, pl.ds(start, CHUNK), :]
        total += ref[row, pl.ds(start - 1, CHUNK), :] + ref[row, pl.ds(start + 1, CHUNK), :]
        return total + pltpu.roll(middle, 1, 1) + pltpu.roll(middle, length - 1, 1)

    last = (sides.shape[0] - 2 * SWEEPS) // step_rows - 1
    for edge_rows, inside, offset, outer in (
        (above, step > 0, 0, top),
        (below, step < last, step_rows + SWEEPS, bottom),
    ):
        @pl.when(inside)
        def _():
            for r in range(SWEEPS):
                punch_row(offset + r, edge_rows, r)

        @pl.when(jnp.logical_not(inside))
        def _():
            for r in range(SWEEPS):
                punch_row(offset + r, outer, r)

    @pl.loop(0, step_rows)
    def _(r):
        punch_row(r + SWEEPS, here, r)

    @pl.loop(1, step_rows + 2 * SWEEPS - 1, unroll=2)
    def _(r):
        for start in range(MARGIN - 8, MARGIN + cols + 8, CHUNK):
            total = neighbours(punched, r, start) * holes(r, start, CHUNK)
            once[r, pl.ds(start, CHUNK), :] = punched[r, pl.ds(start, CHUNK), :] + total

    @pl.loop(0, step_rows)
    def _(r):
        for c in range(0, cols, CHUNK):
            start = MARGIN + c
            total = neighbours(once, r + SWEEPS, start) * holes(r + SWEEPS, start, CHUNK)
            filled = punched[r + SWEEPS, pl.ds(start, CHUNK), :] + total
            first, second = split(filled)
            spot = pl.ds(pl.multiple_of(r * cols + c, CHUNK), CHUNK)
            high[spot, :] = first
            low[spot, :] = second
            wrapped = filled[:, :128]
            for tile in range(1, length // 128):
                wrapped += filled[:, tile * 128 : (tile + 1) * 128]
            folded[pl.ds(c, CHUNK), :] = wrapped
        column = jnp.where(lane == local_row + r, signs, 0.0).astype(jnp.bfloat16)
        first, second = split(folded[...])
        total = jnp.dot(first, column, preferred_element_type=jnp.float32)
        total += jnp.dot(second, column, preferred_element_type=jnp.float32)
        edge[...] += total

    rows_each = 8
    half = given.shape[2]
    order = lax.broadcasted_iota(jnp.int32, (rows_each, cols, half), 1)

    @pl.loop(0, step_rows // rows_each)
    def _(r):
        spot = pl.ds(pl.multiple_of(r * rows_each * cols, CHUNK), rows_each * cols)
        first, second = high[spot, :], low[spot, :]
        total = jnp.dot(first, table_low[...], preferred_element_type=jnp.float32)
        total += jnp.dot(second, table_high[...], preferred_element_type=jnp.float32)
        total += jnp.dot(first, table_high[...], preferred_element_type=jnp.float32)
        total = total.reshape(rows_each, cols, half)

        @pl.when(is_given)
        def _():
            given[pl.ds(r * rows_each, rows_each)] = total

        @pl.when(jnp.logical_not(is_given))
        def _():
            kept[pl.ds(r * rows_each, rows_each)] = total

        signed = jnp.sum(jnp.where(order % 2 == 0, total, -total), axis=1)
        alternate[pl.ds(pl.multiple_of(r * rows_each, rows_each), rows_each), :] = signed


def rounded_parts(table):
    rounded = lax.reduce_precision(table, 8, 7)
    return rounded.astype(jnp.bfloat16), (table - rounded).astype(jnp.bfloat16)


def fill_arrays(intensity, template, row, col, main):
    rows, cols, length = intensity.shape
    united = symmetric_marks(template)
    period = united.shape[0]
    offsets = (jnp.mod(row * rows - SWEEPS, period), jnp.mod(col * cols - MARGIN, period))
    marks = jnp.roll(united, (-offsets[0], -offsets[1]), (0, 1)).astype(jnp.float32) / 6.0
    marks = jnp.tile(marks, (1, 1, 128 // period))
    constants = (marks,) + rounded_parts(main)
    inner, outer = halos(intensity)
    return inner + constants, outer + constants


def filled_spectrum(intensity, arrays, starts, count):
    rows, cols, length = intensity.shape
    half = length // 2
    step_rows = min(STEP_ROWS, count)
    steps = count // step_rows
    pairs = step_rows // SWEEPS
    last = rows // SWEEPS - 1
    whole = lambda array: pl.BlockSpec(array.shape, lambda i, b: (0,) * array.ndim)
    here = lambda i, b: (fill_block(i, b, steps), 0, 0)
    before = lambda i, b: (jnp.maximum(fill_block(i, b, steps) * pairs - 1, 0), 0, 0)
    after = lambda i, b: (jnp.minimum((fill_block(i, b, steps) + 1) * pairs, last), 0, 0)
    padded = (step_rows + 2 * SWEEPS, cols + 2 * MARGIN, length)
    out_block = (step_rows, cols, half)
    out = jax.ShapeDtypeStruct((count, cols, half), jnp.float32)
    return pl.pallas_call(
        fill_kernel,
        grid_spec=pltpu.PrefetchScalarGridSpec(
            num_scalar_prefetch=1,
            grid=(2 * steps,),
            in_specs=[
                pl.BlockSpec((step_rows, cols, length), here),
                pl.BlockSpec((SWEEPS, cols, length), before),
                pl.BlockSpec((SWEEPS, cols, length), after),
            ] + [whole(array) for array in arrays],
            out_specs=[
                pl.BlockSpec(out_block, lambda i, b: (jnp.minimum(i, steps - 1), 0, 0)),
                pl.BlockSpec(out_block, lambda i, b: (jnp.maximum(i - steps, 0), 0, 0)),
                pl.BlockSpec((step_rows, half), lambda i, b: (i, 0)),
                pl.BlockSpec((cols, 128), lambda i, b: (0, 0)),
            ],
            scratch_shapes=[
                pltpu.VMEM(padded, jnp.float32),
                pltpu.VMEM(padded, jnp.float32),
                pltpu.VMEM((step_rows * cols, length), jnp.bfloat16),
                pltpu.VMEM((step_rows * cols, length), jnp.bfloat16),
                pltpu.VMEM((cols, 128), jnp.float32),
            ],
        ),
        out_shape=[
            out,
            out,
            jax.ShapeDtypeStruct((2 * count, half), jnp.float32),
            jax.ShapeDtypeStruct((cols, 128), jnp.float32),
        ],
        compiler_params=pltpu.CompilerParams(vmem_limit_bytes=VMEM_BYTES),
        cost_estimate=pl.CostEstimate(
            flops=count * cols * length * half * 12,
            bytes_accessed=count * cols * (length + half) * 8,
            transcendentals=0,
        ),
    )(jnp.stack(starts) // step_rows, intensity, intensity, intensity, *arrays)


def pack(section, offsets):
    block = offsets[1]
    units = [section[b * block : (b + 1) * block, : (b + 1) * block] for b in range(len(offsets) - 1)]
    return jnp.concatenate(units, axis=1)


def three_dots(left, right):
    total = jnp.dot(left[1], right[0], preferred_element_type=jnp.float32)
    total += jnp.dot(left[0], right[1], preferred_element_type=jnp.float32)
    return total + jnp.dot(left[0], right[0], preferred_element_type=jnp.float32)


def section_kernel(
    offsets, closing, me, weights, kept, got, cols_high, cols_low, rows_high, rows_low,
    rim, corner, before, *refs
):
    step, steps = pl.program_id(0), pl.num_programs(0)
    step_rows = kept.shape[0]
    half, count = rows_high.shape
    planes, block, width = before.shape
    *outs, total, lines, packed = refs
    gy, (_, own, gx, _) = len(outs), outs[0].shape

    def place(layer, values, slot=0):
        packed[slot] = values
        for e in range(own):
            for p in range(gy):
                start = pl.multiple_of((e * gy + (p ^ me[0])) * gx, gx)
                outs[p][layer, e] = packed[slot, pl.ds(start, gx), :]

    @pl.when(step == 0)
    def _():
        total[...] = before[...]

    for r in range(step_rows):
        layer = step * step_rows + r
        values = jnp.concatenate([kept[r], got[r]], axis=0)
        section = three_dots((cols_high[...], cols_low[...]), split(values))
        section = section + section.T
        line = pack(section, offsets)
        place(layer, line, r)
        for m in range(planes):
            total[m] += weights[m, layer] * line
        for m in range(planes - 1):
            row = (m + 1) * (half // planes)
            lines[m, pl.ds(layer, 1), :] = section[row : row + 1]

    @pl.when(step == steps - 1)
    def _():
        for m in range(planes - 1):
            plane = three_dots((rows_high[...], rows_low[...]), split(lines[m]))
            total[m] += pack(plane + plane.T, offsets)
        if closing:
            total[planes - 1] += pack(rim[...] + rim[...].T, offsets)
            for m in range(planes):
                place(count + m, total[m])
            place(count + planes, jnp.zeros((block, width), jnp.float32) + corner[...])


def packed_section(col, kept, got, table_pair, table_rows, marks, rim, corner, before, offsets, shape, closing):
    count, cols, half = kept.shape
    planes, block, width = before.shape
    gx, gy = shape
    step_rows = 4
    layers = count + (planes + 1 if closing else 0)
    whole = lambda array: pl.BlockSpec(array.shape, lambda i: (0,) * array.ndim)
    weights = jnp.stack([table_rows[:, m] for m in marks])
    arrays = rounded_parts(table_pair.T) + rounded_parts(table_rows[:, :half].T)
    arrays += (rim, corner[None], before)
    out = jax.ShapeDtypeStruct((layers, block // (gx * gy), gx, width), jnp.float32)
    outs = [out] * gy + [jax.ShapeDtypeStruct(before.shape, jnp.float32)]
    rows_spec = pl.BlockSpec((step_rows, cols, half), lambda i: (i, 0, 0))
    return pl.pallas_call(
        lambda *refs: section_kernel(offsets, closing, *refs),
        grid=(count // step_rows,),
        in_specs=[pl.BlockSpec(memory_space=pltpu.SMEM)] * 2 + [rows_spec, rows_spec]
        + [whole(array) for array in arrays],
        out_specs=[whole(out) for out in outs],
        out_shape=outs,
        scratch_shapes=[
            pltpu.VMEM((planes, count, half), jnp.float32),
            pltpu.VMEM((step_rows, block, width), jnp.float32),
        ],
        compiler_params=pltpu.CompilerParams(vmem_limit_bytes=VMEM_BYTES),
        cost_estimate=pl.CostEstimate(
            flops=count * 12 * cols * half * half,
            bytes_accessed=count * cols * half * 16,
            transcendentals=0,
        ),
    )(col.reshape(1), weights, kept, got, *arrays)


def on_device(intensity, template):
    rows, cols, length = intensity.shape
    gx, gy = lax.axis_size("gx"), lax.axis_size("gy")
    row, col = lax.axis_index("gx"), lax.axis_index("gy")
    devices, half = gx * gy, length // 2
    block = max(devices, rows)
    blocks, own, slabs = half // block, block // devices, gx // 2
    offsets = [block * b * (b + 1) // 2 for b in range(blocks + 1)]
    width = offsets[blocks]
    table = cosine_table(length)
    main = table[:, :half]

    pair_rows = rows // 2
    parts = row_parts(pair_rows)
    counts = [part.stop - part.start for part in parts]
    core = lax.rem(col, 2)
    inner_arrays, arrays = fill_arrays(intensity, template, row, col, main)
    given_first, kept_first = (1 - core) * pair_rows, core * pair_rows
    pieces = []

    def fill_part(c, after):
        starts = given_first + parts[c].start, kept_first + parts[c].start
        if after is not None:
            starts, after = lax.optimization_barrier((starts, after))
        inner = parts[c].start >= SWEEPS and parts[c].stop <= pair_rows - SWEEPS
        pieces.append(
            filled_spectrum(intensity, inner_arrays if inner else arrays, starts, counts[c])
        )
        return lax.ppermute(pieces[c][0], "gy", swap(gy, 1)), after

    table_cols = lax.dynamic_slice_in_dim(table, col * cols, cols, 0)
    kept_rows = lax.dynamic_slice_in_dim(table, row * rows + kept_first, pair_rows, 0)
    marks = [rows * (m + 1) for m in range(slabs)]
    mates = lax.dynamic_slice_in_dim(main, (col + 1 - 2 * core) * cols, cols, 0)
    table_pair = jnp.concatenate([table_cols[:, :half], mates], axis=0)
    table_parts = main.reshape(gx, 2, pair_rows, half) / 6.0
    table_parts = jnp.where(core == 0, table_parts, table_parts[:, ::-1])
    table_parts = [table_parts[:, :, part] for part in parts]
    side = jnp.zeros((slabs, block, width), jnp.float32)
    rim, corner = jnp.zeros((half, half), jnp.float32), jnp.zeros((width,), jnp.float32)
    values, packed, lines = 0.0, None, None
    for c, count in enumerate(counts):
        closing = c == len(counts) - 1
        got, packed = fill_part(c, packed)
        held = pieces[c][1]
        if c > 0:
            held, got_lines = lax.optimization_barrier((held, exchanged(packed)))
            lines = sent_lines(got_lines, counts[c - 1], lines)
            values = values + first_axis(lines, table_parts[c - 1])
        if closing:
            given_rows = lax.dynamic_slice_in_dim(table, row * rows + given_first, pair_rows, 0)
            ordered_rows = [held_rows[part] for part in parts for held_rows in (given_rows, kept_rows)]
            ordered_rows = jnp.concatenate(ordered_rows, axis=0)
            alternate = jnp.concatenate([piece[2] for piece in pieces], axis=0) / math.sqrt(length)
            edge = [piece[3][:, : piece[2].shape[0]] for piece in pieces]
            edge = jnp.concatenate(edge, axis=1)
            edge = jnp.einsum("ba,bk->ak", edge / math.sqrt(length), table_cols, precision=HIGH)
            edge = edge + jnp.concatenate([alternate, edge[:, half:]], axis=1)
            rim = jnp.einsum("aj,ak->jk", ordered_rows[:, :half], edge[:, :half], precision=HIGH)
            corner = 2.0 * jnp.einsum("a,ak->k", ordered_rows[:, half], edge, precision=HIGH)
            corner = corner + jnp.einsum("aj,a->j", ordered_rows, edge[:, half], precision=HIGH)
            corner = jnp.pad(corner, (0, width - half - 1))

        *packed, side = packed_section(
            col, held, got, table_pair, kept_rows[parts[c]], marks,
            rim, corner, side, offsets, (gx, gy), closing,
        )
    lines = sent_lines(exchanged(packed), counts[-1], lines)
    values = values + first_axis(lines, table_parts[-1])
    side = jnp.sum(lines[:, :, 2 * counts[-1] :], axis=0) / 6.0
    turned = values.reshape(own, blocks, own, devices, width)
    turned = jnp.transpose(turned, (3, 1, 2, 0, 4))
    turned = [turned[:, b, :, :, : offsets[b + 1]] for b in range(blocks)]
    turned = lax.all_to_all(jnp.concatenate(turned, axis=3), ("gy", "gx"), 0, 0, tiled=True)
    turned = jnp.transpose(turned, (1, 2, 0, 3)).reshape(own, block, -1)

    slab = jnp.minimum(row, gx - 1 - row)
    far_row, far_col = row >= slabs, col >= gy // 2
    pick_rows = jnp.arange(rows)
    pick_rows = slab * rows + jnp.where(far_row, rows - pick_rows, pick_rows)
    pick_cols = jnp.arange(cols)
    pick_cols = jnp.where(far_col, (gy - col) * cols - pick_cols, col * cols + pick_cols)

    if rows == block:
        got, piece = [], None
        for messages in slab_messages(values, turned, side, offsets, slabs):
            if piece is not None:
                messages, piece = lax.optimization_barrier((messages, piece))
                got.append(gathered(piece, gy, got[-1] if got else None))
            piece = lax.all_to_all(messages, "gx", 0, 0, tiled=True)
        got.append(gathered(piece, gy, got[-1] if got else None))
        tiles = width // 128
        start = tile_groups(tiles)[0].stop * own * block
        side = jnp.stack([piece[:, start : start + 3 * own * tiles] for piece in got[0]])
        bit = gy // 2
        while bit:
            paired = side.reshape((-1, 2, bit) + side.shape[1:])
            side = jnp.where((col & bit) == 0, paired, paired[:, ::-1]).reshape(side.shape)
            bit //= 2
        side = side.reshape(devices, own, 3, width)
        side = jnp.transpose(side, (2, 1, 0, 3)).reshape(3, block, width)
        next_plane, across = side[0], rim_rows(side[1:], offsets, pick_rows)
        rim_col = col == gy // 2
        rim = across[:, pick_cols]
        return result_block(
            got, next_plane, across, rim, pick_cols, slab, far_row, rim_col, col, offsets
        )

    side = lax.all_gather(side, ("gy", "gx"), axis=0)
    side = jnp.transpose(side, (2, 1, 0, 3)).reshape(slabs + 1, block, width)
    across = rim_rows(side[slabs - 1 :], offsets, pick_rows)
    next_plane = lax.dynamic_index_in_dim(side, slab, 0, keepdims=False)
    sums = axis_order_sums(values, turned, offsets, block)
    messages = []
    for s in range(slabs):
        base, first = s * rows // block, s * rows
        units = []
        for b in range(blocks):
            size = (b + 1) * block
            near = jnp.zeros((own, rows, size))
            far = jnp.zeros((own, block, size))
            if b >= base:
                near = jnp.stack([sums[b][e][first : first + rows, :size] for e in range(own)])
            else:
                far = jnp.stack([sums[base][e][b * block : size, :size] for e in range(own)])
            units.append(jnp.concatenate([near, far], axis=1))
        messages.append(jnp.concatenate(units, axis=2))
    messages = jnp.stack(messages + messages[::-1])
    got = lax.all_to_all(messages, "gx", 0, 0, tiled=True)
    got = lax.all_gather(got, "gy", axis=0, tiled=True)
    got = jnp.swapaxes(got, 0, 1).reshape(block, rows + block, width)
    base = slab * rows // block
    lower = []
    for b in range(blocks):
        lanes = slice(offsets[b], offsets[b + 1])
        near = jnp.swapaxes(got[:, :rows, lanes], 0, 1)
        far = lax.dynamic_slice_in_dim(got[:, rows:, lanes], lax.rem(slab * rows, block), rows, 0)
        lower.append(jnp.where(b >= base, near, far))
    lower = jnp.concatenate(lower, axis=2)
    lower = jnp.concatenate([lower, next_plane[None]], axis=0)
    body = square([lower[:, :, offsets[b] : offsets[b + 1]] for b in range(blocks)], block)
    body = body[pick_rows - slab * rows]
    body = jnp.concatenate([body, across[:, None, :half]], axis=1)[:, pick_cols]
    body = jnp.concatenate([body, across[:, pick_cols][:, :, None]], axis=2)
    return jnp.concatenate([body, jnp.flip(body[:, :, 1:half], 2)], axis=2)


def rim_rows(side, offsets, pick_rows):
    blocks, block = len(offsets) - 1, offsets[1]
    half = blocks * block
    last = square([side[0][:, offsets[b] : offsets[b + 1]] for b in range(blocks)], block)
    rim = side[1, 0, : half + 1]
    last = jnp.concatenate([last, rim[None, :half]], axis=0)
    return jnp.concatenate([last, rim[:, None]], axis=1)[pick_rows]


def axis_order_sums(values, turned, offsets, block):
    start = 0
    sums = []
    for top in range(len(offsets) - 1):
        size = (top + 1) * block
        parts = []
        for e in range(values.shape[0]):
            part = values[e, :size, offsets[top] : offsets[top] + size]
            lower = [turned[e, :, start + offsets[b] : start + offsets[b + 1]] for b in range(top + 1)]
            parts.append(part + part.T + square(lower, block))
        sums.append(parts)
        start += offsets[top + 1]
    return sums


def message_kernel(offsets, slabs, values, turned, side, *messages):
    blocks, block = len(offsets) - 1, offsets[1]
    values, turned = values[...], turned[...]
    own = values.shape[0]
    sums = axis_order_sums(values, turned, offsets, block)
    groups = tile_groups(offsets[-1] // 128)
    side_start = groups[0].stop * own * block
    messages[0][:, side_start:] = jnp.zeros_like(messages[0][:, side_start:])
    for s in range(slabs):
        places = s, 2 * slabs - 1 - s
        for e in range(own):
            units = []
            for b in range(blocks):
                size = (b + 1) * block
                if b >= s:
                    units.append(sums[b][e][s * block : (s + 1) * block, :size])
                else:
                    units.append(sums[s][e][b * block : size, :size])
            line = jnp.concatenate(units, axis=1)
            for group, out in zip(groups, messages):
                for tile in range(group.start, group.stop):
                    start = ((tile - group.start) * own + e) * block
                    for place in places:
                        out[place, start : start + block] = line[:, tile * 128 : (tile + 1) * 128]
            row = side_start + 3 * e * groups[-1].stop
            for plane in (s, slabs - 1, slabs):
                for tile in range(groups[-1].stop):
                    part = side[e, plane : plane + 1, tile * 128 : (tile + 1) * 128]
                    for place in places:
                        messages[0][place, row : row + 1] = part
                    row += 1


def slab_messages(values, turned, side, offsets, slabs):
    own, block, tiles = values.shape[0], offsets[1], offsets[-1] // 128
    sizes = [(group.stop - group.start) * own * block for group in tile_groups(tiles)]
    sizes[0] += -(-3 * own * tiles // 8) * 8
    return pl.pallas_call(
        lambda *refs: message_kernel(offsets, slabs, *refs),
        in_specs=[pl.BlockSpec(memory_space=pltpu.VMEM)] * 3,
        out_specs=[pl.BlockSpec(memory_space=pltpu.VMEM)] * len(sizes),
        out_shape=[jax.ShapeDtypeStruct((2 * slabs, size, 128), jnp.float32) for size in sizes],
        compiler_params=pltpu.CompilerParams(vmem_limit_bytes=VMEM_BYTES),
    )(values, turned, side)


def result_kernel(
    offsets, own, devices, groups, places, next_plane, across, rim, pick, flip, *refs
):
    blocks, block = len(offsets) - 1, offsets[1]
    tiles = offsets[-1] // 128
    peers = (len(refs) - 2) // len(groups) - 1
    pieces, out = refs[: peers * len(groups)], refs[peers * len(groups)]
    held, sems = refs[peers * len(groups) + 1 : -1], refs[-1]
    step_rows, cols, length = out.shape
    half = length // 2
    slab, far_row, rim_col, me = places[0], places[1], places[2], places[3]
    lane = lax.broadcasted_iota(jnp.int32, (block, 128), 1)
    at_rim = lax.broadcasted_iota(jnp.int32, (cols, half), 0) + (1 - rim_col) == 0
    rim_lane = lax.broadcasted_iota(jnp.int32, rim.shape, 1)
    first_lane = lax.broadcasted_iota(jnp.int32, (cols, half), 1) == 0

    @pl.when(pl.program_id(0) == 0)
    def _():
        copies = []
        for g in range(len(groups)):
            for peer in range(peers):
                piece = pieces[g * peers + peer]
                size = piece.shape[0]
                spot = pl.ds(pl.multiple_of((me ^ peer) * size, size), size)
                copies.append(pltpu.make_async_copy(piece, held[g].at[spot], sems.at[g, peer]))
        for copy in copies:
            copy.start()
        for copy in copies:
            copy.wait()

    def left_half(r):
        t = pl.program_id(0) * step_rows + r
        i = jnp.where(far_row == 1, block - t, t)
        inside = (jnp.zeros((block, 128), jnp.int32) + i) < block
        i = jnp.minimum(i, block - 1)
        source = lax.div(i, devices), lax.rem(i, devices)
        parts = []
        for g, group in enumerate(groups):
            stride = held[g].shape[0] // devices
            for tile in range(group.start, group.stop):
                start = (tile - group.start) * own * block
                near = [
                    held[g][pl.ds(start + e * block + i, devices, stride=stride), :]
                    for e in range(own)
                ]
                near = jnp.concatenate(near, axis=0)
                far = pl.multiple_of(source[1] * stride + start + source[0] * block, 8)
                far = held[g][pl.ds(far, block), :]
                kind = jnp.zeros((block, 128), jnp.int32)
                for b in range(1, blocks):
                    kind += (lane + tile * 128 >= offsets[b]).astype(jnp.int32)
                line = jnp.where(kind >= slab, near, far)
                line = jnp.where(inside, line, next_plane[:, pl.ds(tile * 128, 128)])
                parts.append(line)
        line = jnp.concatenate(parts, axis=1)
        plane = square([line[:, offsets[b] : offsets[b + 1]] for b in range(blocks)], block)
        high, low = split(plane)
        left = jnp.dot(pick[...], high, preferred_element_type=jnp.float32)
        left += jnp.dot(pick[...], low, preferred_element_type=jnp.float32)
        left = jnp.where(at_rim, across[pl.ds(t, 1), :], left)
        out[r, :, pl.ds(0, half)] = left
        return left

    together = 4

    @pl.loop(0, step_rows // together)
    def _(c):
        left = [left_half(c * together + n) for n in range(together)]
        high, low = split(jnp.concatenate(left, axis=0))
        right = jnp.dot(high, flip[...], preferred_element_type=jnp.float32)
        right += jnp.dot(low, flip[...], preferred_element_type=jnp.float32)
        for n in range(together):
            r = c * together + n
            t = pl.program_id(0) * step_rows + r
            edge = jnp.sum(jnp.where(rim_lane == t, rim[...], 0.0), axis=1, keepdims=True)
            part = right[n * cols : (n + 1) * cols]
            out[r, :, pl.ds(half, half)] = jnp.where(first_lane, edge, part)


def result_block(got, next_plane, across, rim, pick_cols, slab, far_row, rim_col, col, offsets):
    block = offsets[1]
    gx = got[0][0].shape[0]
    groups = tile_groups(offsets[-1] // 128)
    devices = gx * len(got[0])
    own = block // devices
    rows, half = across.shape[0], across.shape[1] - 1
    cols = pick_cols.shape[0]
    step_rows = 8
    places = jnp.stack([slab, far_row.astype(jnp.int32), rim_col.astype(jnp.int32), col])
    cell = jnp.arange(half)
    pick = (pick_cols[:, None] == cell[None, :]).astype(jnp.bfloat16)
    flip = (cell[:, None] + cell[None, :] == half).astype(jnp.bfloat16)
    rim = jnp.pad(rim.T, ((0, 0), (0, 128 - rows)))
    whole = lambda array: pl.BlockSpec(array.shape, lambda i: (0,) * array.ndim)
    arrays = (next_plane, across[:, :half], rim, pick, flip)
    pieces = [piece.reshape(-1, 128) for group in got for piece in group]
    return pl.pallas_call(
        lambda *refs: result_kernel(offsets, own, devices, groups, *refs),
        grid=(rows // step_rows,),
        in_specs=[pl.BlockSpec(memory_space=pltpu.SMEM)] + [whole(array) for array in arrays]
        + [pl.BlockSpec(memory_space=pl.ANY)] * len(pieces),
        out_specs=pl.BlockSpec((step_rows, cols, 2 * half), lambda i: (i, 0, 0)),
        out_shape=jax.ShapeDtypeStruct((rows, cols, 2 * half), jnp.float32),
        scratch_shapes=[
            pltpu.VMEM((devices * group[0].shape[1], 128), jnp.float32) for group in got
        ] + [pltpu.SemaphoreType.DMA((len(groups), len(got[0])))],
        compiler_params=pltpu.CompilerParams(vmem_limit_bytes=VMEM_BYTES),
    )(places, *arrays, *pieces)


def tile_groups(tiles):
    return [slice(tile, min(tile + 2, tiles)) for tile in range(0, tiles, 2)]


def swap(peers, bit):
    return [(q, q ^ bit) for q in range(peers)]


def gathered(piece, peers, after):
    if after is not None:
        piece, first_hops = lax.optimization_barrier((piece, after[1:3]))
        after[1:3] = first_hops
    pieces, bit = {0: piece}, peers // 2
    while bit:
        for place in list(pieces):
            pieces[place ^ bit] = lax.ppermute(pieces[place], "gy", swap(peers, bit))
        bit //= 2
    return [pieces[place] for place in range(peers)]


def exchanged(packed):
    gy = len(packed)
    return [packed[0]] + [lax.ppermute(packed[p], "gy", swap(gy, p)) for p in range(1, gy)]


def sent_lines(got, count, after):
    gy = len(got)
    lines = [sum(got[p][:count] for p in range(first, gy, 2)) for first in range(2)]
    lines = jnp.concatenate(lines + [sum(piece[count:] for piece in got)], axis=0)
    lines = jnp.transpose(lines, (2, 1, 0, 3))
    if after is not None:
        lines, _ = lax.optimization_barrier((lines, after))
    return lax.all_to_all(lines, "gx", 0, 0, tiled=True)


def first_axis(lines, table):
    gx, _, count, half = table.shape
    table = table.reshape(gx, 2 * count, half)
    return jnp.einsum("geaw,gai->eiw", lines[:, :, : 2 * count], table, precision=HIGH)


def row_parts(rows):
    if rows < 4 * PART_STEP:
        return [slice(0, rows)]
    middle = rows - 2 * PART_STEP
    return [slice(middle, middle + PART_STEP), slice(0, middle), slice(middle + PART_STEP, rows)]


def square(lower, block):
    lines = []
    for b in range(len(lower)):
        parts = [lower[b]]
        for c in range(b + 1, len(lower)):
            part = lower[c][..., b * block : (b + 1) * block]
            parts.append(jnp.swapaxes(part, -1, -2))
        lines.append(jnp.concatenate(parts, axis=-1))
    return jnp.concatenate(lines, axis=-2)


def solution(mesh):
    placed = (P("gx", "gy", None), P())
    return jax.shard_map(
        on_device, mesh=mesh, in_specs=placed, out_specs=P("gx", "gy", None), check_vma=False
    )
```

profile of v0, /device:TPU:0, one launch (start us, length us, event | category | flops | bytes accessed | tf_op | source)
XLA Modules:
  0.0 425.7 jit_solution(15043264713681202148)
XLA Ops:
  0.0 2.6 fusion.46
  3.1 2.0 collective-permute-start.1
  8.9 1.3 copy.120
  10.2 2.1 fusion.10
  14.1 1.4 tile.4
  15.5 1.7 tile.10.marks
  17.9 2.2 fusion.45
  20.1 1.2 pad_maximum_fusion
  21.3 1.7 pad.16.sides
  22.9 18.1 %shard_map.28 = (f32[8,128,256]{2,1,0:T(8,128)}, f32[8,128,256]{2,1,0:T(8,128)}, f32[16,256]{1,0:T(8,128)}, f32[128,128]{1,0:T(8,128)}) custom-call(s32[2]{0:T(128)} %and_select_fusion.2.base, f32[64,128,512]{2,1,0:T(8,128)} %below.5, f32[64,128,512]{2,1,0:T(8,128)} %below.5, f32[64,128,512]{2,1,0:T(8,128)} %below.5, ...), custom_call_target="tpu_custom_call" | custom-call | flops 1610612736 | bytes 6291456 | tf_op jit(solution)/shard_map/pallas_call | solution.py:223
  41.6 4.8 %collective-permute-start.4 = (f32[2,128,512]{2,1,0:T(8,128)S(1)}, f32[2,128,512]{2,1,0:T(8,128)S(1)}, u32[]{:S(2)}, u32[]{:S(2)}) collective-permute-start(f32[2,128,512]{2,1,0:T(8,128)S(1)} %copy-done.2), channel_id=1, source_target_pairs={{4,0},{8,4},{12,8},{16,12},{20,16},{24,20},{28,24},{0,28},{5,1},{9... | collective-permute-start | bytes 1572872 | tf_op jit(solution)/shard_map/ppermute | solution.py:28
  49.0 5.0 %collective-permute-start.6 = (f32[2,4,512]{2,1,0:T(4,128)S(1)}, f32[2,4,512]{2,1,0:T(4,128)S(1)}, u32[]{:S(2)}, u32[]{:S(2)}) collective-permute-start(f32[2,4,512]{2,1,0:T(4,128)S(1)} %get-tuple-element.165), channel_id=1, source_target_pairs={{4,0},{8,4},{12,8},{16,12},{20,16},{24,20},{28,24},{0,28},{5,1},{9... | collective-permute-start | bytes 49160 | tf_op jit(solution)/shard_map/ppermute | solution.py:33
  54.5 13.5 %collective-permute-done.5 = f32[2,4,512]{2,1,0:T(4,128)S(1)} collective-permute-done((f32[2,4,512]{2,1,0:T(4,128)S(1)}, f32[2,4,512]{2,1,0:T(4,128)S(1)}, u32[]{:S(2)}, u32[]{:S(2)}) %collective-permute-start.5) | collective-permute-done | bytes 16416 | tf_op jit(solution)/shard_map/ppermute | solution.py:32
  68.1 2.8 select_maximum_fusion.sides
  73.1 5.5 %shard_map.29 = (f32[8,2,8,640]{3,2,1,0:T(8,128)}, f32[8,2,8,640]{3,2,1,0:T(8,128)}, f32[8,2,8,640]{3,2,1,0:T(8,128)}, f32[8,2,8,640]{3,2,1,0:T(8,128)}, f32[4,64,640]{2,1,0:T(8,128)}) custom-call(s32[1]{0:T(128)} %bitcast.3.refs_0_, f32[4,8]{1,0:T(4,128)} %pad_maximum_fusion.4.refs_1_, f32[8,128,256]{2,1,0:T(8,128)} %get-tuple-element.68.refs_2_, ...), custom_call_target="tpu_custom_call" | custom-call | flops 805306368 | bytes 4194304 | tf_op jit(solution)/shard_map/pallas_call | solution.py:334
  80.8 30.2 %shard_map.30 = (f32[16,128,256]{2,1,0:T(8,128)}, f32[16,128,256]{2,1,0:T(8,128)}, f32[32,256]{1,0:T(8,128)}, f32[128,128]{1,0:T(8,128)}) custom-call(s32[2]{0:T(128)} %and_select_fusion.1.base, f32[64,128,512]{2,1,0:T(8,128)} %below.5, f32[64,128,512]{2,1,0:T(8,128)} %below.5, f32[64,128,512]{2,1,0:T(8,128)} %below.5, f32[2,128,512]{2,1,0:T(8,128)} %copy-done.5, ...), custom_call_target="tpu_custom_call" | custom-call | flops 3221225472 | bytes 12582912 | tf_op jit(solution)/shard_map/pallas_call | solution.py:223
  111.7 1.5 collective-permute-start.8
  114.2 1.4 collective-permute-done.7
  115.6 6.8 %collective-permute-done.8 = f32[8,2,8,640]{3,2,1,0:T(8,128)S(1)} collective-permute-done((f32[8,2,8,640]{3,2,1,0:T(8,128)}, f32[8,2,8,640]{3,2,1,0:T(8,128)S(1)}, u32[]{:S(2)}, u32[]{:S(2)}) %collective-permute-start.8) | collective-permute-done | bytes 327712 | tf_op jit(solution)/shard_map/ppermute | solution.py:703
  122.5 5.3 %collective-permute-done.9 = f32[8,2,8,640]{3,2,1,0:T(8,128)S(1)} collective-permute-done((f32[8,2,8,640]{3,2,1,0:T(8,128)}, f32[8,2,8,640]{3,2,1,0:T(8,128)S(1)}, u32[]{:S(2)}, u32[]{:S(2)}) %collective-permute-start.9) | collective-permute-done | bytes 327712 | tf_op jit(solution)/shard_map/ppermute | solution.py:703
  127.9 1.2 copy.125
  129.2 6.3 %all-to-all-start = ((f32[8,2,16,640]{3,1,2,0:T(2,128)}), f32[8,2,16,640]{3,1,2,0:T(2,128)}, u32[]{:S(2)}, u32[]{:S(2)}) async-start(f32[8,2,16,640]{3,1,2,0:T(2,128)} %copy.125), calls=%async_computation | async-start | bytes 1310720 | tf_op jit(solution)/shard_map/all_to_all | solution.py:713
  137.0 8.2 %shard_map.31 = (f32[16,2,8,640]{3,2,1,0:T(8,128)}, f32[16,2,8,640]{3,2,1,0:T(8,128)}, f32[16,2,8,640]{3,2,1,0:T(8,128)}, f32[16,2,8,640]{3,2,1,0:T(8,128)}, f32[4,64,640]{2,1,0:T(8,128)}) custom-call(s32[1]{0:T(128)} %bitcast.3.refs_0_, f32[4,16]{1,0:T(4,128)} %pad_maximum_fusion.5.refs_1_, f32[16,128,256]{2,1,0:T(8,128)} %get-tuple-element.85.refs_2_, ...), custom_call_target="tpu_custom_call" | custom-call | flops 1610612736 | bytes 8388608 | tf_op jit(solution)/shard_map/pallas_call | solution.py:334
  145.7 1.5 collective-permute-start.12
  147.8 17.6 %shard_map.32 = (f32[8,128,256]{2,1,0:T(8,128)}, f32[8,128,256]{2,1,0:T(8,128)}, f32[16,256]{1,0:T(8,128)}, f32[128,128]{1,0:T(8,128)}) custom-call(s32[2]{0:T(128)} %and_select_fusion.base, f32[64,128,512]{2,1,0:T(8,128)} %below.5, f32[64,128,512]{2,1,0:T(8,128)} %below.5, f32[64,128,512]{2,1,0:T(8,128)} %below.5, f32[2,128,512]{2,1,0:T(8,128)} %copy-done.5, ...), custom_call_target="tpu_custom_call" | custom-call | flops 1610612736 | bytes 6291456 | tf_op jit(solution)/shard_map/pallas_call | solution.py:223
  165.5 1.2 fusion.21
  168.2 7.5 %collective-permute-done.13 = f32[16,2,8,640]{3,2,1,0:T(8,128)S(1)} collective-permute-done((f32[16,2,8,640]{3,2,1,0:T(8,128)}, f32[16,2,8,640]{3,2,1,0:T(8,128)S(1)}, u32[]{:S(2)}, u32[]{:S(2)}) %collective-permute-start.13) | collective-permute-done | bytes 655392 | tf_op jit(solution)/shard_map/ppermute | solution.py:703
  176.0 1.7 copy.129
  177.7 6.3 %all-to-all-start.1 = ((f32[8,2,32,640]{3,1,2,0:T(2,128)}), f32[8,2,32,640]{3,1,2,0:T(2,128)S(1)}, u32[]{:S(2)}, u32[]{:S(2)}) async-start(f32[8,2,32,640]{3,1,2,0:T(2,128)} %copy.129), calls=%async_computation.1 | async-start | bytes 2621440 | tf_op jit(solution)/shard_map/all_to_all | solution.py:713
  185.2 1.0 fusion.26.refs_8_
  186.1 5.9 %shard_map.33 = (f32[13,2,8,640]{3,2,1,0:T(8,128)}, f32[13,2,8,640]{3,2,1,0:T(8,128)}, f32[13,2,8,640]{3,2,1,0:T(8,128)}, f32[13,2,8,640]{3,2,1,0:T(8,128)}, f32[4,64,640]{2,1,0:T(8,128)}) custom-call(s32[1]{0:T(128)} %bitcast.3.refs_0_, f32[4,8]{1,0:T(4,128)} %pad_maximum_fusion.6.refs_1_, f32[8,128,256]{2,1,0:T(8,128)} %get-tuple-element.104.refs_2_, ...), custom_call_target="tpu_custom_call" | custom-call | flops 805306368 | bytes 4194304 | tf_op jit(solution)/shard_map/pallas_call | solution.py:334
  192.0 1.5 collective-permute-start.15
  194.2 13.0 %collective-permute-done.15 = f32[13,2,8,640]{3,2,1,0:T(8,128)S(1)} collective-permute-done((f32[13,2,8,640]{3,2,1,0:T(8,128)}, f32[13,2,8,640]{3,2,1,0:T(8,128)S(1)}, u32[]{:S(2)}, u32[]{:S(2)}) %collective-permute-start.15) | collective-permute-done | bytes 532512 | tf_op jit(solution)/shard_map/ppermute | solution.py:703
  207.2 1.0 slice_add_fusion.1
  208.2 8.7 %collective-permute-done.17 = f32[13,2,8,640]{3,2,1,0:T(8,128)S(1)} collective-permute-done((f32[13,2,8,640]{3,2,1,0:T(8,128)}, f32[13,2,8,640]{3,2,1,0:T(8,128)S(1)}, u32[]{:S(2)}, u32[]{:S(2)}) %collective-permute-start.17) | collective-permute-done | bytes 532512 | tf_op jit(solution)/shard_map/ppermute | solution.py:703
  216.9 1.0 slice_add_fusion.2
  218.0 1.4 copy.131
  219.4 5.7 %all-to-all-start.2 = ((f32[8,2,21,640]{3,1,2,0:T(2,128)}), f32[8,2,21,640]{3,1,2,0:T(2,128)S(1)}, u32[]{:S(2)}, u32[]{:S(2)}) async-start(f32[8,2,21,640]{3,1,2,0:T(2,128)} %copy.131), calls=%async_computation.2 | async-start | bytes 1720320 | tf_op jit(solution)/shard_map/all_to_all | solution.py:713
  225.5 1.2 copy-done.10
  226.7 1.9 convolution_bitcast_fusion
  228.5 19.2 %all-to-all-done.2 = f32[8,2,21,640]{3,1,2,0:T(2,128)S(1)} async-done(((f32[8,2,21,640]{3,1,2,0:T(2,128)}), f32[8,2,21,640]{3,1,2,0:T(2,128)S(1)}, u32[]{:S(2)}, u32[]{:S(2)}) %all-to-all-start.2) | async-done | bytes 860192 | tf_op jit(solution)/shard_map/all_to_all | solution.py:713
  249.1 1.8 fusion.2
  251.0 1.0 copy.162
  252.2 2.4 concatenate.84
  254.6 3.7 all-to-all-start.3
  258.9 18.5 %all-to-all-done.3 = f32[32,2,2,1280]{3,2,1,0:T(2,128)S(1)} async-done(((f32[32,2,2,1280]{3,2,1,0:T(2,128)}), f32[32,2,2,1280]{3,2,1,0:T(2,128)S(1)}, u32[]{:S(2)}, u32[]{:S(2)}) %all-to-all-start.3) | async-done | bytes 655392 | tf_op jit(solution)/shard_map/all_to_all | solution.py:427
  277.4 1.0 copy.134
  278.4 5.6 %shard_map.34 = (f32[8,288,128]{2,1,0:T(8,128)}, f32[8,256,128]{2,1,0:T(8,128)}, f32[8,128,128]{2,1,0:T(8,128)}) custom-call(f32[2,256,640]{2,1,0:T(8,128)} %bitcast.189, f32[2,64,1280]{2,1,0:T(8,128)} %bitcast.196, f32[2,5,640]{2,1,0:T(8,128)} %copy_multiply_fusion.refs_2_), custom_call_target="tpu_custom_call" | custom-call | tf_op jit(solution)/shard_map/pallas_call | solution.py:562
  284.0 32.5 %all_to_all.35 = f32[8,288,128]{2,1,0:T(8,128)S(1)} all-to-all(f32[8,288,128]{2,1,0:T(8,128)} %get-tuple-element.119), channel_id=1, replica_groups=mesh['gx'=8,'gy'=4] {'gx'}, dimensions={0} | all-to-all | bytes 2359296 | tf_op jit(solution)/shard_map/all_to_all | solution.py:443
  316.5 1.2 collective-permute-start.19
  317.7 3.6 all-to-all-start.5
  321.4 21.5 %collective-permute-done.19 = f32[8,288,128]{2,1,0:T(8,128)} collective-permute-done((f32[8,288,128]{2,1,0:T(8,128)S(1)}, f32[8,288,128]{2,1,0:T(8,128)}, u32[]{:S(2)}, u32[]{:S(2)}) %collective-permute-start.19) | collective-permute-done | bytes 1179680 | tf_op jit(solution)/shard_map/ppermute | solution.py:696
  344.9 1.9 all-to-all-done.5
  347.9 3.8 all-to-all-start.6
  351.7 0.9 slice_bitcast_fusion.9
  352.6 0.9 slice_bitcast_fusion.8
  353.5 0.9 slice_bitcast_fusion.2
  355.4 10.8 %all-to-all-done.6 = f32[8,128,128]{2,1,0:T(8,128)S(1)} async-done(((f32[8,128,128]{2,1,0:T(8,128)}), f32[8,128,128]{2,1,0:T(8,128)S(1)}, u32[]{:S(2)}, u32[]{:S(2)}) %all-to-all-start.6) | async-done | bytes 524320 | tf_op jit(solution)/shard_map/all_to_all | solution.py:443
  366.3 4.4 %collective-permute-done.22 = f32[8,256,128]{2,1,0:T(8,128)} collective-permute-done((f32[8,256,128]{2,1,0:T(8,128)S(1)}, f32[8,256,128]{2,1,0:T(8,128)}, u32[]{:S(2)}, u32[]{:S(2)}) %collective-permute-start.22) | collective-permute-done | bytes 1048608 | tf_op jit(solution)/shard_map/ppermute | solution.py:696
  370.7 1.7 collective-permute-start.25
  375.7 7.7 %collective-permute-done.25 = f32[8,128,128]{2,1,0:T(8,128)S(1)} collective-permute-done((f32[8,128,128]{2,1,0:T(8,128)S(1)}, f32[8,128,128]{2,1,0:T(8,128)S(1)}, u32[]{:S(2)}, u32[]{:S(2)}) %collective-permute-start.25) | collective-permute-done | bytes 524320 | tf_op jit(solution)/shard_map/ppermute | solution.py:696
  384.8 1.3 dynamic-update-slice.4
  386.1 1.0 pad_maximum_fusion.2
  391.6 33.9 %shard_map.35 = f32[64,128,512]{2,1,0:T(8,128)} custom-call(s32[4]{0:T(128)} %pad_add_fusion.refs_0_, f32[64,640]{1,0:T(8,128)} %bitcast.208, f32[64,256]{1,0:T(8,128)} %slice.470.refs_2_, f32[128,128]{1,0:T(8,128)} %pad.19.refs_3_, bf16[128,256]{1,0:T(8,128)(2,1)} %fusion.28.refs_4_, bf16[256,256]{1,0:T(8,128)(2,1)} %fusion.20.refs_5_, ...), custom_call_target="tpu_custom_call" | custom-call | tf_op jit(solution)/shard_map/pallas_call | solution.py:667
  (190 shorter events, 38.5 us)
Async XLA Ops:
  0.0 5.1 %slice-start.1 = ((s32[32,32,32]{2,1,0:T(8,128)}), s32[31,32,32]{2,1,0:T(8,128)S(1)}, s32[]{:S(2)}) async-start(s32[32,32,32]{2,1,0:T(8,128)} %param.3), calls=%async_computation.8 | async-start | bytes 1015808 | tf_op jit(solution)/shard_map/jit(_roll_static)/slice | solution.py:41
  2.7 2.5 copy-start.6
  2.7 2.5 slice-start
  2.7 17.4 %collective-permute-start = (f32[64,2,512]{2,1,0:T(2,128)}, f32[64,2,512]{2,1,0:T(2,128)S(1)}, u32[]{:S(2)}, u32[]{:S(2)}) collective-permute-start(f32[64,2,512]{2,1,0:T(2,128)} %get-tuple-element.133), channel_id=1, source_target_pairs={{0,1},{1,2},{2,3},{3,0},{4,5},{5,6},{6,7},{7,4},{8,9},{9,10},{10,1... | collective-permute-start | bytes 786440 | tf_op jit(solution)/shard_map/ppermute | solution.py:29
  3.1 17.0 %collective-permute-start.1 = (f32[64,2,512]{2,1,0:T(2,128)}, f32[64,2,512]{2,1,0:T(2,128)}, u32[]{:S(2)}, u32[]{:S(2)}) collective-permute-start(f32[64,2,512]{2,1,0:T(2,128)} %get-tuple-element.134), channel_id=1, source_target_pairs={{1,0},{2,1},{3,2},{0,3},{5,4},{6,5},{7,6},{4,7},{9,8},{10,9},{11,1... | collective-permute-start | bytes 786440 | tf_op jit(solution)/shard_map/ppermute | solution.py:30
  22.9 18.7 %copy-start.2 = (f32[2,128,512]{2,1,0:T(8,128)S(1)}, f32[2,128,512]{2,1,0:T(8,128)}, u32[]{:S(2)}) copy-start(f32[2,128,512]{2,1,0:T(8,128)} %get-tuple-element.132.top.bottom) | copy-start | bytes 1572868
  41.0 29.9 %collective-permute-start.2 = (f32[8,128,256]{2,1,0:T(8,128)}, f32[8,128,256]{2,1,0:T(8,128)}, u32[]{:S(2)}, u32[]{:S(2)}) collective-permute-start(f32[8,128,256]{2,1,0:T(8,128)} %get-tuple-element.69), channel_id=1, source_target_pairs={{0,1},{1,0},{2,3},{3,2},{4,5},{5,4},{6,7},{7,6},{8,9},{9,8},{10,11... | collective-permute-start | bytes 3145736 | tf_op jit(solution)/shard_map/ppermute | solution.py:382
  41.6 37.6 %collective-permute-start.4 = (f32[2,128,512]{2,1,0:T(8,128)S(1)}, f32[2,128,512]{2,1,0:T(8,128)S(1)}, u32[]{:S(2)}, u32[]{:S(2)}) collective-permute-start(f32[2,128,512]{2,1,0:T(8,128)S(1)} %copy-done.2), channel_id=1, source_target_pairs={{4,0},{8,4},{12,8},{16,12},{20,16},{24,20},{28,24},{0,28},{5,1},{9... | collective-permute-start | bytes 1572872 | tf_op jit(solution)/shard_map/ppermute | solution.py:28
  46.5 32.8 %collective-permute-start.3 = (f32[2,128,512]{2,1,0:T(8,128)}, f32[2,128,512]{2,1,0:T(8,128)S(1)}, u32[]{:S(2)}, u32[]{:S(2)}) collective-permute-start(f32[2,128,512]{2,1,0:T(8,128)} %get-tuple-element.131), channel_id=1, source_target_pairs={{0,4},{4,8},{8,12},{12,16},{16,20},{20,24},{24,28},{28,0},{1,5},{5... | collective-permute-start | bytes 1572872 | tf_op jit(solution)/shard_map/ppermute | solution.py:27
  48.9 19.1 %collective-permute-start.5 = (f32[2,4,512]{2,1,0:T(4,128)S(1)}, f32[2,4,512]{2,1,0:T(4,128)S(1)}, u32[]{:S(2)}, u32[]{:S(2)}) collective-permute-start(f32[2,4,512]{2,1,0:T(4,128)S(1)} %get-tuple-element.164), channel_id=1, source_target_pairs={{0,4},{4,8},{8,12},{12,16},{16,20},{20,24},{24,28},{28,0},{1,5},{5... | collective-permute-start | bytes 49160 | tf_op jit(solution)/shard_map/ppermute | solution.py:32
  49.0 19.1 %collective-permute-start.6 = (f32[2,4,512]{2,1,0:T(4,128)S(1)}, f32[2,4,512]{2,1,0:T(4,128)S(1)}, u32[]{:S(2)}, u32[]{:S(2)}) collective-permute-start(f32[2,4,512]{2,1,0:T(4,128)S(1)} %get-tuple-element.165), channel_id=1, source_target_pairs={{4,0},{8,4},{12,8},{16,12},{20,16},{24,20},{28,24},{0,28},{5,1},{9... | collective-permute-start | bytes 49160 | tf_op jit(solution)/shard_map/ppermute | solution.py:33
  79.2 0.8 copy-start.5
  80.0 0.8 copy-start.4
  111.0 16.8 %copy-start.16 = (f32[8,2,8,640]{3,2,1,0:T(8,128)S(1)}, f32[8,2,8,640]{3,2,1,0:T(8,128)}, u32[]{:S(2)}) copy-start(f32[8,2,8,640]{3,2,1,0:T(8,128)} %get-tuple-element.81) | copy-start | bytes 983044
  111.0 26.0 %collective-permute-start.10 = (f32[16,128,256]{2,1,0:T(8,128)}, f32[16,128,256]{2,1,0:T(8,128)}, u32[]{:S(2)}, u32[]{:S(2)}) collective-permute-start(f32[16,128,256]{2,1,0:T(8,128)} %get-tuple-element.86), channel_id=1, source_target_pairs={{0,1},{1,0},{2,3},{3,2},{4,5},{5,4},{6,7},{7,6},{8,9},{9,8},{10,11... | collective-permute-start | bytes 6291464 | tf_op jit(solution)/shard_map/ppermute | solution.py:382
  111.2 4.4 %collective-permute-start.7 = (f32[8,2,8,640]{3,2,1,0:T(8,128)}, f32[8,2,8,640]{3,2,1,0:T(8,128)S(1)}, u32[]{:S(2)}, u32[]{:S(2)}) collective-permute-start(f32[8,2,8,640]{3,2,1,0:T(8,128)} %get-tuple-element.78), channel_id=1, source_target_pairs={{0,1},{1,0},{2,3},{3,2},{4,5},{5,4},{6,7},{7,6},{8,9},{9,8},{10,11... | collective-permute-start | bytes 983048 | tf_op jit(solution)/shard_map/ppermute | solution.py:703
  111.7 10.8 %collective-permute-start.8 = (f32[8,2,8,640]{3,2,1,0:T(8,128)}, f32[8,2,8,640]{3,2,1,0:T(8,128)S(1)}, u32[]{:S(2)}, u32[]{:S(2)}) collective-permute-start(f32[8,2,8,640]{3,2,1,0:T(8,128)} %get-tuple-element.79), channel_id=1, source_target_pairs={{0,2},{1,3},{2,0},{3,1},{4,6},{5,7},{6,4},{7,5},{8,10},{9,11},{10,... | collective-permute-start | bytes 983048 | tf_op jit(solution)/shard_map/ppermute | solution.py:703
  113.2 14.6 %collective-permute-start.9 = (f32[8,2,8,640]{3,2,1,0:T(8,128)}, f32[8,2,8,640]{3,2,1,0:T(8,128)S(1)}, u32[]{:S(2)}, u32[]{:S(2)}) collective-permute-start(f32[8,2,8,640]{3,2,1,0:T(8,128)} %get-tuple-element.80), channel_id=1, source_target_pairs={{0,3},{1,2},{2,1},{3,0},{4,7},{5,6},{6,5},{7,4},{8,11},{9,10},{10,... | collective-permute-start | bytes 983048 | tf_op jit(solution)/shard_map/ppermute | solution.py:703
  129.2 46.8 %all-to-all-start = ((f32[8,2,16,640]{3,1,2,0:T(2,128)}), f32[8,2,16,640]{3,1,2,0:T(2,128)}, u32[]{:S(2)}, u32[]{:S(2)}) async-start(f32[8,2,16,640]{3,1,2,0:T(2,128)} %copy.125), calls=%async_computation | async-start | bytes 1310720 | tf_op jit(solution)/shard_map/all_to_all | solution.py:713
  145.2 23.0 %collective-permute-start.11 = (f32[16,2,8,640]{3,2,1,0:T(8,128)}, f32[16,2,8,640]{3,2,1,0:T(8,128)S(1)}, u32[]{:S(2)}, u32[]{:S(2)}) collective-permute-start(f32[16,2,8,640]{3,2,1,0:T(8,128)} %get-tuple-element.96), channel_id=1, source_target_pairs={{0,1},{1,0},{2,3},{3,2},{4,5},{5,4},{6,7},{7,6},{8,9},{9,8},{10,11... | collective-permute-start | bytes 1966088 | tf_op jit(solution)/shard_map/ppermute | solution.py:703
  145.7 22.6 %collective-permute-start.12 = (f32[16,2,8,640]{3,2,1,0:T(8,128)}, f32[16,2,8,640]{3,2,1,0:T(8,128)S(1)}, u32[]{:S(2)}, u32[]{:S(2)}) collective-permute-start(f32[16,2,8,640]{3,2,1,0:T(8,128)} %get-tuple-element.97), channel_id=1, source_target_pairs={{0,2},{1,3},{2,0},{3,1},{4,6},{5,7},{6,4},{7,5},{8,10},{9,11},{10,... | collective-permute-start | bytes 1966088 | tf_op jit(solution)/shard_map/ppermute | solution.py:703
  147.1 28.6 %collective-permute-start.13 = (f32[16,2,8,640]{3,2,1,0:T(8,128)}, f32[16,2,8,640]{3,2,1,0:T(8,128)S(1)}, u32[]{:S(2)}, u32[]{:S(2)}) collective-permute-start(f32[16,2,8,640]{3,2,1,0:T(8,128)} %get-tuple-element.98), channel_id=1, source_target_pairs={{0,3},{1,2},{2,1},{3,0},{4,7},{5,6},{6,5},{7,4},{8,11},{9,10},{10,... | collective-permute-start | bytes 1966088 | tf_op jit(solution)/shard_map/ppermute | solution.py:703
  147.8 17.7 %copy-start.17 = (f32[128,128]{1,0:T(8,128)S(1)}, f32[128,128]{1,0:T(8,128)}, u32[]{:S(2)}) copy-start(f32[128,128]{1,0:T(8,128)} %get-tuple-element.106) | copy-start | bytes 196612
  147.8 17.7 %copy-start.18 = (f32[128,128]{1,0:T(8,128)S(1)}, f32[128,128]{1,0:T(8,128)}, u32[]{:S(2)}) copy-start(f32[128,128]{1,0:T(8,128)} %get-tuple-element.107) | copy-start | bytes 196612
  147.8 19.7 %copy-start.19 = (f32[32,256]{1,0:T(8,128)S(1)}, f32[32,256]{1,0:T(8,128)}, u32[]{:S(2)}) copy-start(f32[32,256]{1,0:T(8,128)} %get-tuple-element.110) | copy-start | bytes 98308
  147.8 19.7 %copy-start.20 = (f32[16,256]{1,0:T(8,128)S(1)}, f32[16,256]{1,0:T(8,128)}, u32[]{:S(2)}) copy-start(f32[16,256]{1,0:T(8,128)} %get-tuple-element.109) | copy-start | bytes 49156
  165.5 10.3 %copy-start.12 = (f32[16,2,8,640]{3,2,1,0:T(8,128)S(1)}, f32[16,2,8,640]{3,2,1,0:T(8,128)}, u32[]{:S(2)}) copy-start(f32[16,2,8,640]{3,2,1,0:T(8,128)} %get-tuple-element.99) | copy-start | bytes 1966084
  166.8 19.4 %collective-permute-start.14 = (f32[8,128,256]{2,1,0:T(8,128)}, f32[8,128,256]{2,1,0:T(8,128)}, u32[]{:S(2)}, u32[]{:S(2)}) collective-permute-start(f32[8,128,256]{2,1,0:T(8,128)} %get-tuple-element.105), channel_id=1, source_target_pairs={{0,1},{1,0},{2,3},{3,2},{4,5},{5,4},{6,7},{7,6},{8,9},{9,8},{10,11... | collective-permute-start | bytes 3145736 | tf_op jit(solution)/shard_map/ppermute | solution.py:382
  177.7 40.3 %all-to-all-start.1 = ((f32[8,2,32,640]{3,1,2,0:T(2,128)}), f32[8,2,32,640]{3,1,2,0:T(2,128)S(1)}, u32[]{:S(2)}, u32[]{:S(2)}) async-start(f32[8,2,32,640]{3,1,2,0:T(2,128)} %copy.129), calls=%async_computation.1 | async-start | bytes 2621440 | tf_op jit(solution)/shard_map/all_to_all | solution.py:713
  192.0 15.2 %collective-permute-start.15 = (f32[13,2,8,640]{3,2,1,0:T(8,128)}, f32[13,2,8,640]{3,2,1,0:T(8,128)S(1)}, u32[]{:S(2)}, u32[]{:S(2)}) collective-permute-start(f32[13,2,8,640]{3,2,1,0:T(8,128)} %get-tuple-element.114), channel_id=1, source_target_pairs={{0,2},{1,3},{2,0},{3,1},{4,6},{5,7},{6,4},{7,5},{8,10},{9,11},{10,... | collective-permute-start | bytes 1597448 | tf_op jit(solution)/shard_map/ppermute | solution.py:703
  193.5 14.7 %collective-permute-start.16 = (f32[13,2,8,640]{3,2,1,0:T(8,128)}, f32[13,2,8,640]{3,2,1,0:T(8,128)S(1)}, u32[]{:S(2)}, u32[]{:S(2)}) collective-permute-start(f32[13,2,8,640]{3,2,1,0:T(8,128)} %get-tuple-element.115), channel_id=1, source_target_pairs={{0,1},{1,0},{2,3},{3,2},{4,5},{5,4},{6,7},{7,6},{8,9},{9,8},{10,11... | collective-permute-start | bytes 1597448 | tf_op jit(solution)/shard_map/ppermute | solution.py:703
  193.5 23.4 %collective-permute-start.17 = (f32[13,2,8,640]{3,2,1,0:T(8,128)}, f32[13,2,8,640]{3,2,1,0:T(8,128)S(1)}, u32[]{:S(2)}, u32[]{:S(2)}) collective-permute-start(f32[13,2,8,640]{3,2,1,0:T(8,128)} %get-tuple-element.116), channel_id=1, source_target_pairs={{0,3},{1,2},{2,1},{3,0},{4,7},{5,6},{6,5},{7,4},{8,11},{9,10},{10,... | collective-permute-start | bytes 1597448 | tf_op jit(solution)/shard_map/ppermute | solution.py:703
  218.0 1.4 copy-start.9
  219.4 28.3 %all-to-all-start.2 = ((f32[8,2,21,640]{3,1,2,0:T(2,128)}), f32[8,2,21,640]{3,1,2,0:T(2,128)S(1)}, u32[]{:S(2)}, u32[]{:S(2)}) async-start(f32[8,2,21,640]{3,1,2,0:T(2,128)} %copy.131), calls=%async_computation.2 | async-start | bytes 1720320 | tf_op jit(solution)/shard_map/all_to_all | solution.py:713
  225.3 1.3 copy-start.10
  247.8 1.3 copy-start.21
  250.9 1.1 copy-start.1
  254.6 22.9 %all-to-all-start.3 = ((f32[32,2,2,1280]{3,2,1,0:T(2,128)}), f32[32,2,2,1280]{3,2,1,0:T(2,128)S(1)}, u32[]{:S(2)}, u32[]{:S(2)}) async-start(f32[32,2,2,1280]{3,2,1,0:T(2,128)} %concatenate.84), calls=%async_computation.3 | async-start | bytes 1310720 | tf_op jit(solution)/shard_map/all_to_all | solution.py:427
  316.5 31.4 %copy-start = (f32[8,288,128]{2,1,0:T(8,128)}, f32[8,288,128]{2,1,0:T(8,128)S(1)}, u32[]{:S(2)}) copy-start(f32[8,288,128]{2,1,0:T(8,128)S(1)} %all_to_all.35) | copy-start | bytes 3538948
  316.5 26.4 %collective-permute-start.19 = (f32[8,288,128]{2,1,0:T(8,128)S(1)}, f32[8,288,128]{2,1,0:T(8,128)}, u32[]{:S(2)}, u32[]{:S(2)}) collective-permute-start(f32[8,288,128]{2,1,0:T(8,128)S(1)} %all_to_all.35), channel_id=1, source_target_pairs={{0,2},{1,3},{2,0},{3,1},{4,6},{5,7},{6,4},{7,5},{8,10},{9,11},{10,... | collective-permute-start | bytes 3538952 | tf_op jit(solution)/shard_map/ppermute | solution.py:696
  317.7 29.1 %all-to-all-start.5 = ((f32[8,256,128]{2,1,0:T(8,128)}), f32[8,256,128]{2,1,0:T(8,128)S(1)}, u32[]{:S(2)}, u32[]{:S(2)}) async-start(f32[8,256,128]{2,1,0:T(8,128)} %get-tuple-element.122), calls=%async_computation.5 | async-start | bytes 2097152 | tf_op jit(solution)/shard_map/all_to_all | solution.py:443
  321.2 25.6 %collective-permute-start.18 = (f32[8,288,128]{2,1,0:T(8,128)S(1)}, f32[8,288,128]{2,1,0:T(8,128)S(1)}, u32[]{:S(2)}, u32[]{:S(2)}) collective-permute-start(f32[8,288,128]{2,1,0:T(8,128)S(1)} %all_to_all.35), channel_id=1, source_target_pairs={{0,1},{1,0},{2,3},{3,2},{4,5},{5,4},{6,7},{7,6},{8,9},{9,8},{10,11... | collective-permute-start | bytes 3538952 | tf_op jit(solution)/shard_map/ppermute | solution.py:696
  342.8 10.7 %collective-permute-start.20 = (f32[8,288,128]{2,1,0:T(8,128)}, f32[8,288,128]{2,1,0:T(8,128)}, u32[]{:S(2)}, u32[]{:S(2)}) collective-permute-start(f32[8,288,128]{2,1,0:T(8,128)} %collective-permute-done.19), channel_id=1, source_target_pairs={{0,1},{1,0},{2,3},{3,2},{4,5},{5,4},{6,7},{7,6},{8,9},{9,8},{10,11... | collective-permute-start | bytes 3538952 | tf_op jit(solution)/shard_map/ppermute | solution.py:696
  346.8 7.7 %copy-start.3 = (f32[8,256,128]{2,1,0:T(8,128)}, f32[8,256,128]{2,1,0:T(8,128)S(1)}, u32[]{:S(2)}) copy-start(f32[8,256,128]{2,1,0:T(8,128)S(1)} %all-to-all-done.5) | copy-start | bytes 3145732
  346.8 1.1 copy-start.8
  346.8 23.9 %collective-permute-start.22 = (f32[8,256,128]{2,1,0:T(8,128)S(1)}, f32[8,256,128]{2,1,0:T(8,128)}, u32[]{:S(2)}, u32[]{:S(2)}) collective-permute-start(f32[8,256,128]{2,1,0:T(8,128)S(1)} %all-to-all-done.5), channel_id=1, source_target_pairs={{0,2},{1,3},{2,0},{3,1},{4,6},{5,7},{6,4},{7,5},{8,10},{9,11},{10,... | collective-permute-start | bytes 3145736 | tf_op jit(solution)/shard_map/ppermute | solution.py:696
  347.4 23.3 %collective-permute-start.21 = (f32[8,256,128]{2,1,0:T(8,128)S(1)}, f32[8,256,128]{2,1,0:T(8,128)}, u32[]{:S(2)}, u32[]{:S(2)}) collective-permute-start(f32[8,256,128]{2,1,0:T(8,128)S(1)} %all-to-all-done.5), channel_id=1, source_target_pairs={{0,1},{1,0},{2,3},{3,2},{4,5},{5,4},{6,7},{7,6},{8,9},{9,8},{10,11... | collective-permute-start | bytes 3145736 | tf_op jit(solution)/shard_map/ppermute | solution.py:696
  347.9 18.4 %all-to-all-start.6 = ((f32[8,128,128]{2,1,0:T(8,128)}), f32[8,128,128]{2,1,0:T(8,128)S(1)}, u32[]{:S(2)}, u32[]{:S(2)}) async-start(f32[8,128,128]{2,1,0:T(8,128)} %get-tuple-element.127), calls=%async_computation.6 | async-start | bytes 1048576 | tf_op jit(solution)/shard_map/all_to_all | solution.py:443
  355.3 19.2 %copy-start.15 = (f32[2,2,32,640]{3,2,1,0:T(8,128)}, f32[2,2,32,640]{3,2,1,0:T(8,128)S(1)}, u32[]{:S(2)}) copy-start(f32[2,2,32,640]{3,2,1,0:T(8,128)S(1)} %copy.143) | copy-start | bytes 983044
  366.3 21.5 %copy-start.7 = (f32[8,128,128]{2,1,0:T(8,128)}, f32[8,128,128]{2,1,0:T(8,128)S(1)}, u32[]{:S(2)}) copy-start(f32[8,128,128]{2,1,0:T(8,128)S(1)} %all-to-all-done.6) | copy-start | bytes 1572868
  370.7 12.8 %collective-permute-start.25 = (f32[8,128,128]{2,1,0:T(8,128)S(1)}, f32[8,128,128]{2,1,0:T(8,128)S(1)}, u32[]{:S(2)}, u32[]{:S(2)}) collective-permute-start(f32[8,128,128]{2,1,0:T(8,128)S(1)} %all-to-all-done.6), channel_id=1, source_target_pairs={{0,2},{1,3},{2,0},{3,1},{4,6},{5,7},{6,4},{7,5},{8,10},{9,11},{10,... | collective-permute-start | bytes 1572872 | tf_op jit(solution)/shard_map/ppermute | solution.py:696
  372.4 18.0 %collective-permute-start.23 = (f32[8,256,128]{2,1,0:T(8,128)}, f32[8,256,128]{2,1,0:T(8,128)S(1)}, u32[]{:S(2)}, u32[]{:S(2)}) collective-permute-start(f32[8,256,128]{2,1,0:T(8,128)} %collective-permute-done.22), channel_id=1, source_target_pairs={{0,1},{1,0},{2,3},{3,2},{4,5},{5,4},{6,7},{7,6},{8,9},{9,8},{10,11... | collective-permute-start | bytes 3145736 | tf_op jit(solution)/shard_map/ppermute | solution.py:696
  375.2 15.2 %collective-permute-start.24 = (f32[8,128,128]{2,1,0:T(8,128)S(1)}, f32[8,128,128]{2,1,0:T(8,128)S(1)}, u32[]{:S(2)}, u32[]{:S(2)}) collective-permute-start(f32[8,128,128]{2,1,0:T(8,128)S(1)} %all-to-all-done.6), channel_id=1, source_target_pairs={{0,1},{1,0},{2,3},{3,2},{4,5},{5,4},{6,7},{7,6},{8,9},{9,8},{10,11... | collective-permute-start | bytes 1572872 | tf_op jit(solution)/shard_map/ppermute | solution.py:696
  383.4 6.3 %copy-start.13 = (f32[8,128,128]{2,1,0:T(8,128)}, f32[8,128,128]{2,1,0:T(8,128)S(1)}, u32[]{:S(2)}) copy-start(f32[8,128,128]{2,1,0:T(8,128)S(1)} %collective-permute-done.25) | copy-start | bytes 1572868
  383.4 7.0 %collective-permute-start.26 = (f32[8,128,128]{2,1,0:T(8,128)S(1)}, f32[8,128,128]{2,1,0:T(8,128)}, u32[]{:S(2)}, u32[]{:S(2)}) collective-permute-start(f32[8,128,128]{2,1,0:T(8,128)S(1)} %collective-permute-done.25), channel_id=1, source_target_pairs={{0,1},{1,0},{2,3},{3,2},{4,5},{5,4},{6,7},{7,6},{8,9},{9,8},{10,11... | collective-permute-start | bytes 1572872 | tf_op jit(solution)/shard_map/ppermute | solution.py:696
  390.4 0.8 copy-start.14
  390.4 1.2 copy-start.11
where the time goes:
time: 427 us; the launch traced here: 426 us
  waiting for transfers between devices  140 us (33%)
  Pallas kernels  125 us (29%)
  starting transfers between devices  53.2 us (12%)
  local copies, waits for them, and re-layouts  43.6 us (10%)
  blocking collectives  32.5 us (8%)
  other arithmetic  23 us (5%)
  matrix products  6.99 us (2%)
    pallas_call x3, Pallas kernels, filled_spectrum(): pl.pallas_call(fill_kernel, grid_spec=pltpu.PrefetchScalarGridSpec(num_sc...  65.9 us
    ppermute x9, waiting for transfers between devices, exchanged(): lax.ppermute(packed[p], 'gy', swap(gy, p))  42.8 us
    pallas_call x1, Pallas kernels, result_block(): pl.pallas_call(lambda *refs: result_kernel(offsets, own, devices, groups,...  33.9 us
    ppermute x9, waiting for transfers between devices, gathered(): pieces[place ^ bit] = lax.ppermute(pieces[place], 'gy', swap(peers, bit))  33.6 us
    all_to_all x1, blocking collectives, on_device(): piece = lax.all_to_all(messages, 'gx', 0, 0, tiled=True)  32.5 us
    pallas_call x3, Pallas kernels, packed_section(): pl.pallas_call(lambda *refs: section_kernel(offsets, closing, *refs), gri...  19.6 us
    all_to_all x3, waiting for transfers between devices, sent_lines(): return lax.all_to_all(lines, 'gx', 0, 0, tiled=True)  19.2 us
    all_to_all x1, waiting for transfers between devices, on_device(): lax.all_to_all(jnp.concatenate(turned, axis=3), ('gy', 'gx'), 0, 0, tiled...  18.5 us
  transfers between devices with their start and end apart: 33, of which 14 were waited for; matrix products, arithmetic and copies ran while one was open for 13% of the time, Pallas kernels for 9%

commit v1 on v0

--- a/solution.py
+++ b/solution.py
@@ -32,6 +32,7 @@
     above = lax.ppermute(sides[rows - SWEEPS :], "gx", up)
     below = lax.ppermute(sides[:SWEEPS], "gx", down)
     free = (8 - SWEEPS, 8 - SWEEPS), (0, 0)
+    sides, top, bottom = lax.optimization_barrier((sides, top, bottom))
     inner = jnp.pad(sides, ((SWEEPS, SWEEPS),) + free)
     sides = jnp.pad(jnp.concatenate([above, sides, below], axis=0), ((0, 0),) + free)
     return (block[:SWEEPS], block[:SWEEPS], inner), (top, bottom, sides)
@@ -69,17 +70,12 @@
     return high, low
 
 
-def fill_block(step, base, steps):
-    return jnp.where(step < steps, base[0] + step, base[1] + step - steps)
-
-
 def fill_kernel(
     base, here, above, below, top, bottom, sides, marks, table_high, table_low,
-    given, kept, alternate, edge, punched, once, high, low, folded,
+    spectrum, alternate, edge, punched, once, high, low, folded,
 ):
     step_rows, cols, length = here.shape
-    step = fill_block(pl.program_id(0), base, pl.num_programs(0) // 2)
-    is_given = pl.program_id(0) < pl.num_programs(0) // 2
+    step = pl.program_id(0) + base[0]
     first_row = step * step_rows
     local_row = pl.program_id(0) * step_rows
     period = marks.shape[0]
@@ -165,7 +161,7 @@
         edge[...] += total
 
     rows_each = 8
-    half = given.shape[2]
+    half = spectrum.shape[2]
     order = lax.broadcasted_iota(jnp.int32, (rows_each, cols, half), 1)
 
     @pl.loop(0, step_rows // rows_each)
@@ -176,15 +172,7 @@
         total += jnp.dot(second, table_high[...], preferred_element_type=jnp.float32)
         total += jnp.dot(first, table_high[...], preferred_element_type=jnp.float32)
         total = total.reshape(rows_each, cols, half)
-
-        @pl.when(is_given)
-        def _():
-            given[pl.ds(r * rows_each, rows_each)] = total
-
-        @pl.when(jnp.logical_not(is_given))
-        def _():
-            kept[pl.ds(r * rows_each, rows_each)] = total
-
+        spectrum[pl.ds(r * rows_each, rows_each)] = total
         signed = jnp.sum(jnp.where(order % 2 == 0, total, -total), axis=1)
         alternate[pl.ds(pl.multiple_of(r * rows_each, rows_each), rows_each), :] = signed
 
@@ -206,33 +194,28 @@
     return inner + constants, outer + constants
 
 
-def filled_spectrum(intensity, arrays, starts, count):
+def filled_spectrum(intensity, arrays, first, part):
     rows, cols, length = intensity.shape
-    half = length // 2
-    step_rows = min(STEP_ROWS, count)
-    steps = count // step_rows
+    half, count = length // 2, part.stop - part.start
+    step_rows = STEP_ROWS if part.start % STEP_ROWS == 0 and count % STEP_ROWS == 0 else PART_STEP
     pairs = step_rows // SWEEPS
     last = rows // SWEEPS - 1
     whole = lambda array: pl.BlockSpec(array.shape, lambda i, b: (0,) * array.ndim)
-    here = lambda i, b: (fill_block(i, b, steps), 0, 0)
-    before = lambda i, b: (jnp.maximum(fill_block(i, b, steps) * pairs - 1, 0), 0, 0)
-    after = lambda i, b: (jnp.minimum((fill_block(i, b, steps) + 1) * pairs, last), 0, 0)
+    before = lambda i, b: (jnp.maximum((i + b[0]) * pairs - 1, 0), 0, 0)
+    after = lambda i, b: (jnp.minimum((i + b[0] + 1) * pairs, last), 0, 0)
     padded = (step_rows + 2 * SWEEPS, cols + 2 * MARGIN, length)
-    out_block = (step_rows, cols, half)
-    out = jax.ShapeDtypeStruct((count, cols, half), jnp.float32)
     return pl.pallas_call(
         fill_kernel,
         grid_spec=pltpu.PrefetchScalarGridSpec(
             num_scalar_prefetch=1,
-            grid=(2 * steps,),
+            grid=(count // step_rows,),
             in_specs=[
-                pl.BlockSpec((step_rows, cols, length), here),
+                pl.BlockSpec((step_rows, cols, length), lambda i, b: (i + b[0], 0, 0)),
                 pl.BlockSpec((SWEEPS, cols, length), before),
                 pl.BlockSpec((SWEEPS, cols, length), after),
             ] + [whole(array) for array in arrays],
             out_specs=[
-                pl.BlockSpec(out_block, lambda i, b: (jnp.minimum(i, steps - 1), 0, 0)),
-                pl.BlockSpec(out_block, lambda i, b: (jnp.maximum(i - steps, 0), 0, 0)),
+                pl.BlockSpec((step_rows, cols, half), lambda i, b: (i, 0, 0)),
                 pl.BlockSpec((step_rows, half), lambda i, b: (i, 0)),
                 pl.BlockSpec((cols, 128), lambda i, b: (0, 0)),
             ],
@@ -245,18 +228,17 @@
             ],
         ),
         out_shape=[
-            out,
-            out,
-            jax.ShapeDtypeStruct((2 * count, half), jnp.float32),
+            jax.ShapeDtypeStruct((count, cols, half), jnp.float32),
+            jax.ShapeDtypeStruct((count, half), jnp.float32),
             jax.ShapeDtypeStruct((cols, 128), jnp.float32),
         ],
         compiler_params=pltpu.CompilerParams(vmem_limit_bytes=VMEM_BYTES),
         cost_estimate=pl.CostEstimate(
-            flops=count * cols * length * half * 12,
-            bytes_accessed=count * cols * (length + half) * 8,
+            flops=count * cols * length * half * 6,
+            bytes_accessed=count * cols * (length + half) * 4,
             transcendentals=0,
         ),
-    )(jnp.stack(starts) // step_rows, intensity, intensity, intensity, *arrays)
+    )((first // step_rows).reshape(1), intensity, intensity, intensity, *arrays)
 
 
 def pack(section, offsets):
@@ -369,17 +351,19 @@
     core = lax.rem(col, 2)
     inner_arrays, arrays = fill_arrays(intensity, template, row, col, main)
     given_first, kept_first = (1 - core) * pair_rows, core * pair_rows
-    pieces = []
+    given, kept = [], []
 
     def fill_part(c, after):
-        starts = given_first + parts[c].start, kept_first + parts[c].start
+        part = parts[c]
+        starts = given_first + part.start, kept_first + part.start
         if after is not None:
             starts, after = lax.optimization_barrier((starts, after))
-        inner = parts[c].start >= SWEEPS and parts[c].stop <= pair_rows - SWEEPS
-        pieces.append(
-            filled_spectrum(intensity, inner_arrays if inner else arrays, starts, counts[c])
-        )
-        return lax.ppermute(pieces[c][0], "gy", swap(gy, 1)), after
+        inner = part.start >= SWEEPS and part.stop <= pair_rows - SWEEPS
+        use = inner_arrays if inner else arrays
+        given.append(filled_spectrum(intensity, use, starts[0], part))
+        got = lax.ppermute(given[c][0], "gy", swap(gy, 1))
+        kept.append(filled_spectrum(intensity, use, starts[1], part))
+        return got, after
 
     table_cols = lax.dynamic_slice_in_dim(table, col * cols, cols, 0)
     kept_rows = lax.dynamic_slice_in_dim(table, row * rows + kept_first, pair_rows, 0)
@@ -395,17 +379,17 @@
     for c, count in enumerate(counts):
         closing = c == len(counts) - 1
         got, packed = fill_part(c, packed)
-        held = pieces[c][1]
+        held = kept[c][0]
         if c > 0:
             held, got_lines = lax.optimization_barrier((held, exchanged(packed)))
             lines = sent_lines(got_lines, counts[c - 1], lines)
             values = values + first_axis(lines, table_parts[c - 1])
         if closing:
             given_rows = lax.dynamic_slice_in_dim(table, row * rows + given_first, pair_rows, 0)
-            ordered_rows = [held_rows[part] for part in parts for held_rows in (given_rows, kept_rows)]
+            ordered_rows = [held_rows[part] for held_rows in (given_rows, kept_rows) for part in parts]
             ordered_rows = jnp.concatenate(ordered_rows, axis=0)
-            alternate = jnp.concatenate([piece[2] for piece in pieces], axis=0) / math.sqrt(length)
-            edge = [piece[3][:, : piece[2].shape[0]] for piece in pieces]
+            alternate = jnp.concatenate([piece[1] for piece in given + kept], axis=0) / math.sqrt(length)
+            edge = [piece[2][:, : piece[1].shape[0]] for piece in given + kept]
             edge = jnp.concatenate(edge, axis=1)
             edge = jnp.einsum("ba,bk->ak", edge / math.sqrt(length), table_cols, precision=HIGH)
             edge = edge + jnp.concatenate([alternate, edge[:, half:]], axis=1)
@@ -722,8 +706,7 @@
 def row_parts(rows):
     if rows < 4 * PART_STEP:
         return [slice(0, rows)]
-    middle = rows - 2 * PART_STEP
-    return [slice(middle, middle + PART_STEP), slice(0, middle), slice(middle + PART_STEP, rows)]
+    return [slice(PART_STEP, rows - PART_STEP), slice(0, PART_STEP), slice(rows - PART_STEP, rows)]
 
 
 def square(lower, block):

time: 427 us -> 423 us (level); the launches traced: 426 us -> 415 us
  waiting for transfers between devices: 140 us -> 115 us
  Pallas kernels: 125 us -> 133 us
  other arithmetic: 23 us -> 28.1 us
  local copies, waits for them, and re-layouts: 43.6 us -> 48 us
    ppermute x1, waiting for transfers between devices: 13.5 us -> 0.33 us  [halos(): above = lax.ppermute(sides[rows - SWEEPS:], 'gx', up)]
    ppermute x9, waiting for transfers between devices: 42.8 us -> 29.7 us  [exchanged(): lax.ppermute(packed[p], 'gy', swap(gy, p))]
    pallas_call x3 -> x6, Pallas kernels: 65.9 us -> 73.8 us  [filled_spectrum(): pl.pallas_call(fill_kernel, grid_spec=pltpu.PrefetchScalarGridSpec(num_sc...]
    add x6, other arithmetic: 1.29 us -> 5.66 us  [sent_lines(): sum((got[p][:count] for p in range(first, gy, 2)))]
  transfers between devices with their start and end apart: 33 -> 33, of which waited for: 14 -> 13; matrix products, arithmetic and copies ran while one was open for 13% -> 15% of each run, Pallas kernels for 9% -> 14%
where the time goes in v1:
time: 423 us; the launch traced here: 415 us
  Pallas kernels  133 us (31%)
  waiting for transfers between devices  115 us (27%)
  starting transfers between devices  52.3 us (12%)
  local copies, waits for them, and re-layouts  48 us (11%)
  blocking collectives  32.5 us (8%)
  other arithmetic  28.1 us (7%)
  matrix products  4.91 us (1%)
    pallas_call x6, Pallas kernels, filled_spectrum(): pl.pallas_call(fill_kernel, grid_spec=pltpu.PrefetchScalarGridSpec(num_sc...  73.8 us
    pallas_call x1, Pallas kernels, result_block(): pl.pallas_call(lambda *refs: result_kernel(offsets, own, devices, groups,...  33.9 us
    ppermute x9, waiting for transfers between devices, gathered(): pieces[place ^ bit] = lax.ppermute(pieces[place], 'gy', swap(peers, bit))  33.6 us
    all_to_all x1, blocking collectives, on_device(): piece = lax.all_to_all(messages, 'gx', 0, 0, tiled=True)  32.5 us
    ppermute x9, waiting for transfers between devices, exchanged(): lax.ppermute(packed[p], 'gy', swap(gy, p))  29.7 us
    all_to_all x3, waiting for transfers between devices, sent_lines(): return lax.all_to_all(lines, 'gx', 0, 0, tiled=True)  19.9 us
    pallas_call x3, Pallas kernels, packed_section(): pl.pallas_call(lambda *refs: section_kernel(offsets, closing, *refs), gri...  19.6 us
    all_to_all x1, waiting for transfers between devices, on_device(): lax.all_to_all(jnp.concatenate(turned, axis=3), ('gy', 'gx'), 0, 0, tiled...  18.5 us
  transfers between devices with their start and end apart: 33, of which 13 were waited for; matrix products, arithmetic and copies ran while one was open for 15% of the time, Pallas kernels for 14%

profile of v1, /device:TPU:0, one launch (start us, length us, event | category | flops | bytes accessed | tf_op | source)
XLA Modules:
  0.0 415.4 jit_solution(6992895202932675941)
XLA Ops:
  0.0 2.6 fusion.42
  3.0 2.0 collective-permute-start.1
  5.0 2.1 fusion.41
  7.1 2.3 collective-permute-start.2
  9.4 3.1 collective-permute-start.3
  13.3 1.1 add_maximum_fusion
  15.7 1.2 copy.141
  16.9 1.3 copy.140
  18.2 1.1 copy.139
  19.3 2.1 fusion.10
  21.4 1.8 bitcast_maximum_fusion
  25.3 1.8 copy.145.table_high
  27.1 1.8 copy.146.table_low
  28.9 1.7 tile.4
  30.6 3.1 tile.10.marks
  34.5 4.9 %collective-permute-start.6 = (f32[2,4,512]{2,1,0:T(4,128)S(1)}, f32[2,4,512]{2,1,0:T(4,128)S(1)}, u32[]{:S(2)}, u32[]{:S(2)}) collective-permute-start(f32[2,4,512]{2,1,0:T(4,128)S(1)} %get-tuple-element.185), channel_id=1, source_target_pairs={{4,0},{8,4},{12,8},{16,12},{20,16},{24,20},{28,24},{0,28},{5,1},{9... | collective-permute-start | bytes 49160 | tf_op jit(solution)/shard_map/ppermute | solution.py:33
  39.3 1.2 pad_maximum_fusion
  40.9 2.8 select_maximum_fusion
  43.7 16.8 %shard_map.29 = (f32[16,128,256]{2,1,0:T(8,128)}, f32[16,256]{1,0:T(8,128)}, f32[128,128]{1,0:T(8,128)}) custom-call(s32[1]{0:T(128)} %bitcast.17.base, f32[64,128,512]{2,1,0:T(8,128)} %below.11, f32[64,128,512]{2,1,0:T(8,128)} %below.11, f32[64,128,512]{2,1,0:T(8,128)} %below.11, f32[2,128,512]{2,1,0:T(8,128)} %copy-done, f32[2,128,512]{2,1,0:T(8,128)} %copy-done, ...), custom_call_target="tpu_custom_call" | custom-call | flops 1610612736 | bytes 6291456 | tf_op jit(solution)/shard_map/pallas_call | solution.py:207
  62.8 16.9 %shard_map.28 = (f32[16,128,256]{2,1,0:T(8,128)}, f32[16,256]{1,0:T(8,128)}, f32[128,128]{1,0:T(8,128)}) custom-call(s32[1]{0:T(128)} %bitcast.11.base, f32[64,128,512]{2,1,0:T(8,128)} %below.11, f32[64,128,512]{2,1,0:T(8,128)} %below.11, f32[64,128,512]{2,1,0:T(8,128)} %below.11, f32[2,128,512]{2,1,0:T(8,128)} %copy-done, f32[2,128,512]{2,1,0:T(8,128)} %copy-done, ...), custom_call_target="tpu_custom_call" | custom-call | flops 1610612736 | bytes 6291456 | tf_op jit(solution)/shard_map/pallas_call | solution.py:207
  81.9 8.2 %shard_map.30 = (f32[16,2,8,640]{3,2,1,0:T(8,128)}, f32[16,2,8,640]{3,2,1,0:T(8,128)}, f32[16,2,8,640]{3,2,1,0:T(8,128)}, f32[16,2,8,640]{3,2,1,0:T(8,128)}, f32[4,64,640]{2,1,0:T(8,128)}) custom-call(s32[1]{0:T(128)} %bitcast.3.refs_0_, f32[4,16]{1,0:T(4,128)} %pad_maximum_fusion.4.refs_1_, f32[16,128,256]{2,1,0:T(8,128)} %get-tuple-element.78.refs_2_, ...), custom_call_target="tpu_custom_call" | custom-call | flops 1610612736 | bytes 8388608 | tf_op jit(solution)/shard_map/pallas_call | solution.py:316
  90.1 10.0 %shard_map.32 = (f32[8,128,256]{2,1,0:T(8,128)}, f32[8,256]{1,0:T(8,128)}, f32[128,128]{1,0:T(8,128)}) custom-call(s32[1]{0:T(128)} %bitcast.30.base, f32[64,128,512]{2,1,0:T(8,128)} %below.11, f32[64,128,512]{2,1,0:T(8,128)} %below.11, f32[64,128,512]{2,1,0:T(8,128)} %below.11, f32[2,128,512]{2,1,0:T(8,128)} %copy-done.1, f32[2,128,512]{2,1,0:T(8,128)} %copy-done.2, ...), custom_call_target="tpu_custom_call" | custom-call | flops 805306368 | bytes 3145728 | tf_op jit(solution)/shard_map/pallas_call | solution.py:207
  101.0 1.6 collective-permute-start.8
  105.0 10.1 %shard_map.31 = (f32[8,128,256]{2,1,0:T(8,128)}, f32[8,256]{1,0:T(8,128)}, f32[128,128]{1,0:T(8,128)}) custom-call(s32[1]{0:T(128)} %bitcast.20.base, f32[64,128,512]{2,1,0:T(8,128)} %below.11, f32[64,128,512]{2,1,0:T(8,128)} %below.11, f32[64,128,512]{2,1,0:T(8,128)} %below.11, f32[2,128,512]{2,1,0:T(8,128)} %copy-done.1, f32[2,128,512]{2,1,0:T(8,128)} %copy-done.2, ...), custom_call_target="tpu_custom_call" | custom-call | flops 805306368 | bytes 3145728 | tf_op jit(solution)/shard_map/pallas_call | solution.py:207
  115.1 3.7 collective-permute-done.8
  118.8 12.8 %collective-permute-done.9 = f32[16,2,8,640]{3,2,1,0:T(8,128)} collective-permute-done((f32[16,2,8,640]{3,2,1,0:T(8,128)}, f32[16,2,8,640]{3,2,1,0:T(8,128)}, u32[]{:S(2)}, u32[]{:S(2)}) %collective-permute-start.9) | collective-permute-done | bytes 655392 | tf_op jit(solution)/shard_map/ppermute | solution.py:687
  131.5 1.2 add.243
  132.7 1.2 add.244
  134.0 1.7 copy.151
  135.7 6.4 %all-to-all-start = ((f32[8,2,32,640]{3,1,2,0:T(2,128)}), f32[8,2,32,640]{3,1,2,0:T(2,128)S(1)}, u32[]{:S(2)}, u32[]{:S(2)}) async-start(f32[8,2,32,640]{3,1,2,0:T(2,128)} %copy.151), calls=%async_computation | async-start | bytes 2621440 | tf_op jit(solution)/shard_map/all_to_all | solution.py:697
  142.1 5.6 %shard_map.33 = (f32[8,2,8,640]{3,2,1,0:T(8,128)}, f32[8,2,8,640]{3,2,1,0:T(8,128)}, f32[8,2,8,640]{3,2,1,0:T(8,128)}, f32[8,2,8,640]{3,2,1,0:T(8,128)}, f32[4,64,640]{2,1,0:T(8,128)}) custom-call(s32[1]{0:T(128)} %bitcast.3.refs_0_, f32[4,8]{1,0:T(4,128)} %pad_maximum_fusion.5.refs_1_, f32[8,128,256]{2,1,0:T(8,128)} %get-tuple-element.96.refs_2_, ...), custom_call_target="tpu_custom_call" | custom-call | flops 805306368 | bytes 4194304 | tf_op jit(solution)/shard_map/pallas_call | solution.py:316
  147.9 1.6 collective-permute-start.12
  149.6 10.0 %shard_map.34 = (f32[8,128,256]{2,1,0:T(8,128)}, f32[8,256]{1,0:T(8,128)}, f32[128,128]{1,0:T(8,128)}) custom-call(s32[1]{0:T(128)} %bitcast.32.base, f32[64,128,512]{2,1,0:T(8,128)} %below.11, f32[64,128,512]{2,1,0:T(8,128)} %below.11, f32[64,128,512]{2,1,0:T(8,128)} %below.11, f32[2,128,512]{2,1,0:T(8,128)} %copy-done.1, f32[2,128,512]{2,1,0:T(8,128)} %copy-done.2, ...), custom_call_target="tpu_custom_call" | custom-call | flops 805306368 | bytes 3145728 | tf_op jit(solution)/shard_map/pallas_call | solution.py:207
  159.6 10.1 %shard_map.35 = (f32[8,128,256]{2,1,0:T(8,128)}, f32[8,256]{1,0:T(8,128)}, f32[128,128]{1,0:T(8,128)}) custom-call(s32[1]{0:T(128)} %bitcast.42.base, f32[64,128,512]{2,1,0:T(8,128)} %below.11, f32[64,128,512]{2,1,0:T(8,128)} %below.11, f32[64,128,512]{2,1,0:T(8,128)} %below.11, f32[2,128,512]{2,1,0:T(8,128)} %copy-done.1, f32[2,128,512]{2,1,0:T(8,128)} %copy-done.2, ...), custom_call_target="tpu_custom_call" | custom-call | flops 805306368 | bytes 3145728 | tf_op jit(solution)/shard_map/pallas_call | solution.py:207
  174.4 5.9 %shard_map.36 = (f32[13,2,8,640]{3,2,1,0:T(8,128)}, f32[13,2,8,640]{3,2,1,0:T(8,128)}, f32[13,2,8,640]{3,2,1,0:T(8,128)}, f32[13,2,8,640]{3,2,1,0:T(8,128)}, f32[4,64,640]{2,1,0:T(8,128)}) custom-call(s32[1]{0:T(128)} %bitcast.3.refs_0_, f32[4,8]{1,0:T(4,128)} %pad_maximum_fusion.6.refs_1_, f32[8,128,256]{2,1,0:T(8,128)} %get-tuple-element.115.refs_2_, ...), custom_call_target="tpu_custom_call" | custom-call | flops 805306368 | bytes 4194304 | tf_op jit(solution)/shard_map/pallas_call | solution.py:316
  180.3 1.6 collective-permute-start.15
  183.7 1.3 copy.157
  185.0 5.8 %all-to-all-start.1 = ((f32[8,2,16,640]{3,1,2,0:T(2,128)}), f32[8,2,16,640]{3,1,2,0:T(2,128)S(1)}, u32[]{:S(2)}, u32[]{:S(2)}) async-start(f32[8,2,16,640]{3,1,2,0:T(2,128)} %copy.157), calls=%async_computation.1 | async-start | bytes 1310720 | tf_op jit(solution)/shard_map/all_to_all | solution.py:697
  190.8 4.8 %collective-permute-done.15 = f32[13,2,8,640]{3,2,1,0:T(8,128)} collective-permute-done((f32[13,2,8,640]{3,2,1,0:T(8,128)}, f32[13,2,8,640]{3,2,1,0:T(8,128)}, u32[]{:S(2)}, u32[]{:S(2)}) %collective-permute-start.15) | collective-permute-done | bytes 532512 | tf_op jit(solution)/shard_map/ppermute | solution.py:687
  195.6 1.1 slice_add_fusion.1
  196.7 8.5 %collective-permute-done.17 = f32[13,2,8,640]{3,2,1,0:T(8,128)} collective-permute-done((f32[13,2,8,640]{3,2,1,0:T(8,128)}, f32[13,2,8,640]{3,2,1,0:T(8,128)}, u32[]{:S(2)}, u32[]{:S(2)}) %collective-permute-start.17) | collective-permute-done | bytes 532512 | tf_op jit(solution)/shard_map/ppermute | solution.py:687
  205.2 1.1 slice_add_fusion
  206.3 1.3 slice_add_fusion.2
  208.3 1.4 copy.161
  209.7 5.7 %all-to-all-start.2 = ((f32[8,2,21,640]{3,1,2,0:T(2,128)}), f32[8,2,21,640]{3,1,2,0:T(2,128)S(1)}, u32[]{:S(2)}, u32[]{:S(2)}) async-start(f32[8,2,21,640]{3,1,2,0:T(2,128)} %copy.161), calls=%async_computation.2 | async-start | bytes 1720320 | tf_op jit(solution)/shard_map/all_to_all | solution.py:697
  215.7 1.2 copy-done.10
  216.9 1.9 convolution_bitcast_fusion
  218.8 19.2 %all-to-all-done.2 = f32[8,2,21,640]{3,1,2,0:T(2,128)S(1)} async-done(((f32[8,2,21,640]{3,1,2,0:T(2,128)}), f32[8,2,21,640]{3,1,2,0:T(2,128)S(1)}, u32[]{:S(2)}, u32[]{:S(2)}) %all-to-all-start.2) | async-done | bytes 860192 | tf_op jit(solution)/shard_map/all_to_all | solution.py:697
  241.4 2.4 concatenate.84
  243.8 3.7 all-to-all-start.3
  248.2 18.5 %all-to-all-done.3 = f32[32,2,2,1280]{3,2,1,0:T(2,128)S(1)} async-done(((f32[32,2,2,1280]{3,2,1,0:T(2,128)}), f32[32,2,2,1280]{3,2,1,0:T(2,128)S(1)}, u32[]{:S(2)}, u32[]{:S(2)}) %all-to-all-start.3) | async-done | bytes 655392 | tf_op jit(solution)/shard_map/all_to_all | solution.py:411
  267.7 5.6 %shard_map.37 = (f32[8,288,128]{2,1,0:T(8,128)}, f32[8,256,128]{2,1,0:T(8,128)}, f32[8,128,128]{2,1,0:T(8,128)}) custom-call(f32[2,256,640]{2,1,0:T(8,128)} %bitcast.192, f32[2,64,1280]{2,1,0:T(8,128)} %bitcast.199, f32[2,5,640]{2,1,0:T(8,128)} %copy_multiply_fusion.refs_2_), custom_call_target="tpu_custom_call" | custom-call | tf_op jit(solution)/shard_map/pallas_call | solution.py:546
  273.3 32.5 %all_to_all.35 = f32[8,288,128]{2,1,0:T(8,128)S(1)} all-to-all(f32[8,288,128]{2,1,0:T(8,128)} %get-tuple-element.137), channel_id=1, replica_groups=mesh['gx'=8,'gy'=4] {'gx'}, dimensions={0} | all-to-all | bytes 2359296 | tf_op jit(solution)/shard_map/all_to_all | solution.py:427
  305.8 1.2 collective-permute-start.19
  307.0 3.6 all-to-all-start.5
  310.7 21.5 %collective-permute-done.19 = f32[8,288,128]{2,1,0:T(8,128)} collective-permute-done((f32[8,288,128]{2,1,0:T(8,128)S(1)}, f32[8,288,128]{2,1,0:T(8,128)}, u32[]{:S(2)}, u32[]{:S(2)}) %collective-permute-start.19) | collective-permute-done | bytes 1179680 | tf_op jit(solution)/shard_map/ppermute | solution.py:680
  334.2 1.9 all-to-all-done.5
  337.2 3.5 all-to-all-start.6
  344.5 11.1 %all-to-all-done.6 = f32[8,128,128]{2,1,0:T(8,128)S(1)} async-done(((f32[8,128,128]{2,1,0:T(8,128)}), f32[8,128,128]{2,1,0:T(8,128)S(1)}, u32[]{:S(2)}, u32[]{:S(2)}) %all-to-all-start.6) | async-done | bytes 524320 | tf_op jit(solution)/shard_map/all_to_all | solution.py:427
  355.6 4.4 %collective-permute-done.22 = f32[8,256,128]{2,1,0:T(8,128)} collective-permute-done((f32[8,256,128]{2,1,0:T(8,128)S(1)}, f32[8,256,128]{2,1,0:T(8,128)}, u32[]{:S(2)}, u32[]{:S(2)}) %collective-permute-start.22) | collective-permute-done | bytes 1048608 | tf_op jit(solution)/shard_map/ppermute | solution.py:680
  360.0 1.7 collective-permute-start.25
  365.0 7.8 %collective-permute-done.25 = f32[8,128,128]{2,1,0:T(8,128)S(1)} collective-permute-done((f32[8,128,128]{2,1,0:T(8,128)S(1)}, f32[8,128,128]{2,1,0:T(8,128)S(1)}, u32[]{:S(2)}, u32[]{:S(2)}) %collective-permute-start.25) | collective-permute-done | bytes 524320 | tf_op jit(solution)/shard_map/ppermute | solution.py:680
  374.1 1.3 dynamic-update-slice.4
  381.0 33.9 %shard_map.38 = f32[64,128,512]{2,1,0:T(8,128)} custom-call(s32[4]{0:T(128)} %pad_add_fusion.refs_0_, f32[64,640]{1,0:T(8,128)} %bitcast.211, f32[64,256]{1,0:T(8,128)} %slice.506.refs_2_, f32[128,128]{1,0:T(8,128)} %pad.19.refs_3_, bf16[128,256]{1,0:T(8,128)(2,1)} %fusion.28.refs_4_, bf16[256,256]{1,0:T(8,128)(2,1)} %fusion.20.refs_5_, ...), custom_call_target="tpu_custom_call" | custom-call | tf_op jit(solution)/shard_map/pallas_call | solution.py:651
  (206 shorter events, 43.1 us)
Async XLA Ops:
  2.6 31.1 %collective-permute-start = (f32[64,2,512]{2,1,0:T(2,128)}, f32[64,2,512]{2,1,0:T(2,128)S(1)}, u32[]{:S(2)}, u32[]{:S(2)}) collective-permute-start(f32[64,2,512]{2,1,0:T(2,128)} %get-tuple-element.151), channel_id=1, source_target_pairs={{0,1},{1,2},{2,3},{3,0},{4,5},{5,6},{6,7},{7,4},{8,9},{9,10},{10,1... | collective-permute-start | bytes 786440 | tf_op jit(solution)/shard_map/ppermute | solution.py:29
  3.0 9.5 %slice-start.1 = ((s32[32,32,32]{2,1,0:T(8,128)}), s32[31,32,32]{2,1,0:T(8,128)S(1)}, s32[]{:S(2)}) async-start(s32[32,32,32]{2,1,0:T(8,128)} %param.3), calls=%async_computation.8 | async-start | bytes 1015808 | tf_op jit(solution)/shard_map/jit(_roll_static)/slice | solution.py:42
  3.0 30.6 %collective-permute-start.1 = (f32[64,2,512]{2,1,0:T(2,128)}, f32[64,2,512]{2,1,0:T(2,128)}, u32[]{:S(2)}, u32[]{:S(2)}) collective-permute-start(f32[64,2,512]{2,1,0:T(2,128)} %get-tuple-element.152), channel_id=1, source_target_pairs={{1,0},{2,1},{3,2},{0,3},{5,4},{6,5},{7,6},{4,7},{9,8},{10,9},{11,1... | collective-permute-start | bytes 786440 | tf_op jit(solution)/shard_map/ppermute | solution.py:30
  7.1 7.3 %copy-start = (f32[2,128,512]{2,1,0:T(8,128)}, f32[2,128,512]{2,1,0:T(8,128)S(1)}, u32[]{:S(2)}) copy-start(f32[2,128,512]{2,1,0:T(8,128)S(1)} %get-tuple-element.150.top.bottom) | copy-start | bytes 1572868
  7.1 6.2 %copy-start.6 = (s32[32,32,32]{2,1,0:T(8,128)S(1)}, s32[32,32,32]{2,1,0:T(8,128)}, u32[]{:S(2)}) copy-start(s32[32,32,32]{2,1,0:T(8,128)} %param.3) | copy-start | bytes 393220
  7.1 6.2 %slice-start = ((s32[32,32,32]{2,1,0:T(8,128)}), s32[1,32,32]{2,1,0:T(8,128)S(1)}, s32[]{:S(2)}) async-start(s32[32,32,32]{2,1,0:T(8,128)} %param.3), calls=%async_computation.7 | async-start | bytes 32768 | tf_op jit(solution)/shard_map/jit(_roll_static)/slice | solution.py:42
  7.1 33.4 %collective-permute-start.2 = (f32[2,128,512]{2,1,0:T(8,128)}, f32[2,128,512]{2,1,0:T(8,128)S(1)}, u32[]{:S(2)}, u32[]{:S(2)}) collective-permute-start(f32[2,128,512]{2,1,0:T(8,128)} %get-tuple-element.149), channel_id=1, source_target_pairs={{0,4},{4,8},{8,12},{12,16},{16,20},{20,24},{24,28},{28,0},{1,5},{5... | collective-permute-start | bytes 1572872 | tf_op jit(solution)/shard_map/ppermute | solution.py:27
  9.4 31.1 %collective-permute-start.3 = (f32[2,128,512]{2,1,0:T(8,128)S(1)}, f32[2,128,512]{2,1,0:T(8,128)S(1)}, u32[]{:S(2)}, u32[]{:S(2)}) collective-permute-start(f32[2,128,512]{2,1,0:T(8,128)S(1)} %get-tuple-element.150.top.bottom), channel_id=1, source_target_pairs={{4,0},{8,4},{12,8},{16,12},{20,16},{24,20},{28,24},{0,28},{5,1},{9... | collective-permute-start | bytes 1572872 | tf_op jit(solution)/shard_map/ppermute | solution.py:28
  34.4 6.5 %collective-permute-start.5 = (f32[2,4,512]{2,1,0:T(4,128)S(1)}, f32[2,4,512]{2,1,0:T(4,128)S(1)}, u32[]{:S(2)}, u32[]{:S(2)}) collective-permute-start(f32[2,4,512]{2,1,0:T(4,128)S(1)} %get-tuple-element.184), channel_id=1, source_target_pairs={{0,4},{4,8},{8,12},{12,16},{16,20},{20,24},{24,28},{28,0},{1,5},{5... | collective-permute-start | bytes 49160 | tf_op jit(solution)/shard_map/ppermute | solution.py:32
  34.5 6.4 %collective-permute-start.6 = (f32[2,4,512]{2,1,0:T(4,128)S(1)}, f32[2,4,512]{2,1,0:T(4,128)S(1)}, u32[]{:S(2)}, u32[]{:S(2)}) collective-permute-start(f32[2,4,512]{2,1,0:T(4,128)S(1)} %get-tuple-element.185), channel_id=1, source_target_pairs={{4,0},{8,4},{12,8},{16,12},{20,16},{24,20},{28,24},{0,28},{5,1},{9... | collective-permute-start | bytes 49160 | tf_op jit(solution)/shard_map/ppermute | solution.py:33
  40.5 3.2 copy-start.1
  40.5 3.1 copy-start.2
  60.5 19.2 %collective-permute-start.4 = (f32[16,128,256]{2,1,0:T(8,128)}, f32[16,128,256]{2,1,0:T(8,128)}, u32[]{:S(2)}, u32[]{:S(2)}) collective-permute-start(f32[16,128,256]{2,1,0:T(8,128)} %get-tuple-element.79), channel_id=1, source_target_pairs={{0,1},{1,0},{2,3},{3,2},{4,5},{5,4},{6,7},{7,6},{8,9},{9,8},{10,11... | collective-permute-start | bytes 6291464 | tf_op jit(solution)/shard_map/ppermute | solution.py:364
  100.0 42.1 %collective-permute-start.10 = (f32[8,128,256]{2,1,0:T(8,128)}, f32[8,128,256]{2,1,0:T(8,128)}, u32[]{:S(2)}, u32[]{:S(2)}) collective-permute-start(f32[8,128,256]{2,1,0:T(8,128)} %get-tuple-element.98), channel_id=1, source_target_pairs={{0,1},{1,0},{2,3},{3,2},{4,5},{5,4},{6,7},{7,6},{8,9},{9,8},{10,11... | collective-permute-start | bytes 3145736 | tf_op jit(solution)/shard_map/ppermute | solution.py:364
  100.4 4.5 %copy-start.22 = (f32[16,256]{1,0:T(8,128)S(1)}, f32[16,256]{1,0:T(8,128)}, u32[]{:S(2)}) copy-start(f32[16,256]{1,0:T(8,128)} %get-tuple-element.124) | copy-start | bytes 49156
  100.7 14.4 %collective-permute-start.7 = (f32[16,2,8,640]{3,2,1,0:T(8,128)}, f32[16,2,8,640]{3,2,1,0:T(8,128)S(1)}, u32[]{:S(2)}, u32[]{:S(2)}) collective-permute-start(f32[16,2,8,640]{3,2,1,0:T(8,128)} %get-tuple-element.89), channel_id=1, source_target_pairs={{0,1},{1,0},{2,3},{3,2},{4,5},{5,4},{6,7},{7,6},{8,9},{9,8},{10,11... | collective-permute-start | bytes 1966088 | tf_op jit(solution)/shard_map/ppermute | solution.py:687
  101.0 17.8 %collective-permute-start.8 = (f32[16,2,8,640]{3,2,1,0:T(8,128)}, f32[16,2,8,640]{3,2,1,0:T(8,128)S(1)}, u32[]{:S(2)}, u32[]{:S(2)}) collective-permute-start(f32[16,2,8,640]{3,2,1,0:T(8,128)} %get-tuple-element.90), channel_id=1, source_target_pairs={{0,2},{1,3},{2,0},{3,1},{4,6},{5,7},{6,4},{7,5},{8,10},{9,11},{10,... | collective-permute-start | bytes 1966088 | tf_op jit(solution)/shard_map/ppermute | solution.py:687
  102.6 29.0 %collective-permute-start.9 = (f32[16,2,8,640]{3,2,1,0:T(8,128)}, f32[16,2,8,640]{3,2,1,0:T(8,128)}, u32[]{:S(2)}, u32[]{:S(2)}) collective-permute-start(f32[16,2,8,640]{3,2,1,0:T(8,128)} %get-tuple-element.91), channel_id=1, source_target_pairs={{0,3},{1,2},{2,1},{3,0},{4,7},{5,6},{6,5},{7,4},{8,11},{9,10},{10,... | collective-permute-start | bytes 1966088 | tf_op jit(solution)/shard_map/ppermute | solution.py:687
  105.0 10.1 %copy-start.24 = (f32[8,256]{1,0:T(8,128)S(1)}, f32[8,256]{1,0:T(8,128)}, u32[]{:S(2)}) copy-start(f32[8,256]{1,0:T(8,128)} %get-tuple-element.125) | copy-start | bytes 24580
  105.0 26.6 %copy-start.12 = (f32[16,2,8,640]{3,2,1,0:T(8,128)S(1)}, f32[16,2,8,640]{3,2,1,0:T(8,128)}, u32[]{:S(2)}) copy-start(f32[16,2,8,640]{3,2,1,0:T(8,128)} %get-tuple-element.92) | copy-start | bytes 1966084
  118.8 12.8 %copy-start.13 = (f32[16,2,8,640]{3,2,1,0:T(8,128)}, f32[16,2,8,640]{3,2,1,0:T(8,128)S(1)}, u32[]{:S(2)}) copy-start(f32[16,2,8,640]{3,2,1,0:T(8,128)S(1)} %collective-permute-done.8) | copy-start | bytes 1966084
  135.7 47.9 %all-to-all-start = ((f32[8,2,32,640]{3,1,2,0:T(2,128)}), f32[8,2,32,640]{3,1,2,0:T(2,128)S(1)}, u32[]{:S(2)}, u32[]{:S(2)}) async-start(f32[8,2,32,640]{3,1,2,0:T(2,128)} %copy.151), calls=%async_computation | async-start | bytes 2621440 | tf_op jit(solution)/shard_map/all_to_all | solution.py:697
  147.7 26.7 %collective-permute-start.11 = (f32[8,2,8,640]{3,2,1,0:T(8,128)}, f32[8,2,8,640]{3,2,1,0:T(8,128)S(1)}, u32[]{:S(2)}, u32[]{:S(2)}) collective-permute-start(f32[8,2,8,640]{3,2,1,0:T(8,128)} %get-tuple-element.107), channel_id=1, source_target_pairs={{0,1},{1,0},{2,3},{3,2},{4,5},{5,4},{6,7},{7,6},{8,9},{9,8},{10,11... | collective-permute-start | bytes 983048 | tf_op jit(solution)/shard_map/ppermute | solution.py:687
  147.9 26.5 %collective-permute-start.12 = (f32[8,2,8,640]{3,2,1,0:T(8,128)}, f32[8,2,8,640]{3,2,1,0:T(8,128)S(1)}, u32[]{:S(2)}, u32[]{:S(2)}) collective-permute-start(f32[8,2,8,640]{3,2,1,0:T(8,128)} %get-tuple-element.108), channel_id=1, source_target_pairs={{0,2},{1,3},{2,0},{3,1},{4,6},{5,7},{6,4},{7,5},{8,10},{9,11},{10,... | collective-permute-start | bytes 983048 | tf_op jit(solution)/shard_map/ppermute | solution.py:687
  149.5 24.9 %collective-permute-start.13 = (f32[8,2,8,640]{3,2,1,0:T(8,128)}, f32[8,2,8,640]{3,2,1,0:T(8,128)}, u32[]{:S(2)}, u32[]{:S(2)}) collective-permute-start(f32[8,2,8,640]{3,2,1,0:T(8,128)} %get-tuple-element.109), channel_id=1, source_target_pairs={{0,3},{1,2},{2,1},{3,0},{4,7},{5,6},{6,5},{7,4},{8,11},{9,10},{10,... | collective-permute-start | bytes 983048 | tf_op jit(solution)/shard_map/ppermute | solution.py:687
  159.5 10.7 %copy-start.18 = (f32[128,128]{1,0:T(8,128)S(1)}, f32[128,128]{1,0:T(8,128)}, u32[]{:S(2)}) copy-start(f32[128,128]{1,0:T(8,128)} %get-tuple-element.118) | copy-start | bytes 196612
  159.5 10.7 %copy-start.19 = (f32[128,128]{1,0:T(8,128)S(1)}, f32[128,128]{1,0:T(8,128)}, u32[]{:S(2)}) copy-start(f32[128,128]{1,0:T(8,128)} %get-tuple-element.121) | copy-start | bytes 196612
  159.5 10.7 %copy-start.20 = (f32[128,128]{1,0:T(8,128)S(1)}, f32[128,128]{1,0:T(8,128)}, u32[]{:S(2)}) copy-start(f32[128,128]{1,0:T(8,128)} %get-tuple-element.119) | copy-start | bytes 196612
  159.5 12.4 %copy-start.21 = (f32[16,256]{1,0:T(8,128)S(1)}, f32[16,256]{1,0:T(8,128)}, u32[]{:S(2)}) copy-start(f32[16,256]{1,0:T(8,128)} %get-tuple-element.127) | copy-start | bytes 49156
  159.6 12.4 %copy-start.23 = (f32[8,256]{1,0:T(8,128)S(1)}, f32[8,256]{1,0:T(8,128)}, u32[]{:S(2)}) copy-start(f32[8,256]{1,0:T(8,128)} %get-tuple-element.128) | copy-start | bytes 24580
  159.6 12.4 %copy-start.25 = (f32[8,256]{1,0:T(8,128)S(1)}, f32[8,256]{1,0:T(8,128)}, u32[]{:S(2)}) copy-start(f32[8,256]{1,0:T(8,128)} %get-tuple-element.129) | copy-start | bytes 24580
  169.7 4.7 %collective-permute-start.14 = (f32[8,128,256]{2,1,0:T(8,128)}, f32[8,128,256]{2,1,0:T(8,128)}, u32[]{:S(2)}, u32[]{:S(2)}) collective-permute-start(f32[8,128,256]{2,1,0:T(8,128)} %get-tuple-element.117), channel_id=1, source_target_pairs={{0,1},{1,0},{2,3},{3,2},{4,5},{5,4},{6,7},{7,6},{8,9},{9,8},{10,11... | collective-permute-start | bytes 3145736 | tf_op jit(solution)/shard_map/ppermute | solution.py:364
  174.4 7.5 %copy-start.17 = (f32[8,2,8,640]{3,2,1,0:T(8,128)S(1)}, f32[8,2,8,640]{3,2,1,0:T(8,128)}, u32[]{:S(2)}) copy-start(f32[8,2,8,640]{3,2,1,0:T(8,128)} %get-tuple-element.110) | copy-start | bytes 983044
  180.3 15.3 %collective-permute-start.15 = (f32[13,2,8,640]{3,2,1,0:T(8,128)}, f32[13,2,8,640]{3,2,1,0:T(8,128)}, u32[]{:S(2)}, u32[]{:S(2)}) collective-permute-start(f32[13,2,8,640]{3,2,1,0:T(8,128)} %get-tuple-element.132), channel_id=1, source_target_pairs={{0,2},{1,3},{2,0},{3,1},{4,6},{5,7},{6,4},{7,5},{8,10},{9,11},{10,... | collective-permute-start | bytes 1597448 | tf_op jit(solution)/shard_map/ppermute | solution.py:687
  183.0 13.7 %collective-permute-start.16 = (f32[13,2,8,640]{3,2,1,0:T(8,128)}, f32[13,2,8,640]{3,2,1,0:T(8,128)}, u32[]{:S(2)}, u32[]{:S(2)}) collective-permute-start(f32[13,2,8,640]{3,2,1,0:T(8,128)} %get-tuple-element.133), channel_id=1, source_target_pairs={{0,1},{1,0},{2,3},{3,2},{4,5},{5,4},{6,7},{7,6},{8,9},{9,8},{10,11... | collective-permute-start | bytes 1597448 | tf_op jit(solution)/shard_map/ppermute | solution.py:687
  183.1 22.1 %collective-permute-start.17 = (f32[13,2,8,640]{3,2,1,0:T(8,128)}, f32[13,2,8,640]{3,2,1,0:T(8,128)}, u32[]{:S(2)}, u32[]{:S(2)}) collective-permute-start(f32[13,2,8,640]{3,2,1,0:T(8,128)} %get-tuple-element.134), channel_id=1, source_target_pairs={{0,3},{1,2},{2,1},{3,0},{4,7},{5,6},{6,5},{7,4},{8,11},{9,10},{10,... | collective-permute-start | bytes 1597448 | tf_op jit(solution)/shard_map/ppermute | solution.py:687
  183.7 11.9 %copy-start.9 = (f32[8,2,32,640]{3,1,2,0:T(2,128)}, f32[8,2,32,640]{3,1,2,0:T(2,128)S(1)}, u32[]{:S(2)}) copy-start(f32[8,2,32,640]{3,1,2,0:T(2,128)S(1)} %all-to-all-done) | copy-start | bytes 3932164
  185.0 23.4 %all-to-all-start.1 = ((f32[8,2,16,640]{3,1,2,0:T(2,128)}), f32[8,2,16,640]{3,1,2,0:T(2,128)S(1)}, u32[]{:S(2)}, u32[]{:S(2)}) async-start(f32[8,2,16,640]{3,1,2,0:T(2,128)} %copy.157), calls=%async_computation.1 | async-start | bytes 1310720 | tf_op jit(solution)/shard_map/all_to_all | solution.py:697
  209.7 28.3 %all-to-all-start.2 = ((f32[8,2,21,640]{3,1,2,0:T(2,128)}), f32[8,2,21,640]{3,1,2,0:T(2,128)S(1)}, u32[]{:S(2)}, u32[]{:S(2)}) async-start(f32[8,2,21,640]{3,1,2,0:T(2,128)} %copy.161), calls=%async_computation.2 | async-start | bytes 1720320 | tf_op jit(solution)/shard_map/all_to_all | solution.py:697
  215.6 1.3 copy-start.10
  238.1 1.3 copy-start.26
  240.2 1.1 copy-start.4
  243.8 22.9 %all-to-all-start.3 = ((f32[32,2,2,1280]{3,2,1,0:T(2,128)}), f32[32,2,2,1280]{3,2,1,0:T(2,128)S(1)}, u32[]{:S(2)}, u32[]{:S(2)}) async-start(f32[32,2,2,1280]{3,2,1,0:T(2,128)} %concatenate.84), calls=%async_computation.3 | async-start | bytes 1310720 | tf_op jit(solution)/shard_map/all_to_all | solution.py:411
  305.8 31.4 %copy-start.3 = (f32[8,288,128]{2,1,0:T(8,128)}, f32[8,288,128]{2,1,0:T(8,128)S(1)}, u32[]{:S(2)}) copy-start(f32[8,288,128]{2,1,0:T(8,128)S(1)} %all_to_all.35) | copy-start | bytes 3538948
  305.8 26.4 %collective-permute-start.19 = (f32[8,288,128]{2,1,0:T(8,128)S(1)}, f32[8,288,128]{2,1,0:T(8,128)}, u32[]{:S(2)}, u32[]{:S(2)}) collective-permute-start(f32[8,288,128]{2,1,0:T(8,128)S(1)} %all_to_all.35), channel_id=1, source_target_pairs={{0,2},{1,3},{2,0},{3,1},{4,6},{5,7},{6,4},{7,5},{8,10},{9,11},{10,... | collective-permute-start | bytes 3538952 | tf_op jit(solution)/shard_map/ppermute | solution.py:680
  307.0 29.1 %all-to-all-start.5 = ((f32[8,256,128]{2,1,0:T(8,128)}), f32[8,256,128]{2,1,0:T(8,128)S(1)}, u32[]{:S(2)}, u32[]{:S(2)}) async-start(f32[8,256,128]{2,1,0:T(8,128)} %get-tuple-element.140), calls=%async_computation.5 | async-start | bytes 2097152 | tf_op jit(solution)/shard_map/all_to_all | solution.py:427
  310.5 25.6 %collective-permute-start.18 = (f32[8,288,128]{2,1,0:T(8,128)S(1)}, f32[8,288,128]{2,1,0:T(8,128)S(1)}, u32[]{:S(2)}, u32[]{:S(2)}) collective-permute-start(f32[8,288,128]{2,1,0:T(8,128)S(1)} %all_to_all.35), channel_id=1, source_target_pairs={{0,1},{1,0},{2,3},{3,2},{4,5},{5,4},{6,7},{7,6},{8,9},{9,8},{10,11... | collective-permute-start | bytes 3538952 | tf_op jit(solution)/shard_map/ppermute | solution.py:680
  332.1 10.4 %collective-permute-start.20 = (f32[8,288,128]{2,1,0:T(8,128)}, f32[8,288,128]{2,1,0:T(8,128)}, u32[]{:S(2)}, u32[]{:S(2)}) collective-permute-start(f32[8,288,128]{2,1,0:T(8,128)} %collective-permute-done.19), channel_id=1, source_target_pairs={{0,1},{1,0},{2,3},{3,2},{4,5},{5,4},{6,7},{7,6},{8,9},{9,8},{10,11... | collective-permute-start | bytes 3538952 | tf_op jit(solution)/shard_map/ppermute | solution.py:680
  336.1 7.4 %copy-start.5 = (f32[8,256,128]{2,1,0:T(8,128)}, f32[8,256,128]{2,1,0:T(8,128)S(1)}, u32[]{:S(2)}) copy-start(f32[8,256,128]{2,1,0:T(8,128)S(1)} %all-to-all-done.5) | copy-start | bytes 3145732
  336.1 1.1 copy-start.8
  336.1 23.9 %collective-permute-start.22 = (f32[8,256,128]{2,1,0:T(8,128)S(1)}, f32[8,256,128]{2,1,0:T(8,128)}, u32[]{:S(2)}, u32[]{:S(2)}) collective-permute-start(f32[8,256,128]{2,1,0:T(8,128)S(1)} %all-to-all-done.5), channel_id=1, source_target_pairs={{0,2},{1,3},{2,0},{3,1},{4,6},{5,7},{6,4},{7,5},{8,10},{9,11},{10,... | collective-permute-start | bytes 3145736 | tf_op jit(solution)/shard_map/ppermute | solution.py:680
  336.7 23.3 %collective-permute-start.21 = (f32[8,256,128]{2,1,0:T(8,128)S(1)}, f32[8,256,128]{2,1,0:T(8,128)}, u32[]{:S(2)}, u32[]{:S(2)}) collective-permute-start(f32[8,256,128]{2,1,0:T(8,128)S(1)} %all-to-all-done.5), channel_id=1, source_target_pairs={{0,1},{1,0},{2,3},{3,2},{4,5},{5,4},{6,7},{7,6},{8,9},{9,8},{10,11... | collective-permute-start | bytes 3145736 | tf_op jit(solution)/shard_map/ppermute | solution.py:680
  337.2 18.4 %all-to-all-start.6 = ((f32[8,128,128]{2,1,0:T(8,128)}), f32[8,128,128]{2,1,0:T(8,128)S(1)}, u32[]{:S(2)}, u32[]{:S(2)}) async-start(f32[8,128,128]{2,1,0:T(8,128)} %get-tuple-element.145), calls=%async_computation.6 | async-start | bytes 1048576 | tf_op jit(solution)/shard_map/all_to_all | solution.py:427
  344.4 19.5 %copy-start.16 = (f32[2,2,32,640]{3,2,1,0:T(8,128)}, f32[2,2,32,640]{3,2,1,0:T(8,128)S(1)}, u32[]{:S(2)}) copy-start(f32[2,2,32,640]{3,2,1,0:T(8,128)S(1)} %copy.173) | copy-start | bytes 983044
  355.6 21.5 %copy-start.7 = (f32[8,128,128]{2,1,0:T(8,128)}, f32[8,128,128]{2,1,0:T(8,128)S(1)}, u32[]{:S(2)}) copy-start(f32[8,128,128]{2,1,0:T(8,128)S(1)} %all-to-all-done.6) | copy-start | bytes 1572868
  360.0 12.8 %collective-permute-start.25 = (f32[8,128,128]{2,1,0:T(8,128)S(1)}, f32[8,128,128]{2,1,0:T(8,128)S(1)}, u32[]{:S(2)}, u32[]{:S(2)}) collective-permute-start(f32[8,128,128]{2,1,0:T(8,128)S(1)} %all-to-all-done.6), channel_id=1, source_target_pairs={{0,2},{1,3},{2,0},{3,1},{4,6},{5,7},{6,4},{7,5},{8,10},{9,11},{10,... | collective-permute-start | bytes 1572872 | tf_op jit(solution)/shard_map/ppermute | solution.py:680
  361.7 18.1 %collective-permute-start.23 = (f32[8,256,128]{2,1,0:T(8,128)}, f32[8,256,128]{2,1,0:T(8,128)S(1)}, u32[]{:S(2)}, u32[]{:S(2)}) collective-permute-start(f32[8,256,128]{2,1,0:T(8,128)} %collective-permute-done.22), channel_id=1, source_target_pairs={{0,1},{1,0},{2,3},{3,2},{4,5},{5,4},{6,7},{7,6},{8,9},{9,8},{10,11... | collective-permute-start | bytes 3145736 | tf_op jit(solution)/shard_map/ppermute | solution.py:680
  364.5 15.3 %collective-permute-start.24 = (f32[8,128,128]{2,1,0:T(8,128)S(1)}, f32[8,128,128]{2,1,0:T(8,128)S(1)}, u32[]{:S(2)}, u32[]{:S(2)}) collective-permute-start(f32[8,128,128]{2,1,0:T(8,128)S(1)} %all-to-all-done.6), channel_id=1, source_target_pairs={{0,1},{1,0},{2,3},{3,2},{4,5},{5,4},{6,7},{7,6},{8,9},{9,8},{10,11... | collective-permute-start | bytes 1572872 | tf_op jit(solution)/shard_map/ppermute | solution.py:680
  372.8 6.4 %copy-start.14 = (f32[8,128,128]{2,1,0:T(8,128)}, f32[8,128,128]{2,1,0:T(8,128)S(1)}, u32[]{:S(2)}) copy-start(f32[8,128,128]{2,1,0:T(8,128)S(1)} %collective-permute-done.25) | copy-start | bytes 1572868
  372.8 7.0 %collective-permute-start.26 = (f32[8,128,128]{2,1,0:T(8,128)S(1)}, f32[8,128,128]{2,1,0:T(8,128)}, u32[]{:S(2)}, u32[]{:S(2)}) collective-permute-start(f32[8,128,128]{2,1,0:T(8,128)S(1)} %collective-permute-done.25), channel_id=1, source_target_pairs={{0,1},{1,0},{2,3},{3,2},{4,5},{5,4},{6,7},{7,6},{8,9},{9,8},{10,11... | collective-permute-start | bytes 1572872 | tf_op jit(solution)/shard_map/ppermute | solution.py:680
  379.8 0.8 copy-start.15
  379.8 1.2 copy-start.11

commit v2 on v1

--- a/solution.py
+++ b/solution.py
@@ -2,6 +2,7 @@
 
 import jax
 import jax.numpy as jnp
+import numpy as np
 from jax import lax
 from jax.experimental import pallas as pl
 from jax.experimental.pallas import tpu as pltpu
@@ -20,7 +21,10 @@
     return up, [(j, i) for i, j in up]
 
 
-def halos(block):
+FREE = ((8 - SWEEPS, 8 - SWEEPS), (0, 0))
+
+
+def faces(block):
     rows, cols, _ = block.shape
     up, down = ring("gx")
     right, left = ring("gy")
@@ -28,14 +32,17 @@
     bottom = lax.ppermute(block[:SWEEPS], "gx", down)
     before = lax.ppermute(block[:, cols - SWEEPS :], "gy", right)
     after = lax.ppermute(block[:, :SWEEPS], "gy", left)
-    sides = jnp.concatenate([before, after], axis=1)
-    above = lax.ppermute(sides[rows - SWEEPS :], "gx", up)
-    below = lax.ppermute(sides[:SWEEPS], "gx", down)
-    free = (8 - SWEEPS, 8 - SWEEPS), (0, 0)
-    sides, top, bottom = lax.optimization_barrier((sides, top, bottom))
-    inner = jnp.pad(sides, ((SWEEPS, SWEEPS),) + free)
-    sides = jnp.pad(jnp.concatenate([above, sides, below], axis=0), ((0, 0),) + free)
-    return (block[:SWEEPS], block[:SWEEPS], inner), (top, bottom, sides)
+    return lax.optimization_barrier((top, bottom, jnp.concatenate([before, after], axis=1)))
+
+
+def corners(sides):
+    up, down = ring("gx")
+    above = lax.ppermute(sides[sides.shape[0] - SWEEPS :], "gx", up)
+    return above, lax.ppermute(sides[:SWEEPS], "gx", down)
+
+
+def with_corners(sides, ends):
+    return jnp.pad(jnp.concatenate([ends[0], sides, ends[1]], axis=0), ((0, 0),) + FREE)
 
 
 def mirror(values, axis):
@@ -52,9 +59,9 @@
 
 
 def cosine_table(length):
-    position = jnp.arange(length, dtype=jnp.int32)
-    phases = jnp.mod(position[:, None] * position[None, : length // 2 + 1], length)
-    return jnp.cos(phases.astype(jnp.float32) * (2.0 * math.pi / length)) / math.sqrt(length)
+    position = np.arange(length)
+    phases = np.mod(position[:, None] * position[None, : length // 2 + 1], length)
+    return (np.cos(phases * (2.0 * math.pi / length)) / math.sqrt(length)).astype(np.float32)
 
 
 MARGIN = 16
@@ -182,16 +189,50 @@
     return rounded.astype(jnp.bfloat16), (table - rounded).astype(jnp.bfloat16)
 
 
-def fill_arrays(intensity, template, row, col, main):
-    rows, cols, length = intensity.shape
-    united = symmetric_marks(template)
-    period = united.shape[0]
-    offsets = (jnp.mod(row * rows - SWEEPS, period), jnp.mod(col * cols - MARGIN, period))
-    marks = jnp.roll(united, (-offsets[0], -offsets[1]), (0, 1)).astype(jnp.float32) / 6.0
-    marks = jnp.tile(marks, (1, 1, 128 // period))
-    constants = (marks,) + rounded_parts(main)
-    inner, outer = halos(intensity)
-    return inner + constants, outer + constants
+def marks_kernel(shifts, template, out, held):
+    period = template.shape[0]
+    repeats = held.shape[1] // period
+    line = lax.broadcasted_iota(jnp.int32, (period, period), 0)
+    across = lax.broadcasted_iota(jnp.int32, (period, period), 1)
+    flip = jnp.where((line + across) % period == 0, 1.0, 0.0)
+    for i in range(period):
+        plane = jnp.maximum(template[i], template[-i % period]).astype(jnp.float32)
+        plane = jnp.maximum(plane, jnp.dot(flip, plane, preferred_element_type=jnp.float32))
+        plane = jnp.maximum(plane, jnp.dot(plane, flip, preferred_element_type=jnp.float32))
+        plane = jnp.maximum(plane, plane.T)
+        held[i * period : (i + 1) * period, :] = jnp.concatenate([plane] * repeats, axis=1)
+    for i in range(period):
+        plane = held[i * period : (i + 1) * period, :]
+        turned = held[pl.ds(i, period, stride=period), :]
+        back = turned[:, :period].T
+        plane = jnp.maximum(jnp.maximum(plane, turned), jnp.concatenate([back] * repeats, axis=1))
+        plane = jnp.where(plane == 1.0, 1.0 / 6.0, 0.0)
+        shift = shifts[1]
+        out[(i - shifts[0]) % period] = jnp.concatenate([plane[shift:], plane[:shift]], axis=0)
+
+
+def hole_marks(template, row, col, rows, cols):
+    period = template.shape[0]
+    shape = (period, period, 128)
+    if rows % period == 0 and cols % period == 0:
+        shifts = (-SWEEPS % period, -MARGIN % period)
+        return pl.pallas_call(
+            lambda *refs: marks_kernel(shifts, *refs),
+            in_specs=[pl.BlockSpec(memory_space=pltpu.VMEM)],
+            out_specs=pl.BlockSpec(memory_space=pltpu.VMEM),
+            out_shape=jax.ShapeDtypeStruct(shape, jnp.float32),
+            scratch_shapes=[pltpu.VMEM((period * period, 128), jnp.float32)],
+        )(template)
+    shifts = (jnp.mod(row * rows - SWEEPS, period), jnp.mod(col * cols - MARGIN, period))
+    marks = jnp.roll(symmetric_marks(template), (-shifts[0], -shifts[1]), (0, 1))
+    return jnp.tile(marks.astype(jnp.float32) / 6.0, (1, 1, 128 // period))
+
+
+def fill_constants(intensity, template, row, col, main):
+    rows, cols, _ = intensity.shape
+    high = main.astype(jnp.bfloat16)
+    low = (main - high.astype(np.float32)).astype(jnp.bfloat16)
+    return hole_marks(template, row, col, rows, cols), jnp.asarray(high), jnp.asarray(low)
 
 
 def filled_spectrum(intensity, arrays, first, part):
@@ -342,28 +383,44 @@
     blocks, own, slabs = half // block, block // devices, gx // 2
     offsets = [block * b * (b + 1) // 2 for b in range(blocks + 1)]
     width = offsets[blocks]
-    table = cosine_table(length)
+    table = jnp.asarray(cosine_table(length))
     main = table[:, :half]
 
     pair_rows = rows // 2
     parts = row_parts(pair_rows)
     counts = [part.stop - part.start for part in parts]
     core = lax.rem(col, 2)
-    inner_arrays, arrays = fill_arrays(intensity, template, row, col, main)
+    constants = fill_constants(intensity, template, row, col, cosine_table(length)[:, :half])
+    top, bottom, sides = faces(intensity)
     given_first, kept_first = (1 - core) * pair_rows, core * pair_rows
     given, kept = [], []
-
-    def fill_part(c, after):
+    blank = intensity[:SWEEPS]
+    inner_faces = blank, blank, jnp.pad(sides, ((SWEEPS, SWEEPS),) + FREE)
+    outer_faces = []
+
+    def fill_part(c, packed):
         part = parts[c]
         starts = given_first + part.start, kept_first + part.start
-        if after is not None:
-            starts, after = lax.optimization_barrier((starts, after))
+        if packed is not None:
+            starts, packed = lax.optimization_barrier((starts, packed))
+        lines = None if packed is None else exchanged(packed)
         inner = part.start >= SWEEPS and part.stop <= pair_rows - SWEEPS
-        use = inner_arrays if inner else arrays
-        given.append(filled_spectrum(intensity, use, starts[0], part))
+        if not inner and not outer_faces:
+            outer_faces.extend((top, bottom, with_corners(sides, corners(sides))))
+        use = (inner_faces if inner else tuple(outer_faces)) + constants
+        piece = filled_spectrum(intensity, use, starts[0], part)
+        if inner and not outer_faces:
+            piece, after = lax.optimization_barrier((piece, sides))
+            ends = corners(after)
+        given.append(piece)
         got = lax.ppermute(given[c][0], "gy", swap(gy, 1))
+        if c == 1:
+            starts, lines = lax.optimization_barrier((starts, lines))
         kept.append(filled_spectrum(intensity, use, starts[1], part))
-        return got, after
+        if inner and not outer_faces:
+            kept[c], ends = lax.optimization_barrier((kept[c], ends))
+            outer_faces.extend((top, bottom, with_corners(sides, ends)))
+        return got, lines
 
     table_cols = lax.dynamic_slice_in_dim(table, col * cols, cols, 0)
     kept_rows = lax.dynamic_slice_in_dim(table, row * rows + kept_first, pair_rows, 0)
@@ -378,10 +435,10 @@
     values, packed, lines = 0.0, None, None
     for c, count in enumerate(counts):
         closing = c == len(counts) - 1
-        got, packed = fill_part(c, packed)
+        got, got_lines = fill_part(c, packed)
         held = kept[c][0]
         if c > 0:
-            held, got_lines = lax.optimization_barrier((held, exchanged(packed)))
+            held, got_lines = lax.optimization_barrier((held, got_lines))
             lines = sent_lines(got_lines, counts[c - 1], lines)
             values = values + first_axis(lines, table_parts[c - 1])
         if closing:

time: 423 us -> 420 us (level); the launches traced: 415 us -> 419 us
  waiting for transfers between devices: 115 us -> 140 us
  local copies, waits for them, and re-layouts: 48 us -> 35.4 us
  other arithmetic: 28.1 us -> 19.3 us
    ppermute x6, waiting for transfers between devices: 0.34 us -> 14.1 us  [the longest x1 9.5 us: faces(): top = lax.ppermute(block[rows - SWEEPS:], 'gx', up)]
    ppermute x9, waiting for transfers between devices: 29.7 us -> 39.2 us  [exchanged(): lax.ppermute(packed[p], 'gy', swap(gy, p))]
    another operation x3 -> x1, local copies, waits for them, and re-layouts: 5.34 us -> 0.63 us  [the longest x2 4.75 us: fill_arrays(): marks = jnp.tile(marks, (1, 1, 128 // period))]
  transfers between devices with their start and end apart: 33 -> 33, of which waited for: 13 -> 16; matrix products, arithmetic and copies ran while one was open for 15% -> 10% of each run, Pallas kernels for 14% -> 15%
where the time goes in v2:
time: 420 us; the launch traced here: 419 us
  waiting for transfers between devices  140 us (33%)
  Pallas kernels  136 us (32%)
  starting transfers between devices  49.3 us (12%)
  local copies, waits for them, and re-layouts  35.4 us (8%)
  blocking collectives  32.5 us (8%)
  other arithmetic  19.3 us (5%)
  matrix products  4.95 us (1%)
    pallas_call x6, Pallas kernels, filled_spectrum(): pl.pallas_call(fill_kernel, grid_spec=pltpu.PrefetchScalarGridSpec(num_sc...  73.7 us
    ppermute x9, waiting for transfers between devices, exchanged(): lax.ppermute(packed[p], 'gy', swap(gy, p))  39.2 us
    pallas_call x1, Pallas kernels, result_block(): pl.pallas_call(lambda *refs: result_kernel(offsets, own, devices, groups,...  33.9 us
    ppermute x9, waiting for transfers between devices, gathered(): pieces[place ^ bit] = lax.ppermute(pieces[place], 'gy', swap(peers, bit))  33.7 us
    all_to_all x1, blocking collectives, on_device(): piece = lax.all_to_all(messages, 'gx', 0, 0, tiled=True)  32.5 us
    all_to_all x3, waiting for transfers between devices, sent_lines(): return lax.all_to_all(lines, 'gx', 0, 0, tiled=True)  21.4 us
    pallas_call x3, Pallas kernels, packed_section(): pl.pallas_call(lambda *refs: section_kernel(offsets, closing, *refs), gri...  19.6 us
    all_to_all x1, waiting for transfers between devices, on_device(): lax.all_to_all(jnp.concatenate(turned, axis=3), ('gy', 'gx'), 0, 0, tiled...  18.5 us
  transfers between devices with their start and end apart: 33, of which 16 were waited for; matrix products, arithmetic and copies ran while one was open for 10% of the time, Pallas kernels for 15%

profile of v2, /device:TPU:0, one launch (start us, length us, event | category | flops | bytes accessed | tf_op | source)
XLA Modules:
  0.0 418.7 jit_solution(10156391736295764699)
XLA Ops:
  0.0 1.3 fusion.28
  1.3 3.0 collective-permute-start
  4.3 3.1 collective-permute-start.1
  7.4 1.8 fusion.27
  9.3 1.7 collective-permute-start.3
  11.0 3.5 shard_map.55.marks
  14.6 1.4 collective-permute-done.2
  15.9 1.1 collective-permute-done.3
  17.2 9.5 %collective-permute-done.top = f32[2,128,512]{2,1,0:T(8,128)S(1)} collective-permute-done((f32[2,128,512]{2,1,0:T(8,128)S(1)}, f32[2,128,512]{2,1,0:T(8,128)S(1)}, u32[]{:S(2)}, u32[]{:S(2)}) %collective-permute-start) | collective-permute-done | bytes 524320 | tf_op jit(solution)/shard_map/ppermute | solution.py:31
  26.7 2.2 collective-permute-done.1.bottom
  28.9 1.7 pad.16.sides
  30.6 16.7 %shard_map.57 = (f32[16,128,256]{2,1,0:T(8,128)}, f32[16,256]{1,0:T(8,128)}, f32[128,128]{1,0:T(8,128)}) custom-call(s32[1]{0:T(128)} %bitcast.11.base, f32[64,128,512]{2,1,0:T(8,128)} %below.11, f32[64,128,512]{2,1,0:T(8,128)} %below.11, f32[64,128,512]{2,1,0:T(8,128)} %below.11, f32[2,128,512]{2,1,0:T(8,128)} %copy-done, f32[2,128,512]{2,1,0:T(8,128)} %copy-done, ...), custom_call_target="tpu_custom_call" | custom-call | flops 1610612736 | bytes 6291456 | tf_op jit(solution)/shard_map/pallas_call | solution.py:248
  50.5 3.4 collective-permute-start.5
  53.9 16.8 %shard_map.56 = (f32[16,128,256]{2,1,0:T(8,128)}, f32[16,256]{1,0:T(8,128)}, f32[128,128]{1,0:T(8,128)}) custom-call(s32[1]{0:T(128)} %bitcast.10.base, f32[64,128,512]{2,1,0:T(8,128)} %below.11, f32[64,128,512]{2,1,0:T(8,128)} %below.11, f32[64,128,512]{2,1,0:T(8,128)} %below.11, f32[2,128,512]{2,1,0:T(8,128)} %copy-done, f32[2,128,512]{2,1,0:T(8,128)} %copy-done, ...), custom_call_target="tpu_custom_call" | custom-call | flops 1610612736 | bytes 6291456 | tf_op jit(solution)/shard_map/pallas_call | solution.py:248
  70.7 1.8 select_maximum_fusion.sides
  74.9 8.1 %shard_map.58 = (f32[16,2,8,640]{3,2,1,0:T(8,128)}, f32[16,2,8,640]{3,2,1,0:T(8,128)}, f32[16,2,8,640]{3,2,1,0:T(8,128)}, f32[16,2,8,640]{3,2,1,0:T(8,128)}, f32[4,64,640]{2,1,0:T(8,128)}) custom-call(s32[1]{0:T(128)} %bitcast.3.refs_0_, f32[4,16]{1,0:T(4,128)} %pad_maximum_fusion.4.refs_1_, f32[16,128,256]{2,1,0:T(8,128)} %get-tuple-element.99.refs_2_, ...), custom_call_target="tpu_custom_call" | custom-call | flops 1610612736 | bytes 8388608 | tf_op jit(solution)/shard_map/pallas_call | solution.py:357
  83.1 10.0 %shard_map.60 = (f32[8,128,256]{2,1,0:T(8,128)}, f32[8,256]{1,0:T(8,128)}, f32[128,128]{1,0:T(8,128)}) custom-call(s32[1]{0:T(128)} %bitcast.24.base, f32[64,128,512]{2,1,0:T(8,128)} %below.11, f32[64,128,512]{2,1,0:T(8,128)} %below.11, f32[64,128,512]{2,1,0:T(8,128)} %below.11, f32[2,128,512]{2,1,0:T(8,128)} %copy-done.1, f32[2,128,512]{2,1,0:T(8,128)} %copy-done.2, ...), custom_call_target="tpu_custom_call" | custom-call | flops 805306368 | bytes 3145728 | tf_op jit(solution)/shard_map/pallas_call | solution.py:248
  94.3 1.5 collective-permute-start.8
  97.9 14.2 %collective-permute-done.8 = f32[16,2,8,640]{3,2,1,0:T(8,128)S(1)} collective-permute-done((f32[16,2,8,640]{3,2,1,0:T(8,128)}, f32[16,2,8,640]{3,2,1,0:T(8,128)S(1)}, u32[]{:S(2)}, u32[]{:S(2)}) %collective-permute-start.8) | collective-permute-done | bytes 655392 | tf_op jit(solution)/shard_map/ppermute | solution.py:744
  112.1 12.5 %collective-permute-done.9 = f32[16,2,8,640]{3,2,1,0:T(8,128)} collective-permute-done((f32[16,2,8,640]{3,2,1,0:T(8,128)}, f32[16,2,8,640]{3,2,1,0:T(8,128)}, u32[]{:S(2)}, u32[]{:S(2)}) %collective-permute-start.9) | collective-permute-done | bytes 655392 | tf_op jit(solution)/shard_map/ppermute | solution.py:744
  124.6 10.3 %shard_map.59 = (f32[8,128,256]{2,1,0:T(8,128)}, f32[8,256]{1,0:T(8,128)}, f32[128,128]{1,0:T(8,128)}) custom-call(s32[1]{0:T(128)} %bitcast.14.base, f32[64,128,512]{2,1,0:T(8,128)} %below.11, f32[64,128,512]{2,1,0:T(8,128)} %below.11, f32[64,128,512]{2,1,0:T(8,128)} %below.11, f32[2,128,512]{2,1,0:T(8,128)} %copy-done.1, f32[2,128,512]{2,1,0:T(8,128)} %copy-done.2, ...), custom_call_target="tpu_custom_call" | custom-call | flops 805306368 | bytes 3145728 | tf_op jit(solution)/shard_map/pallas_call | solution.py:248
  134.9 1.0 copy-done.13
  135.9 1.2 add.169
  137.2 1.8 copy.63
  138.9 5.9 %all-to-all-start = ((f32[8,2,32,640]{3,1,2,0:T(2,128)}), f32[8,2,32,640]{3,1,2,0:T(2,128)S(1)}, u32[]{:S(2)}, u32[]{:S(2)}) async-start(f32[8,2,32,640]{3,1,2,0:T(2,128)} %copy.63), calls=%async_computation | async-start | bytes 2621440 | tf_op jit(solution)/shard_map/all_to_all | solution.py:754
  145.8 5.5 %shard_map.61 = (f32[8,2,8,640]{3,2,1,0:T(8,128)}, f32[8,2,8,640]{3,2,1,0:T(8,128)}, f32[8,2,8,640]{3,2,1,0:T(8,128)}, f32[8,2,8,640]{3,2,1,0:T(8,128)}, f32[4,64,640]{2,1,0:T(8,128)}) custom-call(s32[1]{0:T(128)} %bitcast.3.refs_0_, f32[4,8]{1,0:T(4,128)} %pad_maximum_fusion.5.refs_1_, f32[8,128,256]{2,1,0:T(8,128)} %get-tuple-element.125.refs_2_, ...), custom_call_target="tpu_custom_call" | custom-call | flops 805306368 | bytes 4194304 | tf_op jit(solution)/shard_map/pallas_call | solution.py:357
  151.8 1.5 collective-permute-start.12
  153.3 9.9 %shard_map.62 = (f32[8,128,256]{2,1,0:T(8,128)}, f32[8,256]{1,0:T(8,128)}, f32[128,128]{1,0:T(8,128)}) custom-call(s32[1]{0:T(128)} %bitcast.26.base, f32[64,128,512]{2,1,0:T(8,128)} %below.11, f32[64,128,512]{2,1,0:T(8,128)} %below.11, f32[64,128,512]{2,1,0:T(8,128)} %below.11, f32[2,128,512]{2,1,0:T(8,128)} %copy-done.1, f32[2,128,512]{2,1,0:T(8,128)} %copy-done.2, ...), custom_call_target="tpu_custom_call" | custom-call | flops 805306368 | bytes 3145728 | tf_op jit(solution)/shard_map/pallas_call | solution.py:248
  163.2 10.0 %shard_map.63 = (f32[8,128,256]{2,1,0:T(8,128)}, f32[8,256]{1,0:T(8,128)}, f32[128,128]{1,0:T(8,128)}) custom-call(s32[1]{0:T(128)} %bitcast.36.base, f32[64,128,512]{2,1,0:T(8,128)} %below.11, f32[64,128,512]{2,1,0:T(8,128)} %below.11, f32[64,128,512]{2,1,0:T(8,128)} %below.11, f32[2,128,512]{2,1,0:T(8,128)} %copy-done.1, f32[2,128,512]{2,1,0:T(8,128)} %copy-done.2, ...), custom_call_target="tpu_custom_call" | custom-call | flops 805306368 | bytes 3145728 | tf_op jit(solution)/shard_map/pallas_call | solution.py:248
  173.9 1.2 concatenate.54
  179.2 5.9 %shard_map.64 = (f32[13,2,8,640]{3,2,1,0:T(8,128)}, f32[13,2,8,640]{3,2,1,0:T(8,128)}, f32[13,2,8,640]{3,2,1,0:T(8,128)}, f32[13,2,8,640]{3,2,1,0:T(8,128)}, f32[4,64,640]{2,1,0:T(8,128)}) custom-call(s32[1]{0:T(128)} %bitcast.3.refs_0_, f32[4,8]{1,0:T(4,128)} %pad_maximum_fusion.6.refs_1_, f32[8,128,256]{2,1,0:T(8,128)} %get-tuple-element.143.refs_2_, ...), custom_call_target="tpu_custom_call" | custom-call | flops 805306368 | bytes 4194304 | tf_op jit(solution)/shard_map/pallas_call | solution.py:357
  185.1 1.5 collective-permute-start.15
  186.6 1.0 add.172
  187.6 1.0 add.173
  189.4 1.2 copy.65
  190.6 5.7 %all-to-all-start.1 = ((f32[8,2,16,640]{3,1,2,0:T(2,128)}), f32[8,2,16,640]{3,1,2,0:T(2,128)S(1)}, u32[]{:S(2)}, u32[]{:S(2)}) async-start(f32[8,2,16,640]{3,1,2,0:T(2,128)} %copy.65), calls=%async_computation.1 | async-start | bytes 1310720 | tf_op jit(solution)/shard_map/all_to_all | solution.py:754
  196.3 4.0 collective-permute-done.15
  200.4 1.0 slice_add_fusion.1
  201.4 8.5 %collective-permute-done.17 = f32[13,2,8,640]{3,2,1,0:T(8,128)} collective-permute-done((f32[13,2,8,640]{3,2,1,0:T(8,128)}, f32[13,2,8,640]{3,2,1,0:T(8,128)}, u32[]{:S(2)}, u32[]{:S(2)}) %collective-permute-start.17) | collective-permute-done | bytes 532512 | tf_op jit(solution)/shard_map/ppermute | solution.py:744
  209.9 1.1 slice_add_fusion
  211.0 1.2 slice_add_fusion.2
  212.3 1.6 all-to-all-done.1
  213.9 1.4 copy.67
  215.2 4.3 %all-to-all-start.2 = ((f32[8,2,21,640]{3,1,2,0:T(2,128)}), f32[8,2,21,640]{3,1,2,0:T(2,128)S(1)}, u32[]{:S(2)}, u32[]{:S(2)}) async-start(f32[8,2,21,640]{3,1,2,0:T(2,128)} %copy.67), calls=%async_computation.2 | async-start | bytes 1720320 | tf_op jit(solution)/shard_map/all_to_all | solution.py:754
  219.5 1.1 broadcast_select_fusion
  220.7 1.9 convolution_bitcast_fusion
  222.5 19.8 %all-to-all-done.2 = f32[8,2,21,640]{3,1,2,0:T(2,128)S(1)} async-done(((f32[8,2,21,640]{3,1,2,0:T(2,128)}), f32[8,2,21,640]{3,1,2,0:T(2,128)S(1)}, u32[]{:S(2)}, u32[]{:S(2)}) %all-to-all-start.2) | async-done | bytes 860192 | tf_op jit(solution)/shard_map/all_to_all | solution.py:754
  244.5 1.0 copy.97
  245.7 2.4 concatenate.58
  248.1 3.6 all-to-all-start.3
  252.4 18.5 %all-to-all-done.3 = f32[32,2,2,1280]{3,2,1,0:T(2,128)S(1)} async-done(((f32[32,2,2,1280]{3,2,1,0:T(2,128)}), f32[32,2,2,1280]{3,2,1,0:T(2,128)S(1)}, u32[]{:S(2)}, u32[]{:S(2)}) %all-to-all-start.3) | async-done | bytes 655392 | tf_op jit(solution)/shard_map/all_to_all | solution.py:468
  271.9 5.6 %shard_map.65 = (f32[8,288,128]{2,1,0:T(8,128)}, f32[8,256,128]{2,1,0:T(8,128)}, f32[8,128,128]{2,1,0:T(8,128)}) custom-call(f32[2,256,640]{2,1,0:T(8,128)} %bitcast.170, f32[2,64,1280]{2,1,0:T(8,128)} %bitcast.177, f32[2,5,640]{2,1,0:T(8,128)} %copy_multiply_fusion.refs_2_), custom_call_target="tpu_custom_call" | custom-call | tf_op jit(solution)/shard_map/pallas_call | solution.py:603
  277.5 32.5 %all_to_all.35 = f32[8,288,128]{2,1,0:T(8,128)S(1)} all-to-all(f32[8,288,128]{2,1,0:T(8,128)} %get-tuple-element.165), channel_id=1, replica_groups=mesh['gx'=8,'gy'=4] {'gx'}, dimensions={0} | all-to-all | bytes 2359296 | tf_op jit(solution)/shard_map/all_to_all | solution.py:484
  310.0 1.2 collective-permute-start.19
  311.2 3.6 all-to-all-start.5
  314.9 21.5 %collective-permute-done.19 = f32[8,288,128]{2,1,0:T(8,128)} collective-permute-done((f32[8,288,128]{2,1,0:T(8,128)S(1)}, f32[8,288,128]{2,1,0:T(8,128)}, u32[]{:S(2)}, u32[]{:S(2)}) %collective-permute-start.19) | collective-permute-done | bytes 1179680 | tf_op jit(solution)/shard_map/ppermute | solution.py:737
  338.4 1.9 all-to-all-done.5
  340.8 4.0 all-to-all-start.6
  348.6 11.2 %all-to-all-done.6 = f32[8,128,128]{2,1,0:T(8,128)S(1)} async-done(((f32[8,128,128]{2,1,0:T(8,128)}), f32[8,128,128]{2,1,0:T(8,128)S(1)}, u32[]{:S(2)}, u32[]{:S(2)}) %all-to-all-start.6) | async-done | bytes 524320 | tf_op jit(solution)/shard_map/all_to_all | solution.py:484
  359.8 4.4 %collective-permute-done.22 = f32[8,256,128]{2,1,0:T(8,128)} collective-permute-done((f32[8,256,128]{2,1,0:T(8,128)S(1)}, f32[8,256,128]{2,1,0:T(8,128)}, u32[]{:S(2)}, u32[]{:S(2)}) %collective-permute-start.22) | collective-permute-done | bytes 1048608 | tf_op jit(solution)/shard_map/ppermute | solution.py:737
  364.2 1.7 collective-permute-start.25
  369.2 7.8 %collective-permute-done.25 = f32[8,128,128]{2,1,0:T(8,128)S(1)} collective-permute-done((f32[8,128,128]{2,1,0:T(8,128)S(1)}, f32[8,128,128]{2,1,0:T(8,128)S(1)}, u32[]{:S(2)}, u32[]{:S(2)}) %collective-permute-start.25) | collective-permute-done | bytes 524320 | tf_op jit(solution)/shard_map/ppermute | solution.py:737
  377.7 1.3 dynamic-update-slice.4
  384.6 33.9 %shard_map.66 = f32[64,128,512]{2,1,0:T(8,128)} custom-call(s32[4]{0:T(128)} %pad_add_fusion.refs_0_, f32[64,640]{1,0:T(8,128)} %bitcast.187, f32[64,256]{1,0:T(8,128)} %slice.385.refs_2_, f32[128,128]{1,0:T(8,128)} %pad.19.refs_3_, bf16[128,256]{1,0:T(8,128)(2,1)} %fusion.16.refs_4_, bf16[256,256]{1,0:T(8,128)(2,1)} %fusion.8.refs_5_, ...), custom_call_target="tpu_custom_call" | custom-call | tf_op jit(solution)/shard_map/pallas_call | solution.py:708
  (179 shorter events, 36.0 us)
Async XLA Ops:
  1.3 15.9 %copy-start = (f32[2,128,512]{2,1,0:T(8,128)}, f32[2,128,512]{2,1,0:T(8,128)S(1)}, u32[]{:S(2)}) copy-start(f32[2,128,512]{2,1,0:T(8,128)S(1)} %get-tuple-element.180.top.bottom) | copy-start | bytes 1572868
  1.3 25.4 %collective-permute-start = (f32[2,128,512]{2,1,0:T(8,128)S(1)}, f32[2,128,512]{2,1,0:T(8,128)S(1)}, u32[]{:S(2)}, u32[]{:S(2)}) collective-permute-start(f32[2,128,512]{2,1,0:T(8,128)S(1)} %get-tuple-element.179), channel_id=1, source_target_pairs={{0,4},{4,8},{8,12},{12,16},{16,20},{20,24},{24,28},{28,0},{1,5},{5... | collective-permute-start | bytes 1572872 | tf_op jit(solution)/shard_map/ppermute | solution.py:31
  4.3 24.6 %collective-permute-start.1 = (f32[2,128,512]{2,1,0:T(8,128)S(1)}, f32[2,128,512]{2,1,0:T(8,128)S(1)}, u32[]{:S(2)}, u32[]{:S(2)}) collective-permute-start(f32[2,128,512]{2,1,0:T(8,128)S(1)} %get-tuple-element.180.top.bottom), channel_id=1, source_target_pairs={{4,0},{8,4},{12,8},{16,12},{20,16},{24,20},{28,24},{0,28},{5,1},{9... | collective-permute-start | bytes 1572872 | tf_op jit(solution)/shard_map/ppermute | solution.py:32
  9.2 6.7 %collective-permute-start.2 = (f32[64,2,512]{2,1,0:T(2,128)S(1)}, f32[64,2,512]{2,1,0:T(2,128)S(1)}, u32[]{:S(2)}, u32[]{:S(2)}) collective-permute-start(f32[64,2,512]{2,1,0:T(2,128)S(1)} %get-tuple-element.177), channel_id=1, source_target_pairs={{0,1},{1,2},{2,3},{3,0},{4,5},{5,6},{6,7},{7,4},{8,9},{9,10},{10,1... | collective-permute-start | bytes 786440 | tf_op jit(solution)/shard_map/ppermute | solution.py:33
  9.3 7.7 %collective-permute-start.3 = (f32[64,2,512]{2,1,0:T(2,128)S(1)}, f32[64,2,512]{2,1,0:T(2,128)S(1)}, u32[]{:S(2)}, u32[]{:S(2)}) collective-permute-start(f32[64,2,512]{2,1,0:T(2,128)S(1)} %get-tuple-element.178), channel_id=1, source_target_pairs={{1,0},{2,1},{3,2},{0,3},{5,4},{6,5},{7,6},{4,7},{9,8},{10,9},{11,1... | collective-permute-start | bytes 786440 | tf_op jit(solution)/shard_map/ppermute | solution.py:34
  26.7 3.9 copy-start.1
  28.9 1.7 copy-start.2
  30.6 16.8 %copy-start.6 = (f32[512,257]{0,1:T(8,128)S(1)}, f32[512,257]{0,1:T(8,128)}, u32[]{:S(2)}) copy-start(f32[512,257]{0,1:T(8,128)} %constant.112.clone) | copy-start | bytes 1579012
  47.4 25.1 %collective-permute-start.6 = (f32[16,128,256]{2,1,0:T(8,128)}, f32[16,128,256]{2,1,0:T(8,128)S(1)}, u32[]{:S(2)}, u32[]{:S(2)}) collective-permute-start(f32[16,128,256]{2,1,0:T(8,128)} %get-tuple-element.100), channel_id=1, source_target_pairs={{0,1},{1,0},{2,3},{3,2},{4,5},{5,4},{6,7},{7,6},{8,9},{9,8},{10,11... | collective-permute-start | bytes 6291464 | tf_op jit(solution)/shard_map/ppermute | solution.py:416
  50.5 20.2 %collective-permute-start.5 = (f32[2,4,512]{2,1,0:T(4,128)S(1)}, f32[2,4,512]{2,1,0:T(4,128)S(1)}, u32[]{:S(2)}, u32[]{:S(2)}) collective-permute-start(f32[2,4,512]{2,1,0:T(4,128)S(1)} %get-tuple-element.207), channel_id=1, source_target_pairs={{4,0},{8,4},{12,8},{16,12},{20,16},{24,20},{28,24},{0,28},{5,1},{9... | collective-permute-start | bytes 49160 | tf_op jit(solution)/shard_map/ppermute | solution.py:41
  53.9 16.8 %collective-permute-start.4 = (f32[2,4,512]{2,1,0:T(4,128)S(1)}, f32[2,4,512]{2,1,0:T(4,128)S(1)}, u32[]{:S(2)}, u32[]{:S(2)}) collective-permute-start(f32[2,4,512]{2,1,0:T(4,128)S(1)} %get-tuple-element.208), channel_id=1, source_target_pairs={{0,4},{4,8},{8,12},{12,16},{16,20},{20,24},{24,28},{28,0},{1,5},{5... | collective-permute-start | bytes 49160 | tf_op jit(solution)/shard_map/ppermute | solution.py:40
  72.5 2.5 copy-start.25
  93.1 51.8 %collective-permute-start.10 = (f32[8,128,256]{2,1,0:T(8,128)}, f32[8,128,256]{2,1,0:T(8,128)S(1)}, u32[]{:S(2)}, u32[]{:S(2)}) collective-permute-start(f32[8,128,256]{2,1,0:T(8,128)} %get-tuple-element.126), channel_id=1, source_target_pairs={{0,1},{1,0},{2,3},{3,2},{4,5},{5,4},{6,7},{7,6},{8,9},{9,8},{10,11... | collective-permute-start | bytes 3145736 | tf_op jit(solution)/shard_map/ppermute | solution.py:416
  93.3 4.6 %copy-start.21 = (f32[16,256]{1,0:T(8,128)S(1)}, f32[16,256]{1,0:T(8,128)}, u32[]{:S(2)}) copy-start(f32[16,256]{1,0:T(8,128)} %get-tuple-element.152) | copy-start | bytes 49156
  93.3 4.6 %copy-start.23 = (f32[8,256]{1,0:T(8,128)S(1)}, f32[8,256]{1,0:T(8,128)}, u32[]{:S(2)}) copy-start(f32[8,256]{1,0:T(8,128)} %get-tuple-element.153) | copy-start | bytes 24580
  93.8 4.1 collective-permute-start.7
  94.3 17.8 %collective-permute-start.8 = (f32[16,2,8,640]{3,2,1,0:T(8,128)}, f32[16,2,8,640]{3,2,1,0:T(8,128)S(1)}, u32[]{:S(2)}, u32[]{:S(2)}) collective-permute-start(f32[16,2,8,640]{3,2,1,0:T(8,128)} %get-tuple-element.109), channel_id=1, source_target_pairs={{0,2},{1,3},{2,0},{3,1},{4,6},{5,7},{6,4},{7,5},{8,10},{9,11},{10,... | collective-permute-start | bytes 1966088 | tf_op jit(solution)/shard_map/ppermute | solution.py:744
  95.8 28.8 %collective-permute-start.9 = (f32[16,2,8,640]{3,2,1,0:T(8,128)}, f32[16,2,8,640]{3,2,1,0:T(8,128)}, u32[]{:S(2)}, u32[]{:S(2)}) collective-permute-start(f32[16,2,8,640]{3,2,1,0:T(8,128)} %get-tuple-element.110), channel_id=1, source_target_pairs={{0,3},{1,2},{2,1},{3,0},{4,7},{5,6},{6,5},{7,4},{8,11},{9,10},{10,... | collective-permute-start | bytes 1966088 | tf_op jit(solution)/shard_map/ppermute | solution.py:744
  97.9 36.9 %copy-start.12 = (f32[16,2,8,640]{3,2,1,0:T(8,128)}, f32[16,2,8,640]{3,2,1,0:T(8,128)S(1)}, u32[]{:S(2)}) copy-start(f32[16,2,8,640]{3,2,1,0:T(8,128)S(1)} %collective-permute-done.7) | copy-start | bytes 1966084
  112.1 12.5 %copy-start.14 = (f32[16,2,8,640]{3,2,1,0:T(8,128)}, f32[16,2,8,640]{3,2,1,0:T(8,128)S(1)}, u32[]{:S(2)}) copy-start(f32[16,2,8,640]{3,2,1,0:T(8,128)S(1)} %collective-permute-done.8) | copy-start | bytes 1966084
  124.6 10.3 %copy-start.11 = (f32[16,2,8,640]{3,2,1,0:T(8,128)S(1)}, f32[16,2,8,640]{3,2,1,0:T(8,128)}, u32[]{:S(2)}) copy-start(f32[16,2,8,640]{3,2,1,0:T(8,128)} %get-tuple-element.121) | copy-start | bytes 1966084
  124.6 10.3 %copy-start.15 = (f32[16,2,8,640]{3,2,1,0:T(8,128)S(1)}, f32[16,2,8,640]{3,2,1,0:T(8,128)}, u32[]{:S(2)}) copy-start(f32[16,2,8,640]{3,2,1,0:T(8,128)} %copy-done.14) | copy-start | bytes 1966084
  134.8 1.1 copy-start.13
  138.9 50.5 %all-to-all-start = ((f32[8,2,32,640]{3,1,2,0:T(2,128)}), f32[8,2,32,640]{3,1,2,0:T(2,128)S(1)}, u32[]{:S(2)}, u32[]{:S(2)}) async-start(f32[8,2,32,640]{3,1,2,0:T(2,128)} %copy.63), calls=%async_computation | async-start | bytes 2621440 | tf_op jit(solution)/shard_map/all_to_all | solution.py:754
  144.8 1.0 copy-start.8
  151.3 26.8 %collective-permute-start.11 = (f32[8,2,8,640]{3,2,1,0:T(8,128)}, f32[8,2,8,640]{3,2,1,0:T(8,128)S(1)}, u32[]{:S(2)}, u32[]{:S(2)}) collective-permute-start(f32[8,2,8,640]{3,2,1,0:T(8,128)} %get-tuple-element.135), channel_id=1, source_target_pairs={{0,1},{1,0},{2,3},{3,2},{4,5},{5,4},{6,7},{7,6},{8,9},{9,8},{10,11... | collective-permute-start | bytes 983048 | tf_op jit(solution)/shard_map/ppermute | solution.py:744
  151.8 26.4 %collective-permute-start.12 = (f32[8,2,8,640]{3,2,1,0:T(8,128)}, f32[8,2,8,640]{3,2,1,0:T(8,128)}, u32[]{:S(2)}, u32[]{:S(2)}) collective-permute-start(f32[8,2,8,640]{3,2,1,0:T(8,128)} %get-tuple-element.136), channel_id=1, source_target_pairs={{0,2},{1,3},{2,0},{3,1},{4,6},{5,7},{6,4},{7,5},{8,10},{9,11},{10,... | collective-permute-start | bytes 983048 | tf_op jit(solution)/shard_map/ppermute | solution.py:744
  153.3 24.9 %collective-permute-start.13 = (f32[8,2,8,640]{3,2,1,0:T(8,128)}, f32[8,2,8,640]{3,2,1,0:T(8,128)}, u32[]{:S(2)}, u32[]{:S(2)}) collective-permute-start(f32[8,2,8,640]{3,2,1,0:T(8,128)} %get-tuple-element.137), channel_id=1, source_target_pairs={{0,3},{1,2},{2,1},{3,0},{4,7},{5,6},{6,5},{7,4},{8,11},{9,10},{10,... | collective-permute-start | bytes 983048 | tf_op jit(solution)/shard_map/ppermute | solution.py:744
  163.2 12.5 %copy-start.20 = (f32[16,256]{1,0:T(8,128)S(1)}, f32[16,256]{1,0:T(8,128)}, u32[]{:S(2)}) copy-start(f32[16,256]{1,0:T(8,128)} %get-tuple-element.155) | copy-start | bytes 49156
  163.2 12.5 %copy-start.22 = (f32[8,256]{1,0:T(8,128)S(1)}, f32[8,256]{1,0:T(8,128)}, u32[]{:S(2)}) copy-start(f32[8,256]{1,0:T(8,128)} %get-tuple-element.156) | copy-start | bytes 24580
  163.2 12.6 %copy-start.24 = (f32[8,256]{1,0:T(8,128)S(1)}, f32[8,256]{1,0:T(8,128)}, u32[]{:S(2)}) copy-start(f32[8,256]{1,0:T(8,128)} %get-tuple-element.157) | copy-start | bytes 24580
  173.2 4.9 %collective-permute-start.14 = (f32[8,128,256]{2,1,0:T(8,128)}, f32[8,128,256]{2,1,0:T(8,128)S(1)}, u32[]{:S(2)}, u32[]{:S(2)}) collective-permute-start(f32[8,128,256]{2,1,0:T(8,128)} %get-tuple-element.145), channel_id=1, source_target_pairs={{0,1},{1,0},{2,3},{3,2},{4,5},{5,4},{6,7},{7,6},{8,9},{9,8},{10,11... | collective-permute-start | bytes 3145736 | tf_op jit(solution)/shard_map/ppermute | solution.py:416
  178.2 1.0 copy-start.10
  179.2 7.4 %copy-start.19 = (f32[8,2,8,640]{3,2,1,0:T(8,128)S(1)}, f32[8,2,8,640]{3,2,1,0:T(8,128)}, u32[]{:S(2)}) copy-start(f32[8,2,8,640]{3,2,1,0:T(8,128)} %get-tuple-element.138) | copy-start | bytes 983044
  185.1 15.3 %collective-permute-start.15 = (f32[13,2,8,640]{3,2,1,0:T(8,128)}, f32[13,2,8,640]{3,2,1,0:T(8,128)}, u32[]{:S(2)}, u32[]{:S(2)}) collective-permute-start(f32[13,2,8,640]{3,2,1,0:T(8,128)} %get-tuple-element.160), channel_id=1, source_target_pairs={{0,2},{1,3},{2,0},{3,1},{4,6},{5,7},{6,4},{7,5},{8,10},{9,11},{10,... | collective-permute-start | bytes 1597448 | tf_op jit(solution)/shard_map/ppermute | solution.py:744
  188.6 12.8 %collective-permute-start.16 = (f32[13,2,8,640]{3,2,1,0:T(8,128)}, f32[13,2,8,640]{3,2,1,0:T(8,128)}, u32[]{:S(2)}, u32[]{:S(2)}) collective-permute-start(f32[13,2,8,640]{3,2,1,0:T(8,128)} %get-tuple-element.161), channel_id=1, source_target_pairs={{0,1},{1,0},{2,3},{3,2},{4,5},{5,4},{6,7},{7,6},{8,9},{9,8},{10,11... | collective-permute-start | bytes 1597448 | tf_op jit(solution)/shard_map/ppermute | solution.py:744
  188.7 21.2 %collective-permute-start.17 = (f32[13,2,8,640]{3,2,1,0:T(8,128)}, f32[13,2,8,640]{3,2,1,0:T(8,128)}, u32[]{:S(2)}, u32[]{:S(2)}) collective-permute-start(f32[13,2,8,640]{3,2,1,0:T(8,128)} %get-tuple-element.162), channel_id=1, source_target_pairs={{0,3},{1,2},{2,1},{3,0},{4,7},{5,6},{6,5},{7,4},{8,11},{9,10},{10,... | collective-permute-start | bytes 1597448 | tf_op jit(solution)/shard_map/ppermute | solution.py:744
  189.4 11.0 %copy-start.16 = (f32[13,2,8,640]{3,2,1,0:T(8,128)S(1)}, f32[13,2,8,640]{3,2,1,0:T(8,128)}, u32[]{:S(2)}) copy-start(f32[13,2,8,640]{3,2,1,0:T(8,128)} %get-tuple-element.159) | copy-start | bytes 1597444
  190.6 23.3 %all-to-all-start.1 = ((f32[8,2,16,640]{3,1,2,0:T(2,128)}), f32[8,2,16,640]{3,1,2,0:T(2,128)S(1)}, u32[]{:S(2)}, u32[]{:S(2)}) async-start(f32[8,2,16,640]{3,1,2,0:T(2,128)} %copy.65), calls=%async_computation.1 | async-start | bytes 1310720 | tf_op jit(solution)/shard_map/all_to_all | solution.py:754
  215.2 27.1 %all-to-all-start.2 = ((f32[8,2,21,640]{3,1,2,0:T(2,128)}), f32[8,2,21,640]{3,1,2,0:T(2,128)S(1)}, u32[]{:S(2)}, u32[]{:S(2)}) async-start(f32[8,2,21,640]{3,1,2,0:T(2,128)} %copy.67), calls=%async_computation.2 | async-start | bytes 1720320 | tf_op jit(solution)/shard_map/all_to_all | solution.py:754
  242.4 1.3 copy-start.26
  244.5 1.1 copy-start.4
  248.1 22.8 %all-to-all-start.3 = ((f32[32,2,2,1280]{3,2,1,0:T(2,128)}), f32[32,2,2,1280]{3,2,1,0:T(2,128)S(1)}, u32[]{:S(2)}, u32[]{:S(2)}) async-start(f32[32,2,2,1280]{3,2,1,0:T(2,128)} %concatenate.58), calls=%async_computation.3 | async-start | bytes 1310720 | tf_op jit(solution)/shard_map/all_to_all | solution.py:468
  310.0 30.9 %copy-start.3 = (f32[8,288,128]{2,1,0:T(8,128)}, f32[8,288,128]{2,1,0:T(8,128)S(1)}, u32[]{:S(2)}) copy-start(f32[8,288,128]{2,1,0:T(8,128)S(1)} %all_to_all.35) | copy-start | bytes 3538948
  310.0 26.4 %collective-permute-start.19 = (f32[8,288,128]{2,1,0:T(8,128)S(1)}, f32[8,288,128]{2,1,0:T(8,128)}, u32[]{:S(2)}, u32[]{:S(2)}) collective-permute-start(f32[8,288,128]{2,1,0:T(8,128)S(1)} %all_to_all.35), channel_id=1, source_target_pairs={{0,2},{1,3},{2,0},{3,1},{4,6},{5,7},{6,4},{7,5},{8,10},{9,11},{10,... | collective-permute-start | bytes 3538952 | tf_op jit(solution)/shard_map/ppermute | solution.py:737
  311.2 29.1 %all-to-all-start.5 = ((f32[8,256,128]{2,1,0:T(8,128)}), f32[8,256,128]{2,1,0:T(8,128)S(1)}, u32[]{:S(2)}, u32[]{:S(2)}) async-start(f32[8,256,128]{2,1,0:T(8,128)} %get-tuple-element.168), calls=%async_computation.5 | async-start | bytes 2097152 | tf_op jit(solution)/shard_map/all_to_all | solution.py:484
  314.7 25.6 %collective-permute-start.18 = (f32[8,288,128]{2,1,0:T(8,128)S(1)}, f32[8,288,128]{2,1,0:T(8,128)}, u32[]{:S(2)}, u32[]{:S(2)}) collective-permute-start(f32[8,288,128]{2,1,0:T(8,128)S(1)} %all_to_all.35), channel_id=1, source_target_pairs={{0,1},{1,0},{2,3},{3,2},{4,5},{5,4},{6,7},{7,6},{8,9},{9,8},{10,11... | collective-permute-start | bytes 3538952 | tf_op jit(solution)/shard_map/ppermute | solution.py:737
  336.3 10.3 %collective-permute-start.20 = (f32[8,288,128]{2,1,0:T(8,128)}, f32[8,288,128]{2,1,0:T(8,128)}, u32[]{:S(2)}, u32[]{:S(2)}) collective-permute-start(f32[8,288,128]{2,1,0:T(8,128)} %collective-permute-done.19), channel_id=1, source_target_pairs={{0,1},{1,0},{2,3},{3,2},{4,5},{5,4},{6,7},{7,6},{8,9},{9,8},{10,11... | collective-permute-start | bytes 3538952 | tf_op jit(solution)/shard_map/ppermute | solution.py:737
  340.3 7.4 %copy-start.5 = (f32[8,256,128]{2,1,0:T(8,128)}, f32[8,256,128]{2,1,0:T(8,128)S(1)}, u32[]{:S(2)}) copy-start(f32[8,256,128]{2,1,0:T(8,128)S(1)} %all-to-all-done.5) | copy-start | bytes 3145732
  340.3 23.9 %collective-permute-start.22 = (f32[8,256,128]{2,1,0:T(8,128)S(1)}, f32[8,256,128]{2,1,0:T(8,128)}, u32[]{:S(2)}, u32[]{:S(2)}) collective-permute-start(f32[8,256,128]{2,1,0:T(8,128)S(1)} %all-to-all-done.5), channel_id=1, source_target_pairs={{0,2},{1,3},{2,0},{3,1},{4,6},{5,7},{6,4},{7,5},{8,10},{9,11},{10,... | collective-permute-start | bytes 3145736 | tf_op jit(solution)/shard_map/ppermute | solution.py:737
  340.8 23.3 %collective-permute-start.21 = (f32[8,256,128]{2,1,0:T(8,128)S(1)}, f32[8,256,128]{2,1,0:T(8,128)}, u32[]{:S(2)}, u32[]{:S(2)}) collective-permute-start(f32[8,256,128]{2,1,0:T(8,128)S(1)} %all-to-all-done.5), channel_id=1, source_target_pairs={{0,1},{1,0},{2,3},{3,2},{4,5},{5,4},{6,7},{7,6},{8,9},{9,8},{10,11... | collective-permute-start | bytes 3145736 | tf_op jit(solution)/shard_map/ppermute | solution.py:737
  340.8 18.9 %all-to-all-start.6 = ((f32[8,128,128]{2,1,0:T(8,128)}), f32[8,128,128]{2,1,0:T(8,128)S(1)}, u32[]{:S(2)}, u32[]{:S(2)}) async-start(f32[8,128,128]{2,1,0:T(8,128)} %get-tuple-element.173), calls=%async_computation.6 | async-start | bytes 1048576 | tf_op jit(solution)/shard_map/all_to_all | solution.py:484
  359.8 20.9 %copy-start.7 = (f32[8,128,128]{2,1,0:T(8,128)}, f32[8,128,128]{2,1,0:T(8,128)S(1)}, u32[]{:S(2)}) copy-start(f32[8,128,128]{2,1,0:T(8,128)S(1)} %all-to-all-done.6) | copy-start | bytes 1572868
  364.2 12.9 %collective-permute-start.25 = (f32[8,128,128]{2,1,0:T(8,128)S(1)}, f32[8,128,128]{2,1,0:T(8,128)S(1)}, u32[]{:S(2)}, u32[]{:S(2)}) collective-permute-start(f32[8,128,128]{2,1,0:T(8,128)S(1)} %all-to-all-done.6), channel_id=1, source_target_pairs={{0,2},{1,3},{2,0},{3,1},{4,6},{5,7},{6,4},{7,5},{8,10},{9,11},{10,... | collective-permute-start | bytes 1572872 | tf_op jit(solution)/shard_map/ppermute | solution.py:737
  365.9 17.5 %collective-permute-start.23 = (f32[8,256,128]{2,1,0:T(8,128)}, f32[8,256,128]{2,1,0:T(8,128)S(1)}, u32[]{:S(2)}, u32[]{:S(2)}) collective-permute-start(f32[8,256,128]{2,1,0:T(8,128)} %collective-permute-done.22), channel_id=1, source_target_pairs={{0,1},{1,0},{2,3},{3,2},{4,5},{5,4},{6,7},{7,6},{8,9},{9,8},{10,11... | collective-permute-start | bytes 3145736 | tf_op jit(solution)/shard_map/ppermute | solution.py:737
  368.7 14.7 %collective-permute-start.24 = (f32[8,128,128]{2,1,0:T(8,128)S(1)}, f32[8,128,128]{2,1,0:T(8,128)S(1)}, u32[]{:S(2)}, u32[]{:S(2)}) collective-permute-start(f32[8,128,128]{2,1,0:T(8,128)S(1)} %all-to-all-done.6), channel_id=1, source_target_pairs={{0,1},{1,0},{2,3},{3,2},{4,5},{5,4},{6,7},{7,6},{8,9},{9,8},{10,11... | collective-permute-start | bytes 1572872 | tf_op jit(solution)/shard_map/ppermute | solution.py:737
  377.0 5.7 %copy-start.17 = (f32[8,128,128]{2,1,0:T(8,128)}, f32[8,128,128]{2,1,0:T(8,128)S(1)}, u32[]{:S(2)}) copy-start(f32[8,128,128]{2,1,0:T(8,128)S(1)} %collective-permute-done.25) | copy-start | bytes 1572868
  377.0 6.4 %collective-permute-start.26 = (f32[8,128,128]{2,1,0:T(8,128)S(1)}, f32[8,128,128]{2,1,0:T(8,128)}, u32[]{:S(2)}, u32[]{:S(2)}) collective-permute-start(f32[8,128,128]{2,1,0:T(8,128)S(1)} %collective-permute-done.25), channel_id=1, source_target_pairs={{0,1},{1,0},{2,3},{3,2},{4,5},{5,4},{6,7},{7,6},{8,9},{9,8},{10,11... | collective-permute-start | bytes 1572872 | tf_op jit(solution)/shard_map/ppermute | solution.py:737
  383.4 0.8 copy-start.18
  383.4 1.2 copy-start.9

commit v3 on v2

--- a/solution.py
+++ b/solution.py
@@ -32,7 +32,7 @@
     bottom = lax.ppermute(block[:SWEEPS], "gx", down)
     before = lax.ppermute(block[:, cols - SWEEPS :], "gy", right)
     after = lax.ppermute(block[:, :SWEEPS], "gy", left)
-    return lax.optimization_barrier((top, bottom, jnp.concatenate([before, after], axis=1)))
+    return top, bottom, jnp.concatenate([before, after], axis=1)
 
 
 def corners(sides):
@@ -398,29 +398,19 @@
     inner_faces = blank, blank, jnp.pad(sides, ((SWEEPS, SWEEPS),) + FREE)
     outer_faces = []
 
-    def fill_part(c, packed):
+    def fill(c, start):
         part = parts[c]
-        starts = given_first + part.start, kept_first + part.start
-        if packed is not None:
-            starts, packed = lax.optimization_barrier((starts, packed))
-        lines = None if packed is None else exchanged(packed)
         inner = part.start >= SWEEPS and part.stop <= pair_rows - SWEEPS
-        if not inner and not outer_faces:
-            outer_faces.extend((top, bottom, with_corners(sides, corners(sides))))
         use = (inner_faces if inner else tuple(outer_faces)) + constants
-        piece = filled_spectrum(intensity, use, starts[0], part)
-        if inner and not outer_faces:
-            piece, after = lax.optimization_barrier((piece, sides))
-            ends = corners(after)
-        given.append(piece)
-        got = lax.ppermute(given[c][0], "gy", swap(gy, 1))
-        if c == 1:
-            starts, lines = lax.optimization_barrier((starts, lines))
-        kept.append(filled_spectrum(intensity, use, starts[1], part))
-        if inner and not outer_faces:
-            kept[c], ends = lax.optimization_barrier((kept[c], ends))
-            outer_faces.extend((top, bottom, with_corners(sides, ends)))
-        return got, lines
+        return list(filled_spectrum(intensity, use, start + part.start, part))
+
+    if not (parts[0].start >= SWEEPS and parts[0].stop <= pair_rows - SWEEPS):
+        outer_faces.extend((top, bottom, with_corners(sides, corners(sides))))
+    given.append(fill(0, given_first))
+    if not outer_faces:
+        given[0], late_sides = lax.optimization_barrier((given[0], sides))
+        outer_faces.extend((top, bottom, with_corners(sides, corners(late_sides))))
+    kept.append(fill(0, kept_first))
 
     table_cols = lax.dynamic_slice_in_dim(table, col * cols, cols, 0)
     kept_rows = lax.dynamic_slice_in_dim(table, row * rows + kept_first, pair_rows, 0)
@@ -435,10 +425,20 @@
     values, packed, lines = 0.0, None, None
     for c, count in enumerate(counts):
         closing = c == len(counts) - 1
-        got, got_lines = fill_part(c, packed)
+        got_lines = None
+        if c > 0:
+            (starts, packed) = lax.optimization_barrier(((given_first, kept_first), packed))
+            given.append(fill(c, starts[0]))
+            if c == 1:
+                kept.extend(fill(later, starts[1]) for later in range(1, len(counts)))
+            got_lines = exchanged(packed)
+        got = lax.ppermute(given[c][0], "gy", swap(gy, 1))
         held = kept[c][0]
         if c > 0:
-            held, got_lines = lax.optimization_barrier((held, got_lines))
+            behind = [held, got_lines] + [piece[0] for piece in kept[c + 1 :]]
+            held, got_lines, *later = lax.optimization_barrier(behind)
+            for n, spectrum in enumerate(later):
+                kept[c + 1 + n][0] = spectrum
             lines = sent_lines(got_lines, counts[c - 1], lines)
             values = values + first_axis(lines, table_parts[c - 1])
         if closing:

time: 420 us -> 401 us (0.955)
  waiting for transfers between devices: 140 us -> 120 us
    ppermute x1, waiting for transfers between devices: 9.5 us -> 0.01 us  [faces(): top = lax.ppermute(block[rows - SWEEPS:], 'gx', up)]
    ppermute x9, waiting for transfers between devices: 39.2 us -> 34.3 us  [exchanged(): lax.ppermute(packed[p], 'gy', swap(gy, p))]
  transfers between devices with their start and end apart: 33 -> 33, of which waited for: 16 -> 13; matrix products, arithmetic and copies ran while one was open for 10% -> 11% of each run, Pallas kernels for 15% -> 18%
where the time goes in v3:
time: 401 us; the launch traced here: 399 us
  Pallas kernels  136 us (34%)
  waiting for transfers between devices  120 us (30%)
  starting transfers between devices  50.1 us (12%)
  local copies, waits for them, and re-layouts  35.9 us (9%)
  blocking collectives  32.5 us (8%)
  other arithmetic  18.6 us (5%)
  matrix products  4.92 us (1%)
    pallas_call x6, Pallas kernels, filled_spectrum(): pl.pallas_call(fill_kernel, grid_spec=pltpu.PrefetchScalarGridSpec(num_sc...  73.9 us
    ppermute x9, waiting for transfers between devices, exchanged(): lax.ppermute(packed[p], 'gy', swap(gy, p))  34.3 us
    pallas_call x1, Pallas kernels, result_block(): pl.pallas_call(lambda *refs: result_kernel(offsets, own, devices, groups,...  33.9 us
    ppermute x9, waiting for transfers between devices, gathered(): pieces[place ^ bit] = lax.ppermute(pieces[place], 'gy', swap(peers, bit))  33.7 us
    all_to_all x1, blocking collectives, on_device(): piece = lax.all_to_all(messages, 'gx', 0, 0, tiled=True)  32.5 us
    pallas_call x3, Pallas kernels, packed_section(): pl.pallas_call(lambda *refs: section_kernel(offsets, closing, *refs), gri...  19.4 us
    all_to_all x3, waiting for transfers between devices, sent_lines(): return lax.all_to_all(lines, 'gx', 0, 0, tiled=True)  19.3 us
    all_to_all x1, waiting for transfers between devices, on_device(): lax.all_to_all(jnp.concatenate(turned, axis=3), ('gy', 'gx'), 0, 0, tiled...  18.5 us
  transfers between devices with their start and end apart: 33, of which 13 were waited for; matrix products, arithmetic and copies ran while one was open for 11% of the time, Pallas kernels for 18%

profile of v3, /device:TPU:0, one launch (start us, length us, event | category | flops | bytes accessed | tf_op | source)
XLA Modules:
  0.0 399.2 jit_solution(265902609541022998)
XLA Ops:
  0.0 1.8 fusion.28
  2.3 2.0 collective-permute-start.1
  4.3 3.6 shard_map.55.marks
  7.8 2.2 fusion.27
  11.2 1.7 pad.16.sides
  12.8 16.7 %shard_map.57 = (f32[16,128,256]{2,1,0:T(8,128)}, f32[16,256]{1,0:T(8,128)}, f32[128,128]{1,0:T(8,128)}) custom-call(s32[1]{0:T(128)} %bitcast.11.base, f32[64,128,512]{2,1,0:T(8,128)} %below.11, f32[64,128,512]{2,1,0:T(8,128)} %below.11, f32[64,128,512]{2,1,0:T(8,128)} %below.11, f32[2,128,512]{2,1,0:T(8,128)} %get-tuple-element.152.top.bottom, ...), custom_call_target="tpu_custom_call" | custom-call | flops 1610612736 | bytes 6291456 | tf_op jit(solution)/shard_map/pallas_call | solution.py:248
  29.8 5.3 %collective-permute-start.4 = (f32[2,128,512]{2,1,0:T(8,128)S(1)}, f32[2,128,512]{2,1,0:T(8,128)S(1)}, u32[]{:S(2)}, u32[]{:S(2)}) collective-permute-start(f32[2,128,512]{2,1,0:T(8,128)S(1)} %copy-done), channel_id=1, source_target_pairs={{4,0},{8,4},{12,8},{16,12},{20,16},{24,20},{28,24},{0,28},{5,1},{9... | collective-permute-start | bytes 1572872 | tf_op jit(solution)/shard_map/ppermute | solution.py:32
  36.6 0.9 constant_dynamic-slice_fusion.4
  38.5 4.8 %collective-permute-start.6 = (f32[2,4,512]{2,1,0:T(4,128)S(1)}, f32[2,4,512]{2,1,0:T(4,128)S(1)}, u32[]{:S(2)}, u32[]{:S(2)}) collective-permute-start(f32[2,4,512]{2,1,0:T(4,128)S(1)} %get-tuple-element.182), channel_id=1, source_target_pairs={{4,0},{8,4},{12,8},{16,12},{20,16},{24,20},{28,24},{0,28},{5,1},{9... | collective-permute-start | bytes 49160 | tf_op jit(solution)/shard_map/ppermute | solution.py:41
  43.3 16.9 %shard_map.56 = (f32[16,128,256]{2,1,0:T(8,128)}, f32[16,256]{1,0:T(8,128)}, f32[128,128]{1,0:T(8,128)}) custom-call(s32[1]{0:T(128)} %bitcast.10.base, f32[64,128,512]{2,1,0:T(8,128)} %below.11, f32[64,128,512]{2,1,0:T(8,128)} %below.11, f32[64,128,512]{2,1,0:T(8,128)} %below.11, f32[2,128,512]{2,1,0:T(8,128)} %get-tuple-element.152.top.bottom, ...), custom_call_target="tpu_custom_call" | custom-call | flops 1610612736 | bytes 6291456 | tf_op jit(solution)/shard_map/pallas_call | solution.py:248
  60.2 1.9 select_maximum_fusion.sides
  64.3 8.1 %shard_map.58 = (f32[16,2,8,640]{3,2,1,0:T(8,128)}, f32[16,2,8,640]{3,2,1,0:T(8,128)}, f32[16,2,8,640]{3,2,1,0:T(8,128)}, f32[16,2,8,640]{3,2,1,0:T(8,128)}, f32[4,64,640]{2,1,0:T(8,128)}) custom-call(s32[1]{0:T(128)} %bitcast.3.refs_0_, f32[4,16]{1,0:T(4,128)} %pad_maximum_fusion.4.refs_1_, f32[16,128,256]{2,1,0:T(8,128)} %get-tuple-element.78.refs_2_, ...), custom_call_target="tpu_custom_call" | custom-call | flops 1610612736 | bytes 8388608 | tf_op jit(solution)/shard_map/pallas_call | solution.py:357
  73.4 10.0 %shard_map.61 = (f32[8,128,256]{2,1,0:T(8,128)}, f32[8,256]{1,0:T(8,128)}, f32[128,128]{1,0:T(8,128)}) custom-call(s32[1]{0:T(128)} %bitcast.25.base, f32[64,128,512]{2,1,0:T(8,128)} %below.11, f32[64,128,512]{2,1,0:T(8,128)} %below.11, f32[64,128,512]{2,1,0:T(8,128)} %below.11, f32[2,128,512]{2,1,0:T(8,128)} %copy-done.2, f32[2,128,512]{2,1,0:T(8,128)} %copy-done.1, ...), custom_call_target="tpu_custom_call" | custom-call | flops 805306368 | bytes 3145728 | tf_op jit(solution)/shard_map/pallas_call | solution.py:248
  84.3 1.5 collective-permute-start.8
  88.0 10.2 %shard_map.59 = (f32[8,128,256]{2,1,0:T(8,128)}, f32[8,256]{1,0:T(8,128)}, f32[128,128]{1,0:T(8,128)}) custom-call(s32[1]{0:T(128)} %bitcast.14.base, f32[64,128,512]{2,1,0:T(8,128)} %below.11, f32[64,128,512]{2,1,0:T(8,128)} %below.11, f32[64,128,512]{2,1,0:T(8,128)} %below.11, f32[2,128,512]{2,1,0:T(8,128)} %copy-done.2, f32[2,128,512]{2,1,0:T(8,128)} %copy-done.1, ...), custom_call_target="tpu_custom_call" | custom-call | flops 805306368 | bytes 3145728 | tf_op jit(solution)/shard_map/pallas_call | solution.py:248
  98.2 10.0 %shard_map.60 = (f32[8,128,256]{2,1,0:T(8,128)}, f32[8,256]{1,0:T(8,128)}, f32[128,128]{1,0:T(8,128)}) custom-call(s32[1]{0:T(128)} %bitcast.15.base, f32[64,128,512]{2,1,0:T(8,128)} %below.11, f32[64,128,512]{2,1,0:T(8,128)} %below.11, f32[64,128,512]{2,1,0:T(8,128)} %below.11, f32[2,128,512]{2,1,0:T(8,128)} %copy-done.2, f32[2,128,512]{2,1,0:T(8,128)} %copy-done.1, ...), custom_call_target="tpu_custom_call" | custom-call | flops 805306368 | bytes 3145728 | tf_op jit(solution)/shard_map/pallas_call | solution.py:248
  108.3 6.2 %collective-permute-done.9 = f32[16,2,8,640]{3,2,1,0:T(8,128)} collective-permute-done((f32[16,2,8,640]{3,2,1,0:T(8,128)}, f32[16,2,8,640]{3,2,1,0:T(8,128)}, u32[]{:S(2)}, u32[]{:S(2)}) %collective-permute-start.9) | collective-permute-done | bytes 655392 | tf_op jit(solution)/shard_map/ppermute | solution.py:744
  114.5 1.2 add.169
  115.8 1.2 add.170
  117.0 1.8 copy.63
  118.8 3.6 all-to-all-start
  122.4 1.0 copy-done.8
  123.3 5.5 %shard_map.62 = (f32[8,2,8,640]{3,2,1,0:T(8,128)}, f32[8,2,8,640]{3,2,1,0:T(8,128)}, f32[8,2,8,640]{3,2,1,0:T(8,128)}, f32[8,2,8,640]{3,2,1,0:T(8,128)}, f32[4,64,640]{2,1,0:T(8,128)}) custom-call(s32[1]{0:T(128)} %bitcast.3.refs_0_, f32[4,8]{1,0:T(4,128)} %pad_maximum_fusion.5.refs_1_, f32[8,128,256]{2,1,0:T(8,128)} %get-tuple-element.100.refs_2_, ...), custom_call_target="tpu_custom_call" | custom-call | flops 805306368 | bytes 4194304 | tf_op jit(solution)/shard_map/pallas_call | solution.py:357
  128.9 10.1 %shard_map.63 = (f32[8,128,256]{2,1,0:T(8,128)}, f32[8,256]{1,0:T(8,128)}, f32[128,128]{1,0:T(8,128)}) custom-call(s32[1]{0:T(128)} %bitcast.36.base, f32[64,128,512]{2,1,0:T(8,128)} %below.11, f32[64,128,512]{2,1,0:T(8,128)} %below.11, f32[64,128,512]{2,1,0:T(8,128)} %below.11, f32[2,128,512]{2,1,0:T(8,128)} %copy-done.2, f32[2,128,512]{2,1,0:T(8,128)} %copy-done.1, ...), custom_call_target="tpu_custom_call" | custom-call | flops 805306368 | bytes 3145728 | tf_op jit(solution)/shard_map/pallas_call | solution.py:248
  139.7 1.0 concatenate.54
  141.9 1.5 collective-permute-start.12
  144.8 1.0 fusion.14.refs_8_
  145.8 6.9 %collective-permute-done.12 = f32[8,2,8,640]{3,2,1,0:T(8,128)S(1)} collective-permute-done((f32[8,2,8,640]{3,2,1,0:T(8,128)}, f32[8,2,8,640]{3,2,1,0:T(8,128)S(1)}, u32[]{:S(2)}, u32[]{:S(2)}) %collective-permute-start.12) | collective-permute-done | bytes 327712 | tf_op jit(solution)/shard_map/ppermute | solution.py:744
  152.6 6.1 %collective-permute-done.13 = f32[8,2,8,640]{3,2,1,0:T(8,128)S(1)} collective-permute-done((f32[8,2,8,640]{3,2,1,0:T(8,128)}, f32[8,2,8,640]{3,2,1,0:T(8,128)S(1)}, u32[]{:S(2)}, u32[]{:S(2)}) %collective-permute-start.13) | collective-permute-done | bytes 327712 | tf_op jit(solution)/shard_map/ppermute | solution.py:744
  158.8 1.0 copy-done.10
  159.7 5.9 %shard_map.64 = (f32[13,2,8,640]{3,2,1,0:T(8,128)}, f32[13,2,8,640]{3,2,1,0:T(8,128)}, f32[13,2,8,640]{3,2,1,0:T(8,128)}, f32[13,2,8,640]{3,2,1,0:T(8,128)}, f32[4,64,640]{2,1,0:T(8,128)}) custom-call(s32[1]{0:T(128)} %bitcast.3.refs_0_, f32[4,8]{1,0:T(4,128)} %pad_maximum_fusion.6.refs_1_, f32[8,128,256]{2,1,0:T(8,128)} %get-tuple-element.117.refs_2_, ...), custom_call_target="tpu_custom_call" | custom-call | flops 805306368 | bytes 4194304 | tf_op jit(solution)/shard_map/pallas_call | solution.py:357
  165.6 1.6 collective-permute-start.15
  168.1 1.2 copy.65
  169.3 5.6 %all-to-all-start.1 = ((f32[8,2,16,640]{3,1,2,0:T(2,128)}), f32[8,2,16,640]{3,1,2,0:T(2,128)S(1)}, u32[]{:S(2)}, u32[]{:S(2)}) async-start(f32[8,2,16,640]{3,1,2,0:T(2,128)} %copy.65), calls=%async_computation.1 | async-start | bytes 1310720 | tf_op jit(solution)/shard_map/all_to_all | solution.py:754
  174.9 6.0 %collective-permute-done.15 = f32[13,2,8,640]{3,2,1,0:T(8,128)} collective-permute-done((f32[13,2,8,640]{3,2,1,0:T(8,128)}, f32[13,2,8,640]{3,2,1,0:T(8,128)}, u32[]{:S(2)}, u32[]{:S(2)}) %collective-permute-start.15) | collective-permute-done | bytes 532512 | tf_op jit(solution)/shard_map/ppermute | solution.py:744
  180.9 1.0 slice_add_fusion.1
  181.9 9.1 %collective-permute-done.17 = f32[13,2,8,640]{3,2,1,0:T(8,128)} collective-permute-done((f32[13,2,8,640]{3,2,1,0:T(8,128)S(1)}, f32[13,2,8,640]{3,2,1,0:T(8,128)}, u32[]{:S(2)}, u32[]{:S(2)}) %collective-permute-start.17) | collective-permute-done | bytes 532512 | tf_op jit(solution)/shard_map/ppermute | solution.py:744
  191.1 1.1 slice_add_fusion
  192.2 1.2 slice_add_fusion.2
  193.4 1.4 copy.67
  194.8 5.6 %all-to-all-start.2 = ((f32[8,2,21,640]{3,1,2,0:T(2,128)}), f32[8,2,21,640]{3,1,2,0:T(2,128)S(1)}, u32[]{:S(2)}, u32[]{:S(2)}) async-start(f32[8,2,21,640]{3,1,2,0:T(2,128)} %copy.67), calls=%async_computation.2 | async-start | bytes 1720320 | tf_op jit(solution)/shard_map/all_to_all | solution.py:754
  200.5 1.1 broadcast_select_fusion
  201.6 1.9 convolution_bitcast_fusion
  203.5 19.3 %all-to-all-done.2 = f32[8,2,21,640]{3,1,2,0:T(2,128)S(1)} async-done(((f32[8,2,21,640]{3,1,2,0:T(2,128)}), f32[8,2,21,640]{3,1,2,0:T(2,128)S(1)}, u32[]{:S(2)}, u32[]{:S(2)}) %all-to-all-start.2) | async-done | bytes 860192 | tf_op jit(solution)/shard_map/all_to_all | solution.py:754
  225.0 1.0 copy.97
  226.2 2.4 concatenate.58
  228.6 3.7 all-to-all-start.3
  232.9 18.5 %all-to-all-done.3 = f32[32,2,2,1280]{3,2,1,0:T(2,128)S(1)} async-done(((f32[32,2,2,1280]{3,2,1,0:T(2,128)}), f32[32,2,2,1280]{3,2,1,0:T(2,128)S(1)}, u32[]{:S(2)}, u32[]{:S(2)}) %all-to-all-start.3) | async-done | bytes 655392 | tf_op jit(solution)/shard_map/all_to_all | solution.py:468
  251.4 1.0 copy.70
  252.4 5.6 %shard_map.65 = (f32[8,288,128]{2,1,0:T(8,128)}, f32[8,256,128]{2,1,0:T(8,128)}, f32[8,128,128]{2,1,0:T(8,128)}) custom-call(f32[2,256,640]{2,1,0:T(8,128)} %bitcast.170, f32[2,64,1280]{2,1,0:T(8,128)} %bitcast.177, f32[2,5,640]{2,1,0:T(8,128)} %copy_multiply_fusion.refs_2_), custom_call_target="tpu_custom_call" | custom-call | tf_op jit(solution)/shard_map/pallas_call | solution.py:603
  258.0 32.5 %all_to_all.35 = f32[8,288,128]{2,1,0:T(8,128)S(1)} all-to-all(f32[8,288,128]{2,1,0:T(8,128)} %get-tuple-element.139), channel_id=1, replica_groups=mesh['gx'=8,'gy'=4] {'gx'}, dimensions={0} | all-to-all | bytes 2359296 | tf_op jit(solution)/shard_map/all_to_all | solution.py:484
  290.5 1.2 collective-permute-start.19
  291.7 3.6 all-to-all-start.5
  295.4 21.5 %collective-permute-done.19 = f32[8,288,128]{2,1,0:T(8,128)} collective-permute-done((f32[8,288,128]{2,1,0:T(8,128)S(1)}, f32[8,288,128]{2,1,0:T(8,128)}, u32[]{:S(2)}, u32[]{:S(2)}) %collective-permute-start.19) | collective-permute-done | bytes 1179680 | tf_op jit(solution)/shard_map/ppermute | solution.py:737
  318.9 1.9 all-to-all-done.5
  321.3 4.0 %all-to-all-start.6 = ((f32[8,128,128]{2,1,0:T(8,128)}), f32[8,128,128]{2,1,0:T(8,128)S(1)}, u32[]{:S(2)}, u32[]{:S(2)}) async-start(f32[8,128,128]{2,1,0:T(8,128)} %get-tuple-element.147), calls=%async_computation.6 | async-start | bytes 1048576 | tf_op jit(solution)/shard_map/all_to_all | solution.py:484
  326.3 0.9 slice_bitcast_fusion.8
  329.1 11.2 %all-to-all-done.6 = f32[8,128,128]{2,1,0:T(8,128)S(1)} async-done(((f32[8,128,128]{2,1,0:T(8,128)}), f32[8,128,128]{2,1,0:T(8,128)S(1)}, u32[]{:S(2)}, u32[]{:S(2)}) %all-to-all-start.6) | async-done | bytes 524320 | tf_op jit(solution)/shard_map/all_to_all | solution.py:484
  340.3 4.4 %collective-permute-done.22 = f32[8,256,128]{2,1,0:T(8,128)} collective-permute-done((f32[8,256,128]{2,1,0:T(8,128)S(1)}, f32[8,256,128]{2,1,0:T(8,128)}, u32[]{:S(2)}, u32[]{:S(2)}) %collective-permute-start.22) | collective-permute-done | bytes 1048608 | tf_op jit(solution)/shard_map/ppermute | solution.py:737
  344.7 1.7 collective-permute-start.25
  349.7 7.8 %collective-permute-done.25 = f32[8,128,128]{2,1,0:T(8,128)S(1)} collective-permute-done((f32[8,128,128]{2,1,0:T(8,128)S(1)}, f32[8,128,128]{2,1,0:T(8,128)S(1)}, u32[]{:S(2)}, u32[]{:S(2)}) %collective-permute-start.25) | collective-permute-done | bytes 524320 | tf_op jit(solution)/shard_map/ppermute | solution.py:737
  358.3 1.3 dynamic-update-slice.4
  359.6 1.0 pad_maximum_fusion.2
  365.1 33.9 %shard_map.66 = f32[64,128,512]{2,1,0:T(8,128)} custom-call(s32[4]{0:T(128)} %pad_add_fusion.refs_0_, f32[64,640]{1,0:T(8,128)} %bitcast.187, f32[64,256]{1,0:T(8,128)} %slice.385.refs_2_, f32[128,128]{1,0:T(8,128)} %pad.19.refs_3_, bf16[128,256]{1,0:T(8,128)(2,1)} %fusion.16.refs_4_, bf16[256,256]{1,0:T(8,128)(2,1)} %fusion.8.refs_5_, ...), custom_call_target="tpu_custom_call" | custom-call | tf_op jit(solution)/shard_map/pallas_call | solution.py:708
  (185 shorter events, 31.7 us)
Async XLA Ops:
  1.8 8.3 %collective-permute-start = (f32[64,2,512]{2,1,0:T(2,128)S(1)}, f32[64,2,512]{2,1,0:T(2,128)S(1)}, u32[]{:S(2)}, u32[]{:S(2)}) collective-permute-start(f32[64,2,512]{2,1,0:T(2,128)S(1)} %get-tuple-element.153), channel_id=1, source_target_pairs={{0,1},{1,2},{2,3},{3,0},{4,5},{5,6},{6,7},{7,4},{8,9},{9,10},{10,1... | collective-permute-start | bytes 786440 | tf_op jit(solution)/shard_map/ppermute | solution.py:33
  2.3 8.6 %collective-permute-start.1 = (f32[64,2,512]{2,1,0:T(2,128)S(1)}, f32[64,2,512]{2,1,0:T(2,128)S(1)}, u32[]{:S(2)}, u32[]{:S(2)}) collective-permute-start(f32[64,2,512]{2,1,0:T(2,128)S(1)} %get-tuple-element.154), channel_id=1, source_target_pairs={{1,0},{2,1},{3,2},{0,3},{5,4},{6,5},{7,6},{4,7},{9,8},{10,9},{11,1... | collective-permute-start | bytes 786440 | tf_op jit(solution)/shard_map/ppermute | solution.py:34
  12.8 17.0 %copy-start = (f32[2,128,512]{2,1,0:T(8,128)S(1)}, f32[2,128,512]{2,1,0:T(8,128)}, u32[]{:S(2)}) copy-start(f32[2,128,512]{2,1,0:T(8,128)} %get-tuple-element.152.top.bottom) | copy-start | bytes 1572868
  12.8 22.3 %copy-start.6 = (f32[512,257]{0,1:T(8,128)S(1)}, f32[512,257]{0,1:T(8,128)}, u32[]{:S(2)}) copy-start(f32[512,257]{0,1:T(8,128)} %constant.112.clone) | copy-start | bytes 1579012
  29.5 32.5 %collective-permute-start.2 = (f32[16,128,256]{2,1,0:T(8,128)}, f32[16,128,256]{2,1,0:T(8,128)}, u32[]{:S(2)}, u32[]{:S(2)}) collective-permute-start(f32[16,128,256]{2,1,0:T(8,128)} %get-tuple-element.82), channel_id=1, source_target_pairs={{0,1},{1,0},{2,3},{3,2},{4,5},{5,4},{6,7},{7,6},{8,9},{9,8},{10,11... | collective-permute-start | bytes 6291464 | tf_op jit(solution)/shard_map/ppermute | solution.py:435
  29.8 42.7 %collective-permute-start.4 = (f32[2,128,512]{2,1,0:T(8,128)S(1)}, f32[2,128,512]{2,1,0:T(8,128)S(1)}, u32[]{:S(2)}, u32[]{:S(2)}) collective-permute-start(f32[2,128,512]{2,1,0:T(8,128)S(1)} %copy-done), channel_id=1, source_target_pairs={{4,0},{8,4},{12,8},{16,12},{20,16},{24,20},{28,24},{0,28},{5,1},{9... | collective-permute-start | bytes 1572872 | tf_op jit(solution)/shard_map/ppermute | solution.py:32
  35.1 37.3 %collective-permute-start.3 = (f32[2,128,512]{2,1,0:T(8,128)}, f32[2,128,512]{2,1,0:T(8,128)S(1)}, u32[]{:S(2)}, u32[]{:S(2)}) collective-permute-start(f32[2,128,512]{2,1,0:T(8,128)} %get-tuple-element.151), channel_id=1, source_target_pairs={{0,4},{4,8},{8,12},{12,16},{16,20},{20,24},{24,28},{28,0},{1,5},{5... | collective-permute-start | bytes 1572872 | tf_op jit(solution)/shard_map/ppermute | solution.py:31
  38.4 21.7 %collective-permute-start.5 = (f32[2,4,512]{2,1,0:T(4,128)S(1)}, f32[2,4,512]{2,1,0:T(4,128)S(1)}, u32[]{:S(2)}, u32[]{:S(2)}) collective-permute-start(f32[2,4,512]{2,1,0:T(4,128)S(1)} %get-tuple-element.181), channel_id=1, source_target_pairs={{0,4},{4,8},{8,12},{12,16},{16,20},{20,24},{24,28},{28,0},{1,5},{5... | collective-permute-start | bytes 49160 | tf_op jit(solution)/shard_map/ppermute | solution.py:40
  38.5 21.7 %collective-permute-start.6 = (f32[2,4,512]{2,1,0:T(4,128)S(1)}, f32[2,4,512]{2,1,0:T(4,128)S(1)}, u32[]{:S(2)}, u32[]{:S(2)}) collective-permute-start(f32[2,4,512]{2,1,0:T(4,128)S(1)} %get-tuple-element.182), channel_id=1, source_target_pairs={{4,0},{8,4},{12,8},{16,12},{20,16},{24,20},{28,24},{0,28},{5,1},{9... | collective-permute-start | bytes 49160 | tf_op jit(solution)/shard_map/ppermute | solution.py:41
  72.4 0.8 copy-start.2
  72.4 1.0 copy-start.1
  83.4 4.6 %copy-start.24 = (f32[16,256]{1,0:T(8,128)S(1)}, f32[16,256]{1,0:T(8,128)}, u32[]{:S(2)}) copy-start(f32[16,256]{1,0:T(8,128)} %get-tuple-element.126) | copy-start | bytes 49156
  83.4 39.0 %collective-permute-start.10 = (f32[8,128,256]{2,1,0:T(8,128)}, f32[8,128,256]{2,1,0:T(8,128)S(1)}, u32[]{:S(2)}, u32[]{:S(2)}) collective-permute-start(f32[8,128,256]{2,1,0:T(8,128)} %get-tuple-element.102), channel_id=1, source_target_pairs={{0,1},{1,0},{2,3},{3,2},{4,5},{5,4},{6,7},{7,6},{8,9},{9,8},{10,11... | collective-permute-start | bytes 3145736 | tf_op jit(solution)/shard_map/ppermute | solution.py:435
  83.7 24.6 %collective-permute-start.7 = (f32[16,2,8,640]{3,2,1,0:T(8,128)}, f32[16,2,8,640]{3,2,1,0:T(8,128)S(1)}, u32[]{:S(2)}, u32[]{:S(2)}) collective-permute-start(f32[16,2,8,640]{3,2,1,0:T(8,128)} %get-tuple-element.91), channel_id=1, source_target_pairs={{0,1},{1,0},{2,3},{3,2},{4,5},{5,4},{6,7},{7,6},{8,9},{9,8},{10,11... | collective-permute-start | bytes 1966088 | tf_op jit(solution)/shard_map/ppermute | solution.py:744
  84.3 24.0 %collective-permute-start.8 = (f32[16,2,8,640]{3,2,1,0:T(8,128)}, f32[16,2,8,640]{3,2,1,0:T(8,128)}, u32[]{:S(2)}, u32[]{:S(2)}) collective-permute-start(f32[16,2,8,640]{3,2,1,0:T(8,128)} %get-tuple-element.92), channel_id=1, source_target_pairs={{0,2},{1,3},{2,0},{3,1},{4,6},{5,7},{6,4},{7,5},{8,10},{9,11},{10,... | collective-permute-start | bytes 1966088 | tf_op jit(solution)/shard_map/ppermute | solution.py:744
  85.8 28.7 %collective-permute-start.9 = (f32[16,2,8,640]{3,2,1,0:T(8,128)}, f32[16,2,8,640]{3,2,1,0:T(8,128)}, u32[]{:S(2)}, u32[]{:S(2)}) collective-permute-start(f32[16,2,8,640]{3,2,1,0:T(8,128)} %get-tuple-element.93), channel_id=1, source_target_pairs={{0,3},{1,2},{2,1},{3,0},{4,7},{5,6},{6,5},{7,4},{8,11},{9,10},{10,... | collective-permute-start | bytes 1966088 | tf_op jit(solution)/shard_map/ppermute | solution.py:744
  98.2 10.0 %copy-start.25 = (f32[8,256]{1,0:T(8,128)S(1)}, f32[8,256]{1,0:T(8,128)}, u32[]{:S(2)}) copy-start(f32[8,256]{1,0:T(8,128)} %get-tuple-element.127) | copy-start | bytes 24580
  98.2 16.2 %copy-start.11 = (f32[16,2,8,640]{3,2,1,0:T(8,128)S(1)}, f32[16,2,8,640]{3,2,1,0:T(8,128)}, u32[]{:S(2)}) copy-start(f32[16,2,8,640]{3,2,1,0:T(8,128)} %get-tuple-element.95) | copy-start | bytes 1966084
  108.3 6.2 %copy-start.12 = (f32[16,2,8,640]{3,2,1,0:T(8,128)}, f32[16,2,8,640]{3,2,1,0:T(8,128)S(1)}, u32[]{:S(2)}) copy-start(f32[16,2,8,640]{3,2,1,0:T(8,128)S(1)} %collective-permute-done.7) | copy-start | bytes 1966084
  114.5 1.3 copy-start.13
  118.8 49.3 %all-to-all-start = ((f32[8,2,32,640]{3,1,2,0:T(2,128)}), f32[8,2,32,640]{3,1,2,0:T(2,128)S(1)}, u32[]{:S(2)}, u32[]{:S(2)}) async-start(f32[8,2,32,640]{3,1,2,0:T(2,128)} %copy.63), calls=%async_computation | async-start | bytes 2621440 | tf_op jit(solution)/shard_map/all_to_all | solution.py:754
  122.4 1.0 copy-start.8
  128.8 10.9 %copy-start.18 = (f32[128,128]{1,0:T(8,128)S(1)}, f32[128,128]{1,0:T(8,128)}, u32[]{:S(2)}) copy-start(f32[128,128]{1,0:T(8,128)} %get-tuple-element.120) | copy-start | bytes 196612
  128.8 10.9 %copy-start.19 = (f32[128,128]{1,0:T(8,128)S(1)}, f32[128,128]{1,0:T(8,128)}, u32[]{:S(2)}) copy-start(f32[128,128]{1,0:T(8,128)} %get-tuple-element.123) | copy-start | bytes 196612
  128.8 10.9 %copy-start.20 = (f32[128,128]{1,0:T(8,128)S(1)}, f32[128,128]{1,0:T(8,128)}, u32[]{:S(2)}) copy-start(f32[128,128]{1,0:T(8,128)} %get-tuple-element.121) | copy-start | bytes 196612
  128.8 10.9 %copy-start.21 = (f32[128,128]{1,0:T(8,128)S(1)}, f32[128,128]{1,0:T(8,128)}, u32[]{:S(2)}) copy-start(f32[128,128]{1,0:T(8,128)} %get-tuple-element.124) | copy-start | bytes 196612
  128.9 10.9 %copy-start.22 = (f32[128,128]{1,0:T(8,128)S(1)}, f32[128,128]{1,0:T(8,128)}, u32[]{:S(2)}) copy-start(f32[128,128]{1,0:T(8,128)} %get-tuple-element.125) | copy-start | bytes 196612
  128.9 12.6 %copy-start.23 = (f32[16,256]{1,0:T(8,128)S(1)}, f32[16,256]{1,0:T(8,128)}, u32[]{:S(2)}) copy-start(f32[16,256]{1,0:T(8,128)} %get-tuple-element.129) | copy-start | bytes 49156
  128.9 12.6 %copy-start.26 = (f32[8,256]{1,0:T(8,128)S(1)}, f32[8,256]{1,0:T(8,128)}, u32[]{:S(2)}) copy-start(f32[8,256]{1,0:T(8,128)} %get-tuple-element.130) | copy-start | bytes 24580
  128.9 12.6 %copy-start.27 = (f32[8,256]{1,0:T(8,128)S(1)}, f32[8,256]{1,0:T(8,128)}, u32[]{:S(2)}) copy-start(f32[8,256]{1,0:T(8,128)} %get-tuple-element.131) | copy-start | bytes 24580
  139.0 19.8 %collective-permute-start.14 = (f32[8,128,256]{2,1,0:T(8,128)}, f32[8,128,256]{2,1,0:T(8,128)S(1)}, u32[]{:S(2)}, u32[]{:S(2)}) collective-permute-start(f32[8,128,256]{2,1,0:T(8,128)} %get-tuple-element.119), channel_id=1, source_target_pairs={{0,1},{1,0},{2,3},{3,2},{4,5},{5,4},{6,7},{7,6},{8,9},{9,8},{10,11... | collective-permute-start | bytes 3145736 | tf_op jit(solution)/shard_map/ppermute | solution.py:435
  141.8 4.0 %collective-permute-start.11 = (f32[8,2,8,640]{3,2,1,0:T(8,128)}, f32[8,2,8,640]{3,2,1,0:T(8,128)S(1)}, u32[]{:S(2)}, u32[]{:S(2)}) collective-permute-start(f32[8,2,8,640]{3,2,1,0:T(8,128)} %get-tuple-element.109), channel_id=1, source_target_pairs={{0,1},{1,0},{2,3},{3,2},{4,5},{5,4},{6,7},{7,6},{8,9},{9,8},{10,11... | collective-permute-start | bytes 983048 | tf_op jit(solution)/shard_map/ppermute | solution.py:744
  141.9 10.8 %collective-permute-start.12 = (f32[8,2,8,640]{3,2,1,0:T(8,128)}, f32[8,2,8,640]{3,2,1,0:T(8,128)S(1)}, u32[]{:S(2)}, u32[]{:S(2)}) collective-permute-start(f32[8,2,8,640]{3,2,1,0:T(8,128)} %get-tuple-element.110), channel_id=1, source_target_pairs={{0,2},{1,3},{2,0},{3,1},{4,6},{5,7},{6,4},{7,5},{8,10},{9,11},{10,... | collective-permute-start | bytes 983048 | tf_op jit(solution)/shard_map/ppermute | solution.py:744
  143.4 15.3 %collective-permute-start.13 = (f32[8,2,8,640]{3,2,1,0:T(8,128)}, f32[8,2,8,640]{3,2,1,0:T(8,128)S(1)}, u32[]{:S(2)}, u32[]{:S(2)}) collective-permute-start(f32[8,2,8,640]{3,2,1,0:T(8,128)} %get-tuple-element.111), channel_id=1, source_target_pairs={{0,3},{1,2},{2,1},{3,0},{4,7},{5,6},{6,5},{7,4},{8,11},{9,10},{10,... | collective-permute-start | bytes 983048 | tf_op jit(solution)/shard_map/ppermute | solution.py:744
  158.8 1.0 copy-start.10
  159.7 7.4 %copy-start.17 = (f32[8,2,8,640]{3,2,1,0:T(8,128)S(1)}, f32[8,2,8,640]{3,2,1,0:T(8,128)}, u32[]{:S(2)}) copy-start(f32[8,2,8,640]{3,2,1,0:T(8,128)} %get-tuple-element.112) | copy-start | bytes 983044
  165.6 1.7 copy-start.28
  165.6 15.3 %collective-permute-start.15 = (f32[13,2,8,640]{3,2,1,0:T(8,128)}, f32[13,2,8,640]{3,2,1,0:T(8,128)}, u32[]{:S(2)}, u32[]{:S(2)}) collective-permute-start(f32[13,2,8,640]{3,2,1,0:T(8,128)} %get-tuple-element.134), channel_id=1, source_target_pairs={{0,2},{1,3},{2,0},{3,1},{4,6},{5,7},{6,4},{7,5},{8,10},{9,11},{10,... | collective-permute-start | bytes 1597448 | tf_op jit(solution)/shard_map/ppermute | solution.py:744
  167.2 14.7 %collective-permute-start.16 = (f32[13,2,8,640]{3,2,1,0:T(8,128)}, f32[13,2,8,640]{3,2,1,0:T(8,128)}, u32[]{:S(2)}, u32[]{:S(2)}) collective-permute-start(f32[13,2,8,640]{3,2,1,0:T(8,128)} %get-tuple-element.135), channel_id=1, source_target_pairs={{0,1},{1,0},{2,3},{3,2},{4,5},{5,4},{6,7},{7,6},{8,9},{9,8},{10,11... | collective-permute-start | bytes 1597448 | tf_op jit(solution)/shard_map/ppermute | solution.py:744
  167.3 23.7 %collective-permute-start.17 = (f32[13,2,8,640]{3,2,1,0:T(8,128)S(1)}, f32[13,2,8,640]{3,2,1,0:T(8,128)}, u32[]{:S(2)}, u32[]{:S(2)}) collective-permute-start(f32[13,2,8,640]{3,2,1,0:T(8,128)S(1)} %copy-done.28), channel_id=1, source_target_pairs={{0,3},{1,2},{2,1},{3,0},{4,7},{5,6},{6,5},{7,4},{8,11},{9,10},{10,... | collective-permute-start | bytes 1597448 | tf_op jit(solution)/shard_map/ppermute | solution.py:744
  168.1 12.8 %copy-start.14 = (f32[13,2,8,640]{3,2,1,0:T(8,128)S(1)}, f32[13,2,8,640]{3,2,1,0:T(8,128)}, u32[]{:S(2)}) copy-start(f32[13,2,8,640]{3,2,1,0:T(8,128)} %get-tuple-element.133) | copy-start | bytes 1597444
  169.3 24.1 %all-to-all-start.1 = ((f32[8,2,16,640]{3,1,2,0:T(2,128)}), f32[8,2,16,640]{3,1,2,0:T(2,128)S(1)}, u32[]{:S(2)}, u32[]{:S(2)}) async-start(f32[8,2,16,640]{3,1,2,0:T(2,128)} %copy.65), calls=%async_computation.1 | async-start | bytes 1310720 | tf_op jit(solution)/shard_map/all_to_all | solution.py:754
  194.8 28.0 %all-to-all-start.2 = ((f32[8,2,21,640]{3,1,2,0:T(2,128)}), f32[8,2,21,640]{3,1,2,0:T(2,128)S(1)}, u32[]{:S(2)}, u32[]{:S(2)}) async-start(f32[8,2,21,640]{3,1,2,0:T(2,128)} %copy.67), calls=%async_computation.2 | async-start | bytes 1720320 | tf_op jit(solution)/shard_map/all_to_all | solution.py:754
  222.9 1.3 copy-start.29
  225.0 1.1 copy-start.4
  228.6 22.8 %all-to-all-start.3 = ((f32[32,2,2,1280]{3,2,1,0:T(2,128)}), f32[32,2,2,1280]{3,2,1,0:T(2,128)S(1)}, u32[]{:S(2)}, u32[]{:S(2)}) async-start(f32[32,2,2,1280]{3,2,1,0:T(2,128)} %concatenate.58), calls=%async_computation.3 | async-start | bytes 1310720 | tf_op jit(solution)/shard_map/all_to_all | solution.py:468
  290.5 30.9 %copy-start.3 = (f32[8,288,128]{2,1,0:T(8,128)}, f32[8,288,128]{2,1,0:T(8,128)S(1)}, u32[]{:S(2)}) copy-start(f32[8,288,128]{2,1,0:T(8,128)S(1)} %all_to_all.35) | copy-start | bytes 3538948
  290.5 26.4 %collective-permute-start.19 = (f32[8,288,128]{2,1,0:T(8,128)S(1)}, f32[8,288,128]{2,1,0:T(8,128)}, u32[]{:S(2)}, u32[]{:S(2)}) collective-permute-start(f32[8,288,128]{2,1,0:T(8,128)S(1)} %all_to_all.35), channel_id=1, source_target_pairs={{0,2},{1,3},{2,0},{3,1},{4,6},{5,7},{6,4},{7,5},{8,10},{9,11},{10,... | collective-permute-start | bytes 3538952 | tf_op jit(solution)/shard_map/ppermute | solution.py:737
  291.7 29.1 %all-to-all-start.5 = ((f32[8,256,128]{2,1,0:T(8,128)}), f32[8,256,128]{2,1,0:T(8,128)S(1)}, u32[]{:S(2)}, u32[]{:S(2)}) async-start(f32[8,256,128]{2,1,0:T(8,128)} %get-tuple-element.142), calls=%async_computation.5 | async-start | bytes 2097152 | tf_op jit(solution)/shard_map/all_to_all | solution.py:484
  295.2 25.6 %collective-permute-start.18 = (f32[8,288,128]{2,1,0:T(8,128)S(1)}, f32[8,288,128]{2,1,0:T(8,128)}, u32[]{:S(2)}, u32[]{:S(2)}) collective-permute-start(f32[8,288,128]{2,1,0:T(8,128)S(1)} %all_to_all.35), channel_id=1, source_target_pairs={{0,1},{1,0},{2,3},{3,2},{4,5},{5,4},{6,7},{7,6},{8,9},{9,8},{10,11... | collective-permute-start | bytes 3538952 | tf_op jit(solution)/shard_map/ppermute | solution.py:737
  316.8 10.3 %collective-permute-start.20 = (f32[8,288,128]{2,1,0:T(8,128)}, f32[8,288,128]{2,1,0:T(8,128)}, u32[]{:S(2)}, u32[]{:S(2)}) collective-permute-start(f32[8,288,128]{2,1,0:T(8,128)} %collective-permute-done.19), channel_id=1, source_target_pairs={{0,1},{1,0},{2,3},{3,2},{4,5},{5,4},{6,7},{7,6},{8,9},{9,8},{10,11... | collective-permute-start | bytes 3538952 | tf_op jit(solution)/shard_map/ppermute | solution.py:737
  320.8 7.4 %copy-start.5 = (f32[8,256,128]{2,1,0:T(8,128)}, f32[8,256,128]{2,1,0:T(8,128)S(1)}, u32[]{:S(2)}) copy-start(f32[8,256,128]{2,1,0:T(8,128)S(1)} %all-to-all-done.5) | copy-start | bytes 3145732
  320.8 23.9 %collective-permute-start.22 = (f32[8,256,128]{2,1,0:T(8,128)S(1)}, f32[8,256,128]{2,1,0:T(8,128)}, u32[]{:S(2)}, u32[]{:S(2)}) collective-permute-start(f32[8,256,128]{2,1,0:T(8,128)S(1)} %all-to-all-done.5), channel_id=1, source_target_pairs={{0,2},{1,3},{2,0},{3,1},{4,6},{5,7},{6,4},{7,5},{8,10},{9,11},{10,... | collective-permute-start | bytes 3145736 | tf_op jit(solution)/shard_map/ppermute | solution.py:737
  321.3 23.3 %collective-permute-start.21 = (f32[8,256,128]{2,1,0:T(8,128)S(1)}, f32[8,256,128]{2,1,0:T(8,128)}, u32[]{:S(2)}, u32[]{:S(2)}) collective-permute-start(f32[8,256,128]{2,1,0:T(8,128)S(1)} %all-to-all-done.5), channel_id=1, source_target_pairs={{0,1},{1,0},{2,3},{3,2},{4,5},{5,4},{6,7},{7,6},{8,9},{9,8},{10,11... | collective-permute-start | bytes 3145736 | tf_op jit(solution)/shard_map/ppermute | solution.py:737
  321.3 18.9 %all-to-all-start.6 = ((f32[8,128,128]{2,1,0:T(8,128)}), f32[8,128,128]{2,1,0:T(8,128)S(1)}, u32[]{:S(2)}, u32[]{:S(2)}) async-start(f32[8,128,128]{2,1,0:T(8,128)} %get-tuple-element.147), calls=%async_computation.6 | async-start | bytes 1048576 | tf_op jit(solution)/shard_map/all_to_all | solution.py:484
  340.3 20.9 %copy-start.7 = (f32[8,128,128]{2,1,0:T(8,128)}, f32[8,128,128]{2,1,0:T(8,128)S(1)}, u32[]{:S(2)}) copy-start(f32[8,128,128]{2,1,0:T(8,128)S(1)} %all-to-all-done.6) | copy-start | bytes 1572868
  344.7 12.9 %collective-permute-start.25 = (f32[8,128,128]{2,1,0:T(8,128)S(1)}, f32[8,128,128]{2,1,0:T(8,128)S(1)}, u32[]{:S(2)}, u32[]{:S(2)}) collective-permute-start(f32[8,128,128]{2,1,0:T(8,128)S(1)} %all-to-all-done.6), channel_id=1, source_target_pairs={{0,2},{1,3},{2,0},{3,1},{4,6},{5,7},{6,4},{7,5},{8,10},{9,11},{10,... | collective-permute-start | bytes 1572872 | tf_op jit(solution)/shard_map/ppermute | solution.py:737
  346.4 17.5 %collective-permute-start.23 = (f32[8,256,128]{2,1,0:T(8,128)}, f32[8,256,128]{2,1,0:T(8,128)S(1)}, u32[]{:S(2)}, u32[]{:S(2)}) collective-permute-start(f32[8,256,128]{2,1,0:T(8,128)} %collective-permute-done.22), channel_id=1, source_target_pairs={{0,1},{1,0},{2,3},{3,2},{4,5},{5,4},{6,7},{7,6},{8,9},{9,8},{10,11... | collective-permute-start | bytes 3145736 | tf_op jit(solution)/shard_map/ppermute | solution.py:737
  349.2 14.6 %collective-permute-start.24 = (f32[8,128,128]{2,1,0:T(8,128)S(1)}, f32[8,128,128]{2,1,0:T(8,128)S(1)}, u32[]{:S(2)}, u32[]{:S(2)}) collective-permute-start(f32[8,128,128]{2,1,0:T(8,128)S(1)} %all-to-all-done.6), channel_id=1, source_target_pairs={{0,1},{1,0},{2,3},{3,2},{4,5},{5,4},{6,7},{7,6},{8,9},{9,8},{10,11... | collective-permute-start | bytes 1572872 | tf_op jit(solution)/shard_map/ppermute | solution.py:737
  357.6 5.7 %copy-start.15 = (f32[8,128,128]{2,1,0:T(8,128)}, f32[8,128,128]{2,1,0:T(8,128)S(1)}, u32[]{:S(2)}) copy-start(f32[8,128,128]{2,1,0:T(8,128)S(1)} %collective-permute-done.25) | copy-start | bytes 1572868
  357.6 6.3 %collective-permute-start.26 = (f32[8,128,128]{2,1,0:T(8,128)S(1)}, f32[8,128,128]{2,1,0:T(8,128)}, u32[]{:S(2)}, u32[]{:S(2)}) collective-permute-start(f32[8,128,128]{2,1,0:T(8,128)S(1)} %collective-permute-done.25), channel_id=1, source_target_pairs={{0,1},{1,0},{2,3},{3,2},{4,5},{5,4},{6,7},{7,6},{8,9},{9,8},{10,11... | collective-permute-start | bytes 1572872 | tf_op jit(solution)/shard_map/ppermute | solution.py:737
  363.9 0.8 copy-start.16
  363.9 1.2 copy-start.9

commit v4 on v3

--- a/solution.py
+++ b/solution.py
@@ -24,25 +24,22 @@
 FREE = ((8 - SWEEPS, 8 - SWEEPS), (0, 0))
 
 
-def faces(block):
+def side_faces(block):
+    cols = block.shape[1]
+    right, left = ring("gy")
+    before = lax.ppermute(block[:, cols - SWEEPS :], "gy", right)
+    after = lax.ppermute(block[:, :SWEEPS], "gy", left)
+    return jnp.concatenate([before, after], axis=1)
+
+
+def end_faces(block, sides):
     rows, cols, _ = block.shape
     up, down = ring("gx")
-    right, left = ring("gy")
-    top = lax.ppermute(block[rows - SWEEPS :], "gx", up)
-    bottom = lax.ppermute(block[:SWEEPS], "gx", down)
-    before = lax.ppermute(block[:, cols - SWEEPS :], "gy", right)
-    after = lax.ppermute(block[:, :SWEEPS], "gy", left)
-    return top, bottom, jnp.concatenate([before, after], axis=1)
-
-
-def corners(sides):
-    up, down = ring("gx")
-    above = lax.ppermute(sides[sides.shape[0] - SWEEPS :], "gx", up)
-    return above, lax.ppermute(sides[:SWEEPS], "gx", down)
-
-
-def with_corners(sides, ends):
-    return jnp.pad(jnp.concatenate([ends[0], sides, ends[1]], axis=0), ((0, 0),) + FREE)
+    last = jnp.concatenate([block[rows - SWEEPS :], sides[rows - SWEEPS :]], axis=1)
+    first = jnp.concatenate([block[:SWEEPS], sides[:SWEEPS]], axis=1)
+    above, below = lax.ppermute(last, "gx", up), lax.ppermute(first, "gx", down)
+    whole = jnp.concatenate([above[:, cols:], sides, below[:, cols:]], axis=0)
+    return above[:, :cols], below[:, :cols], jnp.pad(whole, ((0, 0),) + FREE)
 
 
 def mirror(values, axis):
@@ -391,7 +388,7 @@
     counts = [part.stop - part.start for part in parts]
     core = lax.rem(col, 2)
     constants = fill_constants(intensity, template, row, col, cosine_table(length)[:, :half])
-    top, bottom, sides = faces(intensity)
+    sides = side_faces(intensity)
     given_first, kept_first = (1 - core) * pair_rows, core * pair_rows
     given, kept = [], []
     blank = intensity[:SWEEPS]
@@ -405,11 +402,11 @@
         return list(filled_spectrum(intensity, use, start + part.start, part))
 
     if not (parts[0].start >= SWEEPS and parts[0].stop <= pair_rows - SWEEPS):
-        outer_faces.extend((top, bottom, with_corners(sides, corners(sides))))
+        outer_faces.extend(end_faces(intensity, sides))
     given.append(fill(0, given_first))
     if not outer_faces:
         given[0], late_sides = lax.optimization_barrier((given[0], sides))
-        outer_faces.extend((top, bottom, with_corners(sides, corners(late_sides))))
+        outer_faces.extend(end_faces(intensity, late_sides))
     kept.append(fill(0, kept_first))
 
     table_cols = lax.dynamic_slice_in_dim(table, col * cols, cols, 0)
@@ -425,18 +422,21 @@
     values, packed, lines = 0.0, None, None
     for c, count in enumerate(counts):
         closing = c == len(counts) - 1
-        got_lines = None
+        if c == 1:
+            start, packed = lax.optimization_barrier((given_first, packed))
+            given.extend(fill(later, start) for later in range(1, len(counts)))
+        sent = given[c][0]
         if c > 0:
-            (starts, packed) = lax.optimization_barrier(((given_first, kept_first), packed))
-            given.append(fill(c, starts[0]))
-            if c == 1:
-                kept.extend(fill(later, starts[1]) for later in range(1, len(counts)))
             got_lines = exchanged(packed)
-        got = lax.ppermute(given[c][0], "gy", swap(gy, 1))
+        if c == 1:
+            start, got_lines = lax.optimization_barrier((kept_first, got_lines))
+            kept.extend(fill(later, start) for later in range(1, len(counts)))
         held = kept[c][0]
         if c > 0:
-            behind = [held, got_lines] + [piece[0] for piece in kept[c + 1 :]]
-            held, got_lines, *later = lax.optimization_barrier(behind)
+            sent, held = lax.optimization_barrier((sent, held))
+        got = lax.ppermute(sent, "gy", swap(gy, 1))
+        if c > 0:
+            held, *later = lax.optimization_barrier([held] + [piece[0] for piece in kept[c + 1 :]])
             for n, spectrum in enumerate(later):
                 kept[c + 1 + n][0] = spectrum
             lines = sent_lines(got_lines, counts[c - 1], lines)

time: 401 us -> 390 us (0.973)
  waiting for transfers between devices: 120 us -> 109 us
  local copies, waits for them, and re-layouts: 35.9 us -> 42.5 us
  starting transfers between devices: 50.1 us -> 44.9 us
    ppermute x9, waiting for transfers between devices: 34.3 us -> 20.2 us  [exchanged(): lax.ppermute(packed[p], 'gy', swap(gy, p))]
    ppermute x9 -> x7, starting transfers between devices: 13.6 us -> 8.62 us  [the longest x1 3.04 us: end_faces(): lax.ppermute(first, 'gx', down)]
    unnamed x68 -> x61, local copies, waits for them, and re-layouts: 6.91 us -> 8.06 us
  transfers between devices with their start and end apart: 33 -> 31, of which waited for: 13 -> 14; matrix products, arithmetic and copies ran while one was open for 11% -> 12% of each run, Pallas kernels for 18% -> 21%
where the time goes in v4:
time: 390 us; the launch traced here: 388 us
  Pallas kernels  137 us (35%)
  waiting for transfers between devices  109 us (28%)
  starting transfers between devices  44.9 us (12%)
  local copies, waits for them, and re-layouts  42.5 us (11%)
  blocking collectives  32.5 us (8%)
  other arithmetic  17.3 us (4%)
  matrix products  4.95 us (1%)
    pallas_call x6, Pallas kernels, filled_spectrum(): pl.pallas_call(fill_kernel, grid_spec=pltpu.PrefetchScalarGridSpec(num_sc...  74 us
    pallas_call x1, Pallas kernels, result_block(): pl.pallas_call(lambda *refs: result_kernel(offsets, own, devices, groups,...  33.9 us
    ppermute x9, waiting for transfers between devices, gathered(): pieces[place ^ bit] = lax.ppermute(pieces[place], 'gy', swap(peers, bit))  33.6 us
    all_to_all x1, blocking collectives, on_device(): piece = lax.all_to_all(messages, 'gx', 0, 0, tiled=True)  32.5 us
    all_to_all x3, waiting for transfers between devices, sent_lines(): return lax.all_to_all(lines, 'gx', 0, 0, tiled=True)  20.5 us
    ppermute x9, waiting for transfers between devices, exchanged(): lax.ppermute(packed[p], 'gy', swap(gy, p))  20.2 us
    pallas_call x3, Pallas kernels, packed_section(): pl.pallas_call(lambda *refs: section_kernel(offsets, closing, *refs), gri...  19.6 us
    all_to_all x1, waiting for transfers between devices, on_device(): lax.all_to_all(jnp.concatenate(turned, axis=3), ('gy', 'gx'), 0, 0, tiled...  18.5 us
  transfers between devices with their start and end apart: 31, of which 14 were waited for; matrix products, arithmetic and copies ran while one was open for 12% of the time, Pallas kernels for 21%

profile of v4, /device:TPU:0, one launch (start us, length us, event | category | flops | bytes accessed | tf_op | source)
XLA Modules:
  0.0 388.2 jit_solution(12978722156033674288)
XLA Ops:
  0.0 1.8 fusion.28
  2.3 2.0 collective-permute-start.1
  4.3 3.6 shard_map.55.marks
  7.8 2.1 fusion.27
  9.9 1.0 collective-permute-done.1
  11.2 1.7 pad.16.sides
  12.8 16.7 %shard_map.57 = (f32[16,128,256]{2,1,0:T(8,128)}, f32[16,256]{1,0:T(8,128)}, f32[128,128]{1,0:T(8,128)}) custom-call(s32[1]{0:T(128)} %bitcast.11.base, f32[64,128,512]{2,1,0:T(8,128)} %below.11, f32[64,128,512]{2,1,0:T(8,128)} %below.11, f32[64,128,512]{2,1,0:T(8,128)} %below.11, f32[2,128,512]{2,1,0:T(8,128)} %get-tuple-element.140.top.bottom, ...), custom_call_target="tpu_custom_call" | custom-call | flops 1610612736 | bytes 6291456 | tf_op jit(solution)/shard_map/pallas_call | solution.py:245
  34.5 1.2 copy.75
  35.8 1.0 pad_maximum_fusion.1
  36.8 2.3 collective-permute-start.6
  39.1 3.0 collective-permute-start.7
  43.8 16.9 %shard_map.56 = (f32[16,128,256]{2,1,0:T(8,128)}, f32[16,256]{1,0:T(8,128)}, f32[128,128]{1,0:T(8,128)}) custom-call(s32[1]{0:T(128)} %bitcast.10.base, f32[64,128,512]{2,1,0:T(8,128)} %below.11, f32[64,128,512]{2,1,0:T(8,128)} %below.11, f32[64,128,512]{2,1,0:T(8,128)} %below.11, f32[2,128,512]{2,1,0:T(8,128)} %get-tuple-element.140.top.bottom, ...), custom_call_target="tpu_custom_call" | custom-call | flops 1610612736 | bytes 6291456 | tf_op jit(solution)/shard_map/pallas_call | solution.py:245
  62.9 8.2 %shard_map.58 = (f32[16,2,8,640]{3,2,1,0:T(8,128)}, f32[16,2,8,640]{3,2,1,0:T(8,128)}, f32[16,2,8,640]{3,2,1,0:T(8,128)}, f32[16,2,8,640]{3,2,1,0:T(8,128)}, f32[4,64,640]{2,1,0:T(8,128)}) custom-call(s32[1]{0:T(128)} %bitcast.3.refs_0_, f32[4,16]{1,0:T(4,128)} %pad_maximum_fusion.6.refs_1_, f32[16,128,256]{2,1,0:T(8,128)} %get-tuple-element.72.refs_2_, ...), custom_call_target="tpu_custom_call" | custom-call | flops 1610612736 | bytes 8388608 | tf_op jit(solution)/shard_map/pallas_call | solution.py:354
  71.1 1.9 collective-permute-start.4
  73.1 1.1 slice.367
  75.8 1.1 slice.368
  78.5 1.8 select_maximum_fusion.sides
  80.3 10.1 %shard_map.59 = (f32[8,128,256]{2,1,0:T(8,128)}, f32[8,256]{1,0:T(8,128)}, f32[128,128]{1,0:T(8,128)}) custom-call(s32[1]{0:T(128)} %bitcast.23.base, f32[64,128,512]{2,1,0:T(8,128)} %below.11, f32[64,128,512]{2,1,0:T(8,128)} %below.11, f32[64,128,512]{2,1,0:T(8,128)} %below.11, f32[2,128,512]{2,1,0:T(8,128)} %copy.102.top, f32[2,128,512]{2,1,0:T(8,128)} %copy.103.bottom, ...), custom_call_target="tpu_custom_call" | custom-call | flops 805306368 | bytes 3145728 | tf_op jit(solution)/shard_map/pallas_call | solution.py:245
  90.4 10.1 %shard_map.63 = (f32[8,128,256]{2,1,0:T(8,128)}, f32[8,256]{1,0:T(8,128)}, f32[128,128]{1,0:T(8,128)}) custom-call(s32[1]{0:T(128)} %bitcast.36.base, f32[64,128,512]{2,1,0:T(8,128)} %below.11, f32[64,128,512]{2,1,0:T(8,128)} %below.11, f32[64,128,512]{2,1,0:T(8,128)} %below.11, f32[2,128,512]{2,1,0:T(8,128)} %copy.102.top, f32[2,128,512]{2,1,0:T(8,128)} %copy.103.bottom, ...), custom_call_target="tpu_custom_call" | custom-call | flops 805306368 | bytes 3145728 | tf_op jit(solution)/shard_map/pallas_call | solution.py:245
  101.2 1.1 collective-permute-done.5
  102.6 1.7 copy.70
  104.3 3.7 all-to-all-start
  108.1 10.1 %shard_map.60 = (f32[8,128,256]{2,1,0:T(8,128)}, f32[8,256]{1,0:T(8,128)}, f32[128,128]{1,0:T(8,128)}) custom-call(s32[1]{0:T(128)} %bitcast.24.base, f32[64,128,512]{2,1,0:T(8,128)} %below.11, f32[64,128,512]{2,1,0:T(8,128)} %below.11, f32[64,128,512]{2,1,0:T(8,128)} %below.11, f32[2,128,512]{2,1,0:T(8,128)} %copy.102.top, f32[2,128,512]{2,1,0:T(8,128)} %copy.103.bottom, ...), custom_call_target="tpu_custom_call" | custom-call | flops 805306368 | bytes 3145728 | tf_op jit(solution)/shard_map/pallas_call | solution.py:245
  118.2 10.1 %shard_map.61 = (f32[8,128,256]{2,1,0:T(8,128)}, f32[8,256]{1,0:T(8,128)}, f32[128,128]{1,0:T(8,128)}) custom-call(s32[1]{0:T(128)} %bitcast.25.base, f32[64,128,512]{2,1,0:T(8,128)} %below.11, f32[64,128,512]{2,1,0:T(8,128)} %below.11, f32[64,128,512]{2,1,0:T(8,128)} %below.11, f32[2,128,512]{2,1,0:T(8,128)} %copy.102.top, f32[2,128,512]{2,1,0:T(8,128)} %copy.103.bottom, ...), custom_call_target="tpu_custom_call" | custom-call | flops 805306368 | bytes 3145728 | tf_op jit(solution)/shard_map/pallas_call | solution.py:245
  128.3 1.0 concatenate.62
  131.4 1.0 fusion.14.refs_8_
  132.4 1.7 collective-permute-done.8.refs_3_
  134.0 1.0 copy-done.8
  135.0 5.4 %shard_map.62 = (f32[8,2,8,640]{3,2,1,0:T(8,128)}, f32[8,2,8,640]{3,2,1,0:T(8,128)}, f32[8,2,8,640]{3,2,1,0:T(8,128)}, f32[8,2,8,640]{3,2,1,0:T(8,128)}, f32[4,64,640]{2,1,0:T(8,128)}) custom-call(s32[1]{0:T(128)} %bitcast.3.refs_0_, f32[4,8]{1,0:T(4,128)} %pad_maximum_fusion.7.refs_1_, f32[8,128,256]{2,1,0:T(8,128)} %get-tuple-element.96.refs_2_, ...), custom_call_target="tpu_custom_call" | custom-call | flops 805306368 | bytes 4194304 | tf_op jit(solution)/shard_map/pallas_call | solution.py:354
  140.4 1.6 collective-permute-start.9
  143.2 1.0 copy-done.7
  144.2 6.0 %shard_map.64 = (f32[13,2,8,640]{3,2,1,0:T(8,128)}, f32[13,2,8,640]{3,2,1,0:T(8,128)}, f32[13,2,8,640]{3,2,1,0:T(8,128)}, f32[13,2,8,640]{3,2,1,0:T(8,128)}, f32[4,64,640]{2,1,0:T(8,128)}) custom-call(s32[1]{0:T(128)} %bitcast.3.refs_0_, f32[4,8]{1,0:T(4,128)} %pad_maximum_fusion.8.refs_1_, f32[8,128,256]{2,1,0:T(8,128)} %get-tuple-element.106.refs_2_, ...), custom_call_target="tpu_custom_call" | custom-call | flops 805306368 | bytes 4194304 | tf_op jit(solution)/shard_map/pallas_call | solution.py:354
  150.1 1.6 collective-permute-start.13
  152.3 5.1 %collective-permute-done.11 = f32[8,2,8,640]{3,2,1,0:T(8,128)S(1)} collective-permute-done((f32[8,2,8,640]{3,2,1,0:T(8,128)}, f32[8,2,8,640]{3,2,1,0:T(8,128)S(1)}, u32[]{:S(2)}, u32[]{:S(2)}) %collective-permute-start.11) | collective-permute-done | bytes 327712 | tf_op jit(solution)/shard_map/ppermute | solution.py:744
  157.5 1.2 copy.79
  158.7 5.9 %all-to-all-start.1 = ((f32[8,2,16,640]{3,1,2,0:T(2,128)}), f32[8,2,16,640]{3,1,2,0:T(2,128)S(1)}, u32[]{:S(2)}, u32[]{:S(2)}) async-start(f32[8,2,16,640]{3,1,2,0:T(2,128)} %copy.79), calls=%async_computation.1 | async-start | bytes 1310720 | tf_op jit(solution)/shard_map/all_to_all | solution.py:754
  164.7 5.1 %collective-permute-done.13 = f32[13,2,8,640]{3,2,1,0:T(8,128)} collective-permute-done((f32[13,2,8,640]{3,2,1,0:T(8,128)}, f32[13,2,8,640]{3,2,1,0:T(8,128)}, u32[]{:S(2)}, u32[]{:S(2)}) %collective-permute-start.13) | collective-permute-done | bytes 532512 | tf_op jit(solution)/shard_map/ppermute | solution.py:744
  169.7 1.0 slice_add_fusion.1
  170.8 8.8 %collective-permute-done.15 = f32[13,2,8,640]{3,2,1,0:T(8,128)} collective-permute-done((f32[13,2,8,640]{3,2,1,0:T(8,128)}, f32[13,2,8,640]{3,2,1,0:T(8,128)}, u32[]{:S(2)}, u32[]{:S(2)}) %collective-permute-start.15) | collective-permute-done | bytes 532512 | tf_op jit(solution)/shard_map/ppermute | solution.py:744
  179.6 1.1 slice_add_fusion
  180.7 1.2 slice_add_fusion.2
  182.8 1.4 copy.81
  184.2 5.1 %all-to-all-start.2 = ((f32[8,2,21,640]{3,1,2,0:T(2,128)}), f32[8,2,21,640]{3,1,2,0:T(2,128)S(1)}, u32[]{:S(2)}, u32[]{:S(2)}) async-start(f32[8,2,21,640]{3,1,2,0:T(2,128)} %copy.81), calls=%async_computation.2 | async-start | bytes 1720320 | tf_op jit(solution)/shard_map/all_to_all | solution.py:754
  189.3 1.1 broadcast_select_fusion
  190.4 1.9 convolution_bitcast_fusion
  192.3 19.7 %all-to-all-done.2 = f32[8,2,21,640]{3,1,2,0:T(2,128)S(1)} async-done(((f32[8,2,21,640]{3,1,2,0:T(2,128)}), f32[8,2,21,640]{3,1,2,0:T(2,128)S(1)}, u32[]{:S(2)}, u32[]{:S(2)}) %all-to-all-start.2) | async-done | bytes 860192 | tf_op jit(solution)/shard_map/all_to_all | solution.py:754
  214.1 1.0 copy.116
  215.4 2.4 concatenate.66
  217.7 3.7 all-to-all-start.3
  222.2 18.5 %all-to-all-done.3 = f32[32,2,2,1280]{3,2,1,0:T(2,128)S(1)} async-done(((f32[32,2,2,1280]{3,2,1,0:T(2,128)}), f32[32,2,2,1280]{3,2,1,0:T(2,128)S(1)}, u32[]{:S(2)}, u32[]{:S(2)}) %all-to-all-start.3) | async-done | bytes 655392 | tf_op jit(solution)/shard_map/all_to_all | solution.py:468
  241.6 5.6 %shard_map.65 = (f32[8,288,128]{2,1,0:T(8,128)}, f32[8,256,128]{2,1,0:T(8,128)}, f32[8,128,128]{2,1,0:T(8,128)}) custom-call(f32[2,256,640]{2,1,0:T(8,128)} %bitcast.170, f32[2,64,1280]{2,1,0:T(8,128)} %bitcast.177, f32[2,5,640]{2,1,0:T(8,128)} %copy_multiply_fusion.refs_2_), custom_call_target="tpu_custom_call" | custom-call | tf_op jit(solution)/shard_map/pallas_call | solution.py:603
  247.2 32.5 %all_to_all.35 = f32[8,288,128]{2,1,0:T(8,128)S(1)} all-to-all(f32[8,288,128]{2,1,0:T(8,128)} %get-tuple-element.127), channel_id=1, replica_groups=mesh['gx'=8,'gy'=4] {'gx'}, dimensions={0} | all-to-all | bytes 2359296 | tf_op jit(solution)/shard_map/all_to_all | solution.py:484
  279.7 1.2 collective-permute-start.17
  280.9 3.6 all-to-all-start.5
  284.6 21.5 %collective-permute-done.17 = f32[8,288,128]{2,1,0:T(8,128)} collective-permute-done((f32[8,288,128]{2,1,0:T(8,128)S(1)}, f32[8,288,128]{2,1,0:T(8,128)}, u32[]{:S(2)}, u32[]{:S(2)}) %collective-permute-start.17) | collective-permute-done | bytes 1179680 | tf_op jit(solution)/shard_map/ppermute | solution.py:737
  308.1 1.9 all-to-all-done.5
  310.5 3.9 %all-to-all-start.6 = ((f32[8,128,128]{2,1,0:T(8,128)}), f32[8,128,128]{2,1,0:T(8,128)S(1)}, u32[]{:S(2)}, u32[]{:S(2)}) async-start(f32[8,128,128]{2,1,0:T(8,128)} %get-tuple-element.135), calls=%async_computation.6 | async-start | bytes 1048576 | tf_op jit(solution)/shard_map/all_to_all | solution.py:484
  318.2 11.2 %all-to-all-done.6 = f32[8,128,128]{2,1,0:T(8,128)S(1)} async-done(((f32[8,128,128]{2,1,0:T(8,128)}), f32[8,128,128]{2,1,0:T(8,128)S(1)}, u32[]{:S(2)}, u32[]{:S(2)}) %all-to-all-start.6) | async-done | bytes 524320 | tf_op jit(solution)/shard_map/all_to_all | solution.py:484
  329.4 4.4 %collective-permute-done.20 = f32[8,256,128]{2,1,0:T(8,128)} collective-permute-done((f32[8,256,128]{2,1,0:T(8,128)S(1)}, f32[8,256,128]{2,1,0:T(8,128)}, u32[]{:S(2)}, u32[]{:S(2)}) %collective-permute-start.20) | collective-permute-done | bytes 1048608 | tf_op jit(solution)/shard_map/ppermute | solution.py:737
  333.8 1.7 collective-permute-start.23
  338.9 7.8 %collective-permute-done.23 = f32[8,128,128]{2,1,0:T(8,128)S(1)} collective-permute-done((f32[8,128,128]{2,1,0:T(8,128)S(1)}, f32[8,128,128]{2,1,0:T(8,128)S(1)}, u32[]{:S(2)}, u32[]{:S(2)}) %collective-permute-start.23) | collective-permute-done | bytes 524320 | tf_op jit(solution)/shard_map/ppermute | solution.py:737
  347.3 1.3 dynamic-update-slice.4
  348.6 1.0 pad_maximum_fusion.4
  354.1 33.9 %shard_map.66 = f32[64,128,512]{2,1,0:T(8,128)} custom-call(s32[4]{0:T(128)} %pad_add_fusion.refs_0_, f32[64,640]{1,0:T(8,128)} %bitcast.187, f32[64,256]{1,0:T(8,128)} %slice.405.refs_2_, f32[128,128]{1,0:T(8,128)} %pad.19.refs_3_, bf16[128,256]{1,0:T(8,128)(2,1)} %fusion.16.refs_4_, bf16[256,256]{1,0:T(8,128)(2,1)} %fusion.8.refs_5_, ...), custom_call_target="tpu_custom_call" | custom-call | tf_op jit(solution)/shard_map/pallas_call | solution.py:708
  (182 shorter events, 37.2 us)
Async XLA Ops:
  1.8 8.1 %collective-permute-start = (f32[64,2,512]{2,1,0:T(2,128)S(1)}, f32[64,2,512]{2,1,0:T(2,128)S(1)}, u32[]{:S(2)}, u32[]{:S(2)}) collective-permute-start(f32[64,2,512]{2,1,0:T(2,128)S(1)} %get-tuple-element.141), channel_id=1, source_target_pairs={{0,1},{1,2},{2,3},{3,0},{4,5},{5,6},{6,7},{7,4},{8,9},{9,10},{10,1... | collective-permute-start | bytes 786440 | tf_op jit(solution)/shard_map/ppermute | solution.py:30
  2.3 8.6 %collective-permute-start.1 = (f32[64,2,512]{2,1,0:T(2,128)S(1)}, f32[64,2,512]{2,1,0:T(2,128)S(1)}, u32[]{:S(2)}, u32[]{:S(2)}) collective-permute-start(f32[64,2,512]{2,1,0:T(2,128)S(1)} %get-tuple-element.142), channel_id=1, source_target_pairs={{1,0},{2,1},{3,2},{0,3},{5,4},{6,5},{7,6},{4,7},{9,8},{10,9},{11,1... | collective-permute-start | bytes 786440 | tf_op jit(solution)/shard_map/ppermute | solution.py:31
  12.8 17.4 %copy-start.4 = (f32[512,257]{0,1:T(8,128)S(1)}, f32[512,257]{0,1:T(8,128)}, u32[]{:S(2)}) copy-start(f32[512,257]{0,1:T(8,128)} %constant.112.clone) | copy-start | bytes 1579012
  29.5 31.2 %collective-permute-start.2 = (f32[16,128,256]{2,1,0:T(8,128)}, f32[16,128,256]{2,1,0:T(8,128)}, u32[]{:S(2)}, u32[]{:S(2)}) collective-permute-start(f32[16,128,256]{2,1,0:T(8,128)} %get-tuple-element.76), channel_id=1, source_target_pairs={{0,1},{1,0},{2,3},{3,2},{4,5},{5,4},{6,7},{7,6},{8,9},{9,8},{10,11... | collective-permute-start | bytes 6291464 | tf_op jit(solution)/shard_map/ppermute | solution.py:437
  32.3 2.2 copy-start
  36.8 36.3 %collective-permute-start.6 = (f32[2,132,512]{2,0,1:T(2,128)}, f32[2,132,512]{2,0,1:T(2,128)}, u32[]{:S(2)}, u32[]{:S(2)}) collective-permute-start(f32[2,132,512]{2,0,1:T(2,128)} %pad_maximum_fusion.1), channel_id=1, source_target_pairs={{0,4},{4,8},{8,12},{12,16},{16,20},{20,24},{24,28},{28,0},{1,5},{5... | collective-permute-start | bytes 1622024 | tf_op jit(solution)/shard_map/ppermute | solution.py:40
  39.1 36.7 %collective-permute-start.7 = (f32[2,132,512]{2,0,1:T(2,128)}, f32[2,132,512]{2,0,1:T(2,128)}, u32[]{:S(2)}, u32[]{:S(2)}) collective-permute-start(f32[2,132,512]{2,0,1:T(2,128)} %copy.75), channel_id=1, source_target_pairs={{4,0},{8,4},{12,8},{16,12},{20,16},{24,20},{28,24},{0,28},{5,1},{9... | collective-permute-start | bytes 1622024 | tf_op jit(solution)/shard_map/ppermute | solution.py:40
  62.9 10.2 %copy-start.19 = (f32[16,256]{1,0:T(8,128)S(1)}, f32[16,256]{1,0:T(8,128)}, u32[]{:S(2)}) copy-start(f32[16,256]{1,0:T(8,128)} %get-tuple-element.114) | copy-start | bytes 49156
  71.1 30.1 %collective-permute-start.3 = (f32[16,2,8,640]{3,2,1,0:T(8,128)}, f32[16,2,8,640]{3,2,1,0:T(8,128)S(1)}, u32[]{:S(2)}, u32[]{:S(2)}) collective-permute-start(f32[16,2,8,640]{3,2,1,0:T(8,128)} %get-tuple-element.82), channel_id=1, source_target_pairs={{0,1},{1,0},{2,3},{3,2},{4,5},{5,4},{6,7},{7,6},{8,9},{9,8},{10,11... | collective-permute-start | bytes 1966088 | tf_op jit(solution)/shard_map/ppermute | solution.py:744
  71.1 30.1 %collective-permute-start.4 = (f32[16,2,8,640]{3,2,1,0:T(8,128)}, f32[16,2,8,640]{3,2,1,0:T(8,128)S(1)}, u32[]{:S(2)}, u32[]{:S(2)}) collective-permute-start(f32[16,2,8,640]{3,2,1,0:T(8,128)} %get-tuple-element.83), channel_id=1, source_target_pairs={{0,2},{1,3},{2,0},{3,1},{4,6},{5,7},{6,4},{7,5},{8,10},{9,11},{10,... | collective-permute-start | bytes 1966088 | tf_op jit(solution)/shard_map/ppermute | solution.py:744
  73.0 29.3 %collective-permute-start.5 = (f32[16,2,8,640]{3,2,1,0:T(8,128)}, f32[16,2,8,640]{3,2,1,0:T(8,128)S(1)}, u32[]{:S(2)}, u32[]{:S(2)}) collective-permute-start(f32[16,2,8,640]{3,2,1,0:T(8,128)} %get-tuple-element.84), channel_id=1, source_target_pairs={{0,3},{1,2},{2,1},{3,0},{4,7},{5,6},{6,5},{7,4},{8,11},{9,10},{10,... | collective-permute-start | bytes 1966088 | tf_op jit(solution)/shard_map/ppermute | solution.py:744
  90.4 10.1 %copy-start.22 = (f32[8,256]{1,0:T(8,128)S(1)}, f32[8,256]{1,0:T(8,128)}, u32[]{:S(2)}) copy-start(f32[8,256]{1,0:T(8,128)} %get-tuple-element.115) | copy-start | bytes 24580
  90.4 11.9 %copy-start.9 = (f32[16,2,8,640]{3,2,1,0:T(8,128)S(1)}, f32[16,2,8,640]{3,2,1,0:T(8,128)}, u32[]{:S(2)}) copy-start(f32[16,2,8,640]{3,2,1,0:T(8,128)} %get-tuple-element.85) | copy-start | bytes 1966084
  104.3 3.7 copy-start.20
  104.3 53.2 %all-to-all-start = ((f32[8,2,32,640]{3,1,2,0:T(2,128)}), f32[8,2,32,640]{3,1,2,0:T(2,128)S(1)}, u32[]{:S(2)}, u32[]{:S(2)}) async-start(f32[8,2,32,640]{3,1,2,0:T(2,128)} %copy.70), calls=%async_computation | async-start | bytes 2621440 | tf_op jit(solution)/shard_map/all_to_all | solution.py:754
  118.2 10.1 %copy-start.14 = (f32[128,128]{1,0:T(8,128)S(1)}, f32[128,128]{1,0:T(8,128)}, u32[]{:S(2)}) copy-start(f32[128,128]{1,0:T(8,128)} %get-tuple-element.108) | copy-start | bytes 196612
  118.2 10.1 %copy-start.15 = (f32[128,128]{1,0:T(8,128)S(1)}, f32[128,128]{1,0:T(8,128)}, u32[]{:S(2)}) copy-start(f32[128,128]{1,0:T(8,128)} %get-tuple-element.111) | copy-start | bytes 196612
  118.2 10.1 %copy-start.16 = (f32[128,128]{1,0:T(8,128)S(1)}, f32[128,128]{1,0:T(8,128)}, u32[]{:S(2)}) copy-start(f32[128,128]{1,0:T(8,128)} %get-tuple-element.109) | copy-start | bytes 196612
  118.2 10.1 %copy-start.17 = (f32[128,128]{1,0:T(8,128)S(1)}, f32[128,128]{1,0:T(8,128)}, u32[]{:S(2)}) copy-start(f32[128,128]{1,0:T(8,128)} %get-tuple-element.110) | copy-start | bytes 196612
  118.2 10.1 %copy-start.18 = (f32[128,128]{1,0:T(8,128)S(1)}, f32[128,128]{1,0:T(8,128)}, u32[]{:S(2)}) copy-start(f32[128,128]{1,0:T(8,128)} %get-tuple-element.112) | copy-start | bytes 196612
  118.2 12.0 %copy-start.21 = (f32[8,256]{1,0:T(8,128)S(1)}, f32[8,256]{1,0:T(8,128)}, u32[]{:S(2)}) copy-start(f32[8,256]{1,0:T(8,128)} %get-tuple-element.118) | copy-start | bytes 24580
  129.6 13.6 %collective-permute-start.12 = (f32[8,128,256]{2,1,0:T(8,128)}, f32[8,128,256]{2,1,0:T(8,128)S(1)}, u32[]{:S(2)}, u32[]{:S(2)}) collective-permute-start(f32[8,128,256]{2,1,0:T(8,128)} %get-tuple-element.107), channel_id=1, source_target_pairs={{0,1},{1,0},{2,3},{3,2},{4,5},{5,4},{6,7},{7,6},{8,9},{9,8},{10,11... | collective-permute-start | bytes 3145736 | tf_op jit(solution)/shard_map/ppermute | solution.py:437
  129.8 4.2 %collective-permute-start.8 = (f32[8,128,256]{2,1,0:T(8,128)}, f32[8,128,256]{2,1,0:T(8,128)S(1)}, u32[]{:S(2)}, u32[]{:S(2)}) collective-permute-start(f32[8,128,256]{2,1,0:T(8,128)} %get-tuple-element.97), channel_id=1, source_target_pairs={{0,1},{1,0},{2,3},{3,2},{4,5},{5,4},{6,7},{7,6},{8,9},{9,8},{10,11... | collective-permute-start | bytes 3145736 | tf_op jit(solution)/shard_map/ppermute | solution.py:437
  134.0 1.0 copy-start.8
  140.4 11.3 %collective-permute-start.9 = (f32[8,2,8,640]{3,2,1,0:T(8,128)}, f32[8,2,8,640]{3,2,1,0:T(8,128)S(1)}, u32[]{:S(2)}, u32[]{:S(2)}) collective-permute-start(f32[8,2,8,640]{3,2,1,0:T(8,128)} %get-tuple-element.100), channel_id=1, source_target_pairs={{0,2},{1,3},{2,0},{3,1},{4,6},{5,7},{6,4},{7,5},{8,10},{9,11},{10,... | collective-permute-start | bytes 983048 | tf_op jit(solution)/shard_map/ppermute | solution.py:744
  142.0 10.3 %collective-permute-start.10 = (f32[8,2,8,640]{3,2,1,0:T(8,128)}, f32[8,2,8,640]{3,2,1,0:T(8,128)S(1)}, u32[]{:S(2)}, u32[]{:S(2)}) collective-permute-start(f32[8,2,8,640]{3,2,1,0:T(8,128)} %get-tuple-element.101), channel_id=1, source_target_pairs={{0,1},{1,0},{2,3},{3,2},{4,5},{5,4},{6,7},{7,6},{8,9},{9,8},{10,11... | collective-permute-start | bytes 983048 | tf_op jit(solution)/shard_map/ppermute | solution.py:744
  142.0 15.4 %collective-permute-start.11 = (f32[8,2,8,640]{3,2,1,0:T(8,128)}, f32[8,2,8,640]{3,2,1,0:T(8,128)S(1)}, u32[]{:S(2)}, u32[]{:S(2)}) collective-permute-start(f32[8,2,8,640]{3,2,1,0:T(8,128)} %get-tuple-element.102), channel_id=1, source_target_pairs={{0,3},{1,2},{2,1},{3,0},{4,7},{5,6},{6,5},{7,4},{8,11},{9,10},{10,... | collective-permute-start | bytes 983048 | tf_op jit(solution)/shard_map/ppermute | solution.py:744
  143.2 1.0 copy-start.7
  144.2 8.1 %copy-start.13 = (f32[8,2,8,640]{3,2,1,0:T(8,128)S(1)}, f32[8,2,8,640]{3,2,1,0:T(8,128)}, u32[]{:S(2)}) copy-start(f32[8,2,8,640]{3,2,1,0:T(8,128)} %get-tuple-element.99) | copy-start | bytes 983044
  150.1 19.6 %collective-permute-start.13 = (f32[13,2,8,640]{3,2,1,0:T(8,128)}, f32[13,2,8,640]{3,2,1,0:T(8,128)}, u32[]{:S(2)}, u32[]{:S(2)}) collective-permute-start(f32[13,2,8,640]{3,2,1,0:T(8,128)} %get-tuple-element.122), channel_id=1, source_target_pairs={{0,2},{1,3},{2,0},{3,1},{4,6},{5,7},{6,4},{7,5},{8,10},{9,11},{10,... | collective-permute-start | bytes 1597448 | tf_op jit(solution)/shard_map/ppermute | solution.py:744
  151.7 19.1 %collective-permute-start.14 = (f32[13,2,8,640]{3,2,1,0:T(8,128)}, f32[13,2,8,640]{3,2,1,0:T(8,128)}, u32[]{:S(2)}, u32[]{:S(2)}) collective-permute-start(f32[13,2,8,640]{3,2,1,0:T(8,128)} %get-tuple-element.123), channel_id=1, source_target_pairs={{0,1},{1,0},{2,3},{3,2},{4,5},{5,4},{6,7},{7,6},{8,9},{9,8},{10,11... | collective-permute-start | bytes 1597448 | tf_op jit(solution)/shard_map/ppermute | solution.py:744
  151.7 27.9 %collective-permute-start.15 = (f32[13,2,8,640]{3,2,1,0:T(8,128)}, f32[13,2,8,640]{3,2,1,0:T(8,128)}, u32[]{:S(2)}, u32[]{:S(2)}) collective-permute-start(f32[13,2,8,640]{3,2,1,0:T(8,128)} %get-tuple-element.124), channel_id=1, source_target_pairs={{0,3},{1,2},{2,1},{3,0},{4,7},{5,6},{6,5},{7,4},{8,11},{9,10},{10,... | collective-permute-start | bytes 1597448 | tf_op jit(solution)/shard_map/ppermute | solution.py:744
  157.5 12.2 %copy-start.10 = (f32[13,2,8,640]{3,2,1,0:T(8,128)S(1)}, f32[13,2,8,640]{3,2,1,0:T(8,128)}, u32[]{:S(2)}) copy-start(f32[13,2,8,640]{3,2,1,0:T(8,128)} %get-tuple-element.121) | copy-start | bytes 1597444
  158.7 24.1 %all-to-all-start.1 = ((f32[8,2,16,640]{3,1,2,0:T(2,128)}), f32[8,2,16,640]{3,1,2,0:T(2,128)S(1)}, u32[]{:S(2)}, u32[]{:S(2)}) async-start(f32[8,2,16,640]{3,1,2,0:T(2,128)} %copy.79), calls=%async_computation.1 | async-start | bytes 1310720 | tf_op jit(solution)/shard_map/all_to_all | solution.py:754
  184.2 27.8 %all-to-all-start.2 = ((f32[8,2,21,640]{3,1,2,0:T(2,128)}), f32[8,2,21,640]{3,1,2,0:T(2,128)S(1)}, u32[]{:S(2)}, u32[]{:S(2)}) async-start(f32[8,2,21,640]{3,1,2,0:T(2,128)} %copy.81), calls=%async_computation.2 | async-start | bytes 1720320 | tf_op jit(solution)/shard_map/all_to_all | solution.py:754
  212.1 1.3 copy-start.23
  214.1 1.1 copy-start.2
  217.7 22.9 %all-to-all-start.3 = ((f32[32,2,2,1280]{3,2,1,0:T(2,128)}), f32[32,2,2,1280]{3,2,1,0:T(2,128)S(1)}, u32[]{:S(2)}, u32[]{:S(2)}) async-start(f32[32,2,2,1280]{3,2,1,0:T(2,128)} %concatenate.66), calls=%async_computation.3 | async-start | bytes 1310720 | tf_op jit(solution)/shard_map/all_to_all | solution.py:468
  279.7 30.9 %copy-start.1 = (f32[8,288,128]{2,1,0:T(8,128)}, f32[8,288,128]{2,1,0:T(8,128)S(1)}, u32[]{:S(2)}) copy-start(f32[8,288,128]{2,1,0:T(8,128)S(1)} %all_to_all.35) | copy-start | bytes 3538948
  279.7 26.4 %collective-permute-start.17 = (f32[8,288,128]{2,1,0:T(8,128)S(1)}, f32[8,288,128]{2,1,0:T(8,128)}, u32[]{:S(2)}, u32[]{:S(2)}) collective-permute-start(f32[8,288,128]{2,1,0:T(8,128)S(1)} %all_to_all.35), channel_id=1, source_target_pairs={{0,2},{1,3},{2,0},{3,1},{4,6},{5,7},{6,4},{7,5},{8,10},{9,11},{10,... | collective-permute-start | bytes 3538952 | tf_op jit(solution)/shard_map/ppermute | solution.py:737
  280.9 29.1 %all-to-all-start.5 = ((f32[8,256,128]{2,1,0:T(8,128)}), f32[8,256,128]{2,1,0:T(8,128)S(1)}, u32[]{:S(2)}, u32[]{:S(2)}) async-start(f32[8,256,128]{2,1,0:T(8,128)} %get-tuple-element.130), calls=%async_computation.5 | async-start | bytes 2097152 | tf_op jit(solution)/shard_map/all_to_all | solution.py:484
  284.4 25.6 %collective-permute-start.16 = (f32[8,288,128]{2,1,0:T(8,128)S(1)}, f32[8,288,128]{2,1,0:T(8,128)}, u32[]{:S(2)}, u32[]{:S(2)}) collective-permute-start(f32[8,288,128]{2,1,0:T(8,128)S(1)} %all_to_all.35), channel_id=1, source_target_pairs={{0,1},{1,0},{2,3},{3,2},{4,5},{5,4},{6,7},{7,6},{8,9},{9,8},{10,11... | collective-permute-start | bytes 3538952 | tf_op jit(solution)/shard_map/ppermute | solution.py:737
  306.0 10.3 %collective-permute-start.18 = (f32[8,288,128]{2,1,0:T(8,128)}, f32[8,288,128]{2,1,0:T(8,128)}, u32[]{:S(2)}, u32[]{:S(2)}) collective-permute-start(f32[8,288,128]{2,1,0:T(8,128)} %collective-permute-done.17), channel_id=1, source_target_pairs={{0,1},{1,0},{2,3},{3,2},{4,5},{5,4},{6,7},{7,6},{8,9},{9,8},{10,11... | collective-permute-start | bytes 3538952 | tf_op jit(solution)/shard_map/ppermute | solution.py:737
  310.0 7.3 %copy-start.3 = (f32[8,256,128]{2,1,0:T(8,128)}, f32[8,256,128]{2,1,0:T(8,128)S(1)}, u32[]{:S(2)}) copy-start(f32[8,256,128]{2,1,0:T(8,128)S(1)} %all-to-all-done.5) | copy-start | bytes 3145732
  310.0 23.8 %collective-permute-start.20 = (f32[8,256,128]{2,1,0:T(8,128)S(1)}, f32[8,256,128]{2,1,0:T(8,128)}, u32[]{:S(2)}, u32[]{:S(2)}) collective-permute-start(f32[8,256,128]{2,1,0:T(8,128)S(1)} %all-to-all-done.5), channel_id=1, source_target_pairs={{0,2},{1,3},{2,0},{3,1},{4,6},{5,7},{6,4},{7,5},{8,10},{9,11},{10,... | collective-permute-start | bytes 3145736 | tf_op jit(solution)/shard_map/ppermute | solution.py:737
  310.5 23.3 %collective-permute-start.19 = (f32[8,256,128]{2,1,0:T(8,128)S(1)}, f32[8,256,128]{2,1,0:T(8,128)}, u32[]{:S(2)}, u32[]{:S(2)}) collective-permute-start(f32[8,256,128]{2,1,0:T(8,128)S(1)} %all-to-all-done.5), channel_id=1, source_target_pairs={{0,1},{1,0},{2,3},{3,2},{4,5},{5,4},{6,7},{7,6},{8,9},{9,8},{10,11... | collective-permute-start | bytes 3145736 | tf_op jit(solution)/shard_map/ppermute | solution.py:737
  310.5 18.9 %all-to-all-start.6 = ((f32[8,128,128]{2,1,0:T(8,128)}), f32[8,128,128]{2,1,0:T(8,128)S(1)}, u32[]{:S(2)}, u32[]{:S(2)}) async-start(f32[8,128,128]{2,1,0:T(8,128)} %get-tuple-element.135), calls=%async_computation.6 | async-start | bytes 1048576 | tf_op jit(solution)/shard_map/all_to_all | solution.py:484
  329.4 20.9 %copy-start.5 = (f32[8,128,128]{2,1,0:T(8,128)}, f32[8,128,128]{2,1,0:T(8,128)S(1)}, u32[]{:S(2)}) copy-start(f32[8,128,128]{2,1,0:T(8,128)S(1)} %all-to-all-done.6) | copy-start | bytes 1572868
  333.8 12.8 %collective-permute-start.23 = (f32[8,128,128]{2,1,0:T(8,128)S(1)}, f32[8,128,128]{2,1,0:T(8,128)S(1)}, u32[]{:S(2)}, u32[]{:S(2)}) collective-permute-start(f32[8,128,128]{2,1,0:T(8,128)S(1)} %all-to-all-done.6), channel_id=1, source_target_pairs={{0,2},{1,3},{2,0},{3,1},{4,6},{5,7},{6,4},{7,5},{8,10},{9,11},{10,... | collective-permute-start | bytes 1572872 | tf_op jit(solution)/shard_map/ppermute | solution.py:737
  335.6 17.4 %collective-permute-start.21 = (f32[8,256,128]{2,1,0:T(8,128)}, f32[8,256,128]{2,1,0:T(8,128)S(1)}, u32[]{:S(2)}, u32[]{:S(2)}) collective-permute-start(f32[8,256,128]{2,1,0:T(8,128)} %collective-permute-done.20), channel_id=1, source_target_pairs={{0,1},{1,0},{2,3},{3,2},{4,5},{5,4},{6,7},{7,6},{8,9},{9,8},{10,11... | collective-permute-start | bytes 3145736 | tf_op jit(solution)/shard_map/ppermute | solution.py:737
  338.4 14.6 %collective-permute-start.22 = (f32[8,128,128]{2,1,0:T(8,128)S(1)}, f32[8,128,128]{2,1,0:T(8,128)S(1)}, u32[]{:S(2)}, u32[]{:S(2)}) collective-permute-start(f32[8,128,128]{2,1,0:T(8,128)S(1)} %all-to-all-done.6), channel_id=1, source_target_pairs={{0,1},{1,0},{2,3},{3,2},{4,5},{5,4},{6,7},{7,6},{8,9},{9,8},{10,11... | collective-permute-start | bytes 1572872 | tf_op jit(solution)/shard_map/ppermute | solution.py:737
  346.6 5.7 %copy-start.11 = (f32[8,128,128]{2,1,0:T(8,128)}, f32[8,128,128]{2,1,0:T(8,128)S(1)}, u32[]{:S(2)}) copy-start(f32[8,128,128]{2,1,0:T(8,128)S(1)} %collective-permute-done.23) | copy-start | bytes 1572868
  346.6 6.4 %collective-permute-start.24 = (f32[8,128,128]{2,1,0:T(8,128)S(1)}, f32[8,128,128]{2,1,0:T(8,128)}, u32[]{:S(2)}, u32[]{:S(2)}) collective-permute-start(f32[8,128,128]{2,1,0:T(8,128)S(1)} %collective-permute-done.23), channel_id=1, source_target_pairs={{0,1},{1,0},{2,3},{3,2},{4,5},{5,4},{6,7},{7,6},{8,9},{9,8},{10,11... | collective-permute-start | bytes 1572872 | tf_op jit(solution)/shard_map/ppermute | solution.py:737
  353.0 0.8 copy-start.12
  353.0 1.1 copy-start.6

commit v5 on v4

--- a/solution.py
+++ b/solution.py
@@ -33,13 +33,11 @@
 
 
 def end_faces(block, sides):
-    rows, cols, _ = block.shape
+    rows = block.shape[0]
     up, down = ring("gx")
     last = jnp.concatenate([block[rows - SWEEPS :], sides[rows - SWEEPS :]], axis=1)
     first = jnp.concatenate([block[:SWEEPS], sides[:SWEEPS]], axis=1)
-    above, below = lax.ppermute(last, "gx", up), lax.ppermute(first, "gx", down)
-    whole = jnp.concatenate([above[:, cols:], sides, below[:, cols:]], axis=0)
-    return above[:, :cols], below[:, :cols], jnp.pad(whole, ((0, 0),) + FREE)
+    return lax.ppermute(last, "gx", up), lax.ppermute(first, "gx", down)
 
 
 def mirror(values, axis):
@@ -79,7 +77,7 @@
     spectrum, alternate, edge, punched, once, high, low, folded,
 ):
     step_rows, cols, length = here.shape
-    step = pl.program_id(0) + base[0]
+    step = base[pl.program_id(0)]
     first_row = step * step_rows
     local_row = pl.program_id(0) * step_rows
     period = marks.shape[0]
@@ -107,11 +105,13 @@
         punched[row, pl.ds(start, values.shape[0]), :] = kept
 
     def punch_row(row, source, index):
-        full = first_row + row
+        for c in range(0, cols, CHUNK):
+            punch(row, MARGIN + c, source[index, pl.ds(c, CHUNK), :])
+
+    def punch_sides(row):
+        full = first_row + row - SWEEPS
         punch(row, MARGIN - 8, sides[full, pl.ds(0, 8), :])
         punch(row, MARGIN + cols, sides[full, pl.ds(8, 8), :])
-        for c in range(0, cols, CHUNK):
-            punch(row, MARGIN + c, source[index, pl.ds(c, CHUNK), :])
 
     def neighbours(ref, row, start):
         middle = ref[row, pl.ds(start, CHUNK), :]
@@ -119,7 +119,7 @@
         total += ref[row, pl.ds(start - 1, CHUNK), :] + ref[row, pl.ds(start + 1, CHUNK), :]
         return total + pltpu.roll(middle, 1, 1) + pltpu.roll(middle, length - 1, 1)
 
-    last = (sides.shape[0] - 2 * SWEEPS) // step_rows - 1
+    last = sides.shape[0] // step_rows - 1
     for edge_rows, inside, offset, outer in (
         (above, step > 0, 0, top),
         (below, step < last, step_rows + SWEEPS, bottom),
@@ -128,15 +128,19 @@
         def _():
             for r in range(SWEEPS):
                 punch_row(offset + r, edge_rows, r)
+                punch_sides(offset + r)
 
         @pl.when(jnp.logical_not(inside))
         def _():
             for r in range(SWEEPS):
                 punch_row(offset + r, outer, r)
+                punch(offset + r, MARGIN - SWEEPS, outer[r, pl.ds(cols, SWEEPS), :])
+                punch(offset + r, MARGIN + cols, outer[r, pl.ds(cols + SWEEPS, SWEEPS), :])
 
     @pl.loop(0, step_rows)
     def _(r):
         punch_row(r + SWEEPS, here, r)
+        punch_sides(r + SWEEPS)
 
     @pl.loop(1, step_rows + 2 * SWEEPS - 1, unroll=2)
     def _(r):
@@ -232,23 +236,27 @@
     return hole_marks(template, row, col, rows, cols), jnp.asarray(high), jnp.asarray(low)
 
 
-def filled_spectrum(intensity, arrays, first, part):
+def filled_spectrum(intensity, arrays, first, parts):
     rows, cols, length = intensity.shape
-    half, count = length // 2, part.stop - part.start
-    step_rows = STEP_ROWS if part.start % STEP_ROWS == 0 and count % STEP_ROWS == 0 else PART_STEP
+    half = length // 2
+    aligned = all(edge % STEP_ROWS == 0 for part in parts for edge in (part.start, part.stop))
+    step_rows = STEP_ROWS if aligned else PART_STEP
+    starts = [start for part in parts for start in range(part.start, part.stop, step_rows)]
+    count = step_rows * len(starts)
+    steps = jnp.stack([(first + start) // step_rows for start in starts])
     pairs = step_rows // SWEEPS
     last = rows // SWEEPS - 1
     whole = lambda array: pl.BlockSpec(array.shape, lambda i, b: (0,) * array.ndim)
-    before = lambda i, b: (jnp.maximum((i + b[0]) * pairs - 1, 0), 0, 0)
-    after = lambda i, b: (jnp.minimum((i + b[0] + 1) * pairs, last), 0, 0)
+    before = lambda i, b: (jnp.maximum(b[i] * pairs - 1, 0), 0, 0)
+    after = lambda i, b: (jnp.minimum((b[i] + 1) * pairs, last), 0, 0)
     padded = (step_rows + 2 * SWEEPS, cols + 2 * MARGIN, length)
     return pl.pallas_call(
         fill_kernel,
         grid_spec=pltpu.PrefetchScalarGridSpec(
             num_scalar_prefetch=1,
-            grid=(count // step_rows,),
+            grid=(len(starts),),
             in_specs=[
-                pl.BlockSpec((step_rows, cols, length), lambda i, b: (i + b[0], 0, 0)),
+                pl.BlockSpec((step_rows, cols, length), lambda i, b: (b[i], 0, 0)),
                 pl.BlockSpec((SWEEPS, cols, length), before),
                 pl.BlockSpec((SWEEPS, cols, length), after),
             ] + [whole(array) for array in arrays],
@@ -276,7 +284,7 @@
             bytes_accessed=count * cols * (length + half) * 4,
             transcendentals=0,
         ),
-    )((first // step_rows).reshape(1), intensity, intensity, intensity, *arrays)
+    )(steps, intensity, intensity, intensity, *arrays)
 
 
 def pack(section, offsets):
@@ -338,8 +346,9 @@
             place(count + planes, jnp.zeros((block, width), jnp.float32) + corner[...])
 
 
-def packed_section(col, kept, got, table_pair, table_rows, marks, rim, corner, before, offsets, shape, closing):
-    count, cols, half = kept.shape
+def packed_section(col, kept, got, first, table_pair, table_rows, marks, rim, corner, before, offsets, shape, closing):
+    _, cols, half = kept.shape
+    count = table_rows.shape[0]
     planes, block, width = before.shape
     gx, gy = shape
     step_rows = 4
@@ -350,7 +359,7 @@
     arrays += (rim, corner[None], before)
     out = jax.ShapeDtypeStruct((layers, block // (gx * gy), gx, width), jnp.float32)
     outs = [out] * gy + [jax.ShapeDtypeStruct(before.shape, jnp.float32)]
-    rows_spec = pl.BlockSpec((step_rows, cols, half), lambda i: (i, 0, 0))
+    rows_spec = pl.BlockSpec((step_rows, cols, half), lambda i: (i + first // step_rows, 0, 0))
     return pl.pallas_call(
         lambda *refs: section_kernel(offsets, closing, *refs),
         grid=(count // step_rows,),
@@ -390,24 +399,22 @@
     constants = fill_constants(intensity, template, row, col, cosine_table(length)[:, :half])
     sides = side_faces(intensity)
     given_first, kept_first = (1 - core) * pair_rows, core * pair_rows
-    given, kept = [], []
-    blank = intensity[:SWEEPS]
-    inner_faces = blank, blank, jnp.pad(sides, ((SWEEPS, SWEEPS),) + FREE)
-    outer_faces = []
-
-    def fill(c, start):
-        part = parts[c]
-        inner = part.start >= SWEEPS and part.stop <= pair_rows - SWEEPS
-        use = (inner_faces if inner else tuple(outer_faces)) + constants
-        return list(filled_spectrum(intensity, use, start + part.start, part))
-
-    if not (parts[0].start >= SWEEPS and parts[0].stop <= pair_rows - SWEEPS):
-        outer_faces.extend(end_faces(intensity, sides))
-    given.append(fill(0, given_first))
-    if not outer_faces:
+    inner = parts[0].start >= SWEEPS and parts[0].stop <= pair_rows - SWEEPS
+    side_columns = jnp.pad(sides, ((0, 0),) + FREE)
+    blank = jnp.zeros((SWEEPS, cols + 2 * SWEEPS, length), jnp.float32)
+    ends = (blank, blank) if inner else end_faces(intensity, sides)
+
+    def fill(some, start):
+        arrays = tuple(ends) + (side_columns,) + constants
+        return list(filled_spectrum(intensity, arrays, start, some))
+
+    given, kept = [fill(parts[:1], given_first)], []
+    outer = ends
+    if inner:
         given[0], late_sides = lax.optimization_barrier((given[0], sides))
-        outer_faces.extend(end_faces(intensity, late_sides))
-    kept.append(fill(0, kept_first))
+        outer = end_faces(intensity, late_sides)
+    kept.append(fill(parts[:1], kept_first))
+    ends = outer
 
     table_cols = lax.dynamic_slice_in_dim(table, col * cols, cols, 0)
     kept_rows = lax.dynamic_slice_in_dim(table, row * rows + kept_first, pair_rows, 0)
@@ -422,23 +429,19 @@
     values, packed, lines = 0.0, None, None
     for c, count in enumerate(counts):
         closing = c == len(counts) - 1
-        if c == 1:
-            start, packed = lax.optimization_barrier((given_first, packed))
-            given.extend(fill(later, start) for later in range(1, len(counts)))
-        sent = given[c][0]
         if c > 0:
+            if c == 1:
+                start, packed = lax.optimization_barrier((given_first, packed))
+                given.append(fill(parts[1:], start))
             got_lines = exchanged(packed)
-        if c == 1:
-            start, got_lines = lax.optimization_barrier((kept_first, got_lines))
-            kept.extend(fill(later, start) for later in range(1, len(counts)))
-        held = kept[c][0]
+            if c == 1:
+                behind = kept_first, got_lines, given[1][0]
+                start, got_lines, given[1][0] = lax.optimization_barrier(behind)
+                kept.append(fill(parts[1:], start))
+        if c < 2:
+            got = lax.ppermute(given[c][0], "gy", swap(gy, 1))
+            held = kept[c][0]
         if c > 0:
-            sent, held = lax.optimization_barrier((sent, held))
-        got = lax.ppermute(sent, "gy", swap(gy, 1))
-        if c > 0:
-            held, *later = lax.optimization_barrier([held] + [piece[0] for piece in kept[c + 1 :]])
-            for n, spectrum in enumerate(later):
-                kept[c + 1 + n][0] = spectrum
             lines = sent_lines(got_lines, counts[c - 1], lines)
             values = values + first_axis(lines, table_parts[c - 1])
         if closing:
@@ -456,7 +459,7 @@
             corner = jnp.pad(corner, (0, width - half - 1))
 
         *packed, side = packed_section(
-            col, held, got, table_pair, kept_rows[parts[c]], marks,
+            col, held, got, sum(counts[1:c]), table_pair, kept_rows[parts[c]], marks,
             rim, corner, side, offsets, (gx, gy), closing,
         )
     lines = sent_lines(exchanged(packed), counts[-1], lines)
@@ -767,14 +770,15 @@
 
 
 def square(lower, block):
-    lines = []
-    for b in range(len(lower)):
-        parts = [lower[b]]
-        for c in range(b + 1, len(lower)):
-            part = lower[c][..., b * block : (b + 1) * block]
-            parts.append(jnp.swapaxes(part, -1, -2))
-        lines.append(jnp.concatenate(parts, axis=-1))
-    return jnp.concatenate(lines, axis=-2)
+    if len(lower) == 1:
+        return lower[0]
+    split_at = len(lower) // 2
+    size = split_at * block
+    first = square(lower[:split_at], block)
+    corner = jnp.concatenate([line[..., :size] for line in lower[split_at:]], axis=-2)
+    last = square([line[..., size:] for line in lower[split_at:]], block)
+    top = jnp.concatenate([first, jnp.swapaxes(corner, -1, -2)], axis=-1)
+    return jnp.concatenate([top, jnp.concatenate([corner, last], axis=-1)], axis=-2)
 
 
 def solution(mesh):

time: 390 us -> 381 us (0.977)
  waiting for transfers between devices: 109 us -> 122 us
  Pallas kernels: 137 us -> 125 us
  local copies, waits for them, and re-layouts: 42.5 us -> 36.3 us
  other arithmetic: 17.3 us -> 12.7 us
    ppermute x9, waiting for transfers between devices: 20.2 us -> 30.8 us  [exchanged(): lax.ppermute(packed[p], 'gy', swap(gy, p))]
    pallas_call x6 -> x4, Pallas kernels: 74 us -> 67.7 us  [filled_spectrum(): pl.pallas_call(fill_kernel, grid_spec=pltpu.PrefetchScalarGridSpec(num_sc...]
    slice x5 -> x0, local copies, waits for them, and re-layouts: 5.67 us -> none  [the longest x2 2.15 us: end_faces(): return (above[:, :cols], below[:, :cols], jnp.pad(whole, ((0, 0),) + FREE))]
    pallas_call x1, Pallas kernels: 33.9 us -> 29.2 us  [result_block(): pl.pallas_call(lambda *refs: result_kernel(offsets, own, devices, groups,...]
    concatenate x5 -> x3, local copies, waits for them, and re-layouts: 4.34 us -> 0.26 us  [the longest x2 0.16 us: square(): top = jnp.concatenate([first, jnp.swapaxes(corner, -1, -2)], axis=-1)]
    unnamed x61 -> x57, local copies, waits for them, and re-layouts: 8.06 us -> 4.59 us
  transfers between devices with their start and end apart: 31 -> 30, of which waited for: 14 -> 14; matrix products, arithmetic and copies ran while one was open for 12% -> 10% of each run, Pallas kernels for 21% -> 19%
where the time goes in v5:
time: 381 us; the launch traced here: 380 us
  Pallas kernels  125 us (33%)
  waiting for transfers between devices  122 us (32%)
  starting transfers between devices  43.5 us (11%)
  local copies, waits for them, and re-layouts  36.3 us (10%)
  blocking collectives  32.5 us (9%)
  other arithmetic  12.7 us (3%)
  matrix products  6.17 us (2%)
    pallas_call x4, Pallas kernels, filled_spectrum(): pl.pallas_call(fill_kernel, grid_spec=pltpu.PrefetchScalarGridSpec(num_sc...  67.7 us
    ppermute x9, waiting for transfers between devices, gathered(): pieces[place ^ bit] = lax.ppermute(pieces[place], 'gy', swap(peers, bit))  35.6 us
    all_to_all x1, blocking collectives, on_device(): piece = lax.all_to_all(messages, 'gx', 0, 0, tiled=True)  32.5 us
    ppermute x9, waiting for transfers between devices, exchanged(): lax.ppermute(packed[p], 'gy', swap(gy, p))  30.8 us
    pallas_call x1, Pallas kernels, result_block(): pl.pallas_call(lambda *refs: result_kernel(offsets, own, devices, groups,...  29.2 us
    all_to_all x3, waiting for transfers between devices, sent_lines(): return lax.all_to_all(lines, 'gx', 0, 0, tiled=True)  22.1 us
    pallas_call x3, Pallas kernels, packed_section(): pl.pallas_call(lambda *refs: section_kernel(offsets, closing, *refs), gri...  19.5 us
    all_to_all x1, waiting for transfers between devices, on_device(): lax.all_to_all(jnp.concatenate(turned, axis=3), ('gy', 'gx'), 0, 0, tiled...  18.2 us
  transfers between devices with their start and end apart: 30, of which 14 were waited for; matrix products, arithmetic and copies ran while one was open for 10% of the time, Pallas kernels for 19%

profile of v5, /device:TPU:0, one launch (start us, length us, event | category | flops | bytes accessed | tf_op | source)
XLA Modules:
  0.0 379.9 jit_solution(17838218892230177029)
XLA Ops:
  0.0 1.8 fusion.33
  2.3 2.0 collective-permute-start.1
  4.3 3.6 shard_map.55.marks
  8.5 2.4 collective-permute-done.1
  11.2 1.6 pad.12.sides
  13.6 17.0 %shard_map.57 = (f32[16,128,256]{2,1,0:T(8,128)}, f32[16,256]{1,0:T(8,128)}, f32[128,128]{1,0:T(8,128)}) custom-call(s32[2]{0:T(128)} %get-tuple-element.160.base, f32[64,128,512]{2,1,0:T(8,128)} %below.7, f32[64,128,512]{2,1,0:T(8,128)} %below.7, f32[64,128,512]{2,1,0:T(8,128)} %below.7, f32[2,132,512]{2,1,0:T(8,128)} %broadcast_in_dim.10.top.bottom, ...), custom_call_target="tpu_custom_call" | custom-call | flops 1610612736 | bytes 6291456 | tf_op jit(solution)/shard_map/pallas_call | solution.py:253
  30.8 1.3 fusion.32
  34.6 0.9 constant_dynamic-slice_fusion.4
  36.3 1.1 pad_maximum_fusion
  37.4 2.3 collective-permute-start.6
  39.7 1.0 pad_maximum_fusion.1
  40.7 3.0 collective-permute-start.7
  43.8 17.1 %shard_map.56 = (f32[16,128,256]{2,1,0:T(8,128)}, f32[16,256]{1,0:T(8,128)}, f32[128,128]{1,0:T(8,128)}) custom-call(s32[2]{0:T(128)} %get-tuple-element.159.base, f32[64,128,512]{2,1,0:T(8,128)} %below.7, f32[64,128,512]{2,1,0:T(8,128)} %below.7, f32[64,128,512]{2,1,0:T(8,128)} %below.7, f32[2,132,512]{2,1,0:T(8,128)} %broadcast_in_dim.10.top.bottom, ...), custom_call_target="tpu_custom_call" | custom-call | flops 1610612736 | bytes 6291456 | tf_op jit(solution)/shard_map/pallas_call | solution.py:253
  62.2 0.9 broadcast_in_dim.23.refs_10_
  63.1 8.1 %shard_map.58 = (f32[16,2,8,640]{3,2,1,0:T(8,128)}, f32[16,2,8,640]{3,2,1,0:T(8,128)}, f32[16,2,8,640]{3,2,1,0:T(8,128)}, f32[16,2,8,640]{3,2,1,0:T(8,128)}, f32[4,64,640]{2,1,0:T(8,128)}) custom-call(s32[1]{0:T(128)} %bitcast.3.refs_0_, f32[4,16]{1,0:T(4,128)} %pad_maximum_fusion.7.refs_1_, f32[16,128,256]{2,1,0:T(8,128)} %get-tuple-element.61.refs_2_, ...), custom_call_target="tpu_custom_call" | custom-call | flops 1610612736 | bytes 8388608 | tf_op jit(solution)/shard_map/pallas_call | solution.py:363
  71.3 1.9 collective-permute-start.4
  73.3 0.9 copy.75.top
  74.2 2.0 copy.76.bottom
  76.9 16.7 %shard_map.59 = (f32[16,128,256]{2,1,0:T(8,128)}, f32[16,256]{1,0:T(8,128)}, f32[128,128]{1,0:T(8,128)}) custom-call(s32[2]{0:T(128)} %pad_add_fusion.3.base, f32[64,128,512]{2,1,0:T(8,128)} %below.7, f32[64,128,512]{2,1,0:T(8,128)} %below.7, f32[64,128,512]{2,1,0:T(8,128)} %below.7, f32[2,132,512]{2,1,0:T(8,128)} %copy.75.top, f32[2,132,512]{2,1,0:T(8,128)} %copy.76.bottom, ...), custom_call_target="tpu_custom_call" | custom-call | flops 1610612736 | bytes 6291456 | tf_op jit(solution)/shard_map/pallas_call | solution.py:253
  93.6 8.9 %collective-permute-done.5 = f32[16,2,8,640]{3,2,1,0:T(8,128)S(1)} collective-permute-done((f32[16,2,8,640]{3,2,1,0:T(8,128)}, f32[16,2,8,640]{3,2,1,0:T(8,128)S(1)}, u32[]{:S(2)}, u32[]{:S(2)}) %collective-permute-start.5) | collective-permute-done | bytes 655392 | tf_op jit(solution)/shard_map/ppermute | solution.py:747
  103.5 0.9 constant_dynamic-slice_fusion.2
  104.4 0.9 constant_dynamic-slice_fusion.7
  105.6 1.8 copy.77
  107.4 4.6 %all-to-all-start = ((f32[8,2,32,640]{3,1,2,0:T(2,128)}), f32[8,2,32,640]{3,1,2,0:T(2,128)}, u32[]{:S(2)}, u32[]{:S(2)}) async-start(f32[8,2,32,640]{3,1,2,0:T(2,128)} %copy.77), calls=%async_computation | async-start | bytes 2621440 | tf_op jit(solution)/shard_map/all_to_all | solution.py:757
  112.1 1.2 concatenate.75
  116.0 16.9 %shard_map.60 = (f32[16,128,256]{2,1,0:T(8,128)}, f32[16,256]{1,0:T(8,128)}, f32[128,128]{1,0:T(8,128)}) custom-call(s32[2]{0:T(128)} %pad_add_fusion.4.base, f32[64,128,512]{2,1,0:T(8,128)} %below.7, f32[64,128,512]{2,1,0:T(8,128)} %below.7, f32[64,128,512]{2,1,0:T(8,128)} %below.7, f32[2,132,512]{2,1,0:T(8,128)} %copy.75.top, f32[2,132,512]{2,1,0:T(8,128)} %copy.76.bottom, ...), custom_call_target="tpu_custom_call" | custom-call | flops 1610612736 | bytes 6291456 | tf_op jit(solution)/shard_map/pallas_call | solution.py:253
  132.9 1.2 fusion.8
  135.4 1.0 fusion.13.refs_8_
  136.4 1.3 copy-done
  137.7 5.5 %shard_map.61 = (f32[8,2,8,640]{3,2,1,0:T(8,128)}, f32[8,2,8,640]{3,2,1,0:T(8,128)}, f32[8,2,8,640]{3,2,1,0:T(8,128)}, f32[8,2,8,640]{3,2,1,0:T(8,128)}, f32[4,64,640]{2,1,0:T(8,128)}) custom-call(s32[1]{0:T(128)} %bitcast.3.refs_0_, f32[4,8]{1,0:T(4,128)} %pad_maximum_fusion.8.refs_1_, f32[16,128,256]{2,1,0:T(8,128)} %get-tuple-element.82.refs_2_, ...), custom_call_target="tpu_custom_call" | custom-call | flops 805306368 | bytes 4194304 | tf_op jit(solution)/shard_map/pallas_call | solution.py:363
  143.2 1.7 collective-permute-start.9
  146.0 5.9 %shard_map.62 = (f32[13,2,8,640]{3,2,1,0:T(8,128)}, f32[13,2,8,640]{3,2,1,0:T(8,128)}, f32[13,2,8,640]{3,2,1,0:T(8,128)}, f32[13,2,8,640]{3,2,1,0:T(8,128)}, f32[4,64,640]{2,1,0:T(8,128)}) custom-call(s32[1]{0:T(128)} %bitcast.3.refs_0_, f32[4,8]{1,0:T(4,128)} %pad_maximum_fusion.9.refs_1_, f32[16,128,256]{2,1,0:T(8,128)} %get-tuple-element.82.refs_2_, ...), custom_call_target="tpu_custom_call" | custom-call | flops 805306368 | bytes 4194304 | tf_op jit(solution)/shard_map/pallas_call | solution.py:363
  151.8 1.7 collective-permute-start.12
  154.0 6.3 %collective-permute-done.11 = f32[8,2,8,640]{3,2,1,0:T(8,128)S(1)} collective-permute-done((f32[8,2,8,640]{3,2,1,0:T(8,128)}, f32[8,2,8,640]{3,2,1,0:T(8,128)S(1)}, u32[]{:S(2)}, u32[]{:S(2)}) %collective-permute-start.11) | collective-permute-done | bytes 327712 | tf_op jit(solution)/shard_map/ppermute | solution.py:747
  160.4 1.2 copy.81
  161.6 5.7 %all-to-all-start.1 = ((f32[8,2,16,640]{3,1,2,0:T(2,128)}), f32[8,2,16,640]{3,1,2,0:T(2,128)S(1)}, u32[]{:S(2)}, u32[]{:S(2)}) async-start(f32[8,2,16,640]{3,1,2,0:T(2,128)} %copy.81), calls=%async_computation.1 | async-start | bytes 1310720 | tf_op jit(solution)/shard_map/all_to_all | solution.py:757
  167.3 5.0 %collective-permute-done.12 = f32[13,2,8,640]{3,2,1,0:T(8,128)S(1)} collective-permute-done((f32[13,2,8,640]{3,2,1,0:T(8,128)}, f32[13,2,8,640]{3,2,1,0:T(8,128)S(1)}, u32[]{:S(2)}, u32[]{:S(2)}) %collective-permute-start.12) | collective-permute-done | bytes 532512 | tf_op jit(solution)/shard_map/ppermute | solution.py:747
  172.4 10.2 %collective-permute-done.14 = f32[13,2,8,640]{3,2,1,0:T(8,128)S(1)} collective-permute-done((f32[13,2,8,640]{3,2,1,0:T(8,128)}, f32[13,2,8,640]{3,2,1,0:T(8,128)S(1)}, u32[]{:S(2)}, u32[]{:S(2)}) %collective-permute-start.14) | collective-permute-done | bytes 532512 | tf_op jit(solution)/shard_map/ppermute | solution.py:747
  182.9 2.4 all-to-all-done.1
  185.3 1.3 copy.83
  186.6 3.6 all-to-all-start.2
  190.4 2.1 convolution_bitcast_fusion
  192.5 19.7 %all-to-all-done.2 = f32[8,2,21,640]{3,1,2,0:T(2,128)S(1)} async-done(((f32[8,2,21,640]{3,1,2,0:T(2,128)}), f32[8,2,21,640]{3,1,2,0:T(2,128)S(1)}, u32[]{:S(2)}, u32[]{:S(2)}) %all-to-all-start.2) | async-done | bytes 860192 | tf_op jit(solution)/shard_map/all_to_all | solution.py:757
  213.8 1.0 copy.117
  215.0 2.4 concatenate.80
  217.4 3.8 all-to-all-start.3
  221.9 18.2 %all-to-all-done.3 = f32[32,2,2,1280]{3,2,1,0:T(2,128)S(1)} async-done(((f32[32,2,2,1280]{3,2,1,0:T(2,128)}), f32[32,2,2,1280]{3,2,1,0:T(2,128)S(1)}, u32[]{:S(2)}, u32[]{:S(2)}) %all-to-all-start.3) | async-done | bytes 655392 | tf_op jit(solution)/shard_map/all_to_all | solution.py:471
  240.1 1.0 copy.86
  241.1 5.4 %shard_map.63 = (f32[8,288,128]{2,1,0:T(8,128)}, f32[8,256,128]{2,1,0:T(8,128)}, f32[8,128,128]{2,1,0:T(8,128)}) custom-call(f32[2,256,640]{2,1,0:T(8,128)} %bitcast.164, f32[2,64,1280]{2,1,0:T(8,128)} %bitcast.173, f32[2,5,640]{2,1,0:T(8,128)} %copy_multiply_fusion.refs_2_), custom_call_target="tpu_custom_call" | custom-call | tf_op jit(solution)/shard_map/pallas_call | solution.py:606
  246.5 32.5 %all_to_all.35 = f32[8,288,128]{2,1,0:T(8,128)S(1)} all-to-all(f32[8,288,128]{2,1,0:T(8,128)} %get-tuple-element.105), channel_id=1, replica_groups=mesh['gx'=8,'gy'=4] {'gx'}, dimensions={0} | all-to-all | bytes 2359296 | tf_op jit(solution)/shard_map/all_to_all | solution.py:487
  279.0 1.2 collective-permute-start.16
  280.2 3.6 all-to-all-start.5
  283.9 21.4 %collective-permute-done.16 = f32[8,288,128]{2,1,0:T(8,128)} collective-permute-done((f32[8,288,128]{2,1,0:T(8,128)S(1)}, f32[8,288,128]{2,1,0:T(8,128)}, u32[]{:S(2)}, u32[]{:S(2)}) %collective-permute-start.16) | collective-permute-done | bytes 1179680 | tf_op jit(solution)/shard_map/ppermute | solution.py:740
  307.4 1.9 all-to-all-done.5
  309.9 3.9 %all-to-all-start.6 = ((f32[8,128,128]{2,1,0:T(8,128)}), f32[8,128,128]{2,1,0:T(8,128)S(1)}, u32[]{:S(2)}, u32[]{:S(2)}) async-start(f32[8,128,128]{2,1,0:T(8,128)} %get-tuple-element.113), calls=%async_computation.6 | async-start | bytes 1048576 | tf_op jit(solution)/shard_map/all_to_all | solution.py:487
  313.8 0.9 slice_bitcast_fusion.9
  314.7 0.9 slice_bitcast_fusion.8
  315.7 0.9 slice_bitcast_fusion.2
  317.4 11.3 %all-to-all-done.6 = f32[8,128,128]{2,1,0:T(8,128)S(1)} async-done(((f32[8,128,128]{2,1,0:T(8,128)}), f32[8,128,128]{2,1,0:T(8,128)S(1)}, u32[]{:S(2)}, u32[]{:S(2)}) %all-to-all-start.6) | async-done | bytes 524320 | tf_op jit(solution)/shard_map/all_to_all | solution.py:487
  328.7 4.4 %collective-permute-done.19 = f32[8,256,128]{2,1,0:T(8,128)} collective-permute-done((f32[8,256,128]{2,1,0:T(8,128)S(1)}, f32[8,256,128]{2,1,0:T(8,128)}, u32[]{:S(2)}, u32[]{:S(2)}) %collective-permute-start.19) | collective-permute-done | bytes 1048608 | tf_op jit(solution)/shard_map/ppermute | solution.py:740
  333.1 1.7 collective-permute-start.22
  336.3 9.7 %collective-permute-done.22 = f32[8,128,128]{2,1,0:T(8,128)S(1)} collective-permute-done((f32[8,128,128]{2,1,0:T(8,128)S(1)}, f32[8,128,128]{2,1,0:T(8,128)S(1)}, u32[]{:S(2)}, u32[]{:S(2)}) %collective-permute-start.22) | collective-permute-done | bytes 524320 | tf_op jit(solution)/shard_map/ppermute | solution.py:740
  349.5 1.0 copy-done.6
  350.5 29.2 %shard_map.64 = f32[64,128,512]{2,1,0:T(8,128)} custom-call(s32[4]{0:T(128)} %pad_add_fusion.refs_0_, f32[64,640]{1,0:T(8,128)} %bitcast.179, f32[64,256]{1,0:T(8,128)} %slice.366.refs_2_, f32[128,128]{1,0:T(8,128)} %pad.14.refs_3_, bf16[128,256]{1,0:T(8,128)(2,1)} %fusion.15.refs_4_, bf16[256,256]{1,0:T(8,128)(2,1)} %fusion.7.refs_5_, ...), custom_call_target="tpu_custom_call" | custom-call | tf_op jit(solution)/shard_map/pallas_call | solution.py:711
  (170 shorter events, 25.6 us)
Async XLA Ops:
  1.8 6.7 %collective-permute-start = (f32[64,2,512]{2,1,0:T(2,128)S(1)}, f32[64,2,512]{2,1,0:T(2,128)S(1)}, u32[]{:S(2)}, u32[]{:S(2)}) collective-permute-start(f32[64,2,512]{2,1,0:T(2,128)S(1)} %get-tuple-element.119), channel_id=1, source_target_pairs={{0,1},{1,2},{2,3},{3,0},{4,5},{5,6},{6,7},{7,4},{8,9},{9,10},{10,1... | collective-permute-start | bytes 786440 | tf_op jit(solution)/shard_map/ppermute | solution.py:30
  2.3 8.6 %collective-permute-start.1 = (f32[64,2,512]{2,1,0:T(2,128)S(1)}, f32[64,2,512]{2,1,0:T(2,128)S(1)}, u32[]{:S(2)}, u32[]{:S(2)}) collective-permute-start(f32[64,2,512]{2,1,0:T(2,128)S(1)} %get-tuple-element.120), channel_id=1, source_target_pairs={{1,0},{2,1},{3,2},{0,3},{5,4},{6,5},{7,6},{4,7},{9,8},{10,9},{11,1... | collective-permute-start | bytes 786440 | tf_op jit(solution)/shard_map/ppermute | solution.py:31
  30.6 30.3 %collective-permute-start.2 = (f32[16,128,256]{2,1,0:T(8,128)}, f32[16,128,256]{2,1,0:T(8,128)}, u32[]{:S(2)}, u32[]{:S(2)}) collective-permute-start(f32[16,128,256]{2,1,0:T(8,128)} %get-tuple-element.65), channel_id=1, source_target_pairs={{0,1},{1,0},{2,3},{3,2},{4,5},{5,4},{6,7},{7,6},{8,9},{9,8},{10,11... | collective-permute-start | bytes 6291464 | tf_op jit(solution)/shard_map/ppermute | solution.py:442
  32.1 1.1 copy-start.4
  37.4 35.9 %collective-permute-start.6 = (f32[2,132,512]{2,0,1:T(2,128)}, f32[2,132,512]{2,0,1:T(2,128)S(1)}, u32[]{:S(2)}, u32[]{:S(2)}) collective-permute-start(f32[2,132,512]{2,0,1:T(2,128)} %pad_maximum_fusion), channel_id=1, source_target_pairs={{0,4},{4,8},{8,12},{12,16},{16,20},{20,24},{24,28},{28,0},{1,5},{5... | collective-permute-start | bytes 1622024 | tf_op jit(solution)/shard_map/ppermute | solution.py:40
  40.7 33.5 %collective-permute-start.7 = (f32[2,132,512]{2,0,1:T(2,128)}, f32[2,132,512]{2,0,1:T(2,128)}, u32[]{:S(2)}, u32[]{:S(2)}) collective-permute-start(f32[2,132,512]{2,0,1:T(2,128)} %pad_maximum_fusion.1), channel_id=1, source_target_pairs={{4,0},{8,4},{12,8},{16,12},{20,16},{24,20},{28,24},{0,28},{5,1},{9... | collective-permute-start | bytes 1622024 | tf_op jit(solution)/shard_map/ppermute | solution.py:40
  71.3 22.3 %collective-permute-start.3 = (f32[16,2,8,640]{3,2,1,0:T(8,128)}, f32[16,2,8,640]{3,2,1,0:T(8,128)S(1)}, u32[]{:S(2)}, u32[]{:S(2)}) collective-permute-start(f32[16,2,8,640]{3,2,1,0:T(8,128)} %get-tuple-element.71), channel_id=1, source_target_pairs={{0,1},{1,0},{2,3},{3,2},{4,5},{5,4},{6,7},{7,6},{8,9},{9,8},{10,11... | collective-permute-start | bytes 1966088 | tf_op jit(solution)/shard_map/ppermute | solution.py:747
  71.3 22.3 %collective-permute-start.4 = (f32[16,2,8,640]{3,2,1,0:T(8,128)}, f32[16,2,8,640]{3,2,1,0:T(8,128)S(1)}, u32[]{:S(2)}, u32[]{:S(2)}) collective-permute-start(f32[16,2,8,640]{3,2,1,0:T(8,128)} %get-tuple-element.72), channel_id=1, source_target_pairs={{0,2},{1,3},{2,0},{3,1},{4,6},{5,7},{6,4},{7,5},{8,10},{9,11},{10,... | collective-permute-start | bytes 1966088 | tf_op jit(solution)/shard_map/ppermute | solution.py:747
  73.2 29.3 %collective-permute-start.5 = (f32[16,2,8,640]{3,2,1,0:T(8,128)}, f32[16,2,8,640]{3,2,1,0:T(8,128)S(1)}, u32[]{:S(2)}, u32[]{:S(2)}) collective-permute-start(f32[16,2,8,640]{3,2,1,0:T(8,128)} %get-tuple-element.73), channel_id=1, source_target_pairs={{0,3},{1,2},{2,1},{3,0},{4,7},{5,6},{6,5},{7,4},{8,11},{9,10},{10,... | collective-permute-start | bytes 1966088 | tf_op jit(solution)/shard_map/ppermute | solution.py:747
  93.6 11.7 %copy-start.7 = (f32[16,2,8,640]{3,2,1,0:T(8,128)S(1)}, f32[16,2,8,640]{3,2,1,0:T(8,128)}, u32[]{:S(2)}) copy-start(f32[16,2,8,640]{3,2,1,0:T(8,128)} %get-tuple-element.77) | copy-start | bytes 1966084
  93.6 8.9 %copy-start.8 = (f32[16,2,8,640]{3,2,1,0:T(8,128)}, f32[16,2,8,640]{3,2,1,0:T(8,128)S(1)}, u32[]{:S(2)}) copy-start(f32[16,2,8,640]{3,2,1,0:T(8,128)S(1)} %collective-permute-done.4) | copy-start | bytes 1966084
  102.5 0.8 copy-start.10
  103.3 2.0 copy-start.9
  103.3 33.0 %collective-permute-start.8 = (f32[16,128,256]{2,1,0:T(8,128)}, f32[16,128,256]{2,1,0:T(8,128)S(1)}, u32[]{:S(2)}, u32[]{:S(2)}) collective-permute-start(f32[16,128,256]{2,1,0:T(8,128)} %get-tuple-element.83), channel_id=1, source_target_pairs={{0,1},{1,0},{2,3},{3,2},{4,5},{5,4},{6,7},{7,6},{8,9},{9,8},{10,11... | collective-permute-start | bytes 6291464 | tf_op jit(solution)/shard_map/ppermute | solution.py:442
  104.4 1.1 copy-start.11
  107.4 4.7 %copy-start.12 = (f32[8,257]{0,1:T(8,128)S(1)}, f32[8,257]{0,1:T(8,128)}, u32[]{:S(2)}) copy-start(f32[8,257]{0,1:T(8,128)} %get-tuple-element.136) | copy-start | bytes 24676
  107.4 4.7 %copy-start.13 = (f32[8,257]{0,1:T(8,128)S(1)}, f32[8,257]{0,1:T(8,128)}, u32[]{:S(2)}) copy-start(f32[8,257]{0,1:T(8,128)} %get-tuple-element.137) | copy-start | bytes 24676
  107.4 4.7 %copy-start.14 = (f32[8,257]{0,1:T(8,128)S(1)}, f32[8,257]{0,1:T(8,128)}, u32[]{:S(2)}) copy-start(f32[8,257]{0,1:T(8,128)} %get-tuple-element.138) | copy-start | bytes 24676
  107.4 53.0 %all-to-all-start = ((f32[8,2,32,640]{3,1,2,0:T(2,128)}), f32[8,2,32,640]{3,1,2,0:T(2,128)}, u32[]{:S(2)}, u32[]{:S(2)}) async-start(f32[8,2,32,640]{3,1,2,0:T(2,128)} %copy.77), calls=%async_computation | async-start | bytes 2621440 | tf_op jit(solution)/shard_map/all_to_all | solution.py:757
  116.0 16.9 %copy-start.20 = (f32[128,128]{1,0:T(8,128)S(1)}, f32[128,128]{1,0:T(8,128)}, u32[]{:S(2)}) copy-start(f32[128,128]{1,0:T(8,128)} %get-tuple-element.90) | copy-start | bytes 196612
  116.0 16.9 %copy-start.21 = (f32[128,128]{1,0:T(8,128)S(1)}, f32[128,128]{1,0:T(8,128)}, u32[]{:S(2)}) copy-start(f32[128,128]{1,0:T(8,128)} %get-tuple-element.92) | copy-start | bytes 196612
  116.0 16.9 %copy-start.22 = (f32[128,128]{1,0:T(8,128)S(1)}, f32[128,128]{1,0:T(8,128)}, u32[]{:S(2)}) copy-start(f32[128,128]{1,0:T(8,128)} %get-tuple-element.91) | copy-start | bytes 196612
  116.0 18.1 %copy-start.23 = (f32[16,256]{1,0:T(8,128)S(1)}, f32[16,256]{1,0:T(8,128)}, u32[]{:S(2)}) copy-start(f32[16,256]{1,0:T(8,128)} %get-tuple-element.94) | copy-start | bytes 49156
  116.0 18.1 %copy-start.24 = (f32[16,256]{1,0:T(8,128)S(1)}, f32[16,256]{1,0:T(8,128)}, u32[]{:S(2)}) copy-start(f32[16,256]{1,0:T(8,128)} %get-tuple-element.96) | copy-start | bytes 49156
  116.0 18.1 %copy-start.25 = (f32[16,256]{1,0:T(8,128)S(1)}, f32[16,256]{1,0:T(8,128)}, u32[]{:S(2)}) copy-start(f32[16,256]{1,0:T(8,128)} %get-tuple-element.95) | copy-start | bytes 49156
  136.4 1.3 copy-start
  143.2 10.8 %collective-permute-start.9 = (f32[8,2,8,640]{3,2,1,0:T(8,128)}, f32[8,2,8,640]{3,2,1,0:T(8,128)S(1)}, u32[]{:S(2)}, u32[]{:S(2)}) collective-permute-start(f32[8,2,8,640]{3,2,1,0:T(8,128)} %get-tuple-element.86), channel_id=1, source_target_pairs={{0,2},{1,3},{2,0},{3,1},{4,6},{5,7},{6,4},{7,5},{8,10},{9,11},{10,... | collective-permute-start | bytes 983048 | tf_op jit(solution)/shard_map/ppermute | solution.py:747
  144.9 9.1 %collective-permute-start.10 = (f32[8,2,8,640]{3,2,1,0:T(8,128)}, f32[8,2,8,640]{3,2,1,0:T(8,128)S(1)}, u32[]{:S(2)}, u32[]{:S(2)}) collective-permute-start(f32[8,2,8,640]{3,2,1,0:T(8,128)} %get-tuple-element.87), channel_id=1, source_target_pairs={{0,1},{1,0},{2,3},{3,2},{4,5},{5,4},{6,7},{7,6},{8,9},{9,8},{10,11... | collective-permute-start | bytes 983048 | tf_op jit(solution)/shard_map/ppermute | solution.py:747
  144.9 15.4 %collective-permute-start.11 = (f32[8,2,8,640]{3,2,1,0:T(8,128)}, f32[8,2,8,640]{3,2,1,0:T(8,128)S(1)}, u32[]{:S(2)}, u32[]{:S(2)}) collective-permute-start(f32[8,2,8,640]{3,2,1,0:T(8,128)} %get-tuple-element.88), channel_id=1, source_target_pairs={{0,3},{1,2},{2,1},{3,0},{4,7},{5,6},{6,5},{7,4},{8,11},{9,10},{10,... | collective-permute-start | bytes 983048 | tf_op jit(solution)/shard_map/ppermute | solution.py:747
  145.9 8.0 %copy-start.19 = (f32[8,2,8,640]{3,2,1,0:T(8,128)S(1)}, f32[8,2,8,640]{3,2,1,0:T(8,128)}, u32[]{:S(2)}) copy-start(f32[8,2,8,640]{3,2,1,0:T(8,128)} %get-tuple-element.85) | copy-start | bytes 983044
  151.8 20.5 %collective-permute-start.12 = (f32[13,2,8,640]{3,2,1,0:T(8,128)}, f32[13,2,8,640]{3,2,1,0:T(8,128)S(1)}, u32[]{:S(2)}, u32[]{:S(2)}) collective-permute-start(f32[13,2,8,640]{3,2,1,0:T(8,128)} %get-tuple-element.100), channel_id=1, source_target_pairs={{0,2},{1,3},{2,0},{3,1},{4,6},{5,7},{6,4},{7,5},{8,10},{9,11},{10,... | collective-permute-start | bytes 1597448 | tf_op jit(solution)/shard_map/ppermute | solution.py:747
  153.6 18.9 %collective-permute-start.13 = (f32[13,2,8,640]{3,2,1,0:T(8,128)}, f32[13,2,8,640]{3,2,1,0:T(8,128)S(1)}, u32[]{:S(2)}, u32[]{:S(2)}) collective-permute-start(f32[13,2,8,640]{3,2,1,0:T(8,128)} %get-tuple-element.101), channel_id=1, source_target_pairs={{0,1},{1,0},{2,3},{3,2},{4,5},{5,4},{6,7},{7,6},{8,9},{9,8},{10,11... | collective-permute-start | bytes 1597448 | tf_op jit(solution)/shard_map/ppermute | solution.py:747
  153.9 28.7 %collective-permute-start.14 = (f32[13,2,8,640]{3,2,1,0:T(8,128)}, f32[13,2,8,640]{3,2,1,0:T(8,128)S(1)}, u32[]{:S(2)}, u32[]{:S(2)}) collective-permute-start(f32[13,2,8,640]{3,2,1,0:T(8,128)} %get-tuple-element.102), channel_id=1, source_target_pairs={{0,3},{1,2},{2,1},{3,0},{4,7},{5,6},{6,5},{7,4},{8,11},{9,10},{10,... | collective-permute-start | bytes 1597448 | tf_op jit(solution)/shard_map/ppermute | solution.py:747
  160.4 12.0 %copy-start.15 = (f32[13,2,8,640]{3,2,1,0:T(8,128)S(1)}, f32[13,2,8,640]{3,2,1,0:T(8,128)}, u32[]{:S(2)}) copy-start(f32[13,2,8,640]{3,2,1,0:T(8,128)} %get-tuple-element.99) | copy-start | bytes 1597444
  161.6 23.7 %all-to-all-start.1 = ((f32[8,2,16,640]{3,1,2,0:T(2,128)}), f32[8,2,16,640]{3,1,2,0:T(2,128)S(1)}, u32[]{:S(2)}, u32[]{:S(2)}) async-start(f32[8,2,16,640]{3,1,2,0:T(2,128)} %copy.81), calls=%async_computation.1 | async-start | bytes 1310720 | tf_op jit(solution)/shard_map/all_to_all | solution.py:757
  182.8 7.4 %copy-start.17 = (f32[8,2,32,256]{3,2,1,0:T(8,128)S(1)}, f32[8,2,32,256]{3,2,1,0:T(8,128)}, u32[]{:S(2)}) copy-start(f32[8,2,32,256]{3,2,1,0:T(8,128)} %constant.142) | copy-start | bytes 1572868
  182.9 7.4 %copy-start.18 = (f32[8,2,32,256]{3,2,1,0:T(8,128)S(1)}, f32[8,2,32,256]{3,2,1,0:T(8,128)}, u32[]{:S(2)}) copy-start(f32[8,2,32,256]{3,2,1,0:T(8,128)} %constant.140) | copy-start | bytes 1572868
  186.6 25.6 %all-to-all-start.2 = ((f32[8,2,21,640]{3,1,2,0:T(2,128)}), f32[8,2,21,640]{3,1,2,0:T(2,128)S(1)}, u32[]{:S(2)}, u32[]{:S(2)}) async-start(f32[8,2,21,640]{3,1,2,0:T(2,128)} %copy.83), calls=%async_computation.2 | async-start | bytes 1720320 | tf_op jit(solution)/shard_map/all_to_all | solution.py:757
  213.8 1.1 copy-start.2
  217.4 22.7 %all-to-all-start.3 = ((f32[32,2,2,1280]{3,2,1,0:T(2,128)}), f32[32,2,2,1280]{3,2,1,0:T(2,128)S(1)}, u32[]{:S(2)}, u32[]{:S(2)}) async-start(f32[32,2,2,1280]{3,2,1,0:T(2,128)} %concatenate.80), calls=%async_computation.3 | async-start | bytes 1310720 | tf_op jit(solution)/shard_map/all_to_all | solution.py:471
  279.0 30.9 %copy-start.1 = (f32[8,288,128]{2,1,0:T(8,128)}, f32[8,288,128]{2,1,0:T(8,128)S(1)}, u32[]{:S(2)}) copy-start(f32[8,288,128]{2,1,0:T(8,128)S(1)} %all_to_all.35) | copy-start | bytes 3538948
  279.0 26.4 %collective-permute-start.16 = (f32[8,288,128]{2,1,0:T(8,128)S(1)}, f32[8,288,128]{2,1,0:T(8,128)}, u32[]{:S(2)}, u32[]{:S(2)}) collective-permute-start(f32[8,288,128]{2,1,0:T(8,128)S(1)} %all_to_all.35), channel_id=1, source_target_pairs={{0,2},{1,3},{2,0},{3,1},{4,6},{5,7},{6,4},{7,5},{8,10},{9,11},{10,... | collective-permute-start | bytes 3538952 | tf_op jit(solution)/shard_map/ppermute | solution.py:740
  280.2 29.1 %all-to-all-start.5 = ((f32[8,256,128]{2,1,0:T(8,128)}), f32[8,256,128]{2,1,0:T(8,128)S(1)}, u32[]{:S(2)}, u32[]{:S(2)}) async-start(f32[8,256,128]{2,1,0:T(8,128)} %get-tuple-element.108), calls=%async_computation.5 | async-start | bytes 2097152 | tf_op jit(solution)/shard_map/all_to_all | solution.py:487
  283.8 25.6 %collective-permute-start.15 = (f32[8,288,128]{2,1,0:T(8,128)S(1)}, f32[8,288,128]{2,1,0:T(8,128)}, u32[]{:S(2)}, u32[]{:S(2)}) collective-permute-start(f32[8,288,128]{2,1,0:T(8,128)S(1)} %all_to_all.35), channel_id=1, source_target_pairs={{0,1},{1,0},{2,3},{3,2},{4,5},{5,4},{6,7},{7,6},{8,9},{9,8},{10,11... | collective-permute-start | bytes 3538952 | tf_op jit(solution)/shard_map/ppermute | solution.py:740
  305.4 10.3 %collective-permute-start.17 = (f32[8,288,128]{2,1,0:T(8,128)}, f32[8,288,128]{2,1,0:T(8,128)}, u32[]{:S(2)}, u32[]{:S(2)}) collective-permute-start(f32[8,288,128]{2,1,0:T(8,128)} %collective-permute-done.16), channel_id=1, source_target_pairs={{0,1},{1,0},{2,3},{3,2},{4,5},{5,4},{6,7},{7,6},{8,9},{9,8},{10,11... | collective-permute-start | bytes 3538952 | tf_op jit(solution)/shard_map/ppermute | solution.py:740
  309.3 7.3 %copy-start.3 = (f32[8,256,128]{2,1,0:T(8,128)}, f32[8,256,128]{2,1,0:T(8,128)S(1)}, u32[]{:S(2)}) copy-start(f32[8,256,128]{2,1,0:T(8,128)S(1)} %all-to-all-done.5) | copy-start | bytes 3145732
  309.3 23.8 %collective-permute-start.19 = (f32[8,256,128]{2,1,0:T(8,128)S(1)}, f32[8,256,128]{2,1,0:T(8,128)}, u32[]{:S(2)}, u32[]{:S(2)}) collective-permute-start(f32[8,256,128]{2,1,0:T(8,128)S(1)} %all-to-all-done.5), channel_id=1, source_target_pairs={{0,2},{1,3},{2,0},{3,1},{4,6},{5,7},{6,4},{7,5},{8,10},{9,11},{10,... | collective-permute-start | bytes 3145736 | tf_op jit(solution)/shard_map/ppermute | solution.py:740
  309.9 23.3 %collective-permute-start.18 = (f32[8,256,128]{2,1,0:T(8,128)S(1)}, f32[8,256,128]{2,1,0:T(8,128)}, u32[]{:S(2)}, u32[]{:S(2)}) collective-permute-start(f32[8,256,128]{2,1,0:T(8,128)S(1)} %all-to-all-done.5), channel_id=1, source_target_pairs={{0,1},{1,0},{2,3},{3,2},{4,5},{5,4},{6,7},{7,6},{8,9},{9,8},{10,11... | collective-permute-start | bytes 3145736 | tf_op jit(solution)/shard_map/ppermute | solution.py:740
  309.9 18.9 %all-to-all-start.6 = ((f32[8,128,128]{2,1,0:T(8,128)}), f32[8,128,128]{2,1,0:T(8,128)S(1)}, u32[]{:S(2)}, u32[]{:S(2)}) async-start(f32[8,128,128]{2,1,0:T(8,128)} %get-tuple-element.113), calls=%async_computation.6 | async-start | bytes 1048576 | tf_op jit(solution)/shard_map/all_to_all | solution.py:487
  328.7 6.9 %copy-start.5 = (f32[8,128,128]{2,1,0:T(8,128)}, f32[8,128,128]{2,1,0:T(8,128)S(1)}, u32[]{:S(2)}) copy-start(f32[8,128,128]{2,1,0:T(8,128)S(1)} %all-to-all-done.6) | copy-start | bytes 1572868
  333.1 12.8 %collective-permute-start.22 = (f32[8,128,128]{2,1,0:T(8,128)S(1)}, f32[8,128,128]{2,1,0:T(8,128)S(1)}, u32[]{:S(2)}, u32[]{:S(2)}) collective-permute-start(f32[8,128,128]{2,1,0:T(8,128)S(1)} %all-to-all-done.6), channel_id=1, source_target_pairs={{0,2},{1,3},{2,0},{3,1},{4,6},{5,7},{6,4},{7,5},{8,10},{9,11},{10,... | collective-permute-start | bytes 1572872 | tf_op jit(solution)/shard_map/ppermute | solution.py:740
  334.9 14.6 %collective-permute-start.20 = (f32[8,256,128]{2,1,0:T(8,128)}, f32[8,256,128]{2,1,0:T(8,128)S(1)}, u32[]{:S(2)}, u32[]{:S(2)}) collective-permute-start(f32[8,256,128]{2,1,0:T(8,128)} %collective-permute-done.19), channel_id=1, source_target_pairs={{0,1},{1,0},{2,3},{3,2},{4,5},{5,4},{6,7},{7,6},{8,9},{9,8},{10,11... | collective-permute-start | bytes 3145736 | tf_op jit(solution)/shard_map/ppermute | solution.py:740
  335.7 13.8 %collective-permute-start.21 = (f32[8,128,128]{2,1,0:T(8,128)S(1)}, f32[8,128,128]{2,1,0:T(8,128)}, u32[]{:S(2)}, u32[]{:S(2)}) collective-permute-start(f32[8,128,128]{2,1,0:T(8,128)S(1)} %all-to-all-done.6), channel_id=1, source_target_pairs={{0,1},{1,0},{2,3},{3,2},{4,5},{5,4},{6,7},{7,6},{8,9},{9,8},{10,11... | collective-permute-start | bytes 1572872 | tf_op jit(solution)/shard_map/ppermute | solution.py:740
  346.0 2.9 copy-start.16
  346.0 3.6 collective-permute-start.23
  349.5 1.0 copy-start.6

commit v6 on v5

--- a/solution.py
+++ b/solution.py
@@ -429,27 +429,31 @@
     values, packed, lines = 0.0, None, None
     for c, count in enumerate(counts):
         closing = c == len(counts) - 1
-        if c > 0:
-            if c == 1:
-                start, packed = lax.optimization_barrier((given_first, packed))
-                given.append(fill(parts[1:], start))
-            got_lines = exchanged(packed)
-            if c == 1:
-                behind = kept_first, got_lines, given[1][0]
-                start, got_lines, given[1][0] = lax.optimization_barrier(behind)
-                kept.append(fill(parts[1:], start))
+        if c == 1:
+            behind = (given_first, kept_first), packed
+            starts, packed = lax.optimization_barrier(behind)
+            given.append(fill(parts[1:], starts[0]))
+            kept.append(fill(parts[1:], starts[1]))
+            behind = given[1][0], kept[1][0]
+            given[1][0], kept[1][0] = lax.optimization_barrier(behind)
         if c < 2:
             got = lax.ppermute(given[c][0], "gy", swap(gy, 1))
             held = kept[c][0]
+        flanks = [piece[1:] for piece in given + kept]
+        if c > 1:
+            flanks, packed = lax.optimization_barrier((flanks, packed))
         if c > 0:
+            got_lines = exchanged(packed)
+            if c == 1:
+                held, got_lines = lax.optimization_barrier((held, got_lines))
             lines = sent_lines(got_lines, counts[c - 1], lines)
             values = values + first_axis(lines, table_parts[c - 1])
         if closing:
             given_rows = lax.dynamic_slice_in_dim(table, row * rows + given_first, pair_rows, 0)
             ordered_rows = [held_rows[part] for held_rows in (given_rows, kept_rows) for part in parts]
             ordered_rows = jnp.concatenate(ordered_rows, axis=0)
-            alternate = jnp.concatenate([piece[1] for piece in given + kept], axis=0) / math.sqrt(length)
-            edge = [piece[2][:, : piece[1].shape[0]] for piece in given + kept]
+            alternate = jnp.concatenate([piece[0] for piece in flanks], axis=0) / math.sqrt(length)
+            edge = [piece[1][:, : piece[0].shape[0]] for piece in flanks]
             edge = jnp.concatenate(edge, axis=1)
             edge = jnp.einsum("ba,bk->ak", edge / math.sqrt(length), table_cols, precision=HIGH)
             edge = edge + jnp.concatenate([alternate, edge[:, half:]], axis=1)

time: 381 us -> 399 us (1.047)
  waiting for transfers between devices: 122 us -> 145 us
    ppermute x9, waiting for transfers between devices: 30.8 us -> 48.3 us  [exchanged(): lax.ppermute(packed[p], 'gy', swap(gy, p))]
  transfers between devices with their start and end apart: 30 -> 30, of which waited for: 14 -> 17; matrix products, arithmetic and copies ran while one was open for 10% -> 9% of each run, Pallas kernels for 19% -> 8%
where the time goes in v6:
time: 399 us; the launch traced here: 398 us
  waiting for transfers between devices  145 us (36%)
  Pallas kernels  126 us (32%)
  starting transfers between devices  41.6 us (10%)
  local copies, waits for them, and re-layouts  33.4 us (8%)
  blocking collectives  32.5 us (8%)
  other arithmetic  13.4 us (3%)
  matrix products  5.31 us (1%)
    pallas_call x4, Pallas kernels, filled_spectrum(): pl.pallas_call(fill_kernel, grid_spec=pltpu.PrefetchScalarGridSpec(num_sc...  67.9 us
    ppermute x9, waiting for transfers between devices, exchanged(): lax.ppermute(packed[p], 'gy', swap(gy, p))  48.3 us
    ppermute x9, waiting for transfers between devices, gathered(): pieces[place ^ bit] = lax.ppermute(pieces[place], 'gy', swap(peers, bit))  35.7 us
    all_to_all x1, blocking collectives, on_device(): piece = lax.all_to_all(messages, 'gx', 0, 0, tiled=True)  32.5 us
    pallas_call x1, Pallas kernels, result_block(): pl.pallas_call(lambda *refs: result_kernel(offsets, own, devices, groups,...  29.2 us
    all_to_all x3, waiting for transfers between devices, sent_lines(): return lax.all_to_all(lines, 'gx', 0, 0, tiled=True)  25.4 us
    pallas_call x3, Pallas kernels, packed_section(): pl.pallas_call(lambda *refs: section_kernel(offsets, closing, *refs), gri...  19.7 us
    all_to_all x1, waiting for transfers between devices, on_device(): lax.all_to_all(jnp.concatenate(turned, axis=3), ('gy', 'gx'), 0, 0, tiled...  18.2 us
  transfers between devices with their start and end apart: 30, of which 17 were waited for; matrix products, arithmetic and copies ran while one was open for 9% of the time, Pallas kernels for 8%

profile of v6, /device:TPU:0, one launch (start us, length us, event | category | flops | bytes accessed | tf_op | source)
XLA Modules:
  0.0 397.8 jit_solution(1838981059400825788)
XLA Ops:
  0.0 1.8 fusion.33
  2.3 2.0 collective-permute-start.1
  4.3 3.6 shard_map.55.marks
  8.5 2.4 collective-permute-done.1
  11.2 1.6 pad.12.sides
  13.6 17.1 %shard_map.57 = (f32[16,128,256]{2,1,0:T(8,128)}, f32[16,256]{1,0:T(8,128)}, f32[128,128]{1,0:T(8,128)}) custom-call(s32[2]{0:T(128)} %get-tuple-element.188.base, f32[64,128,512]{2,1,0:T(8,128)} %below.7, f32[64,128,512]{2,1,0:T(8,128)} %below.7, f32[64,128,512]{2,1,0:T(8,128)} %below.7, f32[2,132,512]{2,1,0:T(8,128)} %broadcast_in_dim.10.top.bottom, ...), custom_call_target="tpu_custom_call" | custom-call | flops 1610612736 | bytes 6291456 | tf_op jit(solution)/shard_map/pallas_call | solution.py:253
  30.8 1.3 fusion.32
  33.5 2.3 collective-permute-start.3
  35.8 1.1 pad_maximum_fusion.1
  36.9 3.1 collective-permute-start.4
  41.3 0.9 constant_dynamic-slice_fusion.4
  42.9 17.1 %shard_map.56 = (f32[16,128,256]{2,1,0:T(8,128)}, f32[16,256]{1,0:T(8,128)}, f32[128,128]{1,0:T(8,128)}) custom-call(s32[2]{0:T(128)} %get-tuple-element.187.base, f32[64,128,512]{2,1,0:T(8,128)} %below.7, f32[64,128,512]{2,1,0:T(8,128)} %below.7, f32[64,128,512]{2,1,0:T(8,128)} %below.7, f32[2,132,512]{2,1,0:T(8,128)} %broadcast_in_dim.10.top.bottom, ...), custom_call_target="tpu_custom_call" | custom-call | flops 1610612736 | bytes 6291456 | tf_op jit(solution)/shard_map/pallas_call | solution.py:253
  60.0 0.9 copy.75.top
  61.0 1.7 collective-permute-done.4
  64.8 0.9 broadcast_in_dim.23.refs_10_
  65.8 8.1 %shard_map.58 = (f32[16,2,8,640]{3,2,1,0:T(8,128)}, f32[16,2,8,640]{3,2,1,0:T(8,128)}, f32[16,2,8,640]{3,2,1,0:T(8,128)}, f32[16,2,8,640]{3,2,1,0:T(8,128)}, f32[4,64,640]{2,1,0:T(8,128)}) custom-call(s32[1]{0:T(128)} %bitcast.3.refs_0_, f32[4,16]{1,0:T(4,128)} %pad_maximum_fusion.7.refs_1_, f32[16,128,256]{2,1,0:T(8,128)} %get-tuple-element.75.refs_2_, ...), custom_call_target="tpu_custom_call" | custom-call | flops 1610612736 | bytes 8388608 | tf_op jit(solution)/shard_map/pallas_call | solution.py:363
  75.0 16.8 %shard_map.60 = (f32[16,128,256]{2,1,0:T(8,128)}, f32[16,256]{1,0:T(8,128)}, f32[128,128]{1,0:T(8,128)}) custom-call(s32[2]{0:T(128)} %pad_add_fusion.4.base, f32[64,128,512]{2,1,0:T(8,128)} %below.7, f32[64,128,512]{2,1,0:T(8,128)} %below.7, f32[64,128,512]{2,1,0:T(8,128)} %below.7, f32[2,132,512]{2,1,0:T(8,128)} %copy.75.top, f32[2,132,512]{2,1,0:T(8,128)} %copy.76.bottom, ...), custom_call_target="tpu_custom_call" | custom-call | flops 1610612736 | bytes 6291456 | tf_op jit(solution)/shard_map/pallas_call | solution.py:253
  91.8 16.9 %shard_map.59 = (f32[16,128,256]{2,1,0:T(8,128)}, f32[16,256]{1,0:T(8,128)}, f32[128,128]{1,0:T(8,128)}) custom-call(s32[2]{0:T(128)} %pad_add_fusion.3.base, f32[64,128,512]{2,1,0:T(8,128)} %below.7, f32[64,128,512]{2,1,0:T(8,128)} %below.7, f32[64,128,512]{2,1,0:T(8,128)} %below.7, f32[2,132,512]{2,1,0:T(8,128)} %copy.75.top, f32[2,132,512]{2,1,0:T(8,128)} %copy.76.bottom, ...), custom_call_target="tpu_custom_call" | custom-call | flops 1610612736 | bytes 6291456 | tf_op jit(solution)/shard_map/pallas_call | solution.py:253
  109.2 1.5 collective-permute-start.6
  110.7 3.1 collective-permute-done.5
  113.8 13.3 %collective-permute-done.6 = f32[16,2,8,640]{3,2,1,0:T(8,128)} collective-permute-done((f32[16,2,8,640]{3,2,1,0:T(8,128)}, f32[16,2,8,640]{3,2,1,0:T(8,128)}, u32[]{:S(2)}, u32[]{:S(2)}) %collective-permute-start.6) | collective-permute-done | bytes 655392 | tf_op jit(solution)/shard_map/ppermute | solution.py:751
  127.1 12.3 %collective-permute-done.7 = f32[16,2,8,640]{3,2,1,0:T(8,128)} collective-permute-done((f32[16,2,8,640]{3,2,1,0:T(8,128)}, f32[16,2,8,640]{3,2,1,0:T(8,128)}, u32[]{:S(2)}, u32[]{:S(2)}) %collective-permute-start.7) | collective-permute-done | bytes 655392 | tf_op jit(solution)/shard_map/ppermute | solution.py:751
  139.4 1.2 add.178
  140.5 1.4 add.179
  142.0 1.7 copy.79
  143.7 4.5 %all-to-all-start = ((f32[8,2,32,640]{3,1,2,0:T(2,128)}), f32[8,2,32,640]{3,1,2,0:T(2,128)}, u32[]{:S(2)}, u32[]{:S(2)}) async-start(f32[8,2,32,640]{3,1,2,0:T(2,128)} %copy.79), calls=%async_computation | async-start | bytes 2621440 | tf_op jit(solution)/shard_map/all_to_all | solution.py:761
  149.2 1.2 concatenate.75
  152.5 1.3 copy-done
  153.9 5.6 %shard_map.61 = (f32[8,2,8,640]{3,2,1,0:T(8,128)}, f32[8,2,8,640]{3,2,1,0:T(8,128)}, f32[8,2,8,640]{3,2,1,0:T(8,128)}, f32[8,2,8,640]{3,2,1,0:T(8,128)}, f32[4,64,640]{2,1,0:T(8,128)}) custom-call(s32[1]{0:T(128)} %bitcast.3.refs_0_, f32[4,8]{1,0:T(4,128)} %pad_maximum_fusion.8.refs_1_, f32[16,128,256]{2,1,0:T(8,128)} %get-tuple-element.106.refs_2_, ...), custom_call_target="tpu_custom_call" | custom-call | flops 805306368 | bytes 4194304 | tf_op jit(solution)/shard_map/pallas_call | solution.py:363
  159.9 1.6 collective-permute-start.9
  162.6 0.9 fusion.13.refs_8_
  164.2 6.0 %shard_map.62 = (f32[13,2,8,640]{3,2,1,0:T(8,128)}, f32[13,2,8,640]{3,2,1,0:T(8,128)}, f32[13,2,8,640]{3,2,1,0:T(8,128)}, f32[13,2,8,640]{3,2,1,0:T(8,128)}, f32[4,64,640]{2,1,0:T(8,128)}) custom-call(s32[1]{0:T(128)} %bitcast.3.refs_0_, f32[4,8]{1,0:T(4,128)} %pad_maximum_fusion.9.refs_1_, f32[16,128,256]{2,1,0:T(8,128)} %get-tuple-element.106.refs_2_, ...), custom_call_target="tpu_custom_call" | custom-call | flops 805306368 | bytes 4194304 | tf_op jit(solution)/shard_map/pallas_call | solution.py:363
  170.2 1.5 collective-permute-start.12
  172.4 4.9 %collective-permute-done.11 = f32[8,2,8,640]{3,2,1,0:T(8,128)S(1)} collective-permute-done((f32[8,2,8,640]{3,2,1,0:T(8,128)}, f32[8,2,8,640]{3,2,1,0:T(8,128)S(1)}, u32[]{:S(2)}, u32[]{:S(2)}) %collective-permute-start.11) | collective-permute-done | bytes 327712 | tf_op jit(solution)/shard_map/ppermute | solution.py:751
  177.4 3.2 all-to-all-done
  180.5 1.2 copy.81
  181.7 3.6 all-to-all-start.1
  185.3 3.9 collective-permute-done.12
  189.2 10.8 %collective-permute-done.14 = f32[13,2,8,640]{3,2,1,0:T(8,128)S(1)} collective-permute-done((f32[13,2,8,640]{3,2,1,0:T(8,128)}, f32[13,2,8,640]{3,2,1,0:T(8,128)S(1)}, u32[]{:S(2)}, u32[]{:S(2)}) %collective-permute-start.14) | collective-permute-done | bytes 532512 | tf_op jit(solution)/shard_map/ppermute | solution.py:751
  200.3 2.6 all-to-all-done.1
  202.9 1.3 copy.83
  204.2 3.6 all-to-all-start.2
  208.0 2.1 convolution_bitcast_fusion
  210.1 19.7 %all-to-all-done.2 = f32[8,2,21,640]{3,1,2,0:T(2,128)S(1)} async-done(((f32[8,2,21,640]{3,1,2,0:T(2,128)}), f32[8,2,21,640]{3,1,2,0:T(2,128)S(1)}, u32[]{:S(2)}, u32[]{:S(2)}) %all-to-all-start.2) | async-done | bytes 860192 | tf_op jit(solution)/shard_map/all_to_all | solution.py:761
  231.4 1.0 copy.117
  232.6 2.4 concatenate.80
  235.0 3.9 all-to-all-start.3
  239.6 18.2 %all-to-all-done.3 = f32[32,2,2,1280]{3,2,1,0:T(2,128)S(1)} async-done(((f32[32,2,2,1280]{3,2,1,0:T(2,128)}), f32[32,2,2,1280]{3,2,1,0:T(2,128)S(1)}, u32[]{:S(2)}, u32[]{:S(2)}) %all-to-all-start.3) | async-done | bytes 655392 | tf_op jit(solution)/shard_map/all_to_all | solution.py:475
  257.8 1.0 copy.86
  258.7 5.5 %shard_map.63 = (f32[8,288,128]{2,1,0:T(8,128)}, f32[8,256,128]{2,1,0:T(8,128)}, f32[8,128,128]{2,1,0:T(8,128)}) custom-call(f32[2,256,640]{2,1,0:T(8,128)} %bitcast.164, f32[2,64,1280]{2,1,0:T(8,128)} %bitcast.173, f32[2,5,640]{2,1,0:T(8,128)} %copy_multiply_fusion.refs_2_), custom_call_target="tpu_custom_call" | custom-call | tf_op jit(solution)/shard_map/pallas_call | solution.py:610
  264.2 32.5 %all_to_all.35 = f32[8,288,128]{2,1,0:T(8,128)S(1)} all-to-all(f32[8,288,128]{2,1,0:T(8,128)} %get-tuple-element.133), channel_id=1, replica_groups=mesh['gx'=8,'gy'=4] {'gx'}, dimensions={0} | all-to-all | bytes 2359296 | tf_op jit(solution)/shard_map/all_to_all | solution.py:491
  296.7 1.2 collective-permute-start.16
  297.9 3.6 all-to-all-start.5
  301.6 21.4 %collective-permute-done.16 = f32[8,288,128]{2,1,0:T(8,128)} collective-permute-done((f32[8,288,128]{2,1,0:T(8,128)S(1)}, f32[8,288,128]{2,1,0:T(8,128)}, u32[]{:S(2)}, u32[]{:S(2)}) %collective-permute-start.16) | collective-permute-done | bytes 1179680 | tf_op jit(solution)/shard_map/ppermute | solution.py:744
  325.1 1.9 all-to-all-done.5
  327.5 4.0 %all-to-all-start.6 = ((f32[8,128,128]{2,1,0:T(8,128)}), f32[8,128,128]{2,1,0:T(8,128)S(1)}, u32[]{:S(2)}, u32[]{:S(2)}) async-start(f32[8,128,128]{2,1,0:T(8,128)} %get-tuple-element.141), calls=%async_computation.6 | async-start | bytes 1048576 | tf_op jit(solution)/shard_map/all_to_all | solution.py:491
  332.5 0.9 slice_bitcast_fusion.8
  333.4 0.9 slice_bitcast_fusion.2
  335.2 11.3 %all-to-all-done.6 = f32[8,128,128]{2,1,0:T(8,128)S(1)} async-done(((f32[8,128,128]{2,1,0:T(8,128)}), f32[8,128,128]{2,1,0:T(8,128)S(1)}, u32[]{:S(2)}, u32[]{:S(2)}) %all-to-all-start.6) | async-done | bytes 524320 | tf_op jit(solution)/shard_map/all_to_all | solution.py:491
  346.5 4.4 %collective-permute-done.19 = f32[8,256,128]{2,1,0:T(8,128)} collective-permute-done((f32[8,256,128]{2,1,0:T(8,128)S(1)}, f32[8,256,128]{2,1,0:T(8,128)}, u32[]{:S(2)}, u32[]{:S(2)}) %collective-permute-start.19) | collective-permute-done | bytes 1048608 | tf_op jit(solution)/shard_map/ppermute | solution.py:744
  350.9 1.7 collective-permute-start.22
  354.0 9.8 %collective-permute-done.22 = f32[8,128,128]{2,1,0:T(8,128)S(1)} collective-permute-done((f32[8,128,128]{2,1,0:T(8,128)S(1)}, f32[8,128,128]{2,1,0:T(8,128)S(1)}, u32[]{:S(2)}, u32[]{:S(2)}) %collective-permute-start.22) | collective-permute-done | bytes 524320 | tf_op jit(solution)/shard_map/ppermute | solution.py:744
  367.4 1.0 copy-done.6
  368.4 29.2 %shard_map.64 = f32[64,128,512]{2,1,0:T(8,128)} custom-call(s32[4]{0:T(128)} %pad_add_fusion.refs_0_, f32[64,640]{1,0:T(8,128)} %bitcast.179, f32[64,256]{1,0:T(8,128)} %slice.366.refs_2_, f32[128,128]{1,0:T(8,128)} %pad.14.refs_3_, bf16[128,256]{1,0:T(8,128)(2,1)} %fusion.15.refs_4_, bf16[256,256]{1,0:T(8,128)(2,1)} %fusion.7.refs_5_, ...), custom_call_target="tpu_custom_call" | custom-call | tf_op jit(solution)/shard_map/pallas_call | solution.py:715
  (160 shorter events, 27.7 us)
Async XLA Ops:
  1.8 6.7 %collective-permute-start = (f32[64,2,512]{2,1,0:T(2,128)S(1)}, f32[64,2,512]{2,1,0:T(2,128)S(1)}, u32[]{:S(2)}, u32[]{:S(2)}) collective-permute-start(f32[64,2,512]{2,1,0:T(2,128)S(1)} %get-tuple-element.147), channel_id=1, source_target_pairs={{0,1},{1,2},{2,3},{3,0},{4,5},{5,6},{6,7},{7,4},{8,9},{9,10},{10,1... | collective-permute-start | bytes 786440 | tf_op jit(solution)/shard_map/ppermute | solution.py:30
  2.3 8.6 %collective-permute-start.1 = (f32[64,2,512]{2,1,0:T(2,128)S(1)}, f32[64,2,512]{2,1,0:T(2,128)S(1)}, u32[]{:S(2)}, u32[]{:S(2)}) collective-permute-start(f32[64,2,512]{2,1,0:T(2,128)S(1)} %get-tuple-element.148), channel_id=1, source_target_pairs={{1,0},{2,1},{3,2},{0,3},{5,4},{6,5},{7,6},{4,7},{9,8},{10,9},{11,1... | collective-permute-start | bytes 786440 | tf_op jit(solution)/shard_map/ppermute | solution.py:31
  30.7 32.8 %collective-permute-start.2 = (f32[16,128,256]{2,1,0:T(8,128)}, f32[16,128,256]{2,1,0:T(8,128)}, u32[]{:S(2)}, u32[]{:S(2)}) collective-permute-start(f32[16,128,256]{2,1,0:T(8,128)} %get-tuple-element.79), channel_id=1, source_target_pairs={{0,1},{1,0},{2,3},{3,2},{4,5},{5,4},{6,7},{7,6},{8,9},{9,8},{10,11... | collective-permute-start | bytes 6291464 | tf_op jit(solution)/shard_map/ppermute | solution.py:440
  32.1 1.1 copy-start.4
  33.5 26.6 %collective-permute-start.3 = (f32[2,132,512]{2,0,1:T(2,128)S(1)}, f32[2,132,512]{2,0,1:T(2,128)S(1)}, u32[]{:S(2)}, u32[]{:S(2)}) collective-permute-start(f32[2,132,512]{2,0,1:T(2,128)S(1)} %pad_maximum_fusion), channel_id=1, source_target_pairs={{0,4},{4,8},{8,12},{12,16},{16,20},{20,24},{24,28},{28,0},{1,5},{5... | collective-permute-start | bytes 1622024 | tf_op jit(solution)/shard_map/ppermute | solution.py:40
  36.9 25.7 %collective-permute-start.4 = (f32[2,132,512]{2,0,1:T(2,128)}, f32[2,132,512]{2,0,1:T(2,128)S(1)}, u32[]{:S(2)}, u32[]{:S(2)}) collective-permute-start(f32[2,132,512]{2,0,1:T(2,128)} %pad_maximum_fusion.1), channel_id=1, source_target_pairs={{4,0},{8,4},{12,8},{16,12},{20,16},{24,20},{28,24},{0,28},{5,1},{9... | collective-permute-start | bytes 1622024 | tf_op jit(solution)/shard_map/ppermute | solution.py:40
  91.8 47.6 %copy-start.7 = (f32[16,2,8,640]{3,2,1,0:T(8,128)S(1)}, f32[16,2,8,640]{3,2,1,0:T(8,128)}, u32[]{:S(2)}) copy-start(f32[16,2,8,640]{3,2,1,0:T(8,128)} %get-tuple-element.94) | copy-start | bytes 1966084
  108.7 43.8 %collective-permute-start.8 = (f32[16,128,256]{2,1,0:T(8,128)}, f32[16,128,256]{2,1,0:T(8,128)S(1)}, u32[]{:S(2)}, u32[]{:S(2)}) collective-permute-start(f32[16,128,256]{2,1,0:T(8,128)} %get-tuple-element.107), channel_id=1, source_target_pairs={{0,1},{1,0},{2,3},{3,2},{4,5},{5,4},{6,7},{7,6},{8,9},{9,8},{10,11... | collective-permute-start | bytes 6291464 | tf_op jit(solution)/shard_map/ppermute | solution.py:440
  108.7 5.1 %collective-permute-start.5 = (f32[16,2,8,640]{3,2,1,0:T(8,128)}, f32[16,2,8,640]{3,2,1,0:T(8,128)}, u32[]{:S(2)}, u32[]{:S(2)}) collective-permute-start(f32[16,2,8,640]{3,2,1,0:T(8,128)} %get-tuple-element.91), channel_id=1, source_target_pairs={{0,1},{1,0},{2,3},{3,2},{4,5},{5,4},{6,7},{7,6},{8,9},{9,8},{10,11... | collective-permute-start | bytes 1966088 | tf_op jit(solution)/shard_map/ppermute | solution.py:751
  109.2 17.9 %collective-permute-start.6 = (f32[16,2,8,640]{3,2,1,0:T(8,128)}, f32[16,2,8,640]{3,2,1,0:T(8,128)}, u32[]{:S(2)}, u32[]{:S(2)}) collective-permute-start(f32[16,2,8,640]{3,2,1,0:T(8,128)} %get-tuple-element.92), channel_id=1, source_target_pairs={{0,2},{1,3},{2,0},{3,1},{4,6},{5,7},{6,4},{7,5},{8,10},{9,11},{10,... | collective-permute-start | bytes 1966088 | tf_op jit(solution)/shard_map/ppermute | solution.py:751
  110.7 28.7 %collective-permute-start.7 = (f32[16,2,8,640]{3,2,1,0:T(8,128)}, f32[16,2,8,640]{3,2,1,0:T(8,128)}, u32[]{:S(2)}, u32[]{:S(2)}) collective-permute-start(f32[16,2,8,640]{3,2,1,0:T(8,128)} %get-tuple-element.93), channel_id=1, source_target_pairs={{0,3},{1,2},{2,1},{3,0},{4,7},{5,6},{6,5},{7,4},{8,11},{9,10},{10,... | collective-permute-start | bytes 1966088 | tf_op jit(solution)/shard_map/ppermute | solution.py:751
  143.7 36.8 %all-to-all-start = ((f32[8,2,32,640]{3,1,2,0:T(2,128)}), f32[8,2,32,640]{3,1,2,0:T(2,128)}, u32[]{:S(2)}, u32[]{:S(2)}) async-start(f32[8,2,32,640]{3,1,2,0:T(2,128)} %copy.79), calls=%async_computation | async-start | bytes 2621440 | tf_op jit(solution)/shard_map/all_to_all | solution.py:761
  152.5 1.3 copy-start
  153.8 5.7 %copy-start.13 = (f32[128,128]{1,0:T(8,128)S(1)}, f32[128,128]{1,0:T(8,128)}, u32[]{:S(2)}) copy-start(f32[128,128]{1,0:T(8,128)} %get-tuple-element.118) | copy-start | bytes 196612
  153.8 5.7 %copy-start.14 = (f32[128,128]{1,0:T(8,128)S(1)}, f32[128,128]{1,0:T(8,128)}, u32[]{:S(2)}) copy-start(f32[128,128]{1,0:T(8,128)} %get-tuple-element.120) | copy-start | bytes 196612
  153.8 5.7 %copy-start.15 = (f32[128,128]{1,0:T(8,128)S(1)}, f32[128,128]{1,0:T(8,128)}, u32[]{:S(2)}) copy-start(f32[128,128]{1,0:T(8,128)} %get-tuple-element.121) | copy-start | bytes 196612
  153.8 5.7 %copy-start.16 = (f32[128,128]{1,0:T(8,128)S(1)}, f32[128,128]{1,0:T(8,128)}, u32[]{:S(2)}) copy-start(f32[128,128]{1,0:T(8,128)} %get-tuple-element.119) | copy-start | bytes 196612
  153.8 8.3 %copy-start.17 = (f32[16,256]{1,0:T(8,128)S(1)}, f32[16,256]{1,0:T(8,128)}, u32[]{:S(2)}) copy-start(f32[16,256]{1,0:T(8,128)} %get-tuple-element.122) | copy-start | bytes 49156
  153.8 8.3 %copy-start.18 = (f32[16,256]{1,0:T(8,128)S(1)}, f32[16,256]{1,0:T(8,128)}, u32[]{:S(2)}) copy-start(f32[16,256]{1,0:T(8,128)} %get-tuple-element.124) | copy-start | bytes 49156
  153.8 8.3 %copy-start.19 = (f32[16,256]{1,0:T(8,128)S(1)}, f32[16,256]{1,0:T(8,128)}, u32[]{:S(2)}) copy-start(f32[16,256]{1,0:T(8,128)} %get-tuple-element.125) | copy-start | bytes 49156
  153.8 8.3 %copy-start.20 = (f32[16,256]{1,0:T(8,128)S(1)}, f32[16,256]{1,0:T(8,128)}, u32[]{:S(2)}) copy-start(f32[16,256]{1,0:T(8,128)} %get-tuple-element.123) | copy-start | bytes 49156
  159.9 11.9 %collective-permute-start.9 = (f32[8,2,8,640]{3,2,1,0:T(8,128)}, f32[8,2,8,640]{3,2,1,0:T(8,128)S(1)}, u32[]{:S(2)}, u32[]{:S(2)}) collective-permute-start(f32[8,2,8,640]{3,2,1,0:T(8,128)} %get-tuple-element.114), channel_id=1, source_target_pairs={{0,2},{1,3},{2,0},{3,1},{4,6},{5,7},{6,4},{7,5},{8,10},{9,11},{10,... | collective-permute-start | bytes 983048 | tf_op jit(solution)/shard_map/ppermute | solution.py:751
  161.5 10.9 %collective-permute-start.10 = (f32[8,2,8,640]{3,2,1,0:T(8,128)}, f32[8,2,8,640]{3,2,1,0:T(8,128)S(1)}, u32[]{:S(2)}, u32[]{:S(2)}) collective-permute-start(f32[8,2,8,640]{3,2,1,0:T(8,128)} %get-tuple-element.115), channel_id=1, source_target_pairs={{0,1},{1,0},{2,3},{3,2},{4,5},{5,4},{6,7},{7,6},{8,9},{9,8},{10,11... | collective-permute-start | bytes 983048 | tf_op jit(solution)/shard_map/ppermute | solution.py:751
  161.9 15.4 %collective-permute-start.11 = (f32[8,2,8,640]{3,2,1,0:T(8,128)}, f32[8,2,8,640]{3,2,1,0:T(8,128)S(1)}, u32[]{:S(2)}, u32[]{:S(2)}) collective-permute-start(f32[8,2,8,640]{3,2,1,0:T(8,128)} %get-tuple-element.116), channel_id=1, source_target_pairs={{0,3},{1,2},{2,1},{3,0},{4,7},{5,6},{6,5},{7,4},{8,11},{9,10},{10,... | collective-permute-start | bytes 983048 | tf_op jit(solution)/shard_map/ppermute | solution.py:751
  164.2 8.1 %copy-start.12 = (f32[8,2,8,640]{3,2,1,0:T(8,128)S(1)}, f32[8,2,8,640]{3,2,1,0:T(8,128)}, u32[]{:S(2)}) copy-start(f32[8,2,8,640]{3,2,1,0:T(8,128)} %get-tuple-element.113) | copy-start | bytes 983044
  170.2 19.0 %collective-permute-start.12 = (f32[13,2,8,640]{3,2,1,0:T(8,128)}, f32[13,2,8,640]{3,2,1,0:T(8,128)S(1)}, u32[]{:S(2)}, u32[]{:S(2)}) collective-permute-start(f32[13,2,8,640]{3,2,1,0:T(8,128)} %get-tuple-element.128), channel_id=1, source_target_pairs={{0,2},{1,3},{2,0},{3,1},{4,6},{5,7},{6,4},{7,5},{8,10},{9,11},{10,... | collective-permute-start | bytes 1597448 | tf_op jit(solution)/shard_map/ppermute | solution.py:751
  171.7 17.6 %collective-permute-start.13 = (f32[13,2,8,640]{3,2,1,0:T(8,128)}, f32[13,2,8,640]{3,2,1,0:T(8,128)S(1)}, u32[]{:S(2)}, u32[]{:S(2)}) collective-permute-start(f32[13,2,8,640]{3,2,1,0:T(8,128)} %get-tuple-element.129), channel_id=1, source_target_pairs={{0,1},{1,0},{2,3},{3,2},{4,5},{5,4},{6,7},{7,6},{8,9},{9,8},{10,11... | collective-permute-start | bytes 1597448 | tf_op jit(solution)/shard_map/ppermute | solution.py:751
  171.8 28.3 %collective-permute-start.14 = (f32[13,2,8,640]{3,2,1,0:T(8,128)}, f32[13,2,8,640]{3,2,1,0:T(8,128)S(1)}, u32[]{:S(2)}, u32[]{:S(2)}) collective-permute-start(f32[13,2,8,640]{3,2,1,0:T(8,128)} %get-tuple-element.130), channel_id=1, source_target_pairs={{0,3},{1,2},{2,1},{3,0},{4,7},{5,6},{6,5},{7,4},{8,11},{9,10},{10,... | collective-permute-start | bytes 1597448 | tf_op jit(solution)/shard_map/ppermute | solution.py:751
  177.4 11.8 %copy-start.8 = (f32[13,2,8,640]{3,2,1,0:T(8,128)S(1)}, f32[13,2,8,640]{3,2,1,0:T(8,128)}, u32[]{:S(2)}) copy-start(f32[13,2,8,640]{3,2,1,0:T(8,128)} %get-tuple-element.127) | copy-start | bytes 1597444
  181.7 21.2 %all-to-all-start.1 = ((f32[8,2,16,640]{3,1,2,0:T(2,128)}), f32[8,2,16,640]{3,1,2,0:T(2,128)S(1)}, u32[]{:S(2)}, u32[]{:S(2)}) async-start(f32[8,2,16,640]{3,1,2,0:T(2,128)} %copy.81), calls=%async_computation.1 | async-start | bytes 1310720 | tf_op jit(solution)/shard_map/all_to_all | solution.py:761
  200.3 7.6 %copy-start.10 = (f32[8,2,32,256]{3,2,1,0:T(8,128)S(1)}, f32[8,2,32,256]{3,2,1,0:T(8,128)}, u32[]{:S(2)}) copy-start(f32[8,2,32,256]{3,2,1,0:T(8,128)} %constant.142) | copy-start | bytes 1572868
  200.3 7.6 %copy-start.11 = (f32[8,2,32,256]{3,2,1,0:T(8,128)S(1)}, f32[8,2,32,256]{3,2,1,0:T(8,128)}, u32[]{:S(2)}) copy-start(f32[8,2,32,256]{3,2,1,0:T(8,128)} %constant.140) | copy-start | bytes 1572868
  204.2 25.6 %all-to-all-start.2 = ((f32[8,2,21,640]{3,1,2,0:T(2,128)}), f32[8,2,21,640]{3,1,2,0:T(2,128)S(1)}, u32[]{:S(2)}, u32[]{:S(2)}) async-start(f32[8,2,21,640]{3,1,2,0:T(2,128)} %copy.83), calls=%async_computation.2 | async-start | bytes 1720320 | tf_op jit(solution)/shard_map/all_to_all | solution.py:761
  231.4 1.1 copy-start.2
  235.0 22.8 %all-to-all-start.3 = ((f32[32,2,2,1280]{3,2,1,0:T(2,128)}), f32[32,2,2,1280]{3,2,1,0:T(2,128)S(1)}, u32[]{:S(2)}, u32[]{:S(2)}) async-start(f32[32,2,2,1280]{3,2,1,0:T(2,128)} %concatenate.80), calls=%async_computation.3 | async-start | bytes 1310720 | tf_op jit(solution)/shard_map/all_to_all | solution.py:475
  296.7 30.9 %copy-start.1 = (f32[8,288,128]{2,1,0:T(8,128)}, f32[8,288,128]{2,1,0:T(8,128)S(1)}, u32[]{:S(2)}) copy-start(f32[8,288,128]{2,1,0:T(8,128)S(1)} %all_to_all.35) | copy-start | bytes 3538948
  296.7 26.4 %collective-permute-start.16 = (f32[8,288,128]{2,1,0:T(8,128)S(1)}, f32[8,288,128]{2,1,0:T(8,128)}, u32[]{:S(2)}, u32[]{:S(2)}) collective-permute-start(f32[8,288,128]{2,1,0:T(8,128)S(1)} %all_to_all.35), channel_id=1, source_target_pairs={{0,2},{1,3},{2,0},{3,1},{4,6},{5,7},{6,4},{7,5},{8,10},{9,11},{10,... | collective-permute-start | bytes 3538952 | tf_op jit(solution)/shard_map/ppermute | solution.py:744
  297.9 29.1 %all-to-all-start.5 = ((f32[8,256,128]{2,1,0:T(8,128)}), f32[8,256,128]{2,1,0:T(8,128)S(1)}, u32[]{:S(2)}, u32[]{:S(2)}) async-start(f32[8,256,128]{2,1,0:T(8,128)} %get-tuple-element.136), calls=%async_computation.5 | async-start | bytes 2097152 | tf_op jit(solution)/shard_map/all_to_all | solution.py:491
  301.4 25.6 %collective-permute-start.15 = (f32[8,288,128]{2,1,0:T(8,128)S(1)}, f32[8,288,128]{2,1,0:T(8,128)}, u32[]{:S(2)}, u32[]{:S(2)}) collective-permute-start(f32[8,288,128]{2,1,0:T(8,128)S(1)} %all_to_all.35), channel_id=1, source_target_pairs={{0,1},{1,0},{2,3},{3,2},{4,5},{5,4},{6,7},{7,6},{8,9},{9,8},{10,11... | collective-permute-start | bytes 3538952 | tf_op jit(solution)/shard_map/ppermute | solution.py:744
  323.0 10.4 %collective-permute-start.17 = (f32[8,288,128]{2,1,0:T(8,128)}, f32[8,288,128]{2,1,0:T(8,128)}, u32[]{:S(2)}, u32[]{:S(2)}) collective-permute-start(f32[8,288,128]{2,1,0:T(8,128)} %collective-permute-done.16), channel_id=1, source_target_pairs={{0,1},{1,0},{2,3},{3,2},{4,5},{5,4},{6,7},{7,6},{8,9},{9,8},{10,11... | collective-permute-start | bytes 3538952 | tf_op jit(solution)/shard_map/ppermute | solution.py:744
  327.0 7.4 %copy-start.3 = (f32[8,256,128]{2,1,0:T(8,128)}, f32[8,256,128]{2,1,0:T(8,128)S(1)}, u32[]{:S(2)}) copy-start(f32[8,256,128]{2,1,0:T(8,128)S(1)} %all-to-all-done.5) | copy-start | bytes 3145732
  327.0 23.9 %collective-permute-start.19 = (f32[8,256,128]{2,1,0:T(8,128)S(1)}, f32[8,256,128]{2,1,0:T(8,128)}, u32[]{:S(2)}, u32[]{:S(2)}) collective-permute-start(f32[8,256,128]{2,1,0:T(8,128)S(1)} %all-to-all-done.5), channel_id=1, source_target_pairs={{0,2},{1,3},{2,0},{3,1},{4,6},{5,7},{6,4},{7,5},{8,10},{9,11},{10,... | collective-permute-start | bytes 3145736 | tf_op jit(solution)/shard_map/ppermute | solution.py:744
  327.5 23.4 %collective-permute-start.18 = (f32[8,256,128]{2,1,0:T(8,128)S(1)}, f32[8,256,128]{2,1,0:T(8,128)}, u32[]{:S(2)}, u32[]{:S(2)}) collective-permute-start(f32[8,256,128]{2,1,0:T(8,128)S(1)} %all-to-all-done.5), channel_id=1, source_target_pairs={{0,1},{1,0},{2,3},{3,2},{4,5},{5,4},{6,7},{7,6},{8,9},{9,8},{10,11... | collective-permute-start | bytes 3145736 | tf_op jit(solution)/shard_map/ppermute | solution.py:744
  327.5 19.0 %all-to-all-start.6 = ((f32[8,128,128]{2,1,0:T(8,128)}), f32[8,128,128]{2,1,0:T(8,128)S(1)}, u32[]{:S(2)}, u32[]{:S(2)}) async-start(f32[8,128,128]{2,1,0:T(8,128)} %get-tuple-element.141), calls=%async_computation.6 | async-start | bytes 1048576 | tf_op jit(solution)/shard_map/all_to_all | solution.py:491
  346.5 6.9 %copy-start.5 = (f32[8,128,128]{2,1,0:T(8,128)}, f32[8,128,128]{2,1,0:T(8,128)S(1)}, u32[]{:S(2)}) copy-start(f32[8,128,128]{2,1,0:T(8,128)S(1)} %all-to-all-done.6) | copy-start | bytes 1572868
  350.9 12.9 %collective-permute-start.22 = (f32[8,128,128]{2,1,0:T(8,128)S(1)}, f32[8,128,128]{2,1,0:T(8,128)S(1)}, u32[]{:S(2)}, u32[]{:S(2)}) collective-permute-start(f32[8,128,128]{2,1,0:T(8,128)S(1)} %all-to-all-done.6), channel_id=1, source_target_pairs={{0,2},{1,3},{2,0},{3,1},{4,6},{5,7},{6,4},{7,5},{8,10},{9,11},{10,... | collective-permute-start | bytes 1572872 | tf_op jit(solution)/shard_map/ppermute | solution.py:744
  352.7 14.7 %collective-permute-start.20 = (f32[8,256,128]{2,1,0:T(8,128)}, f32[8,256,128]{2,1,0:T(8,128)S(1)}, u32[]{:S(2)}, u32[]{:S(2)}) collective-permute-start(f32[8,256,128]{2,1,0:T(8,128)} %collective-permute-done.19), channel_id=1, source_target_pairs={{0,1},{1,0},{2,3},{3,2},{4,5},{5,4},{6,7},{7,6},{8,9},{9,8},{10,11... | collective-permute-start | bytes 3145736 | tf_op jit(solution)/shard_map/ppermute | solution.py:744
  353.4 13.9 %collective-permute-start.21 = (f32[8,128,128]{2,1,0:T(8,128)S(1)}, f32[8,128,128]{2,1,0:T(8,128)}, u32[]{:S(2)}, u32[]{:S(2)}) collective-permute-start(f32[8,128,128]{2,1,0:T(8,128)S(1)} %all-to-all-done.6), channel_id=1, source_target_pairs={{0,1},{1,0},{2,3},{3,2},{4,5},{5,4},{6,7},{7,6},{8,9},{9,8},{10,11... | collective-permute-start | bytes 1572872 | tf_op jit(solution)/shard_map/ppermute | solution.py:744
  363.8 2.9 copy-start.9
  363.8 3.6 collective-permute-start.23
  367.4 1.0 copy-start.6

commit v7 on v6

--- a/solution.py
+++ b/solution.py
@@ -434,18 +434,18 @@
             starts, packed = lax.optimization_barrier(behind)
             given.append(fill(parts[1:], starts[0]))
             kept.append(fill(parts[1:], starts[1]))
-            behind = given[1][0], kept[1][0]
-            given[1][0], kept[1][0] = lax.optimization_barrier(behind)
-        if c < 2:
-            got = lax.ppermute(given[c][0], "gy", swap(gy, 1))
-            held = kept[c][0]
         flanks = [piece[1:] for piece in given + kept]
         if c > 1:
             flanks, packed = lax.optimization_barrier((flanks, packed))
         if c > 0:
             got_lines = exchanged(packed)
-            if c == 1:
-                held, got_lines = lax.optimization_barrier((held, got_lines))
+        if c == 1:
+            behind = given[1][0], kept[1][0], got_lines
+            given[1][0], kept[1][0], got_lines = lax.optimization_barrier(behind)
+        if c < 2:
+            got = lax.ppermute(given[c][0], "gy", swap(gy, 1))
+            held = kept[c][0]
+        if c > 0:
             lines = sent_lines(got_lines, counts[c - 1], lines)
             values = values + first_axis(lines, table_parts[c - 1])
         if closing:

time: 399 us -> 369 us (0.925)
  waiting for transfers between devices: 145 us -> 114 us
    ppermute x9, waiting for transfers between devices: 48.3 us -> 19.2 us  [exchanged(): lax.ppermute(packed[p], 'gy', swap(gy, p))]
  transfers between devices with their start and end apart: 30 -> 30, of which waited for: 17 -> 13; matrix products, arithmetic and copies ran while one was open for 9% -> 10% of each run, Pallas kernels for 8% -> 20%
where the time goes in v7:
time: 369 us; the launch traced here: 368 us
  Pallas kernels  126 us (34%)
  waiting for transfers between devices  114 us (31%)
  starting transfers between devices  42.5 us (12%)
  local copies, waits for them, and re-layouts  34.9 us (9%)
  blocking collectives  32.5 us (9%)
  other arithmetic  11.6 us (3%)
  matrix products  5.32 us (1%)
    pallas_call x4, Pallas kernels, filled_spectrum(): pl.pallas_call(fill_kernel, grid_spec=pltpu.PrefetchScalarGridSpec(num_sc...  67.8 us
    ppermute x9, waiting for transfers between devices, gathered(): pieces[place ^ bit] = lax.ppermute(pieces[place], 'gy', swap(peers, bit))  35.6 us
    all_to_all x1, blocking collectives, on_device(): piece = lax.all_to_all(messages, 'gx', 0, 0, tiled=True)  32.5 us
    pallas_call x1, Pallas kernels, result_block(): pl.pallas_call(lambda *refs: result_kernel(offsets, own, devices, groups,...  29.2 us
    all_to_all x3, waiting for transfers between devices, sent_lines(): return lax.all_to_all(lines, 'gx', 0, 0, tiled=True)  25.3 us
    pallas_call x3, Pallas kernels, packed_section(): pl.pallas_call(lambda *refs: section_kernel(offsets, closing, *refs), gri...  19.8 us
    ppermute x9, waiting for transfers between devices, exchanged(): lax.ppermute(packed[p], 'gy', swap(gy, p))  19.2 us
    all_to_all x1, waiting for transfers between devices, on_device(): lax.all_to_all(jnp.concatenate(turned, axis=3), ('gy', 'gx'), 0, 0, tiled...  18.2 us
  transfers between devices with their start and end apart: 30, of which 13 were waited for; matrix products, arithmetic and copies ran while one was open for 10% of the time, Pallas kernels for 20%

profile of v7, /device:TPU:0, one launch (start us, length us, event | category | flops | bytes accessed | tf_op | source)
XLA Modules:
  0.0 367.5 jit_solution(569748314724837835)
XLA Ops:
  0.0 1.8 fusion.33
  2.3 2.0 collective-permute-start.1
  4.3 3.5 shard_map.55.marks
  8.5 2.4 collective-permute-done.1
  11.2 1.6 pad.12.sides
  12.8 0.9 broadcast_in_dim.10.top.bottom
  13.6 17.0 %shard_map.57 = (f32[16,128,256]{2,1,0:T(8,128)}, f32[16,256]{1,0:T(8,128)}, f32[128,128]{1,0:T(8,128)}) custom-call(s32[2]{0:T(128)} %get-tuple-element.186.base, f32[64,128,512]{2,1,0:T(8,128)} %below.7, f32[64,128,512]{2,1,0:T(8,128)} %below.7, f32[64,128,512]{2,1,0:T(8,128)} %below.7, f32[2,132,512]{2,1,0:T(8,128)} %broadcast_in_dim.10.top.bottom, ...), custom_call_target="tpu_custom_call" | custom-call | flops 1610612736 | bytes 6291456 | tf_op jit(solution)/shard_map/pallas_call | solution.py:253
  30.9 1.3 fusion.32
  34.0 0.9 constant_dynamic-slice_fusion.4
  36.0 2.3 collective-permute-start.3
  38.6 3.3 collective-permute-start.4
  42.4 17.2 %shard_map.56 = (f32[16,128,256]{2,1,0:T(8,128)}, f32[16,256]{1,0:T(8,128)}, f32[128,128]{1,0:T(8,128)}) custom-call(s32[2]{0:T(128)} %get-tuple-element.185.base, f32[64,128,512]{2,1,0:T(8,128)} %below.7, f32[64,128,512]{2,1,0:T(8,128)} %below.7, f32[64,128,512]{2,1,0:T(8,128)} %below.7, f32[2,132,512]{2,1,0:T(8,128)} %broadcast_in_dim.10.top.bottom, ...), custom_call_target="tpu_custom_call" | custom-call | flops 1610612736 | bytes 6291456 | tf_op jit(solution)/shard_map/pallas_call | solution.py:253
  60.9 0.9 broadcast_in_dim.23.refs_10_
  61.9 8.1 %shard_map.58 = (f32[16,2,8,640]{3,2,1,0:T(8,128)}, f32[16,2,8,640]{3,2,1,0:T(8,128)}, f32[16,2,8,640]{3,2,1,0:T(8,128)}, f32[16,2,8,640]{3,2,1,0:T(8,128)}, f32[4,64,640]{2,1,0:T(8,128)}) custom-call(s32[1]{0:T(128)} %bitcast.3.refs_0_, f32[4,16]{1,0:T(4,128)} %pad_maximum_fusion.7.refs_1_, f32[16,128,256]{2,1,0:T(8,128)} %get-tuple-element.74.refs_2_, ...), custom_call_target="tpu_custom_call" | custom-call | flops 1610612736 | bytes 8388608 | tf_op jit(solution)/shard_map/pallas_call | solution.py:363
  70.0 1.9 collective-permute-start.6
  72.0 1.0 copy.75.top
  73.0 0.9 copy.76.bottom
  75.2 16.8 %shard_map.60 = (f32[16,128,256]{2,1,0:T(8,128)}, f32[16,256]{1,0:T(8,128)}, f32[128,128]{1,0:T(8,128)}) custom-call(s32[2]{0:T(128)} %pad_add_fusion.4.base, f32[64,128,512]{2,1,0:T(8,128)} %below.7, f32[64,128,512]{2,1,0:T(8,128)} %below.7, f32[64,128,512]{2,1,0:T(8,128)} %below.7, f32[2,132,512]{2,1,0:T(8,128)} %copy.75.top, f32[2,132,512]{2,1,0:T(8,128)} %copy.76.bottom, ...), custom_call_target="tpu_custom_call" | custom-call | flops 1610612736 | bytes 6291456 | tf_op jit(solution)/shard_map/pallas_call | solution.py:253
  91.9 16.9 %shard_map.59 = (f32[16,128,256]{2,1,0:T(8,128)}, f32[16,256]{1,0:T(8,128)}, f32[128,128]{1,0:T(8,128)}) custom-call(s32[2]{0:T(128)} %pad_add_fusion.3.base, f32[64,128,512]{2,1,0:T(8,128)} %below.7, f32[64,128,512]{2,1,0:T(8,128)} %below.7, f32[64,128,512]{2,1,0:T(8,128)} %below.7, f32[2,132,512]{2,1,0:T(8,128)} %copy.75.top, f32[2,132,512]{2,1,0:T(8,128)} %copy.76.bottom, ...), custom_call_target="tpu_custom_call" | custom-call | flops 1610612736 | bytes 6291456 | tf_op jit(solution)/shard_map/pallas_call | solution.py:253
  110.3 1.3 add.178
  112.0 1.7 copy.79
  113.7 4.5 %all-to-all-start = ((f32[8,2,32,640]{3,1,2,0:T(2,128)}), f32[8,2,32,640]{3,1,2,0:T(2,128)}, u32[]{:S(2)}, u32[]{:S(2)}) async-start(f32[8,2,32,640]{3,1,2,0:T(2,128)} %copy.79), calls=%async_computation | async-start | bytes 2621440 | tf_op jit(solution)/shard_map/all_to_all | solution.py:761
  118.2 0.8 constant_dynamic-slice_fusion.2
  119.2 1.2 concatenate.75
  121.7 0.8 fusion.11
  122.5 1.3 copy-done
  123.9 5.6 %shard_map.61 = (f32[8,2,8,640]{3,2,1,0:T(8,128)}, f32[8,2,8,640]{3,2,1,0:T(8,128)}, f32[8,2,8,640]{3,2,1,0:T(8,128)}, f32[8,2,8,640]{3,2,1,0:T(8,128)}, f32[4,64,640]{2,1,0:T(8,128)}) custom-call(s32[1]{0:T(128)} %bitcast.3.refs_0_, f32[4,8]{1,0:T(4,128)} %pad_maximum_fusion.8.refs_1_, f32[16,128,256]{2,1,0:T(8,128)} %get-tuple-element.104.refs_2_, ...), custom_call_target="tpu_custom_call" | custom-call | flops 805306368 | bytes 4194304 | tf_op jit(solution)/shard_map/pallas_call | solution.py:363
  129.9 1.9 collective-permute-start.9
  132.6 1.0 fusion.13.refs_8_
  134.2 6.0 %shard_map.62 = (f32[13,2,8,640]{3,2,1,0:T(8,128)}, f32[13,2,8,640]{3,2,1,0:T(8,128)}, f32[13,2,8,640]{3,2,1,0:T(8,128)}, f32[13,2,8,640]{3,2,1,0:T(8,128)}, f32[4,64,640]{2,1,0:T(8,128)}) custom-call(s32[1]{0:T(128)} %bitcast.3.refs_0_, f32[4,8]{1,0:T(4,128)} %pad_maximum_fusion.9.refs_1_, f32[16,128,256]{2,1,0:T(8,128)} %get-tuple-element.104.refs_2_, ...), custom_call_target="tpu_custom_call" | custom-call | flops 805306368 | bytes 4194304 | tf_op jit(solution)/shard_map/pallas_call | solution.py:363
  140.2 1.9 collective-permute-start.12
  142.4 4.8 %collective-permute-done.11 = f32[8,2,8,640]{3,2,1,0:T(8,128)S(1)} collective-permute-done((f32[8,2,8,640]{3,2,1,0:T(8,128)}, f32[8,2,8,640]{3,2,1,0:T(8,128)S(1)}, u32[]{:S(2)}, u32[]{:S(2)}) %collective-permute-start.11) | collective-permute-done | bytes 327712 | tf_op jit(solution)/shard_map/ppermute | solution.py:751
  147.3 2.8 all-to-all-done
  150.1 1.2 copy.81
  151.3 3.6 all-to-all-start.1
  154.9 4.3 %collective-permute-done.12 = f32[13,2,8,640]{3,2,1,0:T(8,128)S(1)} collective-permute-done((f32[13,2,8,640]{3,2,1,0:T(8,128)}, f32[13,2,8,640]{3,2,1,0:T(8,128)S(1)}, u32[]{:S(2)}, u32[]{:S(2)}) %collective-permute-start.12) | collective-permute-done | bytes 532512 | tf_op jit(solution)/shard_map/ppermute | solution.py:751
  159.2 10.1 %collective-permute-done.14 = f32[13,2,8,640]{3,2,1,0:T(8,128)S(1)} collective-permute-done((f32[13,2,8,640]{3,2,1,0:T(8,128)}, f32[13,2,8,640]{3,2,1,0:T(8,128)S(1)}, u32[]{:S(2)}, u32[]{:S(2)}) %collective-permute-start.14) | collective-permute-done | bytes 532512 | tf_op jit(solution)/shard_map/ppermute | solution.py:751
  169.5 2.9 all-to-all-done.1
  172.4 1.3 copy.83
  173.8 3.6 all-to-all-start.2
  177.5 2.1 convolution_bitcast_fusion
  179.7 19.7 %all-to-all-done.2 = f32[8,2,21,640]{3,1,2,0:T(2,128)S(1)} async-done(((f32[8,2,21,640]{3,1,2,0:T(2,128)}), f32[8,2,21,640]{3,1,2,0:T(2,128)S(1)}, u32[]{:S(2)}, u32[]{:S(2)}) %all-to-all-start.2) | async-done | bytes 860192 | tf_op jit(solution)/shard_map/all_to_all | solution.py:761
  200.1 0.8 fusion.1
  200.9 1.0 copy.117
  202.2 2.4 concatenate.80
  204.6 4.2 %all-to-all-start.3 = ((f32[32,2,2,1280]{3,2,1,0:T(2,128)}), f32[32,2,2,1280]{3,2,1,0:T(2,128)S(1)}, u32[]{:S(2)}, u32[]{:S(2)}) async-start(f32[32,2,2,1280]{3,2,1,0:T(2,128)} %concatenate.80), calls=%async_computation.3 | async-start | bytes 1310720 | tf_op jit(solution)/shard_map/all_to_all | solution.py:475
  209.5 18.2 %all-to-all-done.3 = f32[32,2,2,1280]{3,2,1,0:T(2,128)S(1)} async-done(((f32[32,2,2,1280]{3,2,1,0:T(2,128)}), f32[32,2,2,1280]{3,2,1,0:T(2,128)S(1)}, u32[]{:S(2)}, u32[]{:S(2)}) %all-to-all-start.3) | async-done | bytes 655392 | tf_op jit(solution)/shard_map/all_to_all | solution.py:475
  227.7 1.0 copy.86
  228.7 5.5 %shard_map.63 = (f32[8,288,128]{2,1,0:T(8,128)}, f32[8,256,128]{2,1,0:T(8,128)}, f32[8,128,128]{2,1,0:T(8,128)}) custom-call(f32[2,256,640]{2,1,0:T(8,128)} %bitcast.164, f32[2,64,1280]{2,1,0:T(8,128)} %bitcast.173, f32[2,5,640]{2,1,0:T(8,128)} %copy_multiply_fusion.refs_2_), custom_call_target="tpu_custom_call" | custom-call | tf_op jit(solution)/shard_map/pallas_call | solution.py:610
  234.1 32.5 %all_to_all.35 = f32[8,288,128]{2,1,0:T(8,128)S(1)} all-to-all(f32[8,288,128]{2,1,0:T(8,128)} %get-tuple-element.131), channel_id=1, replica_groups=mesh['gx'=8,'gy'=4] {'gx'}, dimensions={0} | all-to-all | bytes 2359296 | tf_op jit(solution)/shard_map/all_to_all | solution.py:491
  266.6 1.2 collective-permute-start.16
  267.8 3.6 all-to-all-start.5
  271.5 21.4 %collective-permute-done.16 = f32[8,288,128]{2,1,0:T(8,128)} collective-permute-done((f32[8,288,128]{2,1,0:T(8,128)S(1)}, f32[8,288,128]{2,1,0:T(8,128)}, u32[]{:S(2)}, u32[]{:S(2)}) %collective-permute-start.16) | collective-permute-done | bytes 1179680 | tf_op jit(solution)/shard_map/ppermute | solution.py:744
  295.0 1.9 all-to-all-done.5
  297.5 4.0 %all-to-all-start.6 = ((f32[8,128,128]{2,1,0:T(8,128)}), f32[8,128,128]{2,1,0:T(8,128)S(1)}, u32[]{:S(2)}, u32[]{:S(2)}) async-start(f32[8,128,128]{2,1,0:T(8,128)} %get-tuple-element.139), calls=%async_computation.6 | async-start | bytes 1048576 | tf_op jit(solution)/shard_map/all_to_all | solution.py:491
  301.4 0.9 slice_bitcast_fusion.9
  302.4 0.9 slice_bitcast_fusion.8
  303.3 0.9 slice_bitcast_fusion.2
  305.0 11.3 %all-to-all-done.6 = f32[8,128,128]{2,1,0:T(8,128)S(1)} async-done(((f32[8,128,128]{2,1,0:T(8,128)}), f32[8,128,128]{2,1,0:T(8,128)S(1)}, u32[]{:S(2)}, u32[]{:S(2)}) %all-to-all-start.6) | async-done | bytes 524320 | tf_op jit(solution)/shard_map/all_to_all | solution.py:491
  316.4 4.4 %collective-permute-done.19 = f32[8,256,128]{2,1,0:T(8,128)} collective-permute-done((f32[8,256,128]{2,1,0:T(8,128)S(1)}, f32[8,256,128]{2,1,0:T(8,128)}, u32[]{:S(2)}, u32[]{:S(2)}) %collective-permute-start.19) | collective-permute-done | bytes 1048608 | tf_op jit(solution)/shard_map/ppermute | solution.py:744
  320.8 1.7 collective-permute-start.22
  323.9 9.7 %collective-permute-done.22 = f32[8,128,128]{2,1,0:T(8,128)S(1)} collective-permute-done((f32[8,128,128]{2,1,0:T(8,128)S(1)}, f32[8,128,128]{2,1,0:T(8,128)S(1)}, u32[]{:S(2)}, u32[]{:S(2)}) %collective-permute-start.22) | collective-permute-done | bytes 524320 | tf_op jit(solution)/shard_map/ppermute | solution.py:744
  337.2 1.0 copy-done.6
  338.2 29.2 %shard_map.64 = f32[64,128,512]{2,1,0:T(8,128)} custom-call(s32[4]{0:T(128)} %pad_add_fusion.refs_0_, f32[64,640]{1,0:T(8,128)} %bitcast.179, f32[64,256]{1,0:T(8,128)} %slice.366.refs_2_, f32[128,128]{1,0:T(8,128)} %pad.14.refs_3_, bf16[128,256]{1,0:T(8,128)(2,1)} %fusion.15.refs_4_, bf16[256,256]{1,0:T(8,128)(2,1)} %fusion.7.refs_5_, ...), custom_call_target="tpu_custom_call" | custom-call | tf_op jit(solution)/shard_map/pallas_call | solution.py:715
  (170 shorter events, 23.7 us)
Async XLA Ops:
  1.8 6.7 %collective-permute-start = (f32[64,2,512]{2,1,0:T(2,128)S(1)}, f32[64,2,512]{2,1,0:T(2,128)S(1)}, u32[]{:S(2)}, u32[]{:S(2)}) collective-permute-start(f32[64,2,512]{2,1,0:T(2,128)S(1)} %get-tuple-element.145), channel_id=1, source_target_pairs={{0,1},{1,2},{2,3},{3,0},{4,5},{5,6},{6,7},{7,4},{8,9},{9,10},{10,1... | collective-permute-start | bytes 786440 | tf_op jit(solution)/shard_map/ppermute | solution.py:30
  2.3 8.6 %collective-permute-start.1 = (f32[64,2,512]{2,1,0:T(2,128)S(1)}, f32[64,2,512]{2,1,0:T(2,128)S(1)}, u32[]{:S(2)}, u32[]{:S(2)}) collective-permute-start(f32[64,2,512]{2,1,0:T(2,128)S(1)} %get-tuple-element.146), channel_id=1, source_target_pairs={{1,0},{2,1},{3,2},{0,3},{5,4},{6,5},{7,6},{4,7},{9,8},{10,9},{11,1... | collective-permute-start | bytes 786440 | tf_op jit(solution)/shard_map/ppermute | solution.py:31
  30.7 28.9 %collective-permute-start.2 = (f32[16,128,256]{2,1,0:T(8,128)}, f32[16,128,256]{2,1,0:T(8,128)}, u32[]{:S(2)}, u32[]{:S(2)}) collective-permute-start(f32[16,128,256]{2,1,0:T(8,128)} %get-tuple-element.78), channel_id=1, source_target_pairs={{0,1},{1,0},{2,3},{3,2},{4,5},{5,4},{6,7},{7,6},{8,9},{9,8},{10,11... | collective-permute-start | bytes 6291464 | tf_op jit(solution)/shard_map/ppermute | solution.py:446
  32.2 1.1 copy-start.4
  36.0 36.0 %collective-permute-start.3 = (f32[2,132,512]{2,0,1:T(2,128)S(1)}, f32[2,132,512]{2,0,1:T(2,128)S(1)}, u32[]{:S(2)}, u32[]{:S(2)}) collective-permute-start(f32[2,132,512]{2,0,1:T(2,128)S(1)} %pad_maximum_fusion), channel_id=1, source_target_pairs={{0,4},{4,8},{8,12},{12,16},{16,20},{20,24},{24,28},{28,0},{1,5},{5... | collective-permute-start | bytes 1622024 | tf_op jit(solution)/shard_map/ppermute | solution.py:40
  38.6 34.4 %collective-permute-start.4 = (f32[2,132,512]{2,0,1:T(2,128)S(1)}, f32[2,132,512]{2,0,1:T(2,128)S(1)}, u32[]{:S(2)}, u32[]{:S(2)}) collective-permute-start(f32[2,132,512]{2,0,1:T(2,128)S(1)} %pad_maximum_fusion.1), channel_id=1, source_target_pairs={{4,0},{8,4},{12,8},{16,12},{20,16},{24,20},{28,24},{0,28},{5,1},{9... | collective-permute-start | bytes 1622024 | tf_op jit(solution)/shard_map/ppermute | solution.py:40
  70.0 38.8 %collective-permute-start.5 = (f32[16,2,8,640]{3,2,1,0:T(8,128)}, f32[16,2,8,640]{3,2,1,0:T(8,128)S(1)}, u32[]{:S(2)}, u32[]{:S(2)}) collective-permute-start(f32[16,2,8,640]{3,2,1,0:T(8,128)} %get-tuple-element.89), channel_id=1, source_target_pairs={{0,1},{1,0},{2,3},{3,2},{4,5},{5,4},{6,7},{7,6},{8,9},{9,8},{10,11... | collective-permute-start | bytes 1966088 | tf_op jit(solution)/shard_map/ppermute | solution.py:751
  70.0 38.8 %collective-permute-start.6 = (f32[16,2,8,640]{3,2,1,0:T(8,128)}, f32[16,2,8,640]{3,2,1,0:T(8,128)S(1)}, u32[]{:S(2)}, u32[]{:S(2)}) collective-permute-start(f32[16,2,8,640]{3,2,1,0:T(8,128)} %get-tuple-element.90), channel_id=1, source_target_pairs={{0,2},{1,3},{2,0},{3,1},{4,6},{5,7},{6,4},{7,5},{8,10},{9,11},{10,... | collective-permute-start | bytes 1966088 | tf_op jit(solution)/shard_map/ppermute | solution.py:751
  71.9 36.9 %collective-permute-start.7 = (f32[16,2,8,640]{3,2,1,0:T(8,128)}, f32[16,2,8,640]{3,2,1,0:T(8,128)S(1)}, u32[]{:S(2)}, u32[]{:S(2)}) collective-permute-start(f32[16,2,8,640]{3,2,1,0:T(8,128)} %get-tuple-element.91), channel_id=1, source_target_pairs={{0,3},{1,2},{2,1},{3,0},{4,7},{5,6},{6,5},{7,4},{8,11},{9,10},{10,... | collective-permute-start | bytes 1966088 | tf_op jit(solution)/shard_map/ppermute | solution.py:751
  91.9 18.4 %copy-start.7 = (f32[16,2,8,640]{3,2,1,0:T(8,128)S(1)}, f32[16,2,8,640]{3,2,1,0:T(8,128)}, u32[]{:S(2)}) copy-start(f32[16,2,8,640]{3,2,1,0:T(8,128)} %get-tuple-element.92) | copy-start | bytes 1966084
  108.8 0.8 copy-start.8
  108.8 1.1 copy-start.10
  108.9 1.2 copy-start.11
  110.1 12.4 %collective-permute-start.8 = (f32[16,128,256]{2,1,0:T(8,128)}, f32[16,128,256]{2,1,0:T(8,128)S(1)}, u32[]{:S(2)}, u32[]{:S(2)}) collective-permute-start(f32[16,128,256]{2,1,0:T(8,128)} %get-tuple-element.105), channel_id=1, source_target_pairs={{0,1},{1,0},{2,3},{3,2},{4,5},{5,4},{6,7},{7,6},{8,9},{9,8},{10,11... | collective-permute-start | bytes 6291464 | tf_op jit(solution)/shard_map/ppermute | solution.py:446
  110.3 1.3 copy-start.9
  110.3 1.5 copy-start.12
  113.7 36.4 %all-to-all-start = ((f32[8,2,32,640]{3,1,2,0:T(2,128)}), f32[8,2,32,640]{3,1,2,0:T(2,128)}, u32[]{:S(2)}, u32[]{:S(2)}) async-start(f32[8,2,32,640]{3,1,2,0:T(2,128)} %copy.79), calls=%async_computation | async-start | bytes 2621440 | tf_op jit(solution)/shard_map/all_to_all | solution.py:761
  122.5 1.3 copy-start
  123.8 5.7 %copy-start.18 = (f32[128,128]{1,0:T(8,128)S(1)}, f32[128,128]{1,0:T(8,128)}, u32[]{:S(2)}) copy-start(f32[128,128]{1,0:T(8,128)} %get-tuple-element.116) | copy-start | bytes 196612
  123.8 5.7 %copy-start.19 = (f32[128,128]{1,0:T(8,128)S(1)}, f32[128,128]{1,0:T(8,128)}, u32[]{:S(2)}) copy-start(f32[128,128]{1,0:T(8,128)} %get-tuple-element.118) | copy-start | bytes 196612
  123.8 5.7 %copy-start.20 = (f32[128,128]{1,0:T(8,128)S(1)}, f32[128,128]{1,0:T(8,128)}, u32[]{:S(2)}) copy-start(f32[128,128]{1,0:T(8,128)} %get-tuple-element.119) | copy-start | bytes 196612
  123.8 5.7 %copy-start.21 = (f32[128,128]{1,0:T(8,128)S(1)}, f32[128,128]{1,0:T(8,128)}, u32[]{:S(2)}) copy-start(f32[128,128]{1,0:T(8,128)} %get-tuple-element.117) | copy-start | bytes 196612
  123.8 8.3 %copy-start.22 = (f32[16,256]{1,0:T(8,128)S(1)}, f32[16,256]{1,0:T(8,128)}, u32[]{:S(2)}) copy-start(f32[16,256]{1,0:T(8,128)} %get-tuple-element.120) | copy-start | bytes 49156
  123.8 8.3 %copy-start.23 = (f32[16,256]{1,0:T(8,128)S(1)}, f32[16,256]{1,0:T(8,128)}, u32[]{:S(2)}) copy-start(f32[16,256]{1,0:T(8,128)} %get-tuple-element.122) | copy-start | bytes 49156
  123.9 8.3 %copy-start.24 = (f32[16,256]{1,0:T(8,128)S(1)}, f32[16,256]{1,0:T(8,128)}, u32[]{:S(2)}) copy-start(f32[16,256]{1,0:T(8,128)} %get-tuple-element.123) | copy-start | bytes 49156
  123.9 8.2 %copy-start.25 = (f32[16,256]{1,0:T(8,128)S(1)}, f32[16,256]{1,0:T(8,128)}, u32[]{:S(2)}) copy-start(f32[16,256]{1,0:T(8,128)} %get-tuple-element.121) | copy-start | bytes 49156
  129.9 12.2 %collective-permute-start.9 = (f32[8,2,8,640]{3,2,1,0:T(8,128)}, f32[8,2,8,640]{3,2,1,0:T(8,128)S(1)}, u32[]{:S(2)}, u32[]{:S(2)}) collective-permute-start(f32[8,2,8,640]{3,2,1,0:T(8,128)} %get-tuple-element.112), channel_id=1, source_target_pairs={{0,2},{1,3},{2,0},{3,1},{4,6},{5,7},{6,4},{7,5},{8,10},{9,11},{10,... | collective-permute-start | bytes 983048 | tf_op jit(solution)/shard_map/ppermute | solution.py:751
  131.8 10.6 %collective-permute-start.10 = (f32[8,2,8,640]{3,2,1,0:T(8,128)}, f32[8,2,8,640]{3,2,1,0:T(8,128)S(1)}, u32[]{:S(2)}, u32[]{:S(2)}) collective-permute-start(f32[8,2,8,640]{3,2,1,0:T(8,128)} %get-tuple-element.113), channel_id=1, source_target_pairs={{0,1},{1,0},{2,3},{3,2},{4,5},{5,4},{6,7},{7,6},{8,9},{9,8},{10,11... | collective-permute-start | bytes 983048 | tf_op jit(solution)/shard_map/ppermute | solution.py:751
  131.8 15.4 %collective-permute-start.11 = (f32[8,2,8,640]{3,2,1,0:T(8,128)}, f32[8,2,8,640]{3,2,1,0:T(8,128)S(1)}, u32[]{:S(2)}, u32[]{:S(2)}) collective-permute-start(f32[8,2,8,640]{3,2,1,0:T(8,128)} %get-tuple-element.114), channel_id=1, source_target_pairs={{0,3},{1,2},{2,1},{3,0},{4,7},{5,6},{6,5},{7,4},{8,11},{9,10},{10,... | collective-permute-start | bytes 983048 | tf_op jit(solution)/shard_map/ppermute | solution.py:751
  134.2 8.2 %copy-start.17 = (f32[8,2,8,640]{3,2,1,0:T(8,128)S(1)}, f32[8,2,8,640]{3,2,1,0:T(8,128)}, u32[]{:S(2)}) copy-start(f32[8,2,8,640]{3,2,1,0:T(8,128)} %get-tuple-element.111) | copy-start | bytes 983044
  140.2 18.9 %collective-permute-start.12 = (f32[13,2,8,640]{3,2,1,0:T(8,128)}, f32[13,2,8,640]{3,2,1,0:T(8,128)S(1)}, u32[]{:S(2)}, u32[]{:S(2)}) collective-permute-start(f32[13,2,8,640]{3,2,1,0:T(8,128)} %get-tuple-element.126), channel_id=1, source_target_pairs={{0,2},{1,3},{2,0},{3,1},{4,6},{5,7},{6,4},{7,5},{8,10},{9,11},{10,... | collective-permute-start | bytes 1597448 | tf_op jit(solution)/shard_map/ppermute | solution.py:751
  142.1 17.1 %collective-permute-start.13 = (f32[13,2,8,640]{3,2,1,0:T(8,128)}, f32[13,2,8,640]{3,2,1,0:T(8,128)S(1)}, u32[]{:S(2)}, u32[]{:S(2)}) collective-permute-start(f32[13,2,8,640]{3,2,1,0:T(8,128)} %get-tuple-element.127), channel_id=1, source_target_pairs={{0,1},{1,0},{2,3},{3,2},{4,5},{5,4},{6,7},{7,6},{8,9},{9,8},{10,11... | collective-permute-start | bytes 1597448 | tf_op jit(solution)/shard_map/ppermute | solution.py:751
  142.1 27.2 %collective-permute-start.14 = (f32[13,2,8,640]{3,2,1,0:T(8,128)}, f32[13,2,8,640]{3,2,1,0:T(8,128)S(1)}, u32[]{:S(2)}, u32[]{:S(2)}) collective-permute-start(f32[13,2,8,640]{3,2,1,0:T(8,128)} %get-tuple-element.128), channel_id=1, source_target_pairs={{0,3},{1,2},{2,1},{3,0},{4,7},{5,6},{6,5},{7,4},{8,11},{9,10},{10,... | collective-permute-start | bytes 1597448 | tf_op jit(solution)/shard_map/ppermute | solution.py:751
  147.3 11.8 %copy-start.13 = (f32[13,2,8,640]{3,2,1,0:T(8,128)S(1)}, f32[13,2,8,640]{3,2,1,0:T(8,128)}, u32[]{:S(2)}) copy-start(f32[13,2,8,640]{3,2,1,0:T(8,128)} %get-tuple-element.125) | copy-start | bytes 1597444
  151.3 21.2 %all-to-all-start.1 = ((f32[8,2,16,640]{3,1,2,0:T(2,128)}), f32[8,2,16,640]{3,1,2,0:T(2,128)S(1)}, u32[]{:S(2)}, u32[]{:S(2)}) async-start(f32[8,2,16,640]{3,1,2,0:T(2,128)} %copy.81), calls=%async_computation.1 | async-start | bytes 1310720 | tf_op jit(solution)/shard_map/all_to_all | solution.py:761
  169.5 7.9 %copy-start.15 = (f32[8,2,32,256]{3,2,1,0:T(8,128)S(1)}, f32[8,2,32,256]{3,2,1,0:T(8,128)}, u32[]{:S(2)}) copy-start(f32[8,2,32,256]{3,2,1,0:T(8,128)} %constant.142) | copy-start | bytes 1572868
  169.5 7.9 %copy-start.16 = (f32[8,2,32,256]{3,2,1,0:T(8,128)S(1)}, f32[8,2,32,256]{3,2,1,0:T(8,128)}, u32[]{:S(2)}) copy-start(f32[8,2,32,256]{3,2,1,0:T(8,128)} %constant.140) | copy-start | bytes 1572868
  173.8 25.6 %all-to-all-start.2 = ((f32[8,2,21,640]{3,1,2,0:T(2,128)}), f32[8,2,21,640]{3,1,2,0:T(2,128)S(1)}, u32[]{:S(2)}, u32[]{:S(2)}) async-start(f32[8,2,21,640]{3,1,2,0:T(2,128)} %copy.83), calls=%async_computation.2 | async-start | bytes 1720320 | tf_op jit(solution)/shard_map/all_to_all | solution.py:761
  200.9 1.1 copy-start.2
  204.6 23.1 %all-to-all-start.3 = ((f32[32,2,2,1280]{3,2,1,0:T(2,128)}), f32[32,2,2,1280]{3,2,1,0:T(2,128)S(1)}, u32[]{:S(2)}, u32[]{:S(2)}) async-start(f32[32,2,2,1280]{3,2,1,0:T(2,128)} %concatenate.80), calls=%async_computation.3 | async-start | bytes 1310720 | tf_op jit(solution)/shard_map/all_to_all | solution.py:475
  266.6 30.9 %copy-start.1 = (f32[8,288,128]{2,1,0:T(8,128)}, f32[8,288,128]{2,1,0:T(8,128)S(1)}, u32[]{:S(2)}) copy-start(f32[8,288,128]{2,1,0:T(8,128)S(1)} %all_to_all.35) | copy-start | bytes 3538948
  266.6 26.4 %collective-permute-start.16 = (f32[8,288,128]{2,1,0:T(8,128)S(1)}, f32[8,288,128]{2,1,0:T(8,128)}, u32[]{:S(2)}, u32[]{:S(2)}) collective-permute-start(f32[8,288,128]{2,1,0:T(8,128)S(1)} %all_to_all.35), channel_id=1, source_target_pairs={{0,2},{1,3},{2,0},{3,1},{4,6},{5,7},{6,4},{7,5},{8,10},{9,11},{10,... | collective-permute-start | bytes 3538952 | tf_op jit(solution)/shard_map/ppermute | solution.py:744
  267.8 29.1 %all-to-all-start.5 = ((f32[8,256,128]{2,1,0:T(8,128)}), f32[8,256,128]{2,1,0:T(8,128)S(1)}, u32[]{:S(2)}, u32[]{:S(2)}) async-start(f32[8,256,128]{2,1,0:T(8,128)} %get-tuple-element.134), calls=%async_computation.5 | async-start | bytes 2097152 | tf_op jit(solution)/shard_map/all_to_all | solution.py:491
  271.4 25.6 %collective-permute-start.15 = (f32[8,288,128]{2,1,0:T(8,128)S(1)}, f32[8,288,128]{2,1,0:T(8,128)}, u32[]{:S(2)}, u32[]{:S(2)}) collective-permute-start(f32[8,288,128]{2,1,0:T(8,128)S(1)} %all_to_all.35), channel_id=1, source_target_pairs={{0,1},{1,0},{2,3},{3,2},{4,5},{5,4},{6,7},{7,6},{8,9},{9,8},{10,11... | collective-permute-start | bytes 3538952 | tf_op jit(solution)/shard_map/ppermute | solution.py:744
  293.0 10.3 %collective-permute-start.17 = (f32[8,288,128]{2,1,0:T(8,128)}, f32[8,288,128]{2,1,0:T(8,128)}, u32[]{:S(2)}, u32[]{:S(2)}) collective-permute-start(f32[8,288,128]{2,1,0:T(8,128)} %collective-permute-done.16), channel_id=1, source_target_pairs={{0,1},{1,0},{2,3},{3,2},{4,5},{5,4},{6,7},{7,6},{8,9},{9,8},{10,11... | collective-permute-start | bytes 3538952 | tf_op jit(solution)/shard_map/ppermute | solution.py:744
  296.9 7.3 %copy-start.3 = (f32[8,256,128]{2,1,0:T(8,128)}, f32[8,256,128]{2,1,0:T(8,128)S(1)}, u32[]{:S(2)}) copy-start(f32[8,256,128]{2,1,0:T(8,128)S(1)} %all-to-all-done.5) | copy-start | bytes 3145732
  296.9 23.9 %collective-permute-start.19 = (f32[8,256,128]{2,1,0:T(8,128)S(1)}, f32[8,256,128]{2,1,0:T(8,128)}, u32[]{:S(2)}, u32[]{:S(2)}) collective-permute-start(f32[8,256,128]{2,1,0:T(8,128)S(1)} %all-to-all-done.5), channel_id=1, source_target_pairs={{0,2},{1,3},{2,0},{3,1},{4,6},{5,7},{6,4},{7,5},{8,10},{9,11},{10,... | collective-permute-start | bytes 3145736 | tf_op jit(solution)/shard_map/ppermute | solution.py:744
  297.5 23.3 %collective-permute-start.18 = (f32[8,256,128]{2,1,0:T(8,128)S(1)}, f32[8,256,128]{2,1,0:T(8,128)}, u32[]{:S(2)}, u32[]{:S(2)}) collective-permute-start(f32[8,256,128]{2,1,0:T(8,128)S(1)} %all-to-all-done.5), channel_id=1, source_target_pairs={{0,1},{1,0},{2,3},{3,2},{4,5},{5,4},{6,7},{7,6},{8,9},{9,8},{10,11... | collective-permute-start | bytes 3145736 | tf_op jit(solution)/shard_map/ppermute | solution.py:744
  297.5 18.9 %all-to-all-start.6 = ((f32[8,128,128]{2,1,0:T(8,128)}), f32[8,128,128]{2,1,0:T(8,128)S(1)}, u32[]{:S(2)}, u32[]{:S(2)}) async-start(f32[8,128,128]{2,1,0:T(8,128)} %get-tuple-element.139), calls=%async_computation.6 | async-start | bytes 1048576 | tf_op jit(solution)/shard_map/all_to_all | solution.py:491
  316.4 6.9 %copy-start.5 = (f32[8,128,128]{2,1,0:T(8,128)}, f32[8,128,128]{2,1,0:T(8,128)S(1)}, u32[]{:S(2)}) copy-start(f32[8,128,128]{2,1,0:T(8,128)S(1)} %all-to-all-done.6) | copy-start | bytes 1572868
  320.8 12.8 %collective-permute-start.22 = (f32[8,128,128]{2,1,0:T(8,128)S(1)}, f32[8,128,128]{2,1,0:T(8,128)S(1)}, u32[]{:S(2)}, u32[]{:S(2)}) collective-permute-start(f32[8,128,128]{2,1,0:T(8,128)S(1)} %all-to-all-done.6), channel_id=1, source_target_pairs={{0,2},{1,3},{2,0},{3,1},{4,6},{5,7},{6,4},{7,5},{8,10},{9,11},{10,... | collective-permute-start | bytes 1572872 | tf_op jit(solution)/shard_map/ppermute | solution.py:744
  322.5 14.6 %collective-permute-start.20 = (f32[8,256,128]{2,1,0:T(8,128)}, f32[8,256,128]{2,1,0:T(8,128)S(1)}, u32[]{:S(2)}, u32[]{:S(2)}) collective-permute-start(f32[8,256,128]{2,1,0:T(8,128)} %collective-permute-done.19), channel_id=1, source_target_pairs={{0,1},{1,0},{2,3},{3,2},{4,5},{5,4},{6,7},{7,6},{8,9},{9,8},{10,11... | collective-permute-start | bytes 3145736 | tf_op jit(solution)/shard_map/ppermute | solution.py:744
  323.3 13.8 %collective-permute-start.21 = (f32[8,128,128]{2,1,0:T(8,128)S(1)}, f32[8,128,128]{2,1,0:T(8,128)}, u32[]{:S(2)}, u32[]{:S(2)}) collective-permute-start(f32[8,128,128]{2,1,0:T(8,128)S(1)} %all-to-all-done.6), channel_id=1, source_target_pairs={{0,1},{1,0},{2,3},{3,2},{4,5},{5,4},{6,7},{7,6},{8,9},{9,8},{10,11... | collective-permute-start | bytes 1572872 | tf_op jit(solution)/shard_map/ppermute | solution.py:744
  333.6 2.9 copy-start.14
  333.6 3.6 collective-permute-start.23
  337.2 1.0 copy-start.6

commit v8 on v7

--- a/solution.py
+++ b/solution.py
@@ -300,14 +300,17 @@
 
 
 def section_kernel(
-    offsets, closing, me, weights, kept, got, cols_high, cols_low, rows_high, rows_low,
-    rim, corner, before, *refs
+    offsets, planes, opening, closing, me, weights, kept, got, cols_high, cols_low, rows_high,
+    rows_low, *refs
 ):
     step, steps = pl.program_id(0), pl.num_programs(0)
     step_rows = kept.shape[0]
     half, count = rows_high.shape
-    planes, block, width = before.shape
-    *outs, total, lines, packed = refs
+    before = None if opening else refs[0]
+    refs = refs if opening else refs[1:]
+    rim, corner = refs[:2] if closing else (None, None)
+    *outs, total, lines, packed = refs[2:] if closing else refs
+    block, width = total.shape[1:]
     gy, (_, own, gx, _) = len(outs), outs[0].shape
 
     def place(layer, values, slot=0):
@@ -319,7 +322,7 @@
 
     @pl.when(step == 0)
     def _():
-        total[...] = before[...]
+        total[...] = jnp.zeros_like(total) if opening else before[...]
 
     for r in range(step_rows):
         layer = step * step_rows + r
@@ -349,19 +352,20 @@
 def packed_section(col, kept, got, first, table_pair, table_rows, marks, rim, corner, before, offsets, shape, closing):
     _, cols, half = kept.shape
     count = table_rows.shape[0]
-    planes, block, width = before.shape
+    planes, block, width = len(marks), offsets[1], offsets[-1]
     gx, gy = shape
+    opening = before is None
     step_rows = 4
     layers = count + (planes + 1 if closing else 0)
     whole = lambda array: pl.BlockSpec(array.shape, lambda i: (0,) * array.ndim)
     weights = jnp.stack([table_rows[:, m] for m in marks])
     arrays = rounded_parts(table_pair.T) + rounded_parts(table_rows[:, :half].T)
-    arrays += (rim, corner[None], before)
+    arrays += (() if opening else (before,)) + ((rim, corner[None]) if closing else ())
     out = jax.ShapeDtypeStruct((layers, block // (gx * gy), gx, width), jnp.float32)
-    outs = [out] * gy + [jax.ShapeDtypeStruct(before.shape, jnp.float32)]
+    outs = [out] * gy + [jax.ShapeDtypeStruct((planes, block, width), jnp.float32)]
     rows_spec = pl.BlockSpec((step_rows, cols, half), lambda i: (i + first // step_rows, 0, 0))
     return pl.pallas_call(
-        lambda *refs: section_kernel(offsets, closing, *refs),
+        lambda *refs: section_kernel(offsets, planes, opening, closing, *refs),
         grid=(count // step_rows,),
         in_specs=[pl.BlockSpec(memory_space=pltpu.SMEM)] * 2 + [rows_spec, rows_spec]
         + [whole(array) for array in arrays],
@@ -424,8 +428,7 @@
     table_parts = main.reshape(gx, 2, pair_rows, half) / 6.0
     table_parts = jnp.where(core == 0, table_parts, table_parts[:, ::-1])
     table_parts = [table_parts[:, :, part] for part in parts]
-    side = jnp.zeros((slabs, block, width), jnp.float32)
-    rim, corner = jnp.zeros((half, half), jnp.float32), jnp.zeros((width,), jnp.float32)
+    side = rim = corner = None
     values, packed, lines = 0.0, None, None
     for c, count in enumerate(counts):
         closing = c == len(counts) - 1
@@ -629,8 +632,7 @@
     slab, far_row, rim_col, me = places[0], places[1], places[2], places[3]
     lane = lax.broadcasted_iota(jnp.int32, (block, 128), 1)
     at_rim = lax.broadcasted_iota(jnp.int32, (cols, half), 0) + (1 - rim_col) == 0
-    rim_lane = lax.broadcasted_iota(jnp.int32, rim.shape, 1)
-    first_lane = lax.broadcasted_iota(jnp.int32, (cols, half), 1) == 0
+    first_lane = lax.broadcasted_iota(jnp.int32, (cols, 128), 1) == 0
 
     @pl.when(pl.program_id(0) == 0)
     def _():
@@ -646,7 +648,7 @@
         for copy in copies:
             copy.wait()
 
-    def left_half(r):
+    def left_half(r, may_pass):
         t = pl.program_id(0) * step_rows + r
         i = jnp.where(far_row == 1, block - t, t)
         inside = (jnp.zeros((block, 128), jnp.int32) + i) < block
@@ -662,13 +664,16 @@
                     for e in range(own)
                 ]
                 near = jnp.concatenate(near, axis=0)
-                far = pl.multiple_of(source[1] * stride + start + source[0] * block, 8)
-                far = held[g][pl.ds(far, block), :]
-                kind = jnp.zeros((block, 128), jnp.int32)
-                for b in range(1, blocks):
-                    kind += (lane + tile * 128 >= offsets[b]).astype(jnp.int32)
-                line = jnp.where(kind >= slab, near, far)
-                line = jnp.where(inside, line, next_plane[:, pl.ds(tile * 128, 128)])
+                line = near
+                if tile * 128 < offsets[blocks - 1]:
+                    far = pl.multiple_of(source[1] * stride + start + source[0] * block, 8)
+                    far = held[g][pl.ds(far, block), :]
+                    kind = jnp.zeros((block, 128), jnp.int32)
+                    for b in range(1, blocks):
+                        kind += (lane + tile * 128 >= offsets[b]).astype(jnp.int32)
+                    line = jnp.where(kind >= slab, near, far)
+                if may_pass:
+                    line = jnp.where(inside, line, next_plane[:, pl.ds(tile * 128, 128)])
                 parts.append(line)
         line = jnp.concatenate(parts, axis=1)
         plane = square([line[:, offsets[b] : offsets[b + 1]] for b in range(blocks)], block)
@@ -683,16 +688,17 @@
 
     @pl.loop(0, step_rows // together)
     def _(c):
-        left = [left_half(c * together + n) for n in range(together)]
+        left = [left_half(c * together + n, n == 0) for n in range(together)]
         high, low = split(jnp.concatenate(left, axis=0))
         right = jnp.dot(high, flip[...], preferred_element_type=jnp.float32)
         right += jnp.dot(low, flip[...], preferred_element_type=jnp.float32)
         for n in range(together):
             r = c * together + n
             t = pl.program_id(0) * step_rows + r
-            edge = jnp.sum(jnp.where(rim_lane == t, rim[...], 0.0), axis=1, keepdims=True)
+            edge = pltpu.roll(rim[...], lax.rem(128 - t, 128), 1)
             part = right[n * cols : (n + 1) * cols]
-            out[r, :, pl.ds(half, half)] = jnp.where(first_lane, edge, part)
+            out[r, :, pl.ds(half, 128)] = jnp.where(first_lane, edge, part[:, :128])
+            out[r, :, pl.ds(half + 128, half - 128)] = part[:, 128:]
 
 
 def result_block(got, next_plane, across, rim, pick_cols, slab, far_row, rim_col, col, offsets):

time: 369 us -> 366 us (level)
  transfers between devices with their start and end apart: 30 -> 30, of which waited for: 13 -> 13; matrix products, arithmetic and copies ran while one was open for 10% -> 9% of each run, Pallas kernels for 20% -> 20%
where the time goes in v8:
time: 366 us; the launch traced here: 364 us
  Pallas kernels  125 us (34%)
  waiting for transfers between devices  114 us (31%)
  starting transfers between devices  42.4 us (12%)
  local copies, waits for them, and re-layouts  32.6 us (9%)
  blocking collectives  32.5 us (9%)
  other arithmetic  11.6 us (3%)
  matrix products  5.32 us (1%)
    pallas_call x4, Pallas kernels, filled_spectrum(): pl.pallas_call(fill_kernel, grid_spec=pltpu.PrefetchScalarGridSpec(num_sc...  67.8 us
    ppermute x9, waiting for transfers between devices, gathered(): pieces[place ^ bit] = lax.ppermute(pieces[place], 'gy', swap(peers, bit))  35.6 us
    all_to_all x1, blocking collectives, on_device(): piece = lax.all_to_all(messages, 'gx', 0, 0, tiled=True)  32.5 us
    pallas_call x1, Pallas kernels, result_block(): pl.pallas_call(lambda *refs: result_kernel(offsets, own, devices, groups,...  28.7 us
    all_to_all x3, waiting for transfers between devices, sent_lines(): return lax.all_to_all(lines, 'gx', 0, 0, tiled=True)  25.5 us
    pallas_call x3, Pallas kernels, packed_section(): pl.pallas_call(lambda *refs: section_kernel(offsets, planes, opening, clo...  19.3 us
    ppermute x9, waiting for transfers between devices, exchanged(): lax.ppermute(packed[p], 'gy', swap(gy, p))  19.1 us
    all_to_all x1, waiting for transfers between devices, on_device(): lax.all_to_all(jnp.concatenate(turned, axis=3), ('gy', 'gx'), 0, 0, tiled...  18.2 us
  transfers between devices with their start and end apart: 30, of which 13 were waited for; matrix products, arithmetic and copies ran while one was open for 9% of the time, Pallas kernels for 20%

profile of v8, /device:TPU:0, one launch (start us, length us, event | category | flops | bytes accessed | tf_op | source)
XLA Modules:
  0.0 364.5 jit_solution(13139477179826448667)
XLA Ops:
  0.0 1.8 fusion.33
  2.3 2.0 collective-permute-start.1
  4.3 3.5 shard_map.55.marks
  8.4 2.5 collective-permute-done.1
  11.2 1.6 pad.12.sides
  12.8 0.9 broadcast_in_dim.6.top.bottom
  13.6 17.1 %shard_map.57 = (f32[16,128,256]{2,1,0:T(8,128)}, f32[16,256]{1,0:T(8,128)}, f32[128,128]{1,0:T(8,128)}) custom-call(s32[2]{0:T(128)} %get-tuple-element.186.base, f32[64,128,512]{2,1,0:T(8,128)} %below.7, f32[64,128,512]{2,1,0:T(8,128)} %below.7, f32[64,128,512]{2,1,0:T(8,128)} %below.7, f32[2,132,512]{2,1,0:T(8,128)} %broadcast_in_dim.6.top.bottom, ...), custom_call_target="tpu_custom_call" | custom-call | flops 1610612736 | bytes 6291456 | tf_op jit(solution)/shard_map/pallas_call | solution.py:253
  30.9 1.3 fusion.32
  34.1 0.9 constant_dynamic-slice_fusion.4
  36.0 2.3 collective-permute-start.3
  38.6 3.3 collective-permute-start.4
  42.5 17.2 %shard_map.56 = (f32[16,128,256]{2,1,0:T(8,128)}, f32[16,256]{1,0:T(8,128)}, f32[128,128]{1,0:T(8,128)}) custom-call(s32[2]{0:T(128)} %get-tuple-element.185.base, f32[64,128,512]{2,1,0:T(8,128)} %below.7, f32[64,128,512]{2,1,0:T(8,128)} %below.7, f32[64,128,512]{2,1,0:T(8,128)} %below.7, f32[2,132,512]{2,1,0:T(8,128)} %broadcast_in_dim.6.top.bottom, ...), custom_call_target="tpu_custom_call" | custom-call | flops 1610612736 | bytes 6291456 | tf_op jit(solution)/shard_map/pallas_call | solution.py:253
  59.7 7.8 %shard_map.58 = (f32[16,2,8,640]{3,2,1,0:T(8,128)}, f32[16,2,8,640]{3,2,1,0:T(8,128)}, f32[16,2,8,640]{3,2,1,0:T(8,128)}, f32[16,2,8,640]{3,2,1,0:T(8,128)}, f32[4,64,640]{2,1,0:T(8,128)}) custom-call(s32[1]{0:T(128)} %bitcast.3.refs_0_, f32[4,16]{1,0:T(4,128)} %pad_maximum_fusion.7.refs_1_, f32[16,128,256]{2,1,0:T(8,128)} %get-tuple-element.74.refs_2_, ...), custom_call_target="tpu_custom_call" | custom-call | flops 1610612736 | bytes 8388608 | tf_op jit(solution)/shard_map/pallas_call | solution.py:367
  67.5 1.9 collective-permute-start.6
  69.5 1.0 copy.75.top
  70.4 0.9 copy.76.bottom
  72.7 16.7 %shard_map.60 = (f32[16,128,256]{2,1,0:T(8,128)}, f32[16,256]{1,0:T(8,128)}, f32[128,128]{1,0:T(8,128)}) custom-call(s32[2]{0:T(128)} %pad_add_fusion.4.base, f32[64,128,512]{2,1,0:T(8,128)} %below.7, f32[64,128,512]{2,1,0:T(8,128)} %below.7, f32[64,128,512]{2,1,0:T(8,128)} %below.7, f32[2,132,512]{2,1,0:T(8,128)} %copy.75.top, f32[2,132,512]{2,1,0:T(8,128)} %copy.76.bottom, ...), custom_call_target="tpu_custom_call" | custom-call | flops 1610612736 | bytes 6291456 | tf_op jit(solution)/shard_map/pallas_call | solution.py:253
  89.4 16.9 %shard_map.59 = (f32[16,128,256]{2,1,0:T(8,128)}, f32[16,256]{1,0:T(8,128)}, f32[128,128]{1,0:T(8,128)}) custom-call(s32[2]{0:T(128)} %pad_add_fusion.3.base, f32[64,128,512]{2,1,0:T(8,128)} %below.7, f32[64,128,512]{2,1,0:T(8,128)} %below.7, f32[64,128,512]{2,1,0:T(8,128)} %below.7, f32[2,132,512]{2,1,0:T(8,128)} %copy.75.top, f32[2,132,512]{2,1,0:T(8,128)} %copy.76.bottom, ...), custom_call_target="tpu_custom_call" | custom-call | flops 1610612736 | bytes 6291456 | tf_op jit(solution)/shard_map/pallas_call | solution.py:253
  106.4 0.8 copy-done.8
  107.8 1.3 add.178
  109.5 1.7 copy.79
  111.2 4.5 %all-to-all-start = ((f32[8,2,32,640]{3,1,2,0:T(2,128)}), f32[8,2,32,640]{3,1,2,0:T(2,128)}, u32[]{:S(2)}, u32[]{:S(2)}) async-start(f32[8,2,32,640]{3,1,2,0:T(2,128)} %copy.79), calls=%async_computation | async-start | bytes 2621440 | tf_op jit(solution)/shard_map/all_to_all | solution.py:767
  115.7 0.8 constant_dynamic-slice_fusion.2
  116.7 1.2 concatenate.75
  119.1 0.8 fusion.11
  120.0 1.3 copy-done
  121.4 5.5 %shard_map.61 = (f32[8,2,8,640]{3,2,1,0:T(8,128)}, f32[8,2,8,640]{3,2,1,0:T(8,128)}, f32[8,2,8,640]{3,2,1,0:T(8,128)}, f32[8,2,8,640]{3,2,1,0:T(8,128)}, f32[4,64,640]{2,1,0:T(8,128)}) custom-call(s32[1]{0:T(128)} %bitcast.3.refs_0_, f32[4,8]{1,0:T(4,128)} %pad_maximum_fusion.8.refs_1_, f32[16,128,256]{2,1,0:T(8,128)} %get-tuple-element.104.refs_2_, ...), custom_call_target="tpu_custom_call" | custom-call | flops 805306368 | bytes 4194304 | tf_op jit(solution)/shard_map/pallas_call | solution.py:367
  127.3 1.9 collective-permute-start.9
  130.0 1.0 fusion.13.refs_9_
  131.6 6.0 %shard_map.62 = (f32[13,2,8,640]{3,2,1,0:T(8,128)}, f32[13,2,8,640]{3,2,1,0:T(8,128)}, f32[13,2,8,640]{3,2,1,0:T(8,128)}, f32[13,2,8,640]{3,2,1,0:T(8,128)}, f32[4,64,640]{2,1,0:T(8,128)}) custom-call(s32[1]{0:T(128)} %bitcast.3.refs_0_, f32[4,8]{1,0:T(4,128)} %pad_maximum_fusion.9.refs_1_, f32[16,128,256]{2,1,0:T(8,128)} %get-tuple-element.104.refs_2_, ...), custom_call_target="tpu_custom_call" | custom-call | flops 805306368 | bytes 4194304 | tf_op jit(solution)/shard_map/pallas_call | solution.py:367
  137.6 1.9 collective-permute-start.12
  139.8 4.8 %collective-permute-done.11 = f32[8,2,8,640]{3,2,1,0:T(8,128)S(1)} collective-permute-done((f32[8,2,8,640]{3,2,1,0:T(8,128)}, f32[8,2,8,640]{3,2,1,0:T(8,128)S(1)}, u32[]{:S(2)}, u32[]{:S(2)}) %collective-permute-start.11) | collective-permute-done | bytes 327712 | tf_op jit(solution)/shard_map/ppermute | solution.py:757
  144.7 2.9 all-to-all-done
  147.6 1.2 copy.81
  148.7 3.6 all-to-all-start.1
  152.4 4.1 %collective-permute-done.12 = f32[13,2,8,640]{3,2,1,0:T(8,128)S(1)} collective-permute-done((f32[13,2,8,640]{3,2,1,0:T(8,128)}, f32[13,2,8,640]{3,2,1,0:T(8,128)S(1)}, u32[]{:S(2)}, u32[]{:S(2)}) %collective-permute-start.12) | collective-permute-done | bytes 532512 | tf_op jit(solution)/shard_map/ppermute | solution.py:757
  156.6 10.1 %collective-permute-done.14 = f32[13,2,8,640]{3,2,1,0:T(8,128)S(1)} collective-permute-done((f32[13,2,8,640]{3,2,1,0:T(8,128)}, f32[13,2,8,640]{3,2,1,0:T(8,128)S(1)}, u32[]{:S(2)}, u32[]{:S(2)}) %collective-permute-start.14) | collective-permute-done | bytes 532512 | tf_op jit(solution)/shard_map/ppermute | solution.py:757
  166.9 3.0 all-to-all-done.1
  169.9 1.3 copy.83
  171.2 3.6 all-to-all-start.2
  175.0 2.1 convolution_bitcast_fusion
  177.1 19.7 %all-to-all-done.2 = f32[8,2,21,640]{3,1,2,0:T(2,128)S(1)} async-done(((f32[8,2,21,640]{3,1,2,0:T(2,128)}), f32[8,2,21,640]{3,1,2,0:T(2,128)S(1)}, u32[]{:S(2)}, u32[]{:S(2)}) %all-to-all-start.2) | async-done | bytes 860192 | tf_op jit(solution)/shard_map/all_to_all | solution.py:767
  197.6 0.8 fusion.1
  198.4 1.0 copy.117
  199.6 2.4 concatenate.80
  202.0 4.2 %all-to-all-start.3 = ((f32[32,2,2,1280]{3,2,1,0:T(2,128)}), f32[32,2,2,1280]{3,2,1,0:T(2,128)S(1)}, u32[]{:S(2)}, u32[]{:S(2)}) async-start(f32[32,2,2,1280]{3,2,1,0:T(2,128)} %concatenate.80), calls=%async_computation.3 | async-start | bytes 1310720 | tf_op jit(solution)/shard_map/all_to_all | solution.py:478
  206.9 18.2 %all-to-all-done.3 = f32[32,2,2,1280]{3,2,1,0:T(2,128)S(1)} async-done(((f32[32,2,2,1280]{3,2,1,0:T(2,128)}), f32[32,2,2,1280]{3,2,1,0:T(2,128)S(1)}, u32[]{:S(2)}, u32[]{:S(2)}) %all-to-all-start.3) | async-done | bytes 655392 | tf_op jit(solution)/shard_map/all_to_all | solution.py:478
  225.1 1.0 copy.86
  226.0 5.5 %shard_map.63 = (f32[8,288,128]{2,1,0:T(8,128)}, f32[8,256,128]{2,1,0:T(8,128)}, f32[8,128,128]{2,1,0:T(8,128)}) custom-call(f32[2,256,640]{2,1,0:T(8,128)} %bitcast.164, f32[2,64,1280]{2,1,0:T(8,128)} %bitcast.173, f32[2,5,640]{2,1,0:T(8,128)} %copy_multiply_fusion.refs_2_), custom_call_target="tpu_custom_call" | custom-call | tf_op jit(solution)/shard_map/pallas_call | solution.py:613
  231.5 32.5 %all_to_all.35 = f32[8,288,128]{2,1,0:T(8,128)S(1)} all-to-all(f32[8,288,128]{2,1,0:T(8,128)} %get-tuple-element.131), channel_id=1, replica_groups=mesh['gx'=8,'gy'=4] {'gx'}, dimensions={0} | all-to-all | bytes 2359296 | tf_op jit(solution)/shard_map/all_to_all | solution.py:494
  264.0 1.2 collective-permute-start.16
  265.2 3.6 all-to-all-start.5
  268.9 21.4 %collective-permute-done.16 = f32[8,288,128]{2,1,0:T(8,128)} collective-permute-done((f32[8,288,128]{2,1,0:T(8,128)S(1)}, f32[8,288,128]{2,1,0:T(8,128)}, u32[]{:S(2)}, u32[]{:S(2)}) %collective-permute-start.16) | collective-permute-done | bytes 1179680 | tf_op jit(solution)/shard_map/ppermute | solution.py:750
  292.4 1.9 all-to-all-done.5
  294.8 4.0 %all-to-all-start.6 = ((f32[8,128,128]{2,1,0:T(8,128)}), f32[8,128,128]{2,1,0:T(8,128)S(1)}, u32[]{:S(2)}, u32[]{:S(2)}) async-start(f32[8,128,128]{2,1,0:T(8,128)} %get-tuple-element.139), calls=%async_computation.6 | async-start | bytes 1048576 | tf_op jit(solution)/shard_map/all_to_all | solution.py:494
  298.8 0.9 slice_bitcast_fusion.9
  299.7 0.9 slice_bitcast_fusion.8
  300.7 0.9 slice_bitcast_fusion.2
  302.4 11.3 %all-to-all-done.6 = f32[8,128,128]{2,1,0:T(8,128)S(1)} async-done(((f32[8,128,128]{2,1,0:T(8,128)}), f32[8,128,128]{2,1,0:T(8,128)S(1)}, u32[]{:S(2)}, u32[]{:S(2)}) %all-to-all-start.6) | async-done | bytes 524320 | tf_op jit(solution)/shard_map/all_to_all | solution.py:494
  313.8 4.4 %collective-permute-done.19 = f32[8,256,128]{2,1,0:T(8,128)} collective-permute-done((f32[8,256,128]{2,1,0:T(8,128)S(1)}, f32[8,256,128]{2,1,0:T(8,128)}, u32[]{:S(2)}, u32[]{:S(2)}) %collective-permute-start.19) | collective-permute-done | bytes 1048608 | tf_op jit(solution)/shard_map/ppermute | solution.py:750
  318.2 1.7 collective-permute-start.22
  321.3 9.7 %collective-permute-done.22 = f32[8,128,128]{2,1,0:T(8,128)S(1)} collective-permute-done((f32[8,128,128]{2,1,0:T(8,128)S(1)}, f32[8,128,128]{2,1,0:T(8,128)S(1)}, u32[]{:S(2)}, u32[]{:S(2)}) %collective-permute-start.22) | collective-permute-done | bytes 524320 | tf_op jit(solution)/shard_map/ppermute | solution.py:750
  334.6 1.0 copy-done.6
  335.5 28.7 %shard_map.64 = f32[64,128,512]{2,1,0:T(8,128)} custom-call(s32[4]{0:T(128)} %pad_add_fusion.refs_0_, f32[64,640]{1,0:T(8,128)} %bitcast.179, f32[64,256]{1,0:T(8,128)} %slice.366.refs_2_, f32[128,128]{1,0:T(8,128)} %pad.14.refs_3_, bf16[128,256]{1,0:T(8,128)(2,1)} %fusion.15.refs_4_, bf16[256,256]{1,0:T(8,128)(2,1)} %fusion.7.refs_5_, ...), custom_call_target="tpu_custom_call" | custom-call | tf_op jit(solution)/shard_map/pallas_call | solution.py:721
  (167 shorter events, 21.7 us)
Async XLA Ops:
  1.8 6.6 %collective-permute-start = (f32[64,2,512]{2,1,0:T(2,128)S(1)}, f32[64,2,512]{2,1,0:T(2,128)S(1)}, u32[]{:S(2)}, u32[]{:S(2)}) collective-permute-start(f32[64,2,512]{2,1,0:T(2,128)S(1)} %get-tuple-element.145), channel_id=1, source_target_pairs={{0,1},{1,2},{2,3},{3,0},{4,5},{5,6},{6,7},{7,4},{8,9},{9,10},{10,1... | collective-permute-start | bytes 786440 | tf_op jit(solution)/shard_map/ppermute | solution.py:30
  2.3 8.6 %collective-permute-start.1 = (f32[64,2,512]{2,1,0:T(2,128)S(1)}, f32[64,2,512]{2,1,0:T(2,128)S(1)}, u32[]{:S(2)}, u32[]{:S(2)}) collective-permute-start(f32[64,2,512]{2,1,0:T(2,128)S(1)} %get-tuple-element.146), channel_id=1, source_target_pairs={{1,0},{2,1},{3,2},{0,3},{5,4},{6,5},{7,6},{4,7},{9,8},{10,9},{11,1... | collective-permute-start | bytes 786440 | tf_op jit(solution)/shard_map/ppermute | solution.py:31
  30.7 29.0 %collective-permute-start.2 = (f32[16,128,256]{2,1,0:T(8,128)}, f32[16,128,256]{2,1,0:T(8,128)}, u32[]{:S(2)}, u32[]{:S(2)}) collective-permute-start(f32[16,128,256]{2,1,0:T(8,128)} %get-tuple-element.78), channel_id=1, source_target_pairs={{0,1},{1,0},{2,3},{3,2},{4,5},{5,4},{6,7},{7,6},{8,9},{9,8},{10,11... | collective-permute-start | bytes 6291464 | tf_op jit(solution)/shard_map/ppermute | solution.py:449
  32.2 1.1 copy-start.4
  36.0 33.5 %collective-permute-start.3 = (f32[2,132,512]{2,0,1:T(2,128)S(1)}, f32[2,132,512]{2,0,1:T(2,128)S(1)}, u32[]{:S(2)}, u32[]{:S(2)}) collective-permute-start(f32[2,132,512]{2,0,1:T(2,128)S(1)} %pad_maximum_fusion), channel_id=1, source_target_pairs={{0,4},{4,8},{8,12},{12,16},{16,20},{20,24},{24,28},{28,0},{1,5},{5... | collective-permute-start | bytes 1622024 | tf_op jit(solution)/shard_map/ppermute | solution.py:40
  38.6 31.8 %collective-permute-start.4 = (f32[2,132,512]{2,0,1:T(2,128)S(1)}, f32[2,132,512]{2,0,1:T(2,128)S(1)}, u32[]{:S(2)}, u32[]{:S(2)}) collective-permute-start(f32[2,132,512]{2,0,1:T(2,128)S(1)} %pad_maximum_fusion.1), channel_id=1, source_target_pairs={{4,0},{8,4},{12,8},{16,12},{20,16},{24,20},{28,24},{0,28},{5,1},{9... | collective-permute-start | bytes 1622024 | tf_op jit(solution)/shard_map/ppermute | solution.py:40
  67.5 38.8 %collective-permute-start.5 = (f32[16,2,8,640]{3,2,1,0:T(8,128)}, f32[16,2,8,640]{3,2,1,0:T(8,128)S(1)}, u32[]{:S(2)}, u32[]{:S(2)}) collective-permute-start(f32[16,2,8,640]{3,2,1,0:T(8,128)} %get-tuple-element.89), channel_id=1, source_target_pairs={{0,1},{1,0},{2,3},{3,2},{4,5},{5,4},{6,7},{7,6},{8,9},{9,8},{10,11... | collective-permute-start | bytes 1966088 | tf_op jit(solution)/shard_map/ppermute | solution.py:757
  67.5 38.8 %collective-permute-start.6 = (f32[16,2,8,640]{3,2,1,0:T(8,128)}, f32[16,2,8,640]{3,2,1,0:T(8,128)S(1)}, u32[]{:S(2)}, u32[]{:S(2)}) collective-permute-start(f32[16,2,8,640]{3,2,1,0:T(8,128)} %get-tuple-element.90), channel_id=1, source_target_pairs={{0,2},{1,3},{2,0},{3,1},{4,6},{5,7},{6,4},{7,5},{8,10},{9,11},{10,... | collective-permute-start | bytes 1966088 | tf_op jit(solution)/shard_map/ppermute | solution.py:757
  69.4 36.9 %collective-permute-start.7 = (f32[16,2,8,640]{3,2,1,0:T(8,128)}, f32[16,2,8,640]{3,2,1,0:T(8,128)S(1)}, u32[]{:S(2)}, u32[]{:S(2)}) collective-permute-start(f32[16,2,8,640]{3,2,1,0:T(8,128)} %get-tuple-element.91), channel_id=1, source_target_pairs={{0,3},{1,2},{2,1},{3,0},{4,7},{5,6},{6,5},{7,4},{8,11},{9,10},{10,... | collective-permute-start | bytes 1966088 | tf_op jit(solution)/shard_map/ppermute | solution.py:757
  89.4 18.4 %copy-start.7 = (f32[16,2,8,640]{3,2,1,0:T(8,128)S(1)}, f32[16,2,8,640]{3,2,1,0:T(8,128)}, u32[]{:S(2)}) copy-start(f32[16,2,8,640]{3,2,1,0:T(8,128)} %get-tuple-element.92) | copy-start | bytes 1966084
  106.3 0.8 copy-start.8
  106.3 1.1 copy-start.10
  106.3 1.2 copy-start.11
  107.6 12.4 %collective-permute-start.8 = (f32[16,128,256]{2,1,0:T(8,128)}, f32[16,128,256]{2,1,0:T(8,128)S(1)}, u32[]{:S(2)}, u32[]{:S(2)}) collective-permute-start(f32[16,128,256]{2,1,0:T(8,128)} %get-tuple-element.105), channel_id=1, source_target_pairs={{0,1},{1,0},{2,3},{3,2},{4,5},{5,4},{6,7},{7,6},{8,9},{9,8},{10,11... | collective-permute-start | bytes 6291464 | tf_op jit(solution)/shard_map/ppermute | solution.py:449
  107.8 1.3 copy-start.9
  107.8 1.5 copy-start.12
  111.2 36.4 %all-to-all-start = ((f32[8,2,32,640]{3,1,2,0:T(2,128)}), f32[8,2,32,640]{3,1,2,0:T(2,128)}, u32[]{:S(2)}, u32[]{:S(2)}) async-start(f32[8,2,32,640]{3,1,2,0:T(2,128)} %copy.79), calls=%async_computation | async-start | bytes 2621440 | tf_op jit(solution)/shard_map/all_to_all | solution.py:767
  120.0 1.3 copy-start
  121.3 5.6 %copy-start.18 = (f32[128,128]{1,0:T(8,128)S(1)}, f32[128,128]{1,0:T(8,128)}, u32[]{:S(2)}) copy-start(f32[128,128]{1,0:T(8,128)} %get-tuple-element.117) | copy-start | bytes 196612
  121.3 5.6 %copy-start.19 = (f32[128,128]{1,0:T(8,128)S(1)}, f32[128,128]{1,0:T(8,128)}, u32[]{:S(2)}) copy-start(f32[128,128]{1,0:T(8,128)} %get-tuple-element.119) | copy-start | bytes 196612
  121.3 5.6 %copy-start.20 = (f32[128,128]{1,0:T(8,128)S(1)}, f32[128,128]{1,0:T(8,128)}, u32[]{:S(2)}) copy-start(f32[128,128]{1,0:T(8,128)} %get-tuple-element.120) | copy-start | bytes 196612
  121.3 5.6 %copy-start.21 = (f32[128,128]{1,0:T(8,128)S(1)}, f32[128,128]{1,0:T(8,128)}, u32[]{:S(2)}) copy-start(f32[128,128]{1,0:T(8,128)} %get-tuple-element.118) | copy-start | bytes 196612
  121.3 8.2 %copy-start.22 = (f32[16,256]{1,0:T(8,128)S(1)}, f32[16,256]{1,0:T(8,128)}, u32[]{:S(2)}) copy-start(f32[16,256]{1,0:T(8,128)} %get-tuple-element.121) | copy-start | bytes 49156
  121.3 8.2 %copy-start.23 = (f32[16,256]{1,0:T(8,128)S(1)}, f32[16,256]{1,0:T(8,128)}, u32[]{:S(2)}) copy-start(f32[16,256]{1,0:T(8,128)} %get-tuple-element.123) | copy-start | bytes 49156
  121.3 8.1 %copy-start.24 = (f32[16,256]{1,0:T(8,128)S(1)}, f32[16,256]{1,0:T(8,128)}, u32[]{:S(2)}) copy-start(f32[16,256]{1,0:T(8,128)} %get-tuple-element.124) | copy-start | bytes 49156
  121.3 8.1 %copy-start.25 = (f32[16,256]{1,0:T(8,128)S(1)}, f32[16,256]{1,0:T(8,128)}, u32[]{:S(2)}) copy-start(f32[16,256]{1,0:T(8,128)} %get-tuple-element.122) | copy-start | bytes 49156
  127.3 12.2 %collective-permute-start.9 = (f32[8,2,8,640]{3,2,1,0:T(8,128)}, f32[8,2,8,640]{3,2,1,0:T(8,128)S(1)}, u32[]{:S(2)}, u32[]{:S(2)}) collective-permute-start(f32[8,2,8,640]{3,2,1,0:T(8,128)} %get-tuple-element.112), channel_id=1, source_target_pairs={{0,2},{1,3},{2,0},{3,1},{4,6},{5,7},{6,4},{7,5},{8,10},{9,11},{10,... | collective-permute-start | bytes 983048 | tf_op jit(solution)/shard_map/ppermute | solution.py:757
  129.2 10.6 %collective-permute-start.10 = (f32[8,2,8,640]{3,2,1,0:T(8,128)}, f32[8,2,8,640]{3,2,1,0:T(8,128)S(1)}, u32[]{:S(2)}, u32[]{:S(2)}) collective-permute-start(f32[8,2,8,640]{3,2,1,0:T(8,128)} %get-tuple-element.113), channel_id=1, source_target_pairs={{0,1},{1,0},{2,3},{3,2},{4,5},{5,4},{6,7},{7,6},{8,9},{9,8},{10,11... | collective-permute-start | bytes 983048 | tf_op jit(solution)/shard_map/ppermute | solution.py:757
  129.2 15.4 %collective-permute-start.11 = (f32[8,2,8,640]{3,2,1,0:T(8,128)}, f32[8,2,8,640]{3,2,1,0:T(8,128)S(1)}, u32[]{:S(2)}, u32[]{:S(2)}) collective-permute-start(f32[8,2,8,640]{3,2,1,0:T(8,128)} %get-tuple-element.114), channel_id=1, source_target_pairs={{0,3},{1,2},{2,1},{3,0},{4,7},{5,6},{6,5},{7,4},{8,11},{9,10},{10,... | collective-permute-start | bytes 983048 | tf_op jit(solution)/shard_map/ppermute | solution.py:757
  131.6 8.2 %copy-start.17 = (f32[8,2,8,640]{3,2,1,0:T(8,128)S(1)}, f32[8,2,8,640]{3,2,1,0:T(8,128)}, u32[]{:S(2)}) copy-start(f32[8,2,8,640]{3,2,1,0:T(8,128)} %get-tuple-element.111) | copy-start | bytes 983044
  137.6 18.9 %collective-permute-start.12 = (f32[13,2,8,640]{3,2,1,0:T(8,128)}, f32[13,2,8,640]{3,2,1,0:T(8,128)S(1)}, u32[]{:S(2)}, u32[]{:S(2)}) collective-permute-start(f32[13,2,8,640]{3,2,1,0:T(8,128)} %get-tuple-element.126), channel_id=1, source_target_pairs={{0,2},{1,3},{2,0},{3,1},{4,6},{5,7},{6,4},{7,5},{8,10},{9,11},{10,... | collective-permute-start | bytes 1597448 | tf_op jit(solution)/shard_map/ppermute | solution.py:757
  139.5 17.1 %collective-permute-start.13 = (f32[13,2,8,640]{3,2,1,0:T(8,128)}, f32[13,2,8,640]{3,2,1,0:T(8,128)S(1)}, u32[]{:S(2)}, u32[]{:S(2)}) collective-permute-start(f32[13,2,8,640]{3,2,1,0:T(8,128)} %get-tuple-element.127), channel_id=1, source_target_pairs={{0,1},{1,0},{2,3},{3,2},{4,5},{5,4},{6,7},{7,6},{8,9},{9,8},{10,11... | collective-permute-start | bytes 1597448 | tf_op jit(solution)/shard_map/ppermute | solution.py:757
  139.5 27.2 %collective-permute-start.14 = (f32[13,2,8,640]{3,2,1,0:T(8,128)}, f32[13,2,8,640]{3,2,1,0:T(8,128)S(1)}, u32[]{:S(2)}, u32[]{:S(2)}) collective-permute-start(f32[13,2,8,640]{3,2,1,0:T(8,128)} %get-tuple-element.128), channel_id=1, source_target_pairs={{0,3},{1,2},{2,1},{3,0},{4,7},{5,6},{6,5},{7,4},{8,11},{9,10},{10,... | collective-permute-start | bytes 1597448 | tf_op jit(solution)/shard_map/ppermute | solution.py:757
  144.7 11.8 %copy-start.13 = (f32[13,2,8,640]{3,2,1,0:T(8,128)S(1)}, f32[13,2,8,640]{3,2,1,0:T(8,128)}, u32[]{:S(2)}) copy-start(f32[13,2,8,640]{3,2,1,0:T(8,128)} %get-tuple-element.125) | copy-start | bytes 1597444
  148.7 21.1 %all-to-all-start.1 = ((f32[8,2,16,640]{3,1,2,0:T(2,128)}), f32[8,2,16,640]{3,1,2,0:T(2,128)S(1)}, u32[]{:S(2)}, u32[]{:S(2)}) async-start(f32[8,2,16,640]{3,1,2,0:T(2,128)} %copy.81), calls=%async_computation.1 | async-start | bytes 1310720 | tf_op jit(solution)/shard_map/all_to_all | solution.py:767
  166.9 8.0 %copy-start.15 = (f32[8,2,32,256]{3,2,1,0:T(8,128)S(1)}, f32[8,2,32,256]{3,2,1,0:T(8,128)}, u32[]{:S(2)}) copy-start(f32[8,2,32,256]{3,2,1,0:T(8,128)} %constant.139) | copy-start | bytes 1572868
  166.9 8.0 %copy-start.16 = (f32[8,2,32,256]{3,2,1,0:T(8,128)S(1)}, f32[8,2,32,256]{3,2,1,0:T(8,128)}, u32[]{:S(2)}) copy-start(f32[8,2,32,256]{3,2,1,0:T(8,128)} %constant.137) | copy-start | bytes 1572868
  171.2 25.6 %all-to-all-start.2 = ((f32[8,2,21,640]{3,1,2,0:T(2,128)}), f32[8,2,21,640]{3,1,2,0:T(2,128)S(1)}, u32[]{:S(2)}, u32[]{:S(2)}) async-start(f32[8,2,21,640]{3,1,2,0:T(2,128)} %copy.83), calls=%async_computation.2 | async-start | bytes 1720320 | tf_op jit(solution)/shard_map/all_to_all | solution.py:767
  198.4 1.1 copy-start.2
  202.0 23.1 %all-to-all-start.3 = ((f32[32,2,2,1280]{3,2,1,0:T(2,128)}), f32[32,2,2,1280]{3,2,1,0:T(2,128)S(1)}, u32[]{:S(2)}, u32[]{:S(2)}) async-start(f32[32,2,2,1280]{3,2,1,0:T(2,128)} %concatenate.80), calls=%async_computation.3 | async-start | bytes 1310720 | tf_op jit(solution)/shard_map/all_to_all | solution.py:478
  264.0 30.9 %copy-start.1 = (f32[8,288,128]{2,1,0:T(8,128)}, f32[8,288,128]{2,1,0:T(8,128)S(1)}, u32[]{:S(2)}) copy-start(f32[8,288,128]{2,1,0:T(8,128)S(1)} %all_to_all.35) | copy-start | bytes 3538948
  264.0 26.4 %collective-permute-start.16 = (f32[8,288,128]{2,1,0:T(8,128)S(1)}, f32[8,288,128]{2,1,0:T(8,128)}, u32[]{:S(2)}, u32[]{:S(2)}) collective-permute-start(f32[8,288,128]{2,1,0:T(8,128)S(1)} %all_to_all.35), channel_id=1, source_target_pairs={{0,2},{1,3},{2,0},{3,1},{4,6},{5,7},{6,4},{7,5},{8,10},{9,11},{10,... | collective-permute-start | bytes 3538952 | tf_op jit(solution)/shard_map/ppermute | solution.py:750
  265.2 29.1 %all-to-all-start.5 = ((f32[8,256,128]{2,1,0:T(8,128)}), f32[8,256,128]{2,1,0:T(8,128)S(1)}, u32[]{:S(2)}, u32[]{:S(2)}) async-start(f32[8,256,128]{2,1,0:T(8,128)} %get-tuple-element.134), calls=%async_computation.5 | async-start | bytes 2097152 | tf_op jit(solution)/shard_map/all_to_all | solution.py:494
  268.7 25.6 %collective-permute-start.15 = (f32[8,288,128]{2,1,0:T(8,128)S(1)}, f32[8,288,128]{2,1,0:T(8,128)}, u32[]{:S(2)}, u32[]{:S(2)}) collective-permute-start(f32[8,288,128]{2,1,0:T(8,128)S(1)} %all_to_all.35), channel_id=1, source_target_pairs={{0,1},{1,0},{2,3},{3,2},{4,5},{5,4},{6,7},{7,6},{8,9},{9,8},{10,11... | collective-permute-start | bytes 3538952 | tf_op jit(solution)/shard_map/ppermute | solution.py:750
  290.3 10.3 %collective-permute-start.17 = (f32[8,288,128]{2,1,0:T(8,128)}, f32[8,288,128]{2,1,0:T(8,128)}, u32[]{:S(2)}, u32[]{:S(2)}) collective-permute-start(f32[8,288,128]{2,1,0:T(8,128)} %collective-permute-done.16), channel_id=1, source_target_pairs={{0,1},{1,0},{2,3},{3,2},{4,5},{5,4},{6,7},{7,6},{8,9},{9,8},{10,11... | collective-permute-start | bytes 3538952 | tf_op jit(solution)/shard_map/ppermute | solution.py:750
  294.3 7.3 %copy-start.3 = (f32[8,256,128]{2,1,0:T(8,128)}, f32[8,256,128]{2,1,0:T(8,128)S(1)}, u32[]{:S(2)}) copy-start(f32[8,256,128]{2,1,0:T(8,128)S(1)} %all-to-all-done.5) | copy-start | bytes 3145732
  294.3 23.9 %collective-permute-start.19 = (f32[8,256,128]{2,1,0:T(8,128)S(1)}, f32[8,256,128]{2,1,0:T(8,128)}, u32[]{:S(2)}, u32[]{:S(2)}) collective-permute-start(f32[8,256,128]{2,1,0:T(8,128)S(1)} %all-to-all-done.5), channel_id=1, source_target_pairs={{0,2},{1,3},{2,0},{3,1},{4,6},{5,7},{6,4},{7,5},{8,10},{9,11},{10,... | collective-permute-start | bytes 3145736 | tf_op jit(solution)/shard_map/ppermute | solution.py:750
  294.8 23.3 %collective-permute-start.18 = (f32[8,256,128]{2,1,0:T(8,128)S(1)}, f32[8,256,128]{2,1,0:T(8,128)}, u32[]{:S(2)}, u32[]{:S(2)}) collective-permute-start(f32[8,256,128]{2,1,0:T(8,128)S(1)} %all-to-all-done.5), channel_id=1, source_target_pairs={{0,1},{1,0},{2,3},{3,2},{4,5},{5,4},{6,7},{7,6},{8,9},{9,8},{10,11... | collective-permute-start | bytes 3145736 | tf_op jit(solution)/shard_map/ppermute | solution.py:750
  294.8 18.9 %all-to-all-start.6 = ((f32[8,128,128]{2,1,0:T(8,128)}), f32[8,128,128]{2,1,0:T(8,128)S(1)}, u32[]{:S(2)}, u32[]{:S(2)}) async-start(f32[8,128,128]{2,1,0:T(8,128)} %get-tuple-element.139), calls=%async_computation.6 | async-start | bytes 1048576 | tf_op jit(solution)/shard_map/all_to_all | solution.py:494
  313.8 6.9 %copy-start.5 = (f32[8,128,128]{2,1,0:T(8,128)}, f32[8,128,128]{2,1,0:T(8,128)S(1)}, u32[]{:S(2)}) copy-start(f32[8,128,128]{2,1,0:T(8,128)S(1)} %all-to-all-done.6) | copy-start | bytes 1572868
  318.2 12.8 %collective-permute-start.22 = (f32[8,128,128]{2,1,0:T(8,128)S(1)}, f32[8,128,128]{2,1,0:T(8,128)S(1)}, u32[]{:S(2)}, u32[]{:S(2)}) collective-permute-start(f32[8,128,128]{2,1,0:T(8,128)S(1)} %all-to-all-done.6), channel_id=1, source_target_pairs={{0,2},{1,3},{2,0},{3,1},{4,6},{5,7},{6,4},{7,5},{8,10},{9,11},{10,... | collective-permute-start | bytes 1572872 | tf_op jit(solution)/shard_map/ppermute | solution.py:750
  319.9 14.6 %collective-permute-start.20 = (f32[8,256,128]{2,1,0:T(8,128)}, f32[8,256,128]{2,1,0:T(8,128)S(1)}, u32[]{:S(2)}, u32[]{:S(2)}) collective-permute-start(f32[8,256,128]{2,1,0:T(8,128)} %collective-permute-done.19), channel_id=1, source_target_pairs={{0,1},{1,0},{2,3},{3,2},{4,5},{5,4},{6,7},{7,6},{8,9},{9,8},{10,11... | collective-permute-start | bytes 3145736 | tf_op jit(solution)/shard_map/ppermute | solution.py:750
  320.7 13.8 %collective-permute-start.21 = (f32[8,128,128]{2,1,0:T(8,128)S(1)}, f32[8,128,128]{2,1,0:T(8,128)}, u32[]{:S(2)}, u32[]{:S(2)}) collective-permute-start(f32[8,128,128]{2,1,0:T(8,128)S(1)} %all-to-all-done.6), channel_id=1, source_target_pairs={{0,1},{1,0},{2,3},{3,2},{4,5},{5,4},{6,7},{7,6},{8,9},{9,8},{10,11... | collective-permute-start | bytes 1572872 | tf_op jit(solution)/shard_map/ppermute | solution.py:750
  331.0 2.9 copy-start.14
  331.0 3.6 collective-permute-start.23
  334.5 1.0 copy-start.6

commit v9 on v8

--- a/solution.py
+++ b/solution.py
@@ -73,7 +73,7 @@
 
 
 def fill_kernel(
-    base, here, above, below, top, bottom, sides, marks, table_high, table_low,
+    base, here, above, below, sides, marks, table_high, table_low, top, bottom,
     spectrum, alternate, edge, punched, once, high, low, folded,
 ):
     step_rows, cols, length = here.shape
@@ -124,6 +124,12 @@
         (above, step > 0, 0, top),
         (below, step < last, step_rows + SWEEPS, bottom),
     ):
+        if outer is None:
+            for r in range(SWEEPS):
+                punch_row(offset + r, edge_rows, r)
+                punch_sides(offset + r)
+            continue
+
         @pl.when(inside)
         def _():
             for r in range(SWEEPS):
@@ -250,8 +256,15 @@
     before = lambda i, b: (jnp.maximum(b[i] * pairs - 1, 0), 0, 0)
     after = lambda i, b: (jnp.minimum((b[i] + 1) * pairs, last), 0, 0)
     padded = (step_rows + 2 * SWEEPS, cols + 2 * MARGIN, length)
+    ends = 4 + len(arrays)
+
+    def kernel(*refs):
+        if len(arrays) == 4:
+            refs = refs[:ends] + (None, None) + refs[ends:]
+        fill_kernel(*refs)
+
     return pl.pallas_call(
-        fill_kernel,
+        kernel,
         grid_spec=pltpu.PrefetchScalarGridSpec(
             num_scalar_prefetch=1,
             grid=(len(starts),),
@@ -349,16 +362,15 @@
             place(count + planes, jnp.zeros((block, width), jnp.float32) + corner[...])
 
 
-def packed_section(col, kept, got, first, table_pair, table_rows, marks, rim, corner, before, offsets, shape, closing):
+def packed_section(col, kept, got, first, table_pair, table_rows, weights, rim, corner, before, offsets, shape, closing):
     _, cols, half = kept.shape
     count = table_rows.shape[0]
-    planes, block, width = len(marks), offsets[1], offsets[-1]
+    planes, block, width = weights.shape[0], offsets[1], offsets[-1]
     gx, gy = shape
     opening = before is None
     step_rows = 4
     layers = count + (planes + 1 if closing else 0)
     whole = lambda array: pl.BlockSpec(array.shape, lambda i: (0,) * array.ndim)
-    weights = jnp.stack([table_rows[:, m] for m in marks])
     arrays = rounded_parts(table_pair.T) + rounded_parts(table_rows[:, :half].T)
     arrays += (() if opening else (before,)) + ((rim, corner[None]) if closing else ())
     out = jax.ShapeDtypeStruct((layers, block // (gx * gy), gx, width), jnp.float32)
@@ -405,11 +417,10 @@
     given_first, kept_first = (1 - core) * pair_rows, core * pair_rows
     inner = parts[0].start >= SWEEPS and parts[0].stop <= pair_rows - SWEEPS
     side_columns = jnp.pad(sides, ((0, 0),) + FREE)
-    blank = jnp.zeros((SWEEPS, cols + 2 * SWEEPS, length), jnp.float32)
-    ends = (blank, blank) if inner else end_faces(intensity, sides)
+    ends = () if inner else end_faces(intensity, sides)
 
     def fill(some, start):
-        arrays = tuple(ends) + (side_columns,) + constants
+        arrays = (side_columns,) + constants + tuple(ends)
         return list(filled_spectrum(intensity, arrays, start, some))
 
     given, kept = [fill(parts[:1], given_first)], []
@@ -423,6 +434,10 @@
     table_cols = lax.dynamic_slice_in_dim(table, col * cols, cols, 0)
     kept_rows = lax.dynamic_slice_in_dim(table, row * rows + kept_first, pair_rows, 0)
     marks = [rows * (m + 1) for m in range(slabs)]
+    if all(start % gx == 0 for start in [pair_rows] + [part.start for part in parts]):
+        weights = [jnp.asarray(cosine_table(length)[:count, marks].T) for count in counts]
+    else:
+        weights = [jnp.stack([kept_rows[part, m] for m in marks]) for part in parts]
     mates = lax.dynamic_slice_in_dim(main, (col + 1 - 2 * core) * cols, cols, 0)
     table_pair = jnp.concatenate([table_cols[:, :half], mates], axis=0)
     table_parts = main.reshape(gx, 2, pair_rows, half) / 6.0
@@ -466,7 +481,7 @@
             corner = jnp.pad(corner, (0, width - half - 1))
 
         *packed, side = packed_section(
-            col, held, got, sum(counts[1:c]), table_pair, kept_rows[parts[c]], marks,
+            col, held, got, sum(counts[1:c]), table_pair, kept_rows[parts[c]], weights[c],
             rim, corner, side, offsets, (gx, gy), closing,
         )
     lines = sent_lines(exchanged(packed), counts[-1], lines)

time: 366 us -> 362 us (0.989)
  no operation moved by 1% of the time
where the time goes in v9:
time: 362 us; the launch traced here: 360 us
  Pallas kernels  123 us (34%)
  waiting for transfers between devices  115 us (32%)
  starting transfers between devices  42.2 us (12%)
  blocking collectives  32.5 us (9%)
  local copies, waits for them, and re-layouts  31.3 us (9%)
  other arithmetic  9.64 us (3%)
  matrix products  5.31 us (1%)
    pallas_call x4, Pallas kernels, filled_spectrum(): pl.pallas_call(kernel, grid_spec=pltpu.PrefetchScalarGridSpec(num_scalar_...  66.1 us
    ppermute x9, waiting for transfers between devices, gathered(): pieces[place ^ bit] = lax.ppermute(pieces[place], 'gy', swap(peers, bit))  35.6 us
    all_to_all x1, blocking collectives, on_device(): piece = lax.all_to_all(messages, 'gx', 0, 0, tiled=True)  32.5 us
    pallas_call x1, Pallas kernels, result_block(): pl.pallas_call(lambda *refs: result_kernel(offsets, own, devices, groups,...  28.7 us
    all_to_all x3, waiting for transfers between devices, sent_lines(): return lax.all_to_all(lines, 'gx', 0, 0, tiled=True)  27.8 us
    pallas_call x3, Pallas kernels, packed_section(): pl.pallas_call(lambda *refs: section_kernel(offsets, planes, opening, clo...  19.2 us
    all_to_all x1, waiting for transfers between devices, on_device(): lax.all_to_all(jnp.concatenate(turned, axis=3), ('gy', 'gx'), 0, 0, tiled...  18.2 us
    ppermute x9, waiting for transfers between devices, exchanged(): lax.ppermute(packed[p], 'gy', swap(gy, p))  18 us
  transfers between devices with their start and end apart: 30, of which 13 were waited for; matrix products, arithmetic and copies ran while one was open for 9% of the time, Pallas kernels for 20%

profile of v9, /device:TPU:0, one launch (start us, length us, event | category | flops | bytes accessed | tf_op | source)
XLA Modules:
  0.0 360.3 jit_solution(9559247013188464218)
XLA Ops:
  0.0 1.8 fusion.33
  2.3 2.0 collective-permute-start.1
  4.3 3.6 shard_map.82.refs_5_
  8.5 2.4 collective-permute-done.1
  11.2 1.6 pad.12.refs_4_
  12.8 16.2 %shard_map.84 = (f32[16,128,256]{2,1,0:T(8,128)}, f32[16,256]{1,0:T(8,128)}, f32[128,128]{1,0:T(8,128)}) custom-call(s32[2]{0:T(128)} %get-tuple-element.174.refs_0_, f32[64,128,512]{2,1,0:T(8,128)} %refs_3_.7, f32[64,128,512]{2,1,0:T(8,128)} %refs_3_.7, f32[64,128,512]{2,1,0:T(8,128)} %refs_3_.7, f32[64,16,512]{2,1,0:T(8,128)} %pad.12.refs_4_, ...), custom_call_target="tpu_custom_call" | custom-call | flops 1610612736 | bytes 6291456 | tf_op jit(solution)/shard_map/pallas_call | solution.py:266
  29.0 1.3 fusion.32
  31.4 0.9 constant_dynamic-slice_fusion.4
  33.3 2.3 collective-permute-start.3
  35.9 3.3 collective-permute-start.4
  39.2 0.8 fusion.10
  39.9 16.2 %shard_map.83 = (f32[16,128,256]{2,1,0:T(8,128)}, f32[16,256]{1,0:T(8,128)}, f32[128,128]{1,0:T(8,128)}) custom-call(s32[2]{0:T(128)} %get-tuple-element.173.refs_0_, f32[64,128,512]{2,1,0:T(8,128)} %refs_3_.7, f32[64,128,512]{2,1,0:T(8,128)} %refs_3_.7, f32[64,128,512]{2,1,0:T(8,128)} %refs_3_.7, f32[64,16,512]{2,1,0:T(8,128)} %pad.12.refs_4_, ...), custom_call_target="tpu_custom_call" | custom-call | flops 1610612736 | bytes 6291456 | tf_op jit(solution)/shard_map/pallas_call | solution.py:266
  56.2 7.8 %shard_map.85 = (f32[16,2,8,640]{3,2,1,0:T(8,128)}, f32[16,2,8,640]{3,2,1,0:T(8,128)}, f32[16,2,8,640]{3,2,1,0:T(8,128)}, f32[16,2,8,640]{3,2,1,0:T(8,128)}, f32[4,64,640]{2,1,0:T(8,128)}) custom-call(s32[1]{0:T(128)} %bitcast.3.refs_0_, f32[4,16]{1,0:T(4,128)} %constant.132.clone.refs_1_, f32[16,128,256]{2,1,0:T(8,128)} %get-tuple-element.74.refs_2_, ...), custom_call_target="tpu_custom_call" | custom-call | flops 1610612736 | bytes 8388608 | tf_op jit(solution)/shard_map/pallas_call | solution.py:379
  63.9 1.9 collective-permute-start.6
  65.9 1.0 copy.78.refs_8_
  66.9 0.9 copy.79.refs_9_
  69.0 16.8 %shard_map.87 = (f32[16,128,256]{2,1,0:T(8,128)}, f32[16,256]{1,0:T(8,128)}, f32[128,128]{1,0:T(8,128)}) custom-call(s32[2]{0:T(128)} %pad_add_fusion.4.refs_0_, f32[64,128,512]{2,1,0:T(8,128)} %refs_3_.7, f32[64,128,512]{2,1,0:T(8,128)} %refs_3_.7, f32[64,128,512]{2,1,0:T(8,128)} %refs_3_.7, f32[64,16,512]{2,1,0:T(8,128)} %pad.12.refs_4_, ...), custom_call_target="tpu_custom_call" | custom-call | flops 1610612736 | bytes 6291456 | tf_op jit(solution)/shard_map/pallas_call | solution.py:266
  85.8 16.9 %shard_map.86 = (f32[16,128,256]{2,1,0:T(8,128)}, f32[16,256]{1,0:T(8,128)}, f32[128,128]{1,0:T(8,128)}) custom-call(s32[2]{0:T(128)} %pad_add_fusion.3.refs_0_, f32[64,128,512]{2,1,0:T(8,128)} %refs_3_.7, f32[64,128,512]{2,1,0:T(8,128)} %refs_3_.7, f32[64,128,512]{2,1,0:T(8,128)} %refs_3_.7, f32[64,16,512]{2,1,0:T(8,128)} %pad.12.refs_4_, ...), custom_call_target="tpu_custom_call" | custom-call | flops 1610612736 | bytes 6291456 | tf_op jit(solution)/shard_map/pallas_call | solution.py:266
  102.8 0.8 copy-done.8
  104.0 1.2 add.178
  105.3 1.7 copy.82
  107.1 4.5 %all-to-all-start = ((f32[8,2,32,640]{3,1,2,0:T(2,128)}), f32[8,2,32,640]{3,1,2,0:T(2,128)}, u32[]{:S(2)}, u32[]{:S(2)}) async-start(f32[8,2,32,640]{3,1,2,0:T(2,128)} %copy.82), calls=%async_computation | async-start | bytes 2621440 | tf_op jit(solution)/shard_map/all_to_all | solution.py:782
  111.6 0.8 constant_dynamic-slice_fusion.1
  112.6 1.2 concatenate.75
  113.9 0.8 fusion.11
  114.7 1.3 copy-done
  116.1 5.5 %shard_map.88 = (f32[8,2,8,640]{3,2,1,0:T(8,128)}, f32[8,2,8,640]{3,2,1,0:T(8,128)}, f32[8,2,8,640]{3,2,1,0:T(8,128)}, f32[8,2,8,640]{3,2,1,0:T(8,128)}, f32[4,64,640]{2,1,0:T(8,128)}) custom-call(s32[1]{0:T(128)} %bitcast.3.refs_0_, f32[4,8]{1,0:T(4,128)} %constant.133.clone.refs_1_, f32[16,128,256]{2,1,0:T(8,128)} %get-tuple-element.104.refs_2_, ...), custom_call_target="tpu_custom_call" | custom-call | flops 805306368 | bytes 4194304 | tf_op jit(solution)/shard_map/pallas_call | solution.py:379
  122.0 1.9 collective-permute-start.9
  124.8 0.9 fusion.13.refs_9_
  126.3 6.0 %shard_map.89 = (f32[13,2,8,640]{3,2,1,0:T(8,128)}, f32[13,2,8,640]{3,2,1,0:T(8,128)}, f32[13,2,8,640]{3,2,1,0:T(8,128)}, f32[13,2,8,640]{3,2,1,0:T(8,128)}, f32[4,64,640]{2,1,0:T(8,128)}) custom-call(s32[1]{0:T(128)} %bitcast.3.refs_0_, f32[4,8]{1,0:T(4,128)} %constant.133.clone.refs_1_, f32[16,128,256]{2,1,0:T(8,128)} %get-tuple-element.104.refs_2_, ...), custom_call_target="tpu_custom_call" | custom-call | flops 805306368 | bytes 4194304 | tf_op jit(solution)/shard_map/pallas_call | solution.py:379
  132.3 1.8 collective-permute-start.12
  134.5 4.8 %collective-permute-done.11 = f32[8,2,8,640]{3,2,1,0:T(8,128)S(1)} collective-permute-done((f32[8,2,8,640]{3,2,1,0:T(8,128)}, f32[8,2,8,640]{3,2,1,0:T(8,128)S(1)}, u32[]{:S(2)}, u32[]{:S(2)}) %collective-permute-start.11) | collective-permute-done | bytes 327712 | tf_op jit(solution)/shard_map/ppermute | solution.py:772
  139.4 4.0 %all-to-all-done = f32[8,2,32,640]{3,1,2,0:T(2,128)} async-done(((f32[8,2,32,640]{3,1,2,0:T(2,128)}), f32[8,2,32,640]{3,1,2,0:T(2,128)}, u32[]{:S(2)}, u32[]{:S(2)}) %all-to-all-start) | async-done | bytes 1310752 | tf_op jit(solution)/shard_map/all_to_all | solution.py:782
  143.5 1.2 copy.84
  144.6 3.6 %all-to-all-start.1 = ((f32[8,2,16,640]{3,1,2,0:T(2,128)}), f32[8,2,16,640]{3,1,2,0:T(2,128)S(1)}, u32[]{:S(2)}, u32[]{:S(2)}) async-start(f32[8,2,16,640]{3,1,2,0:T(2,128)} %copy.84), calls=%async_computation.1 | async-start | bytes 1310720 | tf_op jit(solution)/shard_map/all_to_all | solution.py:782
  148.3 3.0 collective-permute-done.12
  151.3 10.1 %collective-permute-done.14 = f32[13,2,8,640]{3,2,1,0:T(8,128)S(1)} collective-permute-done((f32[13,2,8,640]{3,2,1,0:T(8,128)}, f32[13,2,8,640]{3,2,1,0:T(8,128)S(1)}, u32[]{:S(2)}, u32[]{:S(2)}) %collective-permute-start.14) | collective-permute-done | bytes 532512 | tf_op jit(solution)/shard_map/ppermute | solution.py:772
  161.6 4.1 %all-to-all-done.1 = f32[8,2,16,640]{3,1,2,0:T(2,128)S(1)} async-done(((f32[8,2,16,640]{3,1,2,0:T(2,128)}), f32[8,2,16,640]{3,1,2,0:T(2,128)S(1)}, u32[]{:S(2)}, u32[]{:S(2)}) %all-to-all-start.1) | async-done | bytes 655392 | tf_op jit(solution)/shard_map/all_to_all | solution.py:782
  165.8 1.3 copy.86
  167.1 3.6 %all-to-all-start.2 = ((f32[8,2,21,640]{3,1,2,0:T(2,128)}), f32[8,2,21,640]{3,1,2,0:T(2,128)S(1)}, u32[]{:S(2)}, u32[]{:S(2)}) async-start(f32[8,2,21,640]{3,1,2,0:T(2,128)} %copy.86), calls=%async_computation.2 | async-start | bytes 1720320 | tf_op jit(solution)/shard_map/all_to_all | solution.py:782
  170.9 2.1 convolution_bitcast_fusion
  173.0 19.7 %all-to-all-done.2 = f32[8,2,21,640]{3,1,2,0:T(2,128)S(1)} async-done(((f32[8,2,21,640]{3,1,2,0:T(2,128)}), f32[8,2,21,640]{3,1,2,0:T(2,128)S(1)}, u32[]{:S(2)}, u32[]{:S(2)}) %all-to-all-start.2) | async-done | bytes 860192 | tf_op jit(solution)/shard_map/all_to_all | solution.py:782
  193.5 0.8 fusion.1
  194.3 1.0 copy.120
  195.5 2.4 concatenate.80
  197.9 4.1 %all-to-all-start.3 = ((f32[32,2,2,1280]{3,2,1,0:T(2,128)}), f32[32,2,2,1280]{3,2,1,0:T(2,128)S(1)}, u32[]{:S(2)}, u32[]{:S(2)}) async-start(f32[32,2,2,1280]{3,2,1,0:T(2,128)} %concatenate.80), calls=%async_computation.3 | async-start | bytes 1310720 | tf_op jit(solution)/shard_map/all_to_all | solution.py:493
  202.7 18.2 %all-to-all-done.3 = f32[32,2,2,1280]{3,2,1,0:T(2,128)S(1)} async-done(((f32[32,2,2,1280]{3,2,1,0:T(2,128)}), f32[32,2,2,1280]{3,2,1,0:T(2,128)S(1)}, u32[]{:S(2)}, u32[]{:S(2)}) %all-to-all-start.3) | async-done | bytes 655392 | tf_op jit(solution)/shard_map/all_to_all | solution.py:493
  220.9 1.0 copy.89
  221.9 5.5 %shard_map.90 = (f32[8,288,128]{2,1,0:T(8,128)}, f32[8,256,128]{2,1,0:T(8,128)}, f32[8,128,128]{2,1,0:T(8,128)}) custom-call(f32[2,256,640]{2,1,0:T(8,128)} %bitcast.140, f32[2,64,1280]{2,1,0:T(8,128)} %bitcast.149, f32[2,5,640]{2,1,0:T(8,128)} %copy_multiply_fusion.refs_2_), custom_call_target="tpu_custom_call" | custom-call | tf_op jit(solution)/shard_map/pallas_call | solution.py:628
  227.4 32.5 %all_to_all.35 = f32[8,288,128]{2,1,0:T(8,128)S(1)} all-to-all(f32[8,288,128]{2,1,0:T(8,128)} %get-tuple-element.131), channel_id=1, replica_groups=mesh['gx'=8,'gy'=4] {'gx'}, dimensions={0} | all-to-all | bytes 2359296 | tf_op jit(solution)/shard_map/all_to_all | solution.py:509
  259.9 1.2 collective-permute-start.16
  261.0 3.6 all-to-all-start.5
  264.8 21.4 %collective-permute-done.16 = f32[8,288,128]{2,1,0:T(8,128)} collective-permute-done((f32[8,288,128]{2,1,0:T(8,128)S(1)}, f32[8,288,128]{2,1,0:T(8,128)}, u32[]{:S(2)}, u32[]{:S(2)}) %collective-permute-start.16) | collective-permute-done | bytes 1179680 | tf_op jit(solution)/shard_map/ppermute | solution.py:765
  288.2 1.9 all-to-all-done.5
  290.7 4.0 %all-to-all-start.6 = ((f32[8,128,128]{2,1,0:T(8,128)}), f32[8,128,128]{2,1,0:T(8,128)S(1)}, u32[]{:S(2)}, u32[]{:S(2)}) async-start(f32[8,128,128]{2,1,0:T(8,128)} %get-tuple-element.139), calls=%async_computation.6 | async-start | bytes 1048576 | tf_op jit(solution)/shard_map/all_to_all | solution.py:509
  294.7 0.9 slice_bitcast_fusion.9
  295.6 0.9 slice_bitcast_fusion.8
  296.5 0.9 slice_bitcast_fusion.2
  298.3 11.3 %all-to-all-done.6 = f32[8,128,128]{2,1,0:T(8,128)S(1)} async-done(((f32[8,128,128]{2,1,0:T(8,128)}), f32[8,128,128]{2,1,0:T(8,128)S(1)}, u32[]{:S(2)}, u32[]{:S(2)}) %all-to-all-start.6) | async-done | bytes 524320 | tf_op jit(solution)/shard_map/all_to_all | solution.py:509
  309.6 4.4 %collective-permute-done.19 = f32[8,256,128]{2,1,0:T(8,128)} collective-permute-done((f32[8,256,128]{2,1,0:T(8,128)S(1)}, f32[8,256,128]{2,1,0:T(8,128)}, u32[]{:S(2)}, u32[]{:S(2)}) %collective-permute-start.19) | collective-permute-done | bytes 1048608 | tf_op jit(solution)/shard_map/ppermute | solution.py:765
  314.0 1.7 collective-permute-start.22
  317.1 9.7 %collective-permute-done.22 = f32[8,128,128]{2,1,0:T(8,128)S(1)} collective-permute-done((f32[8,128,128]{2,1,0:T(8,128)S(1)}, f32[8,128,128]{2,1,0:T(8,128)S(1)}, u32[]{:S(2)}, u32[]{:S(2)}) %collective-permute-start.22) | collective-permute-done | bytes 524320 | tf_op jit(solution)/shard_map/ppermute | solution.py:765
  330.4 1.0 copy-done.6
  331.4 28.7 %shard_map.91 = f32[64,128,512]{2,1,0:T(8,128)} custom-call(s32[4]{0:T(128)} %pad_add_fusion.refs_0_, f32[64,640]{1,0:T(8,128)} %bitcast.155, f32[64,256]{1,0:T(8,128)} %slice.306.refs_2_, f32[128,128]{1,0:T(8,128)} %pad.14.refs_3_, bf16[128,256]{1,0:T(8,128)(2,1)} %fusion.15.refs_4_, bf16[256,256]{1,0:T(8,128)(2,1)} %fusion.7.refs_5_, ...), custom_call_target="tpu_custom_call" | custom-call | tf_op jit(solution)/shard_map/pallas_call | solution.py:736
  (157 shorter events, 18.3 us)
Async XLA Ops:
  1.8 6.7 %collective-permute-start = (f32[64,2,512]{2,1,0:T(2,128)S(1)}, f32[64,2,512]{2,1,0:T(2,128)S(1)}, u32[]{:S(2)}, u32[]{:S(2)}) collective-permute-start(f32[64,2,512]{2,1,0:T(2,128)S(1)} %get-tuple-element.145), channel_id=1, source_target_pairs={{0,1},{1,2},{2,3},{3,0},{4,5},{5,6},{6,7},{7,4},{8,9},{9,10},{10,1... | collective-permute-start | bytes 786440 | tf_op jit(solution)/shard_map/ppermute | solution.py:30
  2.3 8.6 %collective-permute-start.1 = (f32[64,2,512]{2,1,0:T(2,128)S(1)}, f32[64,2,512]{2,1,0:T(2,128)S(1)}, u32[]{:S(2)}, u32[]{:S(2)}) collective-permute-start(f32[64,2,512]{2,1,0:T(2,128)S(1)} %get-tuple-element.146), channel_id=1, source_target_pairs={{1,0},{2,1},{3,2},{0,3},{5,4},{6,5},{7,6},{4,7},{9,8},{10,9},{11,1... | collective-permute-start | bytes 786440 | tf_op jit(solution)/shard_map/ppermute | solution.py:31
  29.0 27.2 %collective-permute-start.2 = (f32[16,128,256]{2,1,0:T(8,128)}, f32[16,128,256]{2,1,0:T(8,128)}, u32[]{:S(2)}, u32[]{:S(2)}) collective-permute-start(f32[16,128,256]{2,1,0:T(8,128)} %get-tuple-element.78), channel_id=1, source_target_pairs={{0,1},{1,0},{2,3},{3,2},{4,5},{5,4},{6,7},{7,6},{8,9},{9,8},{10,11... | collective-permute-start | bytes 6291464 | tf_op jit(solution)/shard_map/ppermute | solution.py:464
  30.3 1.1 copy-start.4
  33.3 32.6 %collective-permute-start.3 = (f32[2,132,512]{2,0,1:T(2,128)S(1)}, f32[2,132,512]{2,0,1:T(2,128)S(1)}, u32[]{:S(2)}, u32[]{:S(2)}) collective-permute-start(f32[2,132,512]{2,0,1:T(2,128)S(1)} %pad_maximum_fusion), channel_id=1, source_target_pairs={{0,4},{4,8},{8,12},{12,16},{16,20},{20,24},{24,28},{28,0},{1,5},{5... | collective-permute-start | bytes 1622024 | tf_op jit(solution)/shard_map/ppermute | solution.py:40
  35.9 31.0 %collective-permute-start.4 = (f32[2,132,512]{2,0,1:T(2,128)S(1)}, f32[2,132,512]{2,0,1:T(2,128)S(1)}, u32[]{:S(2)}, u32[]{:S(2)}) collective-permute-start(f32[2,132,512]{2,0,1:T(2,128)S(1)} %pad_maximum_fusion.1), channel_id=1, source_target_pairs={{4,0},{8,4},{12,8},{16,12},{20,16},{24,20},{28,24},{0,28},{5,1},{9... | collective-permute-start | bytes 1622024 | tf_op jit(solution)/shard_map/ppermute | solution.py:40
  63.9 38.8 %collective-permute-start.5 = (f32[16,2,8,640]{3,2,1,0:T(8,128)}, f32[16,2,8,640]{3,2,1,0:T(8,128)S(1)}, u32[]{:S(2)}, u32[]{:S(2)}) collective-permute-start(f32[16,2,8,640]{3,2,1,0:T(8,128)} %get-tuple-element.89), channel_id=1, source_target_pairs={{0,1},{1,0},{2,3},{3,2},{4,5},{5,4},{6,7},{7,6},{8,9},{9,8},{10,11... | collective-permute-start | bytes 1966088 | tf_op jit(solution)/shard_map/ppermute | solution.py:772
  63.9 38.8 %collective-permute-start.6 = (f32[16,2,8,640]{3,2,1,0:T(8,128)}, f32[16,2,8,640]{3,2,1,0:T(8,128)S(1)}, u32[]{:S(2)}, u32[]{:S(2)}) collective-permute-start(f32[16,2,8,640]{3,2,1,0:T(8,128)} %get-tuple-element.90), channel_id=1, source_target_pairs={{0,2},{1,3},{2,0},{3,1},{4,6},{5,7},{6,4},{7,5},{8,10},{9,11},{10,... | collective-permute-start | bytes 1966088 | tf_op jit(solution)/shard_map/ppermute | solution.py:772
  65.8 36.9 %collective-permute-start.7 = (f32[16,2,8,640]{3,2,1,0:T(8,128)}, f32[16,2,8,640]{3,2,1,0:T(8,128)S(1)}, u32[]{:S(2)}, u32[]{:S(2)}) collective-permute-start(f32[16,2,8,640]{3,2,1,0:T(8,128)} %get-tuple-element.91), channel_id=1, source_target_pairs={{0,3},{1,2},{2,1},{3,0},{4,7},{5,6},{6,5},{7,4},{8,11},{9,10},{10,... | collective-permute-start | bytes 1966088 | tf_op jit(solution)/shard_map/ppermute | solution.py:772
  85.8 18.2 %copy-start.7 = (f32[16,2,8,640]{3,2,1,0:T(8,128)S(1)}, f32[16,2,8,640]{3,2,1,0:T(8,128)}, u32[]{:S(2)}) copy-start(f32[16,2,8,640]{3,2,1,0:T(8,128)} %get-tuple-element.92) | copy-start | bytes 1966084
  102.7 0.9 copy-start.8
  102.7 1.0 copy-start.9
  103.8 1.4 copy-start.10
  103.8 10.9 %collective-permute-start.8 = (f32[16,128,256]{2,1,0:T(8,128)}, f32[16,128,256]{2,1,0:T(8,128)S(1)}, u32[]{:S(2)}, u32[]{:S(2)}) collective-permute-start(f32[16,128,256]{2,1,0:T(8,128)} %get-tuple-element.105), channel_id=1, source_target_pairs={{0,1},{1,0},{2,3},{3,2},{4,5},{5,4},{6,7},{7,6},{8,9},{9,8},{10,11... | collective-permute-start | bytes 6291464 | tf_op jit(solution)/shard_map/ppermute | solution.py:464
  107.1 36.4 %all-to-all-start = ((f32[8,2,32,640]{3,1,2,0:T(2,128)}), f32[8,2,32,640]{3,1,2,0:T(2,128)}, u32[]{:S(2)}, u32[]{:S(2)}) async-start(f32[8,2,32,640]{3,1,2,0:T(2,128)} %copy.82), calls=%async_computation | async-start | bytes 2621440 | tf_op jit(solution)/shard_map/all_to_all | solution.py:782
  114.7 1.3 copy-start
  116.0 5.6 %copy-start.16 = (f32[128,128]{1,0:T(8,128)S(1)}, f32[128,128]{1,0:T(8,128)}, u32[]{:S(2)}) copy-start(f32[128,128]{1,0:T(8,128)} %get-tuple-element.117) | copy-start | bytes 196612
  116.0 5.6 %copy-start.17 = (f32[128,128]{1,0:T(8,128)S(1)}, f32[128,128]{1,0:T(8,128)}, u32[]{:S(2)}) copy-start(f32[128,128]{1,0:T(8,128)} %get-tuple-element.119) | copy-start | bytes 196612
  116.0 5.6 %copy-start.18 = (f32[128,128]{1,0:T(8,128)S(1)}, f32[128,128]{1,0:T(8,128)}, u32[]{:S(2)}) copy-start(f32[128,128]{1,0:T(8,128)} %get-tuple-element.120) | copy-start | bytes 196612
  116.0 5.6 %copy-start.19 = (f32[128,128]{1,0:T(8,128)S(1)}, f32[128,128]{1,0:T(8,128)}, u32[]{:S(2)}) copy-start(f32[128,128]{1,0:T(8,128)} %get-tuple-element.118) | copy-start | bytes 196612
  116.0 8.2 %copy-start.20 = (f32[16,256]{1,0:T(8,128)S(1)}, f32[16,256]{1,0:T(8,128)}, u32[]{:S(2)}) copy-start(f32[16,256]{1,0:T(8,128)} %get-tuple-element.121) | copy-start | bytes 49156
  116.1 8.2 %copy-start.21 = (f32[16,256]{1,0:T(8,128)S(1)}, f32[16,256]{1,0:T(8,128)}, u32[]{:S(2)}) copy-start(f32[16,256]{1,0:T(8,128)} %get-tuple-element.123) | copy-start | bytes 49156
  116.1 8.2 %copy-start.22 = (f32[16,256]{1,0:T(8,128)S(1)}, f32[16,256]{1,0:T(8,128)}, u32[]{:S(2)}) copy-start(f32[16,256]{1,0:T(8,128)} %get-tuple-element.124) | copy-start | bytes 49156
  116.1 8.2 %copy-start.23 = (f32[16,256]{1,0:T(8,128)S(1)}, f32[16,256]{1,0:T(8,128)}, u32[]{:S(2)}) copy-start(f32[16,256]{1,0:T(8,128)} %get-tuple-element.122) | copy-start | bytes 49156
  122.0 12.1 %collective-permute-start.9 = (f32[8,2,8,640]{3,2,1,0:T(8,128)}, f32[8,2,8,640]{3,2,1,0:T(8,128)S(1)}, u32[]{:S(2)}, u32[]{:S(2)}) collective-permute-start(f32[8,2,8,640]{3,2,1,0:T(8,128)} %get-tuple-element.112), channel_id=1, source_target_pairs={{0,2},{1,3},{2,0},{3,1},{4,6},{5,7},{6,4},{7,5},{8,10},{9,11},{10,... | collective-permute-start | bytes 983048 | tf_op jit(solution)/shard_map/ppermute | solution.py:772
  123.9 10.6 %collective-permute-start.10 = (f32[8,2,8,640]{3,2,1,0:T(8,128)}, f32[8,2,8,640]{3,2,1,0:T(8,128)S(1)}, u32[]{:S(2)}, u32[]{:S(2)}) collective-permute-start(f32[8,2,8,640]{3,2,1,0:T(8,128)} %get-tuple-element.113), channel_id=1, source_target_pairs={{0,1},{1,0},{2,3},{3,2},{4,5},{5,4},{6,7},{7,6},{8,9},{9,8},{10,11... | collective-permute-start | bytes 983048 | tf_op jit(solution)/shard_map/ppermute | solution.py:772
  123.9 15.4 %collective-permute-start.11 = (f32[8,2,8,640]{3,2,1,0:T(8,128)}, f32[8,2,8,640]{3,2,1,0:T(8,128)S(1)}, u32[]{:S(2)}, u32[]{:S(2)}) collective-permute-start(f32[8,2,8,640]{3,2,1,0:T(8,128)} %get-tuple-element.114), channel_id=1, source_target_pairs={{0,3},{1,2},{2,1},{3,0},{4,7},{5,6},{6,5},{7,4},{8,11},{9,10},{10,... | collective-permute-start | bytes 983048 | tf_op jit(solution)/shard_map/ppermute | solution.py:772
  126.3 8.1 %copy-start.15 = (f32[8,2,8,640]{3,2,1,0:T(8,128)S(1)}, f32[8,2,8,640]{3,2,1,0:T(8,128)}, u32[]{:S(2)}) copy-start(f32[8,2,8,640]{3,2,1,0:T(8,128)} %get-tuple-element.111) | copy-start | bytes 983044
  132.3 18.9 %collective-permute-start.12 = (f32[13,2,8,640]{3,2,1,0:T(8,128)}, f32[13,2,8,640]{3,2,1,0:T(8,128)S(1)}, u32[]{:S(2)}, u32[]{:S(2)}) collective-permute-start(f32[13,2,8,640]{3,2,1,0:T(8,128)} %get-tuple-element.126), channel_id=1, source_target_pairs={{0,2},{1,3},{2,0},{3,1},{4,6},{5,7},{6,4},{7,5},{8,10},{9,11},{10,... | collective-permute-start | bytes 1597448 | tf_op jit(solution)/shard_map/ppermute | solution.py:772
  134.1 17.2 %collective-permute-start.13 = (f32[13,2,8,640]{3,2,1,0:T(8,128)}, f32[13,2,8,640]{3,2,1,0:T(8,128)S(1)}, u32[]{:S(2)}, u32[]{:S(2)}) collective-permute-start(f32[13,2,8,640]{3,2,1,0:T(8,128)} %get-tuple-element.127), channel_id=1, source_target_pairs={{0,1},{1,0},{2,3},{3,2},{4,5},{5,4},{6,7},{7,6},{8,9},{9,8},{10,11... | collective-permute-start | bytes 1597448 | tf_op jit(solution)/shard_map/ppermute | solution.py:772
  134.1 27.3 %collective-permute-start.14 = (f32[13,2,8,640]{3,2,1,0:T(8,128)}, f32[13,2,8,640]{3,2,1,0:T(8,128)S(1)}, u32[]{:S(2)}, u32[]{:S(2)}) collective-permute-start(f32[13,2,8,640]{3,2,1,0:T(8,128)} %get-tuple-element.128), channel_id=1, source_target_pairs={{0,3},{1,2},{2,1},{3,0},{4,7},{5,6},{6,5},{7,4},{8,11},{9,10},{10,... | collective-permute-start | bytes 1597448 | tf_op jit(solution)/shard_map/ppermute | solution.py:772
  139.4 11.8 %copy-start.11 = (f32[13,2,8,640]{3,2,1,0:T(8,128)S(1)}, f32[13,2,8,640]{3,2,1,0:T(8,128)}, u32[]{:S(2)}) copy-start(f32[13,2,8,640]{3,2,1,0:T(8,128)} %get-tuple-element.125) | copy-start | bytes 1597444
  144.6 21.1 %all-to-all-start.1 = ((f32[8,2,16,640]{3,1,2,0:T(2,128)}), f32[8,2,16,640]{3,1,2,0:T(2,128)S(1)}, u32[]{:S(2)}, u32[]{:S(2)}) async-start(f32[8,2,16,640]{3,1,2,0:T(2,128)} %copy.84), calls=%async_computation.1 | async-start | bytes 1310720 | tf_op jit(solution)/shard_map/all_to_all | solution.py:782
  161.6 9.1 %copy-start.13 = (f32[8,2,32,256]{3,2,1,0:T(8,128)S(1)}, f32[8,2,32,256]{3,2,1,0:T(8,128)}, u32[]{:S(2)}) copy-start(f32[8,2,32,256]{3,2,1,0:T(8,128)} %constant.144) | copy-start | bytes 1572868
  161.6 9.1 %copy-start.14 = (f32[8,2,32,256]{3,2,1,0:T(8,128)S(1)}, f32[8,2,32,256]{3,2,1,0:T(8,128)}, u32[]{:S(2)}) copy-start(f32[8,2,32,256]{3,2,1,0:T(8,128)} %constant.142) | copy-start | bytes 1572868
  167.1 25.6 %all-to-all-start.2 = ((f32[8,2,21,640]{3,1,2,0:T(2,128)}), f32[8,2,21,640]{3,1,2,0:T(2,128)S(1)}, u32[]{:S(2)}, u32[]{:S(2)}) async-start(f32[8,2,21,640]{3,1,2,0:T(2,128)} %copy.86), calls=%async_computation.2 | async-start | bytes 1720320 | tf_op jit(solution)/shard_map/all_to_all | solution.py:782
  194.3 1.1 copy-start.2
  197.9 23.0 %all-to-all-start.3 = ((f32[32,2,2,1280]{3,2,1,0:T(2,128)}), f32[32,2,2,1280]{3,2,1,0:T(2,128)S(1)}, u32[]{:S(2)}, u32[]{:S(2)}) async-start(f32[32,2,2,1280]{3,2,1,0:T(2,128)} %concatenate.80), calls=%async_computation.3 | async-start | bytes 1310720 | tf_op jit(solution)/shard_map/all_to_all | solution.py:493
  259.9 30.9 %copy-start.1 = (f32[8,288,128]{2,1,0:T(8,128)}, f32[8,288,128]{2,1,0:T(8,128)S(1)}, u32[]{:S(2)}) copy-start(f32[8,288,128]{2,1,0:T(8,128)S(1)} %all_to_all.35) | copy-start | bytes 3538948
  259.9 26.4 %collective-permute-start.16 = (f32[8,288,128]{2,1,0:T(8,128)S(1)}, f32[8,288,128]{2,1,0:T(8,128)}, u32[]{:S(2)}, u32[]{:S(2)}) collective-permute-start(f32[8,288,128]{2,1,0:T(8,128)S(1)} %all_to_all.35), channel_id=1, source_target_pairs={{0,2},{1,3},{2,0},{3,1},{4,6},{5,7},{6,4},{7,5},{8,10},{9,11},{10,... | collective-permute-start | bytes 3538952 | tf_op jit(solution)/shard_map/ppermute | solution.py:765
  261.0 29.1 %all-to-all-start.5 = ((f32[8,256,128]{2,1,0:T(8,128)}), f32[8,256,128]{2,1,0:T(8,128)S(1)}, u32[]{:S(2)}, u32[]{:S(2)}) async-start(f32[8,256,128]{2,1,0:T(8,128)} %get-tuple-element.134), calls=%async_computation.5 | async-start | bytes 2097152 | tf_op jit(solution)/shard_map/all_to_all | solution.py:509
  264.6 25.6 %collective-permute-start.15 = (f32[8,288,128]{2,1,0:T(8,128)S(1)}, f32[8,288,128]{2,1,0:T(8,128)}, u32[]{:S(2)}, u32[]{:S(2)}) collective-permute-start(f32[8,288,128]{2,1,0:T(8,128)S(1)} %all_to_all.35), channel_id=1, source_target_pairs={{0,1},{1,0},{2,3},{3,2},{4,5},{5,4},{6,7},{7,6},{8,9},{9,8},{10,11... | collective-permute-start | bytes 3538952 | tf_op jit(solution)/shard_map/ppermute | solution.py:765
  286.2 10.3 %collective-permute-start.17 = (f32[8,288,128]{2,1,0:T(8,128)}, f32[8,288,128]{2,1,0:T(8,128)}, u32[]{:S(2)}, u32[]{:S(2)}) collective-permute-start(f32[8,288,128]{2,1,0:T(8,128)} %collective-permute-done.16), channel_id=1, source_target_pairs={{0,1},{1,0},{2,3},{3,2},{4,5},{5,4},{6,7},{7,6},{8,9},{9,8},{10,11... | collective-permute-start | bytes 3538952 | tf_op jit(solution)/shard_map/ppermute | solution.py:765
  290.2 7.3 %copy-start.3 = (f32[8,256,128]{2,1,0:T(8,128)}, f32[8,256,128]{2,1,0:T(8,128)S(1)}, u32[]{:S(2)}) copy-start(f32[8,256,128]{2,1,0:T(8,128)S(1)} %all-to-all-done.5) | copy-start | bytes 3145732
  290.2 23.8 %collective-permute-start.19 = (f32[8,256,128]{2,1,0:T(8,128)S(1)}, f32[8,256,128]{2,1,0:T(8,128)}, u32[]{:S(2)}, u32[]{:S(2)}) collective-permute-start(f32[8,256,128]{2,1,0:T(8,128)S(1)} %all-to-all-done.5), channel_id=1, source_target_pairs={{0,2},{1,3},{2,0},{3,1},{4,6},{5,7},{6,4},{7,5},{8,10},{9,11},{10,... | collective-permute-start | bytes 3145736 | tf_op jit(solution)/shard_map/ppermute | solution.py:765
  290.7 23.3 %collective-permute-start.18 = (f32[8,256,128]{2,1,0:T(8,128)S(1)}, f32[8,256,128]{2,1,0:T(8,128)}, u32[]{:S(2)}, u32[]{:S(2)}) collective-permute-start(f32[8,256,128]{2,1,0:T(8,128)S(1)} %all-to-all-done.5), channel_id=1, source_target_pairs={{0,1},{1,0},{2,3},{3,2},{4,5},{5,4},{6,7},{7,6},{8,9},{9,8},{10,11... | collective-permute-start | bytes 3145736 | tf_op jit(solution)/shard_map/ppermute | solution.py:765
  290.7 18.9 %all-to-all-start.6 = ((f32[8,128,128]{2,1,0:T(8,128)}), f32[8,128,128]{2,1,0:T(8,128)S(1)}, u32[]{:S(2)}, u32[]{:S(2)}) async-start(f32[8,128,128]{2,1,0:T(8,128)} %get-tuple-element.139), calls=%async_computation.6 | async-start | bytes 1048576 | tf_op jit(solution)/shard_map/all_to_all | solution.py:509
  309.6 6.9 %copy-start.5 = (f32[8,128,128]{2,1,0:T(8,128)}, f32[8,128,128]{2,1,0:T(8,128)S(1)}, u32[]{:S(2)}) copy-start(f32[8,128,128]{2,1,0:T(8,128)S(1)} %all-to-all-done.6) | copy-start | bytes 1572868
  314.0 12.8 %collective-permute-start.22 = (f32[8,128,128]{2,1,0:T(8,128)S(1)}, f32[8,128,128]{2,1,0:T(8,128)S(1)}, u32[]{:S(2)}, u32[]{:S(2)}) collective-permute-start(f32[8,128,128]{2,1,0:T(8,128)S(1)} %all-to-all-done.6), channel_id=1, source_target_pairs={{0,2},{1,3},{2,0},{3,1},{4,6},{5,7},{6,4},{7,5},{8,10},{9,11},{10,... | collective-permute-start | bytes 1572872 | tf_op jit(solution)/shard_map/ppermute | solution.py:765
  315.7 14.7 %collective-permute-start.20 = (f32[8,256,128]{2,1,0:T(8,128)}, f32[8,256,128]{2,1,0:T(8,128)S(1)}, u32[]{:S(2)}, u32[]{:S(2)}) collective-permute-start(f32[8,256,128]{2,1,0:T(8,128)} %collective-permute-done.19), channel_id=1, source_target_pairs={{0,1},{1,0},{2,3},{3,2},{4,5},{5,4},{6,7},{7,6},{8,9},{9,8},{10,11... | collective-permute-start | bytes 3145736 | tf_op jit(solution)/shard_map/ppermute | solution.py:765
  316.5 13.9 %collective-permute-start.21 = (f32[8,128,128]{2,1,0:T(8,128)S(1)}, f32[8,128,128]{2,1,0:T(8,128)}, u32[]{:S(2)}, u32[]{:S(2)}) collective-permute-start(f32[8,128,128]{2,1,0:T(8,128)S(1)} %all-to-all-done.6), channel_id=1, source_target_pairs={{0,1},{1,0},{2,3},{3,2},{4,5},{5,4},{6,7},{7,6},{8,9},{9,8},{10,11... | collective-permute-start | bytes 1572872 | tf_op jit(solution)/shard_map/ppermute | solution.py:765
  326.8 2.9 copy-start.12
  326.8 3.6 collective-permute-start.23
  330.4 1.0 copy-start.6

commit v10 on v9

--- a/solution.py
+++ b/solution.py
@@ -21,15 +21,12 @@
     return up, [(j, i) for i, j in up]
 
 
-FREE = ((8 - SWEEPS, 8 - SWEEPS), (0, 0))
-
-
 def side_faces(block):
     cols = block.shape[1]
     right, left = ring("gy")
     before = lax.ppermute(block[:, cols - SWEEPS :], "gy", right)
     after = lax.ppermute(block[:, :SWEEPS], "gy", left)
-    return jnp.concatenate([before, after], axis=1)
+    return before, after
 
 
 def end_faces(block, sides):
@@ -362,16 +359,16 @@
             place(count + planes, jnp.zeros((block, width), jnp.float32) + corner[...])
 
 
-def packed_section(col, kept, got, first, table_pair, table_rows, weights, rim, corner, before, offsets, shape, closing):
+def packed_section(col, kept, got, first, pair_table, row_table, weights, rim, corner, before, offsets, shape, closing):
     _, cols, half = kept.shape
-    count = table_rows.shape[0]
+    count = row_table[0].shape[1]
     planes, block, width = weights.shape[0], offsets[1], offsets[-1]
     gx, gy = shape
     opening = before is None
     step_rows = 4
     layers = count + (planes + 1 if closing else 0)
     whole = lambda array: pl.BlockSpec(array.shape, lambda i: (0,) * array.ndim)
-    arrays = rounded_parts(table_pair.T) + rounded_parts(table_rows[:, :half].T)
+    arrays = pair_table + row_table
     arrays += (() if opening else (before,)) + ((rim, corner[None]) if closing else ())
     out = jax.ShapeDtypeStruct((layers, block // (gx * gy), gx, width), jnp.float32)
     outs = [out] * gy + [jax.ShapeDtypeStruct((planes, block, width), jnp.float32)]
@@ -412,11 +409,20 @@
     parts = row_parts(pair_rows)
     counts = [part.stop - part.start for part in parts]
     core = lax.rem(col, 2)
+    given_first, kept_first = (1 - core) * pair_rows, core * pair_rows
     constants = fill_constants(intensity, template, row, col, cosine_table(length)[:, :half])
-    sides = side_faces(intensity)
-    given_first, kept_first = (1 - core) * pair_rows, core * pair_rows
+    table_cols = lax.dynamic_slice_in_dim(table, col * cols, cols, 0)
+    kept_rows = lax.dynamic_slice_in_dim(table, row * rows + kept_first, pair_rows, 0)
+    mates = lax.dynamic_slice_in_dim(main, (col + 1 - 2 * core) * cols, cols, 0)
+    table_pair = jnp.concatenate([table_cols[:, :half], mates], axis=0)
+    pair_tables = rounded_parts(table_pair.T), rounded_parts(kept_rows[parts[0], :half].T)
+    before, after = side_faces(intensity)
+    before, after, pair_tables = lax.optimization_barrier((before, after, pair_tables))
+    sides = jnp.concatenate([before, after], axis=1)
     inner = parts[0].start >= SWEEPS and parts[0].stop <= pair_rows - SWEEPS
-    side_columns = jnp.pad(sides, ((0, 0),) + FREE)
+    room = 8 - SWEEPS
+    side_columns = jnp.pad(before, ((0, 0), (room, 8), (0, 0)))
+    side_columns = side_columns + jnp.pad(after, ((0, 0), (8, room), (0, 0)))
     ends = () if inner else end_faces(intensity, sides)
 
     def fill(some, start):
@@ -431,15 +437,11 @@
     kept.append(fill(parts[:1], kept_first))
     ends = outer
 
-    table_cols = lax.dynamic_slice_in_dim(table, col * cols, cols, 0)
-    kept_rows = lax.dynamic_slice_in_dim(table, row * rows + kept_first, pair_rows, 0)
     marks = [rows * (m + 1) for m in range(slabs)]
     if all(start % gx == 0 for start in [pair_rows] + [part.start for part in parts]):
         weights = [jnp.asarray(cosine_table(length)[:count, marks].T) for count in counts]
     else:
         weights = [jnp.stack([kept_rows[part, m] for m in marks]) for part in parts]
-    mates = lax.dynamic_slice_in_dim(main, (col + 1 - 2 * core) * cols, cols, 0)
-    table_pair = jnp.concatenate([table_cols[:, :half], mates], axis=0)
     table_parts = main.reshape(gx, 2, pair_rows, half) / 6.0
     table_parts = jnp.where(core == 0, table_parts, table_parts[:, ::-1])
     table_parts = [table_parts[:, :, part] for part in parts]
@@ -480,8 +482,11 @@
             corner = corner + jnp.einsum("aj,a->j", ordered_rows, edge[:, half], precision=HIGH)
             corner = jnp.pad(corner, (0, width - half - 1))
 
+        row_table = pair_tables[1]
+        if c > 0:
+            row_table = rounded_parts(kept_rows[parts[c], :half].T)
         *packed, side = packed_section(
-            col, held, got, sum(counts[1:c]), table_pair, kept_rows[parts[c]], weights[c],
+            col, held, got, sum(counts[1:c]), pair_tables[0], row_table, weights[c],
             rim, corner, side, offsets, (gx, gy), closing,
         )
     lines = sent_lines(exchanged(packed), counts[-1], lines)

time: 362 us -> 360 us (level)
  no operation moved by 1% of the time
where the time goes in v10:
time: 360 us; the launch traced here: 359 us
  Pallas kernels  123 us (34%)
  waiting for transfers between devices  114 us (32%)
  starting transfers between devices  41.3 us (11%)
  blocking collectives  32.5 us (9%)
  local copies, waits for them, and re-layouts  30.9 us (9%)
  other arithmetic  11.3 us (3%)
  matrix products  5.32 us (1%)
    pallas_call x4, Pallas kernels, filled_spectrum(): pl.pallas_call(kernel, grid_spec=pltpu.PrefetchScalarGridSpec(num_scalar_...  66.2 us
    ppermute x9, waiting for transfers between devices, gathered(): pieces[place ^ bit] = lax.ppermute(pieces[place], 'gy', swap(peers, bit))  35.6 us
    all_to_all x1, blocking collectives, on_device(): piece = lax.all_to_all(messages, 'gx', 0, 0, tiled=True)  32.5 us
    pallas_call x1, Pallas kernels, result_block(): pl.pallas_call(lambda *refs: result_kernel(offsets, own, devices, groups,...  28.7 us
    all_to_all x3, waiting for transfers between devices, sent_lines(): return lax.all_to_all(lines, 'gx', 0, 0, tiled=True)  28.2 us
    pallas_call x3, Pallas kernels, packed_section(): pl.pallas_call(lambda *refs: section_kernel(offsets, planes, opening, clo...  19.3 us
    all_to_all x1, waiting for transfers between devices, on_device(): lax.all_to_all(jnp.concatenate(turned, axis=3), ('gy', 'gx'), 0, 0, tiled...  18.2 us
    ppermute x9, waiting for transfers between devices, exchanged(): lax.ppermute(packed[p], 'gy', swap(gy, p))  17.5 us
  transfers between devices with their start and end apart: 30, of which 13 were waited for; matrix products, arithmetic and copies ran while one was open for 9% of the time, Pallas kernels for 20%

profile of v10, /device:TPU:0, one launch (start us, length us, event | category | flops | bytes accessed | tf_op | source)
XLA Modules:
  0.0 359.2 jit_solution(7740594935739747506)
XLA Ops:
  0.0 1.9 fusion.33
  1.9 2.4 collective-permute-start.1
  5.7 3.6 shard_map.82.refs_5_
  9.3 0.9 constant_dynamic-slice_fusion.4
  10.9 1.1 collective-permute-done
  12.2 1.6 pad_add_fusion.refs_4_
  13.9 16.2 %shard_map.84 = (f32[16,128,256]{2,1,0:T(8,128)}, f32[16,256]{1,0:T(8,128)}, f32[128,128]{1,0:T(8,128)}) custom-call(s32[2]{0:T(128)} %get-tuple-element.186.refs_0_, f32[64,128,512]{2,1,0:T(8,128)} %refs_3_.7, f32[64,128,512]{2,1,0:T(8,128)} %refs_3_.7, f32[64,128,512]{2,1,0:T(8,128)} %refs_3_.7, f32[64,16,512]{2,1,0:T(8,128)} %pad_add_fusion.refs_4_, ...), custom_call_target="tpu_custom_call" | custom-call | flops 1610612736 | bytes 6291456 | tf_op jit(solution)/shard_map/pallas_call | solution.py:263
  30.1 1.3 fusion.32
  32.5 1.6 collective-permute-start.3
  34.3 3.5 collective-permute-start.4
  37.8 16.3 %shard_map.83 = (f32[16,128,256]{2,1,0:T(8,128)}, f32[16,256]{1,0:T(8,128)}, f32[128,128]{1,0:T(8,128)}) custom-call(s32[2]{0:T(128)} %get-tuple-element.185.refs_0_, f32[64,128,512]{2,1,0:T(8,128)} %refs_3_.7, f32[64,128,512]{2,1,0:T(8,128)} %refs_3_.7, f32[64,128,512]{2,1,0:T(8,128)} %refs_3_.7, f32[64,16,512]{2,1,0:T(8,128)} %pad_add_fusion.refs_4_, ...), custom_call_target="tpu_custom_call" | custom-call | flops 1610612736 | bytes 6291456 | tf_op jit(solution)/shard_map/pallas_call | solution.py:263
  54.0 1.3 copy-done.24
  55.3 7.8 %shard_map.85 = (f32[16,2,8,640]{3,2,1,0:T(8,128)}, f32[16,2,8,640]{3,2,1,0:T(8,128)}, f32[16,2,8,640]{3,2,1,0:T(8,128)}, f32[16,2,8,640]{3,2,1,0:T(8,128)}, f32[4,64,640]{2,1,0:T(8,128)}) custom-call(s32[1]{0:T(128)} %bitcast.3.refs_0_, f32[4,16]{1,0:T(4,128)} %constant.132.clone.refs_1_, f32[16,128,256]{2,1,0:T(8,128)} %get-tuple-element.82.refs_2_, ...), custom_call_target="tpu_custom_call" | custom-call | flops 1610612736 | bytes 8388608 | tf_op jit(solution)/shard_map/pallas_call | solution.py:376
  63.2 1.5 collective-permute-start.6
  65.0 0.9 copy.78.refs_8_
  65.9 0.9 copy.79.refs_9_
  68.1 16.8 %shard_map.87 = (f32[16,128,256]{2,1,0:T(8,128)}, f32[16,256]{1,0:T(8,128)}, f32[128,128]{1,0:T(8,128)}) custom-call(s32[2]{0:T(128)} %pad_add_fusion.5.refs_0_, f32[64,128,512]{2,1,0:T(8,128)} %refs_3_.7, f32[64,128,512]{2,1,0:T(8,128)} %refs_3_.7, f32[64,128,512]{2,1,0:T(8,128)} %refs_3_.7, f32[64,16,512]{2,1,0:T(8,128)} %pad_add_fusion.refs_4_, ...), custom_call_target="tpu_custom_call" | custom-call | flops 1610612736 | bytes 6291456 | tf_op jit(solution)/shard_map/pallas_call | solution.py:263
  84.9 16.9 %shard_map.86 = (f32[16,128,256]{2,1,0:T(8,128)}, f32[16,256]{1,0:T(8,128)}, f32[128,128]{1,0:T(8,128)}) custom-call(s32[2]{0:T(128)} %pad_add_fusion.4.refs_0_, f32[64,128,512]{2,1,0:T(8,128)} %refs_3_.7, f32[64,128,512]{2,1,0:T(8,128)} %refs_3_.7, f32[64,128,512]{2,1,0:T(8,128)} %refs_3_.7, f32[64,16,512]{2,1,0:T(8,128)} %pad_add_fusion.refs_4_, ...), custom_call_target="tpu_custom_call" | custom-call | flops 1610612736 | bytes 6291456 | tf_op jit(solution)/shard_map/pallas_call | solution.py:263
  101.8 0.8 copy-done.8
  103.2 1.2 add.184
  104.5 1.7 copy.82
  106.3 4.5 %all-to-all-start = ((f32[8,2,32,640]{3,1,2,0:T(2,128)}), f32[8,2,32,640]{3,1,2,0:T(2,128)}, u32[]{:S(2)}, u32[]{:S(2)}) async-start(f32[8,2,32,640]{3,1,2,0:T(2,128)} %copy.82), calls=%async_computation | async-start | bytes 2621440 | tf_op jit(solution)/shard_map/all_to_all | solution.py:787
  110.8 0.8 constant_dynamic-slice_fusion.1
  111.8 1.2 concatenate.75
  113.1 0.8 fusion.11
  113.9 1.3 copy-done
  115.3 5.5 %shard_map.88 = (f32[8,2,8,640]{3,2,1,0:T(8,128)}, f32[8,2,8,640]{3,2,1,0:T(8,128)}, f32[8,2,8,640]{3,2,1,0:T(8,128)}, f32[8,2,8,640]{3,2,1,0:T(8,128)}, f32[4,64,640]{2,1,0:T(8,128)}) custom-call(s32[1]{0:T(128)} %bitcast.3.refs_0_, f32[4,8]{1,0:T(4,128)} %constant.133.clone.refs_1_, f32[16,128,256]{2,1,0:T(8,128)} %get-tuple-element.116.refs_2_, ...), custom_call_target="tpu_custom_call" | custom-call | flops 805306368 | bytes 4194304 | tf_op jit(solution)/shard_map/pallas_call | solution.py:376
  121.2 1.6 collective-permute-start.9
  124.0 1.0 fusion.13.refs_9_
  125.5 6.0 %shard_map.89 = (f32[13,2,8,640]{3,2,1,0:T(8,128)}, f32[13,2,8,640]{3,2,1,0:T(8,128)}, f32[13,2,8,640]{3,2,1,0:T(8,128)}, f32[13,2,8,640]{3,2,1,0:T(8,128)}, f32[4,64,640]{2,1,0:T(8,128)}) custom-call(s32[1]{0:T(128)} %bitcast.3.refs_0_, f32[4,8]{1,0:T(4,128)} %constant.133.clone.refs_1_, f32[16,128,256]{2,1,0:T(8,128)} %get-tuple-element.116.refs_2_, ...), custom_call_target="tpu_custom_call" | custom-call | flops 805306368 | bytes 4194304 | tf_op jit(solution)/shard_map/pallas_call | solution.py:376
  131.5 1.5 collective-permute-start.12
  133.7 4.5 %collective-permute-done.11 = f32[8,2,8,640]{3,2,1,0:T(8,128)S(1)} collective-permute-done((f32[8,2,8,640]{3,2,1,0:T(8,128)}, f32[8,2,8,640]{3,2,1,0:T(8,128)S(1)}, u32[]{:S(2)}, u32[]{:S(2)}) %collective-permute-start.11) | collective-permute-done | bytes 327712 | tf_op jit(solution)/shard_map/ppermute | solution.py:777
  138.3 4.3 %all-to-all-done = f32[8,2,32,640]{3,1,2,0:T(2,128)} async-done(((f32[8,2,32,640]{3,1,2,0:T(2,128)}), f32[8,2,32,640]{3,1,2,0:T(2,128)}, u32[]{:S(2)}, u32[]{:S(2)}) %all-to-all-start) | async-done | bytes 1310752 | tf_op jit(solution)/shard_map/all_to_all | solution.py:787
  142.6 1.2 copy.84
  143.7 3.6 %all-to-all-start.1 = ((f32[8,2,16,640]{3,1,2,0:T(2,128)}), f32[8,2,16,640]{3,1,2,0:T(2,128)S(1)}, u32[]{:S(2)}, u32[]{:S(2)}) async-start(f32[8,2,16,640]{3,1,2,0:T(2,128)} %copy.84), calls=%async_computation.1 | async-start | bytes 1310720 | tf_op jit(solution)/shard_map/all_to_all | solution.py:787
  147.4 3.1 collective-permute-done.12
  150.5 9.9 %collective-permute-done.14 = f32[13,2,8,640]{3,2,1,0:T(8,128)S(1)} collective-permute-done((f32[13,2,8,640]{3,2,1,0:T(8,128)}, f32[13,2,8,640]{3,2,1,0:T(8,128)S(1)}, u32[]{:S(2)}, u32[]{:S(2)}) %collective-permute-start.14) | collective-permute-done | bytes 532512 | tf_op jit(solution)/shard_map/ppermute | solution.py:777
  160.6 4.2 %all-to-all-done.1 = f32[8,2,16,640]{3,1,2,0:T(2,128)S(1)} async-done(((f32[8,2,16,640]{3,1,2,0:T(2,128)}), f32[8,2,16,640]{3,1,2,0:T(2,128)S(1)}, u32[]{:S(2)}, u32[]{:S(2)}) %all-to-all-start.1) | async-done | bytes 655392 | tf_op jit(solution)/shard_map/all_to_all | solution.py:787
  164.9 1.3 copy.86
  166.2 3.6 %all-to-all-start.2 = ((f32[8,2,21,640]{3,1,2,0:T(2,128)}), f32[8,2,21,640]{3,1,2,0:T(2,128)S(1)}, u32[]{:S(2)}, u32[]{:S(2)}) async-start(f32[8,2,21,640]{3,1,2,0:T(2,128)} %copy.86), calls=%async_computation.2 | async-start | bytes 1720320 | tf_op jit(solution)/shard_map/all_to_all | solution.py:787
  170.0 2.1 convolution_bitcast_fusion
  172.1 19.7 %all-to-all-done.2 = f32[8,2,21,640]{3,1,2,0:T(2,128)S(1)} async-done(((f32[8,2,21,640]{3,1,2,0:T(2,128)}), f32[8,2,21,640]{3,1,2,0:T(2,128)S(1)}, u32[]{:S(2)}, u32[]{:S(2)}) %all-to-all-start.2) | async-done | bytes 860192 | tf_op jit(solution)/shard_map/all_to_all | solution.py:787
  192.6 0.8 fusion.1
  193.4 1.0 copy.120
  194.6 2.4 concatenate.80
  197.0 3.9 %all-to-all-start.3 = ((f32[32,2,2,1280]{3,2,1,0:T(2,128)}), f32[32,2,2,1280]{3,2,1,0:T(2,128)S(1)}, u32[]{:S(2)}, u32[]{:S(2)}) async-start(f32[32,2,2,1280]{3,2,1,0:T(2,128)} %concatenate.80), calls=%async_computation.3 | async-start | bytes 1310720 | tf_op jit(solution)/shard_map/all_to_all | solution.py:498
  201.6 18.2 %all-to-all-done.3 = f32[32,2,2,1280]{3,2,1,0:T(2,128)S(1)} async-done(((f32[32,2,2,1280]{3,2,1,0:T(2,128)}), f32[32,2,2,1280]{3,2,1,0:T(2,128)S(1)}, u32[]{:S(2)}, u32[]{:S(2)}) %all-to-all-start.3) | async-done | bytes 655392 | tf_op jit(solution)/shard_map/all_to_all | solution.py:498
  219.8 1.0 copy.89
  220.7 5.5 %shard_map.90 = (f32[8,288,128]{2,1,0:T(8,128)}, f32[8,256,128]{2,1,0:T(8,128)}, f32[8,128,128]{2,1,0:T(8,128)}) custom-call(f32[2,256,640]{2,1,0:T(8,128)} %bitcast.140, f32[2,64,1280]{2,1,0:T(8,128)} %bitcast.149, f32[2,5,640]{2,1,0:T(8,128)} %copy_multiply_fusion.refs_2_), custom_call_target="tpu_custom_call" | custom-call | tf_op jit(solution)/shard_map/pallas_call | solution.py:633
  226.2 32.5 %all_to_all.35 = f32[8,288,128]{2,1,0:T(8,128)S(1)} all-to-all(f32[8,288,128]{2,1,0:T(8,128)} %get-tuple-element.143), channel_id=1, replica_groups=mesh['gx'=8,'gy'=4] {'gx'}, dimensions={0} | all-to-all | bytes 2359296 | tf_op jit(solution)/shard_map/all_to_all | solution.py:514
  258.7 1.2 collective-permute-start.16
  259.9 3.6 all-to-all-start.5
  263.6 21.4 %collective-permute-done.16 = f32[8,288,128]{2,1,0:T(8,128)} collective-permute-done((f32[8,288,128]{2,1,0:T(8,128)S(1)}, f32[8,288,128]{2,1,0:T(8,128)}, u32[]{:S(2)}, u32[]{:S(2)}) %collective-permute-start.16) | collective-permute-done | bytes 1179680 | tf_op jit(solution)/shard_map/ppermute | solution.py:770
  287.1 1.9 all-to-all-done.5
  289.6 4.0 %all-to-all-start.6 = ((f32[8,128,128]{2,1,0:T(8,128)}), f32[8,128,128]{2,1,0:T(8,128)S(1)}, u32[]{:S(2)}, u32[]{:S(2)}) async-start(f32[8,128,128]{2,1,0:T(8,128)} %get-tuple-element.151), calls=%async_computation.6 | async-start | bytes 1048576 | tf_op jit(solution)/shard_map/all_to_all | solution.py:514
  293.5 0.9 slice_bitcast_fusion.9
  294.5 0.9 slice_bitcast_fusion.8
  295.4 0.9 slice_bitcast_fusion.2
  297.1 11.3 %all-to-all-done.6 = f32[8,128,128]{2,1,0:T(8,128)S(1)} async-done(((f32[8,128,128]{2,1,0:T(8,128)}), f32[8,128,128]{2,1,0:T(8,128)S(1)}, u32[]{:S(2)}, u32[]{:S(2)}) %all-to-all-start.6) | async-done | bytes 524320 | tf_op jit(solution)/shard_map/all_to_all | solution.py:514
  308.5 4.4 %collective-permute-done.19 = f32[8,256,128]{2,1,0:T(8,128)} collective-permute-done((f32[8,256,128]{2,1,0:T(8,128)S(1)}, f32[8,256,128]{2,1,0:T(8,128)}, u32[]{:S(2)}, u32[]{:S(2)}) %collective-permute-start.19) | collective-permute-done | bytes 1048608 | tf_op jit(solution)/shard_map/ppermute | solution.py:770
  312.9 1.7 collective-permute-start.22
  316.0 9.7 %collective-permute-done.22 = f32[8,128,128]{2,1,0:T(8,128)S(1)} collective-permute-done((f32[8,128,128]{2,1,0:T(8,128)S(1)}, f32[8,128,128]{2,1,0:T(8,128)S(1)}, u32[]{:S(2)}, u32[]{:S(2)}) %collective-permute-start.22) | collective-permute-done | bytes 524320 | tf_op jit(solution)/shard_map/ppermute | solution.py:770
  329.3 1.0 copy-done.6
  330.3 28.7 %shard_map.91 = f32[64,128,512]{2,1,0:T(8,128)} custom-call(s32[4]{0:T(128)} %pad_add_fusion.1.refs_0_, f32[64,640]{1,0:T(8,128)} %bitcast.155, f32[64,256]{1,0:T(8,128)} %slice.300.refs_2_, f32[128,128]{1,0:T(8,128)} %pad.19.refs_3_, bf16[128,256]{1,0:T(8,128)(2,1)} %fusion.15.refs_4_, bf16[256,256]{1,0:T(8,128)(2,1)} %fusion.7.refs_5_, ...), custom_call_target="tpu_custom_call" | custom-call | tf_op jit(solution)/shard_map/pallas_call | solution.py:741
  (159 shorter events, 19.5 us)
Async XLA Ops:
  0.0 4.3 %copy-start.4 = (f32[512,257]{0,1:T(8,128)S(1)}, f32[512,257]{0,1:T(8,128)}, u32[]{:S(2)}) copy-start(f32[512,257]{0,1:T(8,128)} %constant.129.clone) | copy-start | bytes 1579012
  1.9 9.1 %collective-permute-start.1 = (f32[64,2,512]{2,1,0:T(2,128)S(1)}, f32[64,2,512]{2,1,0:T(2,128)S(1)}, u32[]{:S(2)}, u32[]{:S(2)}) collective-permute-start(f32[64,2,512]{2,1,0:T(2,128)S(1)} %get-tuple-element.157), channel_id=1, source_target_pairs={{1,0},{2,1},{3,2},{0,3},{5,4},{6,5},{7,6},{4,7},{9,8},{10,9},{11,1... | collective-permute-start | bytes 786440 | tf_op jit(solution)/shard_map/ppermute | solution.py:28
  4.3 7.7 %collective-permute-start = (f32[64,2,512]{2,1,0:T(2,128)S(1)}, f32[64,2,512]{2,1,0:T(2,128)S(1)}, u32[]{:S(2)}, u32[]{:S(2)}) collective-permute-start(f32[64,2,512]{2,1,0:T(2,128)S(1)} %get-tuple-element.158), channel_id=1, source_target_pairs={{0,1},{1,2},{2,3},{3,0},{4,5},{5,6},{6,7},{7,4},{8,9},{9,10},{10,1... | collective-permute-start | bytes 786440 | tf_op jit(solution)/shard_map/ppermute | solution.py:27
  30.1 23.9 %collective-permute-start.2 = (f32[16,128,256]{2,1,0:T(8,128)}, f32[16,128,256]{2,1,0:T(8,128)S(1)}, u32[]{:S(2)}, u32[]{:S(2)}) collective-permute-start(f32[16,128,256]{2,1,0:T(8,128)} %get-tuple-element.86), channel_id=1, source_target_pairs={{0,1},{1,0},{2,3},{3,2},{4,5},{5,4},{6,7},{7,6},{8,9},{9,8},{10,11... | collective-permute-start | bytes 6291464 | tf_op jit(solution)/shard_map/ppermute | solution.py:466
  32.5 32.5 %collective-permute-start.3 = (f32[2,132,512]{2,0,1:T(2,128)S(1)}, f32[2,132,512]{2,0,1:T(2,128)S(1)}, u32[]{:S(2)}, u32[]{:S(2)}) collective-permute-start(f32[2,132,512]{2,0,1:T(2,128)S(1)} %pad_maximum_fusion), channel_id=1, source_target_pairs={{0,4},{4,8},{8,12},{12,16},{16,20},{20,24},{24,28},{28,0},{1,5},{5... | collective-permute-start | bytes 1622024 | tf_op jit(solution)/shard_map/ppermute | solution.py:37
  34.3 31.6 %collective-permute-start.4 = (f32[2,132,512]{2,0,1:T(2,128)S(1)}, f32[2,132,512]{2,0,1:T(2,128)S(1)}, u32[]{:S(2)}, u32[]{:S(2)}) collective-permute-start(f32[2,132,512]{2,0,1:T(2,128)S(1)} %pad_maximum_fusion.1), channel_id=1, source_target_pairs={{4,0},{8,4},{12,8},{16,12},{20,16},{24,20},{28,24},{0,28},{5,1},{9... | collective-permute-start | bytes 1622024 | tf_op jit(solution)/shard_map/ppermute | solution.py:37
  54.0 1.3 copy-start.24
  63.1 38.7 %collective-permute-start.5 = (f32[16,2,8,640]{3,2,1,0:T(8,128)}, f32[16,2,8,640]{3,2,1,0:T(8,128)S(1)}, u32[]{:S(2)}, u32[]{:S(2)}) collective-permute-start(f32[16,2,8,640]{3,2,1,0:T(8,128)} %get-tuple-element.101), channel_id=1, source_target_pairs={{0,1},{1,0},{2,3},{3,2},{4,5},{5,4},{6,7},{7,6},{8,9},{9,8},{10,11... | collective-permute-start | bytes 1966088 | tf_op jit(solution)/shard_map/ppermute | solution.py:777
  63.2 38.6 %collective-permute-start.6 = (f32[16,2,8,640]{3,2,1,0:T(8,128)}, f32[16,2,8,640]{3,2,1,0:T(8,128)S(1)}, u32[]{:S(2)}, u32[]{:S(2)}) collective-permute-start(f32[16,2,8,640]{3,2,1,0:T(8,128)} %get-tuple-element.102), channel_id=1, source_target_pairs={{0,2},{1,3},{2,0},{3,1},{4,6},{5,7},{6,4},{7,5},{8,10},{9,11},{10,... | collective-permute-start | bytes 1966088 | tf_op jit(solution)/shard_map/ppermute | solution.py:777
  64.7 37.1 %collective-permute-start.7 = (f32[16,2,8,640]{3,2,1,0:T(8,128)}, f32[16,2,8,640]{3,2,1,0:T(8,128)S(1)}, u32[]{:S(2)}, u32[]{:S(2)}) collective-permute-start(f32[16,2,8,640]{3,2,1,0:T(8,128)} %get-tuple-element.103), channel_id=1, source_target_pairs={{0,3},{1,2},{2,1},{3,0},{4,7},{5,6},{6,5},{7,4},{8,11},{9,10},{10,... | collective-permute-start | bytes 1966088 | tf_op jit(solution)/shard_map/ppermute | solution.py:777
  84.9 18.3 %copy-start.7 = (f32[16,2,8,640]{3,2,1,0:T(8,128)S(1)}, f32[16,2,8,640]{3,2,1,0:T(8,128)}, u32[]{:S(2)}) copy-start(f32[16,2,8,640]{3,2,1,0:T(8,128)} %get-tuple-element.104) | copy-start | bytes 1966084
  101.8 0.9 copy-start.8
  101.8 1.0 copy-start.9
  102.8 1.5 copy-start.10
  102.8 11.1 %collective-permute-start.8 = (f32[16,128,256]{2,1,0:T(8,128)}, f32[16,128,256]{2,1,0:T(8,128)S(1)}, u32[]{:S(2)}, u32[]{:S(2)}) collective-permute-start(f32[16,128,256]{2,1,0:T(8,128)} %get-tuple-element.117), channel_id=1, source_target_pairs={{0,1},{1,0},{2,3},{3,2},{4,5},{5,4},{6,7},{7,6},{8,9},{9,8},{10,11... | collective-permute-start | bytes 6291464 | tf_op jit(solution)/shard_map/ppermute | solution.py:466
  106.3 36.3 %all-to-all-start = ((f32[8,2,32,640]{3,1,2,0:T(2,128)}), f32[8,2,32,640]{3,1,2,0:T(2,128)}, u32[]{:S(2)}, u32[]{:S(2)}) async-start(f32[8,2,32,640]{3,1,2,0:T(2,128)} %copy.82), calls=%async_computation | async-start | bytes 2621440 | tf_op jit(solution)/shard_map/all_to_all | solution.py:787
  113.9 1.3 copy-start
  115.3 5.6 %copy-start.16 = (f32[128,128]{1,0:T(8,128)S(1)}, f32[128,128]{1,0:T(8,128)}, u32[]{:S(2)}) copy-start(f32[128,128]{1,0:T(8,128)} %get-tuple-element.129) | copy-start | bytes 196612
  115.3 5.6 %copy-start.17 = (f32[128,128]{1,0:T(8,128)S(1)}, f32[128,128]{1,0:T(8,128)}, u32[]{:S(2)}) copy-start(f32[128,128]{1,0:T(8,128)} %get-tuple-element.131) | copy-start | bytes 196612
  115.3 5.6 %copy-start.18 = (f32[128,128]{1,0:T(8,128)S(1)}, f32[128,128]{1,0:T(8,128)}, u32[]{:S(2)}) copy-start(f32[128,128]{1,0:T(8,128)} %get-tuple-element.132) | copy-start | bytes 196612
  115.3 5.6 %copy-start.19 = (f32[128,128]{1,0:T(8,128)S(1)}, f32[128,128]{1,0:T(8,128)}, u32[]{:S(2)}) copy-start(f32[128,128]{1,0:T(8,128)} %get-tuple-element.130) | copy-start | bytes 196612
  115.3 8.2 %copy-start.20 = (f32[16,256]{1,0:T(8,128)S(1)}, f32[16,256]{1,0:T(8,128)}, u32[]{:S(2)}) copy-start(f32[16,256]{1,0:T(8,128)} %get-tuple-element.133) | copy-start | bytes 49156
  115.3 8.2 %copy-start.21 = (f32[16,256]{1,0:T(8,128)S(1)}, f32[16,256]{1,0:T(8,128)}, u32[]{:S(2)}) copy-start(f32[16,256]{1,0:T(8,128)} %get-tuple-element.135) | copy-start | bytes 49156
  115.3 8.2 %copy-start.22 = (f32[16,256]{1,0:T(8,128)S(1)}, f32[16,256]{1,0:T(8,128)}, u32[]{:S(2)}) copy-start(f32[16,256]{1,0:T(8,128)} %get-tuple-element.136) | copy-start | bytes 49156
  115.3 8.2 %copy-start.23 = (f32[16,256]{1,0:T(8,128)S(1)}, f32[16,256]{1,0:T(8,128)}, u32[]{:S(2)}) copy-start(f32[16,256]{1,0:T(8,128)} %get-tuple-element.134) | copy-start | bytes 49156
  121.2 11.8 %collective-permute-start.9 = (f32[8,2,8,640]{3,2,1,0:T(8,128)}, f32[8,2,8,640]{3,2,1,0:T(8,128)S(1)}, u32[]{:S(2)}, u32[]{:S(2)}) collective-permute-start(f32[8,2,8,640]{3,2,1,0:T(8,128)} %get-tuple-element.124), channel_id=1, source_target_pairs={{0,2},{1,3},{2,0},{3,1},{4,6},{5,7},{6,4},{7,5},{8,10},{9,11},{10,... | collective-permute-start | bytes 983048 | tf_op jit(solution)/shard_map/ppermute | solution.py:777
  122.8 10.9 %collective-permute-start.10 = (f32[8,2,8,640]{3,2,1,0:T(8,128)}, f32[8,2,8,640]{3,2,1,0:T(8,128)S(1)}, u32[]{:S(2)}, u32[]{:S(2)}) collective-permute-start(f32[8,2,8,640]{3,2,1,0:T(8,128)} %get-tuple-element.125), channel_id=1, source_target_pairs={{0,1},{1,0},{2,3},{3,2},{4,5},{5,4},{6,7},{7,6},{8,9},{9,8},{10,11... | collective-permute-start | bytes 983048 | tf_op jit(solution)/shard_map/ppermute | solution.py:777
  122.8 15.4 %collective-permute-start.11 = (f32[8,2,8,640]{3,2,1,0:T(8,128)}, f32[8,2,8,640]{3,2,1,0:T(8,128)S(1)}, u32[]{:S(2)}, u32[]{:S(2)}) collective-permute-start(f32[8,2,8,640]{3,2,1,0:T(8,128)} %get-tuple-element.126), channel_id=1, source_target_pairs={{0,3},{1,2},{2,1},{3,0},{4,7},{5,6},{6,5},{7,4},{8,11},{9,10},{10,... | collective-permute-start | bytes 983048 | tf_op jit(solution)/shard_map/ppermute | solution.py:777
  125.5 8.1 %copy-start.15 = (f32[8,2,8,640]{3,2,1,0:T(8,128)S(1)}, f32[8,2,8,640]{3,2,1,0:T(8,128)}, u32[]{:S(2)}) copy-start(f32[8,2,8,640]{3,2,1,0:T(8,128)} %get-tuple-element.123) | copy-start | bytes 983044
  131.5 19.0 %collective-permute-start.12 = (f32[13,2,8,640]{3,2,1,0:T(8,128)}, f32[13,2,8,640]{3,2,1,0:T(8,128)S(1)}, u32[]{:S(2)}, u32[]{:S(2)}) collective-permute-start(f32[13,2,8,640]{3,2,1,0:T(8,128)} %get-tuple-element.138), channel_id=1, source_target_pairs={{0,2},{1,3},{2,0},{3,1},{4,6},{5,7},{6,4},{7,5},{8,10},{9,11},{10,... | collective-permute-start | bytes 1597448 | tf_op jit(solution)/shard_map/ppermute | solution.py:777
  133.0 17.5 %collective-permute-start.13 = (f32[13,2,8,640]{3,2,1,0:T(8,128)}, f32[13,2,8,640]{3,2,1,0:T(8,128)S(1)}, u32[]{:S(2)}, u32[]{:S(2)}) collective-permute-start(f32[13,2,8,640]{3,2,1,0:T(8,128)} %get-tuple-element.139), channel_id=1, source_target_pairs={{0,1},{1,0},{2,3},{3,2},{4,5},{5,4},{6,7},{7,6},{8,9},{9,8},{10,11... | collective-permute-start | bytes 1597448 | tf_op jit(solution)/shard_map/ppermute | solution.py:777
  133.0 27.4 %collective-permute-start.14 = (f32[13,2,8,640]{3,2,1,0:T(8,128)}, f32[13,2,8,640]{3,2,1,0:T(8,128)S(1)}, u32[]{:S(2)}, u32[]{:S(2)}) collective-permute-start(f32[13,2,8,640]{3,2,1,0:T(8,128)} %get-tuple-element.140), channel_id=1, source_target_pairs={{0,3},{1,2},{2,1},{3,0},{4,7},{5,6},{6,5},{7,4},{8,11},{9,10},{10,... | collective-permute-start | bytes 1597448 | tf_op jit(solution)/shard_map/ppermute | solution.py:777
  138.3 12.2 %copy-start.11 = (f32[13,2,8,640]{3,2,1,0:T(8,128)S(1)}, f32[13,2,8,640]{3,2,1,0:T(8,128)}, u32[]{:S(2)}) copy-start(f32[13,2,8,640]{3,2,1,0:T(8,128)} %get-tuple-element.137) | copy-start | bytes 1597444
  143.7 21.1 %all-to-all-start.1 = ((f32[8,2,16,640]{3,1,2,0:T(2,128)}), f32[8,2,16,640]{3,1,2,0:T(2,128)S(1)}, u32[]{:S(2)}, u32[]{:S(2)}) async-start(f32[8,2,16,640]{3,1,2,0:T(2,128)} %copy.84), calls=%async_computation.1 | async-start | bytes 1310720 | tf_op jit(solution)/shard_map/all_to_all | solution.py:787
  160.6 9.3 %copy-start.13 = (f32[8,2,32,256]{3,2,1,0:T(8,128)S(1)}, f32[8,2,32,256]{3,2,1,0:T(8,128)}, u32[]{:S(2)}) copy-start(f32[8,2,32,256]{3,2,1,0:T(8,128)} %constant.146) | copy-start | bytes 1572868
  160.6 9.3 %copy-start.14 = (f32[8,2,32,256]{3,2,1,0:T(8,128)S(1)}, f32[8,2,32,256]{3,2,1,0:T(8,128)}, u32[]{:S(2)}) copy-start(f32[8,2,32,256]{3,2,1,0:T(8,128)} %constant.144) | copy-start | bytes 1572868
  166.2 25.6 %all-to-all-start.2 = ((f32[8,2,21,640]{3,1,2,0:T(2,128)}), f32[8,2,21,640]{3,1,2,0:T(2,128)S(1)}, u32[]{:S(2)}, u32[]{:S(2)}) async-start(f32[8,2,21,640]{3,1,2,0:T(2,128)} %copy.86), calls=%async_computation.2 | async-start | bytes 1720320 | tf_op jit(solution)/shard_map/all_to_all | solution.py:787
  193.4 1.1 copy-start.2
  197.0 22.8 %all-to-all-start.3 = ((f32[32,2,2,1280]{3,2,1,0:T(2,128)}), f32[32,2,2,1280]{3,2,1,0:T(2,128)S(1)}, u32[]{:S(2)}, u32[]{:S(2)}) async-start(f32[32,2,2,1280]{3,2,1,0:T(2,128)} %concatenate.80), calls=%async_computation.3 | async-start | bytes 1310720 | tf_op jit(solution)/shard_map/all_to_all | solution.py:498
  258.7 30.9 %copy-start.1 = (f32[8,288,128]{2,1,0:T(8,128)}, f32[8,288,128]{2,1,0:T(8,128)S(1)}, u32[]{:S(2)}) copy-start(f32[8,288,128]{2,1,0:T(8,128)S(1)} %all_to_all.35) | copy-start | bytes 3538948
  258.7 26.4 %collective-permute-start.16 = (f32[8,288,128]{2,1,0:T(8,128)S(1)}, f32[8,288,128]{2,1,0:T(8,128)}, u32[]{:S(2)}, u32[]{:S(2)}) collective-permute-start(f32[8,288,128]{2,1,0:T(8,128)S(1)} %all_to_all.35), channel_id=1, source_target_pairs={{0,2},{1,3},{2,0},{3,1},{4,6},{5,7},{6,4},{7,5},{8,10},{9,11},{10,... | collective-permute-start | bytes 3538952 | tf_op jit(solution)/shard_map/ppermute | solution.py:770
  259.9 29.1 %all-to-all-start.5 = ((f32[8,256,128]{2,1,0:T(8,128)}), f32[8,256,128]{2,1,0:T(8,128)S(1)}, u32[]{:S(2)}, u32[]{:S(2)}) async-start(f32[8,256,128]{2,1,0:T(8,128)} %get-tuple-element.146), calls=%async_computation.5 | async-start | bytes 2097152 | tf_op jit(solution)/shard_map/all_to_all | solution.py:514
  263.5 25.6 %collective-permute-start.15 = (f32[8,288,128]{2,1,0:T(8,128)S(1)}, f32[8,288,128]{2,1,0:T(8,128)}, u32[]{:S(2)}, u32[]{:S(2)}) collective-permute-start(f32[8,288,128]{2,1,0:T(8,128)S(1)} %all_to_all.35), channel_id=1, source_target_pairs={{0,1},{1,0},{2,3},{3,2},{4,5},{5,4},{6,7},{7,6},{8,9},{9,8},{10,11... | collective-permute-start | bytes 3538952 | tf_op jit(solution)/shard_map/ppermute | solution.py:770
  285.1 10.3 %collective-permute-start.17 = (f32[8,288,128]{2,1,0:T(8,128)}, f32[8,288,128]{2,1,0:T(8,128)}, u32[]{:S(2)}, u32[]{:S(2)}) collective-permute-start(f32[8,288,128]{2,1,0:T(8,128)} %collective-permute-done.16), channel_id=1, source_target_pairs={{0,1},{1,0},{2,3},{3,2},{4,5},{5,4},{6,7},{7,6},{8,9},{9,8},{10,11... | collective-permute-start | bytes 3538952 | tf_op jit(solution)/shard_map/ppermute | solution.py:770
  289.0 7.3 %copy-start.3 = (f32[8,256,128]{2,1,0:T(8,128)}, f32[8,256,128]{2,1,0:T(8,128)S(1)}, u32[]{:S(2)}) copy-start(f32[8,256,128]{2,1,0:T(8,128)S(1)} %all-to-all-done.5) | copy-start | bytes 3145732
  289.0 23.8 %collective-permute-start.19 = (f32[8,256,128]{2,1,0:T(8,128)S(1)}, f32[8,256,128]{2,1,0:T(8,128)}, u32[]{:S(2)}, u32[]{:S(2)}) collective-permute-start(f32[8,256,128]{2,1,0:T(8,128)S(1)} %all-to-all-done.5), channel_id=1, source_target_pairs={{0,2},{1,3},{2,0},{3,1},{4,6},{5,7},{6,4},{7,5},{8,10},{9,11},{10,... | collective-permute-start | bytes 3145736 | tf_op jit(solution)/shard_map/ppermute | solution.py:770
  289.6 23.3 %collective-permute-start.18 = (f32[8,256,128]{2,1,0:T(8,128)S(1)}, f32[8,256,128]{2,1,0:T(8,128)}, u32[]{:S(2)}, u32[]{:S(2)}) collective-permute-start(f32[8,256,128]{2,1,0:T(8,128)S(1)} %all-to-all-done.5), channel_id=1, source_target_pairs={{0,1},{1,0},{2,3},{3,2},{4,5},{5,4},{6,7},{7,6},{8,9},{9,8},{10,11... | collective-permute-start | bytes 3145736 | tf_op jit(solution)/shard_map/ppermute | solution.py:770
  289.6 18.9 %all-to-all-start.6 = ((f32[8,128,128]{2,1,0:T(8,128)}), f32[8,128,128]{2,1,0:T(8,128)S(1)}, u32[]{:S(2)}, u32[]{:S(2)}) async-start(f32[8,128,128]{2,1,0:T(8,128)} %get-tuple-element.151), calls=%async_computation.6 | async-start | bytes 1048576 | tf_op jit(solution)/shard_map/all_to_all | solution.py:514
  308.5 6.9 %copy-start.5 = (f32[8,128,128]{2,1,0:T(8,128)}, f32[8,128,128]{2,1,0:T(8,128)S(1)}, u32[]{:S(2)}) copy-start(f32[8,128,128]{2,1,0:T(8,128)S(1)} %all-to-all-done.6) | copy-start | bytes 1572868
  312.9 12.8 %collective-permute-start.22 = (f32[8,128,128]{2,1,0:T(8,128)S(1)}, f32[8,128,128]{2,1,0:T(8,128)S(1)}, u32[]{:S(2)}, u32[]{:S(2)}) collective-permute-start(f32[8,128,128]{2,1,0:T(8,128)S(1)} %all-to-all-done.6), channel_id=1, source_target_pairs={{0,2},{1,3},{2,0},{3,1},{4,6},{5,7},{6,4},{7,5},{8,10},{9,11},{10,... | collective-permute-start | bytes 1572872 | tf_op jit(solution)/shard_map/ppermute | solution.py:770
  314.6 14.7 %collective-permute-start.20 = (f32[8,256,128]{2,1,0:T(8,128)}, f32[8,256,128]{2,1,0:T(8,128)S(1)}, u32[]{:S(2)}, u32[]{:S(2)}) collective-permute-start(f32[8,256,128]{2,1,0:T(8,128)} %collective-permute-done.19), channel_id=1, source_target_pairs={{0,1},{1,0},{2,3},{3,2},{4,5},{5,4},{6,7},{7,6},{8,9},{9,8},{10,11... | collective-permute-start | bytes 3145736 | tf_op jit(solution)/shard_map/ppermute | solution.py:770
  315.4 13.9 %collective-permute-start.21 = (f32[8,128,128]{2,1,0:T(8,128)S(1)}, f32[8,128,128]{2,1,0:T(8,128)}, u32[]{:S(2)}, u32[]{:S(2)}) collective-permute-start(f32[8,128,128]{2,1,0:T(8,128)S(1)} %all-to-all-done.6), channel_id=1, source_target_pairs={{0,1},{1,0},{2,3},{3,2},{4,5},{5,4},{6,7},{7,6},{8,9},{9,8},{10,11... | collective-permute-start | bytes 1572872 | tf_op jit(solution)/shard_map/ppermute | solution.py:770
  325.7 2.9 copy-start.12
  325.7 3.6 collective-permute-start.23
  329.3 1.0 copy-start.6

commit v11 on v10

--- a/solution.py
+++ b/solution.py
@@ -372,11 +372,12 @@
     arrays += (() if opening else (before,)) + ((rim, corner[None]) if closing else ())
     out = jax.ShapeDtypeStruct((layers, block // (gx * gy), gx, width), jnp.float32)
     outs = [out] * gy + [jax.ShapeDtypeStruct((planes, block, width), jnp.float32)]
+    kept_spec = pl.BlockSpec((step_rows, cols, half), lambda i: (i, 0, 0))
     rows_spec = pl.BlockSpec((step_rows, cols, half), lambda i: (i + first // step_rows, 0, 0))
     return pl.pallas_call(
         lambda *refs: section_kernel(offsets, planes, opening, closing, *refs),
         grid=(count // step_rows,),
-        in_specs=[pl.BlockSpec(memory_space=pltpu.SMEM)] * 2 + [rows_spec, rows_spec]
+        in_specs=[pl.BlockSpec(memory_space=pltpu.SMEM)] * 2 + [kept_spec, rows_spec]
         + [whole(array) for array in arrays],
         out_specs=[whole(out) for out in outs],
         out_shape=outs,
@@ -453,7 +454,7 @@
             behind = (given_first, kept_first), packed
             starts, packed = lax.optimization_barrier(behind)
             given.append(fill(parts[1:], starts[0]))
-            kept.append(fill(parts[1:], starts[1]))
+            kept.extend(fill([part], starts[1]) for part in parts[1:])
         flanks = [piece[1:] for piece in given + kept]
         if c > 1:
             flanks, packed = lax.optimization_barrier((flanks, packed))
@@ -464,7 +465,6 @@
             given[1][0], kept[1][0], got_lines = lax.optimization_barrier(behind)
         if c < 2:
             got = lax.ppermute(given[c][0], "gy", swap(gy, 1))
-            held = kept[c][0]
         if c > 0:
             lines = sent_lines(got_lines, counts[c - 1], lines)
             values = values + first_axis(lines, table_parts[c - 1])
@@ -486,7 +486,7 @@
         if c > 0:
             row_table = rounded_parts(kept_rows[parts[c], :half].T)
         *packed, side = packed_section(
-            col, held, got, sum(counts[1:c]), pair_tables[0], row_table, weights[c],
+            col, kept[c][0], got, sum(counts[1:c]), pair_tables[0], row_table, weights[c],
             rim, corner, side, offsets, (gx, gy), closing,
         )
     lines = sent_lines(exchanged(packed), counts[-1], lines)

time: 360 us -> 367 us (1.019)
    all_to_all x3, waiting for transfers between devices: 28.2 us -> 34.7 us  [sent_lines(): return lax.all_to_all(lines, 'gx', 0, 0, tiled=True)]
    pallas_call x4 -> x5, Pallas kernels: 66.2 us -> 69.4 us  [filled_spectrum(): pl.pallas_call(kernel, grid_spec=pltpu.PrefetchScalarGridSpec(num_scalar_...]
  transfers between devices with their start and end apart: 30 -> 30, of which waited for: 13 -> 12; matrix products, arithmetic and copies ran while one was open for 9% -> 8% of each run, Pallas kernels for 20% -> 21%
where the time goes in v11:
time: 367 us; the launch traced here: 366 us
  Pallas kernels  126 us (34%)
  waiting for transfers between devices  117 us (32%)
  starting transfers between devices  40.7 us (11%)
  local copies, waits for them, and re-layouts  33.1 us (9%)
  blocking collectives  32.5 us (9%)
  other arithmetic  9.61 us (3%)
  matrix products  5.23 us (1%)
    pallas_call x5, Pallas kernels, filled_spectrum(): pl.pallas_call(kernel, grid_spec=pltpu.PrefetchScalarGridSpec(num_scalar_...  69.4 us
    ppermute x9, waiting for transfers between devices, gathered(): pieces[place ^ bit] = lax.ppermute(pieces[place], 'gy', swap(peers, bit))  35.6 us
    all_to_all x3, waiting for transfers between devices, sent_lines(): return lax.all_to_all(lines, 'gx', 0, 0, tiled=True)  34.7 us
    all_to_all x1, blocking collectives, on_device(): piece = lax.all_to_all(messages, 'gx', 0, 0, tiled=True)  32.5 us
    pallas_call x1, Pallas kernels, result_block(): pl.pallas_call(lambda *refs: result_kernel(offsets, own, devices, groups,...  28.7 us
    pallas_call x3, Pallas kernels, packed_section(): pl.pallas_call(lambda *refs: section_kernel(offsets, planes, opening, clo...  19.2 us
    all_to_all x1, waiting for transfers between devices, on_device(): lax.all_to_all(jnp.concatenate(turned, axis=3), ('gy', 'gx'), 0, 0, tiled...  18.5 us
    ppermute x9, waiting for transfers between devices, exchanged(): lax.ppermute(packed[p], 'gy', swap(gy, p))  14 us
  transfers between devices with their start and end apart: 30, of which 12 were waited for; matrix products, arithmetic and copies ran while one was open for 8% of the time, Pallas kernels for 21%

profile of v11, /device:TPU:0, one launch (start us, length us, event | category | flops | bytes accessed | tf_op | source)
XLA Modules:
  0.0 365.7 jit_solution(2530337984904909259)
XLA Ops:
  0.0 1.9 fusion.27
  1.9 2.4 collective-permute-start.1
  5.7 3.6 shard_map.82.refs_5_
  9.3 0.9 constant_dynamic-slice_fusion.4
  10.9 1.1 collective-permute-done
  12.2 1.6 pad_add_fusion.refs_4_
  13.9 16.2 %shard_map.84 = (f32[16,128,256]{2,1,0:T(8,128)}, f32[16,256]{1,0:T(8,128)}, f32[128,128]{1,0:T(8,128)}) custom-call(s32[2]{0:T(128)} %get-tuple-element.196.refs_0_, f32[64,128,512]{2,1,0:T(8,128)} %refs_3_.9, f32[64,128,512]{2,1,0:T(8,128)} %refs_3_.9, f32[64,128,512]{2,1,0:T(8,128)} %refs_3_.9, f32[64,16,512]{2,1,0:T(8,128)} %pad_add_fusion.refs_4_, ...), custom_call_target="tpu_custom_call" | custom-call | flops 1610612736 | bytes 6291456 | tf_op jit(solution)/shard_map/pallas_call | solution.py:263
  30.1 1.3 fusion.26
  32.5 1.6 collective-permute-start.3
  34.3 3.3 collective-permute-start.4
  37.6 16.2 %shard_map.83 = (f32[16,128,256]{2,1,0:T(8,128)}, f32[16,256]{1,0:T(8,128)}, f32[128,128]{1,0:T(8,128)}) custom-call(s32[2]{0:T(128)} %get-tuple-element.195.refs_0_, f32[64,128,512]{2,1,0:T(8,128)} %refs_3_.9, f32[64,128,512]{2,1,0:T(8,128)} %refs_3_.9, f32[64,128,512]{2,1,0:T(8,128)} %refs_3_.9, f32[64,16,512]{2,1,0:T(8,128)} %pad_add_fusion.refs_4_, ...), custom_call_target="tpu_custom_call" | custom-call | flops 1610612736 | bytes 6291456 | tf_op jit(solution)/shard_map/pallas_call | solution.py:263
  53.8 1.3 copy-done.27
  55.2 7.8 %shard_map.85 = (f32[16,2,8,640]{3,2,1,0:T(8,128)}, f32[16,2,8,640]{3,2,1,0:T(8,128)}, f32[16,2,8,640]{3,2,1,0:T(8,128)}, f32[16,2,8,640]{3,2,1,0:T(8,128)}, f32[4,64,640]{2,1,0:T(8,128)}) custom-call(s32[1]{0:T(128)} %bitcast.3.refs_0_, f32[4,16]{1,0:T(4,128)} %constant.132.clone.refs_1_, f32[16,128,256]{2,1,0:T(8,128)} %get-tuple-element.87.refs_2_, ...), custom_call_target="tpu_custom_call" | custom-call | flops 1610612736 | bytes 8388608 | tf_op jit(solution)/shard_map/pallas_call | solution.py:377
  63.0 1.5 collective-permute-start.6
  64.8 0.9 copy.80.refs_8_
  65.7 0.9 copy.81.refs_9_
  66.6 10.2 %shard_map.87 = (f32[8,128,256]{2,1,0:T(8,128)}, f32[8,256]{1,0:T(8,128)}, f32[128,128]{1,0:T(8,128)}) custom-call(s32[1]{0:T(128)} %bitcast.14.refs_0_, f32[64,128,512]{2,1,0:T(8,128)} %refs_3_.9, f32[64,128,512]{2,1,0:T(8,128)} %refs_3_.9, f32[64,128,512]{2,1,0:T(8,128)} %refs_3_.9, f32[64,16,512]{2,1,0:T(8,128)} %pad_add_fusion.refs_4_, ...), custom_call_target="tpu_custom_call" | custom-call | flops 805306368 | bytes 3145728 | tf_op jit(solution)/shard_map/pallas_call | solution.py:263
  77.5 16.8 %shard_map.86 = (f32[16,128,256]{2,1,0:T(8,128)}, f32[16,256]{1,0:T(8,128)}, f32[128,128]{1,0:T(8,128)}) custom-call(s32[2]{0:T(128)} %pad_add_fusion.4.refs_0_, f32[64,128,512]{2,1,0:T(8,128)} %refs_3_.9, f32[64,128,512]{2,1,0:T(8,128)} %refs_3_.9, f32[64,128,512]{2,1,0:T(8,128)} %refs_3_.9, f32[64,16,512]{2,1,0:T(8,128)} %pad_add_fusion.refs_4_, ...), custom_call_target="tpu_custom_call" | custom-call | flops 1610612736 | bytes 6291456 | tf_op jit(solution)/shard_map/pallas_call | solution.py:263
  94.3 0.8 copy-done.8
  95.6 0.9 constant_dynamic-slice_fusion.1
  96.5 1.0 constant_dynamic-slice_fusion.6
  97.5 1.5 concatenate.75
  99.0 0.8 fusion.11
  99.8 10.1 %shard_map.88 = (f32[8,128,256]{2,1,0:T(8,128)}, f32[8,256]{1,0:T(8,128)}, f32[128,128]{1,0:T(8,128)}) custom-call(s32[1]{0:T(128)} %bitcast.20.refs_0_, f32[64,128,512]{2,1,0:T(8,128)} %refs_3_.9, f32[64,128,512]{2,1,0:T(8,128)} %refs_3_.9, f32[64,128,512]{2,1,0:T(8,128)} %refs_3_.9, f32[64,16,512]{2,1,0:T(8,128)} %pad_add_fusion.refs_4_, ...), custom_call_target="tpu_custom_call" | custom-call | flops 805306368 | bytes 3145728 | tf_op jit(solution)/shard_map/pallas_call | solution.py:263
  110.0 1.0 copy-done.11
  111.1 1.8 copy.84
  112.9 4.3 %all-to-all-start = ((f32[8,2,32,640]{3,1,2,0:T(2,128)}), f32[8,2,32,640]{3,1,2,0:T(2,128)}, u32[]{:S(2)}, u32[]{:S(2)}) async-start(f32[8,2,32,640]{3,1,2,0:T(2,128)} %copy.84), calls=%async_computation | async-start | bytes 2621440 | tf_op jit(solution)/shard_map/all_to_all | solution.py:787
  117.2 1.3 copy-done
  118.6 5.5 %shard_map.89 = (f32[8,2,8,640]{3,2,1,0:T(8,128)}, f32[8,2,8,640]{3,2,1,0:T(8,128)}, f32[8,2,8,640]{3,2,1,0:T(8,128)}, f32[8,2,8,640]{3,2,1,0:T(8,128)}, f32[4,64,640]{2,1,0:T(8,128)}) custom-call(s32[1]{0:T(128)} %bitcast.3.refs_0_, f32[4,8]{1,0:T(4,128)} %constant.133.clone.refs_1_, f32[8,128,256]{2,1,0:T(8,128)} %get-tuple-element.123.refs_2_, ...), custom_call_target="tpu_custom_call" | custom-call | flops 805306368 | bytes 4194304 | tf_op jit(solution)/shard_map/pallas_call | solution.py:377
  124.6 1.6 collective-permute-start.9
  127.4 1.0 fusion.13.refs_9_
  128.9 5.9 %shard_map.90 = (f32[13,2,8,640]{3,2,1,0:T(8,128)}, f32[13,2,8,640]{3,2,1,0:T(8,128)}, f32[13,2,8,640]{3,2,1,0:T(8,128)}, f32[13,2,8,640]{3,2,1,0:T(8,128)}, f32[4,64,640]{2,1,0:T(8,128)}) custom-call(s32[1]{0:T(128)} %bitcast.3.refs_0_, f32[4,8]{1,0:T(4,128)} %constant.133.clone.refs_1_, f32[8,128,256]{2,1,0:T(8,128)} %get-tuple-element.135.refs_2_, ...), custom_call_target="tpu_custom_call" | custom-call | flops 805306368 | bytes 4194304 | tf_op jit(solution)/shard_map/pallas_call | solution.py:377
  134.9 1.5 collective-permute-start.12
  137.1 4.5 %collective-permute-done.11 = f32[8,2,8,640]{3,2,1,0:T(8,128)S(1)} collective-permute-done((f32[8,2,8,640]{3,2,1,0:T(8,128)}, f32[8,2,8,640]{3,2,1,0:T(8,128)S(1)}, u32[]{:S(2)}, u32[]{:S(2)}) %collective-permute-start.11) | collective-permute-done | bytes 327712 | tf_op jit(solution)/shard_map/ppermute | solution.py:777
  141.7 7.5 %all-to-all-done = f32[8,2,32,640]{3,1,2,0:T(2,128)} async-done(((f32[8,2,32,640]{3,1,2,0:T(2,128)}), f32[8,2,32,640]{3,1,2,0:T(2,128)}, u32[]{:S(2)}, u32[]{:S(2)}) %all-to-all-start) | async-done | bytes 1310752 | tf_op jit(solution)/shard_map/all_to_all | solution.py:787
  149.2 1.2 copy.88
  150.4 3.8 %all-to-all-start.1 = ((f32[8,2,16,640]{3,1,2,0:T(2,128)}), f32[8,2,16,640]{3,1,2,0:T(2,128)S(1)}, u32[]{:S(2)}, u32[]{:S(2)}) async-start(f32[8,2,16,640]{3,1,2,0:T(2,128)} %copy.88), calls=%async_computation.1 | async-start | bytes 1310720 | tf_op jit(solution)/shard_map/all_to_all | solution.py:787
  154.2 9.5 %collective-permute-done.14 = f32[13,2,8,640]{3,2,1,0:T(8,128)S(1)} collective-permute-done((f32[13,2,8,640]{3,2,1,0:T(8,128)}, f32[13,2,8,640]{3,2,1,0:T(8,128)S(1)}, u32[]{:S(2)}, u32[]{:S(2)}) %collective-permute-start.14) | collective-permute-done | bytes 532512 | tf_op jit(solution)/shard_map/ppermute | solution.py:777
  163.9 7.5 %all-to-all-done.1 = f32[8,2,16,640]{3,1,2,0:T(2,128)S(1)} async-done(((f32[8,2,16,640]{3,1,2,0:T(2,128)}), f32[8,2,16,640]{3,1,2,0:T(2,128)S(1)}, u32[]{:S(2)}, u32[]{:S(2)}) %all-to-all-start.1) | async-done | bytes 655392 | tf_op jit(solution)/shard_map/all_to_all | solution.py:787
  171.5 1.3 copy.90
  172.8 3.6 all-to-all-start.2
  176.6 2.1 convolution_bitcast_fusion
  178.7 19.7 %all-to-all-done.2 = f32[8,2,21,640]{3,1,2,0:T(2,128)S(1)} async-done(((f32[8,2,21,640]{3,1,2,0:T(2,128)}), f32[8,2,21,640]{3,1,2,0:T(2,128)S(1)}, u32[]{:S(2)}, u32[]{:S(2)}) %all-to-all-start.2) | async-done | bytes 860192 | tf_op jit(solution)/shard_map/all_to_all | solution.py:787
  200.0 1.0 copy.124
  201.2 2.4 concatenate.80
  203.6 3.6 all-to-all-start.3
  207.9 18.5 %all-to-all-done.3 = f32[32,2,2,1280]{3,2,1,0:T(2,128)S(1)} async-done(((f32[32,2,2,1280]{3,2,1,0:T(2,128)}), f32[32,2,2,1280]{3,2,1,0:T(2,128)S(1)}, u32[]{:S(2)}, u32[]{:S(2)}) %all-to-all-start.3) | async-done | bytes 655392 | tf_op jit(solution)/shard_map/all_to_all | solution.py:498
  226.4 1.0 copy.93
  227.4 5.5 %shard_map.91 = (f32[8,288,128]{2,1,0:T(8,128)}, f32[8,256,128]{2,1,0:T(8,128)}, f32[8,128,128]{2,1,0:T(8,128)}) custom-call(f32[2,256,640]{2,1,0:T(8,128)} %bitcast.141, f32[2,64,1280]{2,1,0:T(8,128)} %bitcast.150, f32[2,5,640]{2,1,0:T(8,128)} %copy_multiply_fusion.refs_2_), custom_call_target="tpu_custom_call" | custom-call | tf_op jit(solution)/shard_map/pallas_call | solution.py:633
  232.8 32.5 %all_to_all.35 = f32[8,288,128]{2,1,0:T(8,128)S(1)} all-to-all(f32[8,288,128]{2,1,0:T(8,128)} %get-tuple-element.153), channel_id=1, replica_groups=mesh['gx'=8,'gy'=4] {'gx'}, dimensions={0} | all-to-all | bytes 2359296 | tf_op jit(solution)/shard_map/all_to_all | solution.py:514
  265.3 1.2 collective-permute-start.16
  266.5 3.6 all-to-all-start.5
  270.2 21.5 %collective-permute-done.16 = f32[8,288,128]{2,1,0:T(8,128)} collective-permute-done((f32[8,288,128]{2,1,0:T(8,128)S(1)}, f32[8,288,128]{2,1,0:T(8,128)}, u32[]{:S(2)}, u32[]{:S(2)}) %collective-permute-start.16) | collective-permute-done | bytes 1179680 | tf_op jit(solution)/shard_map/ppermute | solution.py:770
  293.7 1.9 all-to-all-done.5
  296.2 4.0 %all-to-all-start.6 = ((f32[8,128,128]{2,1,0:T(8,128)}), f32[8,128,128]{2,1,0:T(8,128)S(1)}, u32[]{:S(2)}, u32[]{:S(2)}) async-start(f32[8,128,128]{2,1,0:T(8,128)} %get-tuple-element.161), calls=%async_computation.6 | async-start | bytes 1048576 | tf_op jit(solution)/shard_map/all_to_all | solution.py:514
  300.1 0.9 slice_bitcast_fusion.9
  301.0 0.9 slice_bitcast_fusion.8
  302.0 0.9 slice_bitcast_fusion.2
  303.7 11.3 %all-to-all-done.6 = f32[8,128,128]{2,1,0:T(8,128)S(1)} async-done(((f32[8,128,128]{2,1,0:T(8,128)}), f32[8,128,128]{2,1,0:T(8,128)S(1)}, u32[]{:S(2)}, u32[]{:S(2)}) %all-to-all-start.6) | async-done | bytes 524320 | tf_op jit(solution)/shard_map/all_to_all | solution.py:514
  315.1 4.4 %collective-permute-done.19 = f32[8,256,128]{2,1,0:T(8,128)} collective-permute-done((f32[8,256,128]{2,1,0:T(8,128)S(1)}, f32[8,256,128]{2,1,0:T(8,128)}, u32[]{:S(2)}, u32[]{:S(2)}) %collective-permute-start.19) | collective-permute-done | bytes 1048608 | tf_op jit(solution)/shard_map/ppermute | solution.py:770
  319.5 1.7 collective-permute-start.22
  322.6 9.7 %collective-permute-done.22 = f32[8,128,128]{2,1,0:T(8,128)S(1)} collective-permute-done((f32[8,128,128]{2,1,0:T(8,128)S(1)}, f32[8,128,128]{2,1,0:T(8,128)S(1)}, u32[]{:S(2)}, u32[]{:S(2)}) %collective-permute-start.22) | collective-permute-done | bytes 524320 | tf_op jit(solution)/shard_map/ppermute | solution.py:770
  335.9 1.0 copy-done.6
  336.8 28.7 %shard_map.92 = f32[64,128,512]{2,1,0:T(8,128)} custom-call(s32[4]{0:T(128)} %pad_add_fusion.1.refs_0_, f32[64,640]{1,0:T(8,128)} %bitcast.156, f32[64,256]{1,0:T(8,128)} %slice.304.refs_2_, f32[128,128]{1,0:T(8,128)} %pad.19.refs_3_, bf16[128,256]{1,0:T(8,128)(2,1)} %fusion.15.refs_4_, bf16[256,256]{1,0:T(8,128)(2,1)} %fusion.7.refs_5_, ...), custom_call_target="tpu_custom_call" | custom-call | tf_op jit(solution)/shard_map/pallas_call | solution.py:741
  (170 shorter events, 19.5 us)
Async XLA Ops:
  0.0 4.3 %copy-start.4 = (f32[512,257]{0,1:T(8,128)S(1)}, f32[512,257]{0,1:T(8,128)}, u32[]{:S(2)}) copy-start(f32[512,257]{0,1:T(8,128)} %constant.129.clone) | copy-start | bytes 1579012
  1.9 9.1 %collective-permute-start.1 = (f32[64,2,512]{2,1,0:T(2,128)S(1)}, f32[64,2,512]{2,1,0:T(2,128)S(1)}, u32[]{:S(2)}, u32[]{:S(2)}) collective-permute-start(f32[64,2,512]{2,1,0:T(2,128)S(1)} %get-tuple-element.167), channel_id=1, source_target_pairs={{1,0},{2,1},{3,2},{0,3},{5,4},{6,5},{7,6},{4,7},{9,8},{10,9},{11,1... | collective-permute-start | bytes 786440 | tf_op jit(solution)/shard_map/ppermute | solution.py:28
  4.3 7.7 %collective-permute-start = (f32[64,2,512]{2,1,0:T(2,128)S(1)}, f32[64,2,512]{2,1,0:T(2,128)S(1)}, u32[]{:S(2)}, u32[]{:S(2)}) collective-permute-start(f32[64,2,512]{2,1,0:T(2,128)S(1)} %get-tuple-element.168), channel_id=1, source_target_pairs={{0,1},{1,2},{2,3},{3,0},{4,5},{5,6},{6,7},{7,4},{8,9},{9,10},{10,1... | collective-permute-start | bytes 786440 | tf_op jit(solution)/shard_map/ppermute | solution.py:27
  30.1 23.7 %collective-permute-start.2 = (f32[16,128,256]{2,1,0:T(8,128)}, f32[16,128,256]{2,1,0:T(8,128)S(1)}, u32[]{:S(2)}, u32[]{:S(2)}) collective-permute-start(f32[16,128,256]{2,1,0:T(8,128)} %get-tuple-element.91), channel_id=1, source_target_pairs={{0,1},{1,0},{2,3},{3,2},{4,5},{5,4},{6,7},{7,6},{8,9},{9,8},{10,11... | collective-permute-start | bytes 6291464 | tf_op jit(solution)/shard_map/ppermute | solution.py:467
  32.5 32.3 %collective-permute-start.3 = (f32[2,132,512]{2,0,1:T(2,128)S(1)}, f32[2,132,512]{2,0,1:T(2,128)S(1)}, u32[]{:S(2)}, u32[]{:S(2)}) collective-permute-start(f32[2,132,512]{2,0,1:T(2,128)S(1)} %pad_maximum_fusion), channel_id=1, source_target_pairs={{0,4},{4,8},{8,12},{12,16},{16,20},{20,24},{24,28},{28,0},{1,5},{5... | collective-permute-start | bytes 1622024 | tf_op jit(solution)/shard_map/ppermute | solution.py:37
  34.3 31.4 %collective-permute-start.4 = (f32[2,132,512]{2,0,1:T(2,128)S(1)}, f32[2,132,512]{2,0,1:T(2,128)S(1)}, u32[]{:S(2)}, u32[]{:S(2)}) collective-permute-start(f32[2,132,512]{2,0,1:T(2,128)S(1)} %pad_maximum_fusion.1), channel_id=1, source_target_pairs={{4,0},{8,4},{12,8},{16,12},{20,16},{24,20},{28,24},{0,28},{5,1},{9... | collective-permute-start | bytes 1622024 | tf_op jit(solution)/shard_map/ppermute | solution.py:37
  53.8 1.3 copy-start.27
  62.9 31.3 %collective-permute-start.5 = (f32[16,2,8,640]{3,2,1,0:T(8,128)}, f32[16,2,8,640]{3,2,1,0:T(8,128)S(1)}, u32[]{:S(2)}, u32[]{:S(2)}) collective-permute-start(f32[16,2,8,640]{3,2,1,0:T(8,128)} %get-tuple-element.106), channel_id=1, source_target_pairs={{0,1},{1,0},{2,3},{3,2},{4,5},{5,4},{6,7},{7,6},{8,9},{9,8},{10,11... | collective-permute-start | bytes 1966088 | tf_op jit(solution)/shard_map/ppermute | solution.py:777
  63.0 31.2 %collective-permute-start.6 = (f32[16,2,8,640]{3,2,1,0:T(8,128)}, f32[16,2,8,640]{3,2,1,0:T(8,128)S(1)}, u32[]{:S(2)}, u32[]{:S(2)}) collective-permute-start(f32[16,2,8,640]{3,2,1,0:T(8,128)} %get-tuple-element.107), channel_id=1, source_target_pairs={{0,2},{1,3},{2,0},{3,1},{4,6},{5,7},{6,4},{7,5},{8,10},{9,11},{10,... | collective-permute-start | bytes 1966088 | tf_op jit(solution)/shard_map/ppermute | solution.py:777
  64.5 29.8 %collective-permute-start.7 = (f32[16,2,8,640]{3,2,1,0:T(8,128)}, f32[16,2,8,640]{3,2,1,0:T(8,128)S(1)}, u32[]{:S(2)}, u32[]{:S(2)}) collective-permute-start(f32[16,2,8,640]{3,2,1,0:T(8,128)} %get-tuple-element.108), channel_id=1, source_target_pairs={{0,3},{1,2},{2,1},{3,0},{4,7},{5,6},{6,5},{7,4},{8,11},{9,10},{10,... | collective-permute-start | bytes 1966088 | tf_op jit(solution)/shard_map/ppermute | solution.py:777
  94.2 0.8 copy-start.8
  94.3 1.0 copy-start.10
  95.3 21.9 %collective-permute-start.8 = (f32[16,128,256]{2,1,0:T(8,128)}, f32[16,128,256]{2,1,0:T(8,128)S(1)}, u32[]{:S(2)}, u32[]{:S(2)}) collective-permute-start(f32[16,128,256]{2,1,0:T(8,128)} %get-tuple-element.124), channel_id=1, source_target_pairs={{0,1},{1,0},{2,3},{3,2},{4,5},{5,4},{6,7},{7,6},{8,9},{9,8},{10,11... | collective-permute-start | bytes 6291464 | tf_op jit(solution)/shard_map/ppermute | solution.py:467
  99.8 10.1 %copy-start.7 = (f32[16,2,8,640]{3,2,1,0:T(8,128)S(1)}, f32[16,2,8,640]{3,2,1,0:T(8,128)}, u32[]{:S(2)}) copy-start(f32[16,2,8,640]{3,2,1,0:T(8,128)} %get-tuple-element.109) | copy-start | bytes 1966084
  99.8 10.1 %copy-start.9 = (f32[16,2,8,640]{3,2,1,0:T(8,128)S(1)}, f32[16,2,8,640]{3,2,1,0:T(8,128)}, u32[]{:S(2)}) copy-start(f32[16,2,8,640]{3,2,1,0:T(8,128)} %copy-done.8) | copy-start | bytes 1966084
  109.9 1.1 copy-start.11
  112.9 36.3 %all-to-all-start = ((f32[8,2,32,640]{3,1,2,0:T(2,128)}), f32[8,2,32,640]{3,1,2,0:T(2,128)}, u32[]{:S(2)}, u32[]{:S(2)}) async-start(f32[8,2,32,640]{3,1,2,0:T(2,128)} %copy.84), calls=%async_computation | async-start | bytes 2621440 | tf_op jit(solution)/shard_map/all_to_all | solution.py:787
  117.2 1.3 copy-start
  118.5 5.6 %copy-start.17 = (f32[128,128]{1,0:T(8,128)S(1)}, f32[128,128]{1,0:T(8,128)}, u32[]{:S(2)}) copy-start(f32[128,128]{1,0:T(8,128)} %get-tuple-element.137) | copy-start | bytes 196612
  118.5 5.6 %copy-start.18 = (f32[128,128]{1,0:T(8,128)S(1)}, f32[128,128]{1,0:T(8,128)}, u32[]{:S(2)}) copy-start(f32[128,128]{1,0:T(8,128)} %get-tuple-element.139) | copy-start | bytes 196612
  118.5 5.6 %copy-start.19 = (f32[128,128]{1,0:T(8,128)S(1)}, f32[128,128]{1,0:T(8,128)}, u32[]{:S(2)}) copy-start(f32[128,128]{1,0:T(8,128)} %get-tuple-element.140) | copy-start | bytes 196612
  118.5 5.6 %copy-start.20 = (f32[128,128]{1,0:T(8,128)S(1)}, f32[128,128]{1,0:T(8,128)}, u32[]{:S(2)}) copy-start(f32[128,128]{1,0:T(8,128)} %get-tuple-element.138) | copy-start | bytes 196612
  118.5 5.6 %copy-start.21 = (f32[128,128]{1,0:T(8,128)S(1)}, f32[128,128]{1,0:T(8,128)}, u32[]{:S(2)}) copy-start(f32[128,128]{1,0:T(8,128)} %get-tuple-element.141) | copy-start | bytes 196612
  118.5 8.3 %copy-start.22 = (f32[16,256]{1,0:T(8,128)S(1)}, f32[16,256]{1,0:T(8,128)}, u32[]{:S(2)}) copy-start(f32[16,256]{1,0:T(8,128)} %get-tuple-element.142) | copy-start | bytes 49156
  118.5 8.2 %copy-start.24 = (f32[16,256]{1,0:T(8,128)S(1)}, f32[16,256]{1,0:T(8,128)}, u32[]{:S(2)}) copy-start(f32[16,256]{1,0:T(8,128)} %get-tuple-element.143) | copy-start | bytes 49156
  118.6 8.2 %copy-start.23 = (f32[16,256]{1,0:T(8,128)S(1)}, f32[16,256]{1,0:T(8,128)}, u32[]{:S(2)}) copy-start(f32[16,256]{1,0:T(8,128)} %get-tuple-element.144) | copy-start | bytes 49156
  118.6 8.3 %copy-start.25 = (f32[8,256]{1,0:T(8,128)S(1)}, f32[8,256]{1,0:T(8,128)}, u32[]{:S(2)}) copy-start(f32[8,256]{1,0:T(8,128)} %get-tuple-element.145) | copy-start | bytes 24580
  118.6 8.3 %copy-start.26 = (f32[8,256]{1,0:T(8,128)S(1)}, f32[8,256]{1,0:T(8,128)}, u32[]{:S(2)}) copy-start(f32[8,256]{1,0:T(8,128)} %get-tuple-element.146) | copy-start | bytes 24580
  124.6 11.8 %collective-permute-start.9 = (f32[8,2,8,640]{3,2,1,0:T(8,128)}, f32[8,2,8,640]{3,2,1,0:T(8,128)S(1)}, u32[]{:S(2)}, u32[]{:S(2)}) collective-permute-start(f32[8,2,8,640]{3,2,1,0:T(8,128)} %get-tuple-element.131), channel_id=1, source_target_pairs={{0,2},{1,3},{2,0},{3,1},{4,6},{5,7},{6,4},{7,5},{8,10},{9,11},{10,... | collective-permute-start | bytes 983048 | tf_op jit(solution)/shard_map/ppermute | solution.py:777
  126.2 10.9 %collective-permute-start.10 = (f32[8,2,8,640]{3,2,1,0:T(8,128)}, f32[8,2,8,640]{3,2,1,0:T(8,128)S(1)}, u32[]{:S(2)}, u32[]{:S(2)}) collective-permute-start(f32[8,2,8,640]{3,2,1,0:T(8,128)} %get-tuple-element.132), channel_id=1, source_target_pairs={{0,1},{1,0},{2,3},{3,2},{4,5},{5,4},{6,7},{7,6},{8,9},{9,8},{10,11... | collective-permute-start | bytes 983048 | tf_op jit(solution)/shard_map/ppermute | solution.py:777
  126.2 15.4 %collective-permute-start.11 = (f32[8,2,8,640]{3,2,1,0:T(8,128)}, f32[8,2,8,640]{3,2,1,0:T(8,128)S(1)}, u32[]{:S(2)}, u32[]{:S(2)}) collective-permute-start(f32[8,2,8,640]{3,2,1,0:T(8,128)} %get-tuple-element.133), channel_id=1, source_target_pairs={{0,3},{1,2},{2,1},{3,0},{4,7},{5,6},{6,5},{7,4},{8,11},{9,10},{10,... | collective-permute-start | bytes 983048 | tf_op jit(solution)/shard_map/ppermute | solution.py:777
  128.9 8.1 %copy-start.16 = (f32[8,2,8,640]{3,2,1,0:T(8,128)S(1)}, f32[8,2,8,640]{3,2,1,0:T(8,128)}, u32[]{:S(2)}) copy-start(f32[8,2,8,640]{3,2,1,0:T(8,128)} %get-tuple-element.130) | copy-start | bytes 983044
  134.9 19.3 %collective-permute-start.12 = (f32[13,2,8,640]{3,2,1,0:T(8,128)}, f32[13,2,8,640]{3,2,1,0:T(8,128)S(1)}, u32[]{:S(2)}, u32[]{:S(2)}) collective-permute-start(f32[13,2,8,640]{3,2,1,0:T(8,128)} %get-tuple-element.148), channel_id=1, source_target_pairs={{0,2},{1,3},{2,0},{3,1},{4,6},{5,7},{6,4},{7,5},{8,10},{9,11},{10,... | collective-permute-start | bytes 1597448 | tf_op jit(solution)/shard_map/ppermute | solution.py:777
  136.4 17.8 %collective-permute-start.13 = (f32[13,2,8,640]{3,2,1,0:T(8,128)}, f32[13,2,8,640]{3,2,1,0:T(8,128)S(1)}, u32[]{:S(2)}, u32[]{:S(2)}) collective-permute-start(f32[13,2,8,640]{3,2,1,0:T(8,128)} %get-tuple-element.149), channel_id=1, source_target_pairs={{0,1},{1,0},{2,3},{3,2},{4,5},{5,4},{6,7},{7,6},{8,9},{9,8},{10,11... | collective-permute-start | bytes 1597448 | tf_op jit(solution)/shard_map/ppermute | solution.py:777
  136.4 27.4 %collective-permute-start.14 = (f32[13,2,8,640]{3,2,1,0:T(8,128)}, f32[13,2,8,640]{3,2,1,0:T(8,128)S(1)}, u32[]{:S(2)}, u32[]{:S(2)}) collective-permute-start(f32[13,2,8,640]{3,2,1,0:T(8,128)} %get-tuple-element.150), channel_id=1, source_target_pairs={{0,3},{1,2},{2,1},{3,0},{4,7},{5,6},{6,5},{7,4},{8,11},{9,10},{10,... | collective-permute-start | bytes 1597448 | tf_op jit(solution)/shard_map/ppermute | solution.py:777
  141.7 12.5 %copy-start.12 = (f32[13,2,8,640]{3,2,1,0:T(8,128)S(1)}, f32[13,2,8,640]{3,2,1,0:T(8,128)}, u32[]{:S(2)}) copy-start(f32[13,2,8,640]{3,2,1,0:T(8,128)} %get-tuple-element.147) | copy-start | bytes 1597444
  150.4 21.1 %all-to-all-start.1 = ((f32[8,2,16,640]{3,1,2,0:T(2,128)}), f32[8,2,16,640]{3,1,2,0:T(2,128)S(1)}, u32[]{:S(2)}, u32[]{:S(2)}) async-start(f32[8,2,16,640]{3,1,2,0:T(2,128)} %copy.88), calls=%async_computation.1 | async-start | bytes 1310720 | tf_op jit(solution)/shard_map/all_to_all | solution.py:787
  163.9 12.5 %copy-start.14 = (f32[8,2,32,256]{3,2,1,0:T(8,128)S(1)}, f32[8,2,32,256]{3,2,1,0:T(8,128)}, u32[]{:S(2)}) copy-start(f32[8,2,32,256]{3,2,1,0:T(8,128)} %constant.146) | copy-start | bytes 1572868
  163.9 12.5 %copy-start.15 = (f32[8,2,32,256]{3,2,1,0:T(8,128)S(1)}, f32[8,2,32,256]{3,2,1,0:T(8,128)}, u32[]{:S(2)}) copy-start(f32[8,2,32,256]{3,2,1,0:T(8,128)} %constant.144) | copy-start | bytes 1572868
  172.8 25.6 %all-to-all-start.2 = ((f32[8,2,21,640]{3,1,2,0:T(2,128)}), f32[8,2,21,640]{3,1,2,0:T(2,128)S(1)}, u32[]{:S(2)}, u32[]{:S(2)}) async-start(f32[8,2,21,640]{3,1,2,0:T(2,128)} %copy.90), calls=%async_computation.2 | async-start | bytes 1720320 | tf_op jit(solution)/shard_map/all_to_all | solution.py:787
  200.0 1.1 copy-start.2
  203.6 22.8 %all-to-all-start.3 = ((f32[32,2,2,1280]{3,2,1,0:T(2,128)}), f32[32,2,2,1280]{3,2,1,0:T(2,128)S(1)}, u32[]{:S(2)}, u32[]{:S(2)}) async-start(f32[32,2,2,1280]{3,2,1,0:T(2,128)} %concatenate.80), calls=%async_computation.3 | async-start | bytes 1310720 | tf_op jit(solution)/shard_map/all_to_all | solution.py:498
  265.3 30.9 %copy-start.1 = (f32[8,288,128]{2,1,0:T(8,128)}, f32[8,288,128]{2,1,0:T(8,128)S(1)}, u32[]{:S(2)}) copy-start(f32[8,288,128]{2,1,0:T(8,128)S(1)} %all_to_all.35) | copy-start | bytes 3538948
  265.3 26.4 %collective-permute-start.16 = (f32[8,288,128]{2,1,0:T(8,128)S(1)}, f32[8,288,128]{2,1,0:T(8,128)}, u32[]{:S(2)}, u32[]{:S(2)}) collective-permute-start(f32[8,288,128]{2,1,0:T(8,128)S(1)} %all_to_all.35), channel_id=1, source_target_pairs={{0,2},{1,3},{2,0},{3,1},{4,6},{5,7},{6,4},{7,5},{8,10},{9,11},{10,... | collective-permute-start | bytes 3538952 | tf_op jit(solution)/shard_map/ppermute | solution.py:770
  266.5 29.1 %all-to-all-start.5 = ((f32[8,256,128]{2,1,0:T(8,128)}), f32[8,256,128]{2,1,0:T(8,128)S(1)}, u32[]{:S(2)}, u32[]{:S(2)}) async-start(f32[8,256,128]{2,1,0:T(8,128)} %get-tuple-element.156), calls=%async_computation.5 | async-start | bytes 2097152 | tf_op jit(solution)/shard_map/all_to_all | solution.py:514
  270.1 25.6 %collective-permute-start.15 = (f32[8,288,128]{2,1,0:T(8,128)S(1)}, f32[8,288,128]{2,1,0:T(8,128)}, u32[]{:S(2)}, u32[]{:S(2)}) collective-permute-start(f32[8,288,128]{2,1,0:T(8,128)S(1)} %all_to_all.35), channel_id=1, source_target_pairs={{0,1},{1,0},{2,3},{3,2},{4,5},{5,4},{6,7},{7,6},{8,9},{9,8},{10,11... | collective-permute-start | bytes 3538952 | tf_op jit(solution)/shard_map/ppermute | solution.py:770
  291.7 10.3 %collective-permute-start.17 = (f32[8,288,128]{2,1,0:T(8,128)}, f32[8,288,128]{2,1,0:T(8,128)}, u32[]{:S(2)}, u32[]{:S(2)}) collective-permute-start(f32[8,288,128]{2,1,0:T(8,128)} %collective-permute-done.16), channel_id=1, source_target_pairs={{0,1},{1,0},{2,3},{3,2},{4,5},{5,4},{6,7},{7,6},{8,9},{9,8},{10,11... | collective-permute-start | bytes 3538952 | tf_op jit(solution)/shard_map/ppermute | solution.py:770
  295.6 7.3 %copy-start.3 = (f32[8,256,128]{2,1,0:T(8,128)}, f32[8,256,128]{2,1,0:T(8,128)S(1)}, u32[]{:S(2)}) copy-start(f32[8,256,128]{2,1,0:T(8,128)S(1)} %all-to-all-done.5) | copy-start | bytes 3145732
  295.6 23.8 %collective-permute-start.19 = (f32[8,256,128]{2,1,0:T(8,128)S(1)}, f32[8,256,128]{2,1,0:T(8,128)}, u32[]{:S(2)}, u32[]{:S(2)}) collective-permute-start(f32[8,256,128]{2,1,0:T(8,128)S(1)} %all-to-all-done.5), channel_id=1, source_target_pairs={{0,2},{1,3},{2,0},{3,1},{4,6},{5,7},{6,4},{7,5},{8,10},{9,11},{10,... | collective-permute-start | bytes 3145736 | tf_op jit(solution)/shard_map/ppermute | solution.py:770
  296.2 23.3 %collective-permute-start.18 = (f32[8,256,128]{2,1,0:T(8,128)S(1)}, f32[8,256,128]{2,1,0:T(8,128)}, u32[]{:S(2)}, u32[]{:S(2)}) collective-permute-start(f32[8,256,128]{2,1,0:T(8,128)S(1)} %all-to-all-done.5), channel_id=1, source_target_pairs={{0,1},{1,0},{2,3},{3,2},{4,5},{5,4},{6,7},{7,6},{8,9},{9,8},{10,11... | collective-permute-start | bytes 3145736 | tf_op jit(solution)/shard_map/ppermute | solution.py:770
  296.2 18.9 %all-to-all-start.6 = ((f32[8,128,128]{2,1,0:T(8,128)}), f32[8,128,128]{2,1,0:T(8,128)S(1)}, u32[]{:S(2)}, u32[]{:S(2)}) async-start(f32[8,128,128]{2,1,0:T(8,128)} %get-tuple-element.161), calls=%async_computation.6 | async-start | bytes 1048576 | tf_op jit(solution)/shard_map/all_to_all | solution.py:514
  315.1 6.9 %copy-start.5 = (f32[8,128,128]{2,1,0:T(8,128)}, f32[8,128,128]{2,1,0:T(8,128)S(1)}, u32[]{:S(2)}) copy-start(f32[8,128,128]{2,1,0:T(8,128)S(1)} %all-to-all-done.6) | copy-start | bytes 1572868
  319.5 12.8 %collective-permute-start.22 = (f32[8,128,128]{2,1,0:T(8,128)S(1)}, f32[8,128,128]{2,1,0:T(8,128)S(1)}, u32[]{:S(2)}, u32[]{:S(2)}) collective-permute-start(f32[8,128,128]{2,1,0:T(8,128)S(1)} %all-to-all-done.6), channel_id=1, source_target_pairs={{0,2},{1,3},{2,0},{3,1},{4,6},{5,7},{6,4},{7,5},{8,10},{9,11},{10,... | collective-permute-start | bytes 1572872 | tf_op jit(solution)/shard_map/ppermute | solution.py:770
  321.2 14.6 %collective-permute-start.20 = (f32[8,256,128]{2,1,0:T(8,128)}, f32[8,256,128]{2,1,0:T(8,128)S(1)}, u32[]{:S(2)}, u32[]{:S(2)}) collective-permute-start(f32[8,256,128]{2,1,0:T(8,128)} %collective-permute-done.19), channel_id=1, source_target_pairs={{0,1},{1,0},{2,3},{3,2},{4,5},{5,4},{6,7},{7,6},{8,9},{9,8},{10,11... | collective-permute-start | bytes 3145736 | tf_op jit(solution)/shard_map/ppermute | solution.py:770
  322.0 13.8 %collective-permute-start.21 = (f32[8,128,128]{2,1,0:T(8,128)S(1)}, f32[8,128,128]{2,1,0:T(8,128)}, u32[]{:S(2)}, u32[]{:S(2)}) collective-permute-start(f32[8,128,128]{2,1,0:T(8,128)S(1)} %all-to-all-done.6), channel_id=1, source_target_pairs={{0,1},{1,0},{2,3},{3,2},{4,5},{5,4},{6,7},{7,6},{8,9},{9,8},{10,11... | collective-permute-start | bytes 1572872 | tf_op jit(solution)/shard_map/ppermute | solution.py:770
  332.3 2.9 copy-start.13
  332.3 3.6 collective-permute-start.23
  335.8 1.0 copy-start.6
